TPU v7x, 32 devices: a whole 2x2x4 slice. The times are simulated.
32 devices in a mesh: ctx: 16 (over z, y, core), tp: 2 (over x).
Axes of the slice: x: 2, y: 2, z: 4, core: 2. Of those that a mesh axis runs over, the one named last changes fastest.
Arguments:
- queries: bfloat16 [2048, 8192], P('ctx', 'tp'), may hold values from -8 to 8
- keys: bfloat16 [2048, 1024], P('ctx', 'tp'), may hold values from -4 to 4
- values: bfloat16 [2048, 1024], P('ctx', 'tp'), may hold values from -4 to 4
- attn_out: bfloat16 [2048, 8192], P('ctx', 'tp'), may hold values from -4 to 4, as said below
- out_grad: bfloat16 [2048, 8192], P(('ctx', 'tp')), may hold values from -24 to 24
- logsumexp: float32 [64, 2048], P('tp', 'ctx'), may hold values from -50 to 50, as said below
- position_ids: int32 [3, 2048], P(None, 'ctx'), may hold values from 0 to 2047, as said below
- block_map: int32 [32], replicated, may hold values from 0 to 31, as said below
- span_blocks: int32 [4, 2], replicated, may hold values from 0 to 31, as said below
Outputs:
- grad_q: bfloat16 [2048, 8192], P('ctx', 'tp')
- key_gradient: bfloat16 [2048, 1024], P('ctx', 'tp')
- value_gradient: bfloat16 [2048, 1024], P('ctx', 'tp')
Inputs may be any that keep to these rules, and one draw needn't show every extreme that they name: `block_map`: a permutation of the sequence blocks. `span_blocks`: spans ascend in sequence order and do not intersect; each row is a start block and an end block past the span's last; the first span starts at block 0 and the last ends at block 31. `position_ids`: given inputs, not renumbered after spans: text rows carry their sequence position in all three ids; a row of a visual span carries the span's first position plus its frame, grid row and grid column. `attn_out`: the output of the forward pass for these queries, keys and values. `logsumexp`: the log of each row's softmax total over its allowed keys, from the forward pass.
All inputs are finite; a program needn't handle non-finite values.
Results may differ from a plain program's by a relative error of at most 0.011.
Values may be sent and summed in bfloat16 or wider, within the bound.
No kernel may reach another device: no remote copies, remote signals or barrier semaphores. Data moves between devices by JAX's collectives and lax.ppermute only.
A program may use at most 64 MiB of HBM per device.

v0:
```python
import math

import jax
import jax.numpy as jnp
from jax import lax
from jax.sharding import PartitionSpec as P

HEAD_SIZE = 128
BLOCKS_DEV = 2


THETA = 1000000.0


def passed_along(block, axis, distance):
    devices = range(lax.axis_size(axis))
    route = [((i - distance) % len(devices), i) for i in devices]
    return lax.ppermute(block, axis, route)


def rope_tables(position_ids, width):
    half_width = width // 2
    pair_index = jnp.arange(half_width, dtype=jnp.int32)
    first_cut = width // 8
    second_cut = first_cut + 3 * width // 16
    inverse = jnp.exp(pair_index.astype(jnp.float32) * jnp.float32(-2.0 * math.log(THETA) / width))
    picked = jnp.where(
        pair_index[None, :] < first_cut,
        position_ids[0][:, None],
        jnp.where(
            pair_index[None, :] < second_cut, position_ids[1][:, None], position_ids[2][:, None]
        ),
    )
    angles = picked.astype(jnp.float32) * inverse[None, :]
    cosine_table = jnp.concatenate([jnp.cos(angles), jnp.cos(angles)], axis=-1)
    sine_lookup = jnp.concatenate([jnp.sin(angles), jnp.sin(angles)], axis=-1)
    return (cosine_table, sine_lookup)


def apply_rotation(field, cosine_table, sine_lookup):
    half_width = field.shape[-1] // 2
    turned = jnp.concatenate([-field[..., half_width:], field[..., :half_width]], axis=-1)
    return field * cosine_table[:, None, :] + turned * sine_lookup[:, None, :]


def reverse_rotation(field, cosine_table, sine_lookup):
    half_width = field.shape[-1] // 2
    scaled = field * sine_lookup[:, None, :]
    turned = jnp.concatenate([scaled[..., half_width:], -scaled[..., :half_width]], axis=-1)
    return field * cosine_table[:, None, :] + turned


def heads_first(field, kv_heads, query_group_width):
    row_count = field.shape[0]
    return field.reshape(row_count, kv_heads, query_group_width, HEAD_SIZE).transpose(1, 2, 0, 3)


def shards(
    queries, keys, values, attn_out, out_grad, logsumexp, position_ids, block_map, span_blocks
):
    row_count = queries.shape[0]
    kv_heads = keys.shape[1] // HEAD_SIZE
    q_heads = queries.shape[1] // HEAD_SIZE
    query_group_width = q_heads // kv_heads
    block_len = row_count // BLOCKS_DEV
    score_scale = 1.0 / math.sqrt(HEAD_SIZE)
    cycle_size = lax.axis_size("ctx")
    own_index = lax.axis_index("ctx")
    grad_heads = lax.all_to_all(out_grad, "tp", split_axis=1, concat_axis=0, tiled=True)
    cosine_table, sine_lookup = rope_tables(position_ids, HEAD_SIZE)
    q_flat = apply_rotation(
        queries.astype(jnp.float32).reshape(row_count, q_heads, HEAD_SIZE),
        cosine_table,
        sine_lookup,
    ).astype(jnp.bfloat16)
    q_rot = heads_first(q_flat.reshape(row_count, q_heads * HEAD_SIZE), kv_heads, query_group_width)
    rotated_keys = apply_rotation(
        keys.astype(jnp.float32).reshape(row_count, kv_heads, HEAD_SIZE), cosine_table, sine_lookup
    ).astype(jnp.bfloat16)
    value_heads = values.reshape(row_count, kv_heads, HEAD_SIZE).transpose(1, 0, 2)
    d_heads = heads_first(grad_heads, kv_heads, query_group_width)
    delta_rows = jnp.sum(
        grad_heads.astype(jnp.float32).reshape(row_count, q_heads, HEAD_SIZE)
        * attn_out.astype(jnp.float32).reshape(row_count, q_heads, HEAD_SIZE),
        axis=-1,
    )
    delta_rows = delta_rows.T.reshape(kv_heads, query_group_width, row_count)
    lse_rows = logsumexp.reshape(kv_heads, query_group_width, row_count)
    kv_pair = jnp.stack([rotated_keys.transpose(1, 0, 2), value_heads])
    every_block = jnp.arange(block_map.shape[0], dtype=jnp.int32)
    inside = (every_block[:, None] >= span_blocks[None, :, 0]) & (
        every_block[:, None] < span_blocks[None, :, 1]
    )
    numbers = jnp.arange(span_blocks.shape[0], dtype=jnp.int32)[None, :] + 1
    block_span = jnp.sum(jnp.where(inside, numbers, 0), axis=1) - 1

    def token_info(owner):
        seq_blocks = lax.dynamic_slice_in_dim(block_map, owner * BLOCKS_DEV, BLOCKS_DEV)
        matched = seq_blocks[:, None] == every_block[None, :]
        spans_of = jnp.sum(jnp.where(matched, block_span[None, :], 0), axis=1)
        positions = (
            seq_blocks[:, None] * block_len + jnp.arange(block_len, dtype=jnp.int32)[None, :]
        ).reshape(row_count)
        row_spans = jnp.repeat(spans_of, block_len)
        return (seq_blocks, spans_of, positions, row_spans)

    mine = token_info(own_index)

    def visit_block(dq_total, grads_total, pair_now, owner):
        my_blocks, my_spans, my_pos, my_row_spans = mine
        their_blocks, their_spans, their_pos, their_row_spans = token_info(owner)
        block_shared = (my_spans[:, None] == their_spans[None, :]) & (my_spans[:, None] >= 0)
        is_live = jnp.any((their_blocks[None, :] <= my_blocks[:, None]) | block_shared)
        k_part = pair_now[0]
        v_part = pair_now[1]

        def compute(unused):
            shared = (my_row_spans[:, None] == their_row_spans[None, :]) & (
                my_row_spans[:, None] >= 0
            )
            allowed = (their_pos[None, :] <= my_pos[:, None]) | shared
            scores = (
                jnp.einsum("kgqd,kcd->kgqc", q_rot, k_part, preferred_element_type=jnp.float32)
                * score_scale
            )
            attn_probs = jnp.exp(jnp.where(allowed, scores - lse_rows[..., None], -jnp.inf))
            value_grad = jnp.einsum(
                "kgqc,kgqd->kcd",
                attn_probs.astype(jnp.bfloat16),
                d_heads,
                preferred_element_type=jnp.float32,
            )
            grad_p = jnp.einsum(
                "kgqd,kcd->kgqc", d_heads, v_part, preferred_element_type=jnp.float32
            )
            grad_s = (attn_probs * (grad_p - delta_rows[..., None])).astype(jnp.bfloat16)
            query_grad = jnp.einsum(
                "kgqc,kcd->kgqd", grad_s, k_part, preferred_element_type=jnp.float32
            )
            key_grad = jnp.einsum(
                "kgqc,kgqd->kcd", grad_s, q_rot, preferred_element_type=jnp.float32
            )
            return (dq_total + query_grad, grads_total + jnp.stack([key_grad, value_grad]))

        def nothing(unused):
            return (dq_total, grads_total)

        return lax.cond(is_live, compute, nothing, 0)

    zero_q = jnp.zeros((kv_heads, query_group_width, row_count, HEAD_SIZE), jnp.float32)
    zero_kv = jnp.zeros((2, kv_heads, row_count, HEAD_SIZE), jnp.float32)
    dq_total, local_grads = visit_block(zero_q, zero_kv, kv_pair, own_index)

    def advance(offset, loop_state):
        pair_now, grads_now, dq_now = loop_state
        pair_now = passed_along(pair_now, "ctx", 1)
        grads_now = passed_along(grads_now, "ctx", 1)
        dq_now, grads_now = visit_block(
            dq_now, grads_now, pair_now, (own_index - offset) % cycle_size
        )
        return (pair_now, grads_now, dq_now)

    pair_end, grads_end, dq_total = lax.fori_loop(
        1, cycle_size, advance, (kv_pair, local_grads, dq_total)
    )
    grads_total = passed_along(grads_end, "ctx", 1)
    dq_rot = (dq_total * score_scale).transpose(2, 0, 1, 3).reshape(row_count, q_heads, HEAD_SIZE)
    grad_q = (
        reverse_rotation(dq_rot, cosine_table, sine_lookup)
        .astype(jnp.bfloat16)
        .reshape(row_count, q_heads * HEAD_SIZE)
    )
    rotated_key_gradient = (grads_total[0] * score_scale).transpose(1, 0, 2)
    key_gradient = (
        reverse_rotation(rotated_key_gradient, cosine_table, sine_lookup)
        .astype(jnp.bfloat16)
        .reshape(row_count, kv_heads * HEAD_SIZE)
    )
    value_gradient = (
        grads_total[1]
        .transpose(1, 0, 2)
        .astype(jnp.bfloat16)
        .reshape(row_count, kv_heads * HEAD_SIZE)
    )
    return (grad_q, key_gradient, value_gradient)


def solution(mesh):
    return jax.shard_map(
        shards,
        mesh=mesh,
        in_specs=(
            P("ctx", "tp"),
            P("ctx", "tp"),
            P("ctx", "tp"),
            P("ctx", "tp"),
            P(("ctx", "tp"), None),
            P("tp", "ctx"),
            P(None, "ctx"),
            P(),
            P(),
        ),
        out_specs=(P("ctx", "tp"), P("ctx", "tp"), P("ctx", "tp")),
        check_vma=False,
    )
```

profile of v0, /device:TPU:0, one launch (start us, length us, event | category | flops | bytes accessed | tf_op | source)
XLA Modules:
  0.0 440.7 jit_solution(2682618504753706451)
XLA Ops:
  0.7 2.3 copy.132
  3.0 4.3 all-to-all-start
  30.1 2.9 fusion.24
  33.0 2.3 copy.84
  39.8 10.9 %conditional.2 = (f32[4,8,128,128]{3,2,1,0:T(8,128)S(1)}, f32[2,4,128,128]{3,2,1,0:T(8,128)}) conditional(s32[]{:T(128)} %convert_element_type.73, () %tuple.50, (s32[2]{0:T(128)}, s32[2]{0:T(128)}, bf16[4,8,128,128]{2,3,1,0:T(8,128)(2,1)}, bf16[4,128,128]{1,2,0:T(8,128)(2,1)S(1)}, f32[32,128]{1,0:T(8,128)}, ...), branch_computations={%region_4.5_spmd, %region_5.6_spmd} | conditional | flops 674955520 | bytes 30381400 | solution.py:148
  41.5 3.5 select_exponential_fusion
  45.0 2.1 multiply_convert_fusion
  50.7 376.8 %while.21 = (s32[]{:T(128)}, bf16[2,4,128,128]{3,2,1,0:T(8,128)(2,1)}, f32[2,4,128,128]{3,2,1,0:T(8,128)}, f32[4,8,128,128]{3,2,1,0:T(8,128)S(1)}, s32[]{:T(128)...) while((s32[]{:T(128)}, ...), condition=%wide.region_11.12_spmd.clone.clone, body=%wide.region_6.11_spmd.clone.clone.sunk | while | flops 675611264 | bytes 29305948 | solution.py:163
  50.8 2.5 collective-permute-start
  57.4 8.0 %collective-permute-done = bf16[2,4,128,128]{3,2,1,0:T(8,128)(2,1)S(1)} collective-permute-done((bf16[2,4,128,128]{3,2,1,0:T(8,128)(2,1)}, bf16[2,4,128,128]{3,2,1,0:T(8,128)(2,1)S(1)}, u32[]{:S(2)}, u32[]{:S(2)}) %collective-permute-start) | collective-permute-done | bytes 262176 | tf_op jit(solution)/shard_map/while/body/eval_jaxpr/ppermute | solution.py:18
  66.2 8.5 %conditional.6 = ((f32[4,8,128,128]{3,2,1,0:T(8,128)S(1)}, f32[2,4,128,128]{3,2,1,0:T(8,128)})) conditional(s32[]{:T(128)} %convert_element_type.112, (f32[4,8,128,128]{3,2,1,0:T(8,128)S(1)}, f32[2,4,128,128]{3,2,1,0:T(8,128)}) %tuple.91, (s32[2]{0:T(128)S(1)}, s32[2,64]{1,0:T(2,128)S(1)}, s32[2]{0:T(128)}, s32[2]{0:T(128)}, s32[2]{0:T(128)S(1)}, ...), branch_computations={%region_9.9_spmd, %region_10.10_spmd} | conditional | flops 675611008 | bytes 24586084 | solution.py:148
  72.3 1.9 maximum_add_fusion
  80.8 10.1 %collective-permute-done = bf16[2,4,128,128]{3,2,1,0:T(8,128)(2,1)S(1)} collective-permute-done((bf16[2,4,128,128]{3,2,1,0:T(8,128)(2,1)}, bf16[2,4,128,128]{3,2,1,0:T(8,128)(2,1)S(1)}, u32[]{:S(2)}, u32[]{:S(2)}) %collective-permute-start) | collective-permute-done | bytes 262176 | tf_op jit(solution)/shard_map/while/body/eval_jaxpr/ppermute | solution.py:18
  91.6 8.5 %conditional.6 = ((f32[4,8,128,128]{3,2,1,0:T(8,128)S(1)}, f32[2,4,128,128]{3,2,1,0:T(8,128)})) conditional(s32[]{:T(128)} %convert_element_type.112, (f32[4,8,128,128]{3,2,1,0:T(8,128)S(1)}, f32[2,4,128,128]{3,2,1,0:T(8,128)}) %tuple.91, (s32[2]{0:T(128)S(1)}, s32[2,64]{1,0:T(2,128)S(1)}, s32[2]{0:T(128)}, s32[2]{0:T(128)}, s32[2]{0:T(128)S(1)}, ...), branch_computations={%region_9.9_spmd, %region_10.10_spmd} | conditional | flops 675611008 | bytes 24586084 | solution.py:148
  97.7 1.9 maximum_add_fusion
  106.2 10.1 %collective-permute-done = bf16[2,4,128,128]{3,2,1,0:T(8,128)(2,1)S(1)} collective-permute-done((bf16[2,4,128,128]{3,2,1,0:T(8,128)(2,1)}, bf16[2,4,128,128]{3,2,1,0:T(8,128)(2,1)S(1)}, u32[]{:S(2)}, u32[]{:S(2)}) %collective-permute-start) | collective-permute-done | bytes 262176 | tf_op jit(solution)/shard_map/while/body/eval_jaxpr/ppermute | solution.py:18
  117.1 8.5 %conditional.6 = ((f32[4,8,128,128]{3,2,1,0:T(8,128)S(1)}, f32[2,4,128,128]{3,2,1,0:T(8,128)})) conditional(s32[]{:T(128)} %convert_element_type.112, (f32[4,8,128,128]{3,2,1,0:T(8,128)S(1)}, f32[2,4,128,128]{3,2,1,0:T(8,128)}) %tuple.91, (s32[2]{0:T(128)S(1)}, s32[2,64]{1,0:T(2,128)S(1)}, s32[2]{0:T(128)}, s32[2]{0:T(128)}, s32[2]{0:T(128)S(1)}, ...), branch_computations={%region_9.9_spmd, %region_10.10_spmd} | conditional | flops 675611008 | bytes 24586084 | solution.py:148
  123.1 1.9 maximum_add_fusion
  131.6 10.1 %collective-permute-done = bf16[2,4,128,128]{3,2,1,0:T(8,128)(2,1)S(1)} collective-permute-done((bf16[2,4,128,128]{3,2,1,0:T(8,128)(2,1)}, bf16[2,4,128,128]{3,2,1,0:T(8,128)(2,1)S(1)}, u32[]{:S(2)}, u32[]{:S(2)}) %collective-permute-start) | collective-permute-done | bytes 262176 | tf_op jit(solution)/shard_map/while/body/eval_jaxpr/ppermute | solution.py:18
  142.5 8.5 %conditional.6 = ((f32[4,8,128,128]{3,2,1,0:T(8,128)S(1)}, f32[2,4,128,128]{3,2,1,0:T(8,128)})) conditional(s32[]{:T(128)} %convert_element_type.112, (f32[4,8,128,128]{3,2,1,0:T(8,128)S(1)}, f32[2,4,128,128]{3,2,1,0:T(8,128)}) %tuple.91, (s32[2]{0:T(128)S(1)}, s32[2,64]{1,0:T(2,128)S(1)}, s32[2]{0:T(128)}, s32[2]{0:T(128)}, s32[2]{0:T(128)S(1)}, ...), branch_computations={%region_9.9_spmd, %region_10.10_spmd} | conditional | flops 675611008 | bytes 24586084 | solution.py:148
  148.5 1.9 maximum_add_fusion
  157.1 10.1 %collective-permute-done = bf16[2,4,128,128]{3,2,1,0:T(8,128)(2,1)S(1)} collective-permute-done((bf16[2,4,128,128]{3,2,1,0:T(8,128)(2,1)}, bf16[2,4,128,128]{3,2,1,0:T(8,128)(2,1)S(1)}, u32[]{:S(2)}, u32[]{:S(2)}) %collective-permute-start) | collective-permute-done | bytes 262176 | tf_op jit(solution)/shard_map/while/body/eval_jaxpr/ppermute | solution.py:18
  167.9 8.5 %conditional.6 = ((f32[4,8,128,128]{3,2,1,0:T(8,128)S(1)}, f32[2,4,128,128]{3,2,1,0:T(8,128)})) conditional(s32[]{:T(128)} %convert_element_type.112, (f32[4,8,128,128]{3,2,1,0:T(8,128)S(1)}, f32[2,4,128,128]{3,2,1,0:T(8,128)}) %tuple.91, (s32[2]{0:T(128)S(1)}, s32[2,64]{1,0:T(2,128)S(1)}, s32[2]{0:T(128)}, s32[2]{0:T(128)}, s32[2]{0:T(128)S(1)}, ...), branch_computations={%region_9.9_spmd, %region_10.10_spmd} | conditional | flops 675611008 | bytes 24586084 | solution.py:148
  174.0 1.9 maximum_add_fusion
  182.5 10.1 %collective-permute-done = bf16[2,4,128,128]{3,2,1,0:T(8,128)(2,1)S(1)} collective-permute-done((bf16[2,4,128,128]{3,2,1,0:T(8,128)(2,1)}, bf16[2,4,128,128]{3,2,1,0:T(8,128)(2,1)S(1)}, u32[]{:S(2)}, u32[]{:S(2)}) %collective-permute-start) | collective-permute-done | bytes 262176 | tf_op jit(solution)/shard_map/while/body/eval_jaxpr/ppermute | solution.py:18
  193.4 8.5 %conditional.6 = ((f32[4,8,128,128]{3,2,1,0:T(8,128)S(1)}, f32[2,4,128,128]{3,2,1,0:T(8,128)})) conditional(s32[]{:T(128)} %convert_element_type.112, (f32[4,8,128,128]{3,2,1,0:T(8,128)S(1)}, f32[2,4,128,128]{3,2,1,0:T(8,128)}) %tuple.91, (s32[2]{0:T(128)S(1)}, s32[2,64]{1,0:T(2,128)S(1)}, s32[2]{0:T(128)}, s32[2]{0:T(128)}, s32[2]{0:T(128)S(1)}, ...), branch_computations={%region_9.9_spmd, %region_10.10_spmd} | conditional | flops 675611008 | bytes 24586084 | solution.py:148
  199.4 1.9 maximum_add_fusion
  207.9 10.1 %collective-permute-done = bf16[2,4,128,128]{3,2,1,0:T(8,128)(2,1)S(1)} collective-permute-done((bf16[2,4,128,128]{3,2,1,0:T(8,128)(2,1)}, bf16[2,4,128,128]{3,2,1,0:T(8,128)(2,1)S(1)}, u32[]{:S(2)}, u32[]{:S(2)}) %collective-permute-start) | collective-permute-done | bytes 262176 | tf_op jit(solution)/shard_map/while/body/eval_jaxpr/ppermute | solution.py:18
  218.8 8.5 %conditional.6 = ((f32[4,8,128,128]{3,2,1,0:T(8,128)S(1)}, f32[2,4,128,128]{3,2,1,0:T(8,128)})) conditional(s32[]{:T(128)} %convert_element_type.112, (f32[4,8,128,128]{3,2,1,0:T(8,128)S(1)}, f32[2,4,128,128]{3,2,1,0:T(8,128)}) %tuple.91, (s32[2]{0:T(128)S(1)}, s32[2,64]{1,0:T(2,128)S(1)}, s32[2]{0:T(128)}, s32[2]{0:T(128)}, s32[2]{0:T(128)S(1)}, ...), branch_computations={%region_9.9_spmd, %region_10.10_spmd} | conditional | flops 675611008 | bytes 24586084 | solution.py:148
  224.8 1.9 maximum_add_fusion
  233.4 10.1 %collective-permute-done = bf16[2,4,128,128]{3,2,1,0:T(8,128)(2,1)S(1)} collective-permute-done((bf16[2,4,128,128]{3,2,1,0:T(8,128)(2,1)}, bf16[2,4,128,128]{3,2,1,0:T(8,128)(2,1)S(1)}, u32[]{:S(2)}, u32[]{:S(2)}) %collective-permute-start) | collective-permute-done | bytes 262176 | tf_op jit(solution)/shard_map/while/body/eval_jaxpr/ppermute | solution.py:18
  244.2 8.5 %conditional.6 = ((f32[4,8,128,128]{3,2,1,0:T(8,128)S(1)}, f32[2,4,128,128]{3,2,1,0:T(8,128)})) conditional(s32[]{:T(128)} %convert_element_type.112, (f32[4,8,128,128]{3,2,1,0:T(8,128)S(1)}, f32[2,4,128,128]{3,2,1,0:T(8,128)}) %tuple.91, (s32[2]{0:T(128)S(1)}, s32[2,64]{1,0:T(2,128)S(1)}, s32[2]{0:T(128)}, s32[2]{0:T(128)}, s32[2]{0:T(128)S(1)}, ...), branch_computations={%region_9.9_spmd, %region_10.10_spmd} | conditional | flops 675611008 | bytes 24586084 | solution.py:148
  250.3 1.9 maximum_add_fusion
  258.8 10.1 %collective-permute-done = bf16[2,4,128,128]{3,2,1,0:T(8,128)(2,1)S(1)} collective-permute-done((bf16[2,4,128,128]{3,2,1,0:T(8,128)(2,1)}, bf16[2,4,128,128]{3,2,1,0:T(8,128)(2,1)S(1)}, u32[]{:S(2)}, u32[]{:S(2)}) %collective-permute-start) | collective-permute-done | bytes 262176 | tf_op jit(solution)/shard_map/while/body/eval_jaxpr/ppermute | solution.py:18
  269.6 8.5 %conditional.6 = ((f32[4,8,128,128]{3,2,1,0:T(8,128)S(1)}, f32[2,4,128,128]{3,2,1,0:T(8,128)})) conditional(s32[]{:T(128)} %convert_element_type.112, (f32[4,8,128,128]{3,2,1,0:T(8,128)S(1)}, f32[2,4,128,128]{3,2,1,0:T(8,128)}) %tuple.91, (s32[2]{0:T(128)S(1)}, s32[2,64]{1,0:T(2,128)S(1)}, s32[2]{0:T(128)}, s32[2]{0:T(128)}, s32[2]{0:T(128)S(1)}, ...), branch_computations={%region_9.9_spmd, %region_10.10_spmd} | conditional | flops 675611008 | bytes 24586084 | solution.py:148
  284.2 10.1 %collective-permute-done = bf16[2,4,128,128]{3,2,1,0:T(8,128)(2,1)S(1)} collective-permute-done((bf16[2,4,128,128]{3,2,1,0:T(8,128)(2,1)}, bf16[2,4,128,128]{3,2,1,0:T(8,128)(2,1)S(1)}, u32[]{:S(2)}, u32[]{:S(2)}) %collective-permute-start) | collective-permute-done | bytes 262176 | tf_op jit(solution)/shard_map/while/body/eval_jaxpr/ppermute | solution.py:18
  295.1 8.5 %conditional.6 = ((f32[4,8,128,128]{3,2,1,0:T(8,128)S(1)}, f32[2,4,128,128]{3,2,1,0:T(8,128)})) conditional(s32[]{:T(128)} %convert_element_type.112, (f32[4,8,128,128]{3,2,1,0:T(8,128)S(1)}, f32[2,4,128,128]{3,2,1,0:T(8,128)}) %tuple.91, (s32[2]{0:T(128)S(1)}, s32[2,64]{1,0:T(2,128)S(1)}, s32[2]{0:T(128)}, s32[2]{0:T(128)}, s32[2]{0:T(128)S(1)}, ...), branch_computations={%region_9.9_spmd, %region_10.10_spmd} | conditional | flops 675611008 | bytes 24586084 | solution.py:148
  309.7 10.1 %collective-permute-done = bf16[2,4,128,128]{3,2,1,0:T(8,128)(2,1)S(1)} collective-permute-done((bf16[2,4,128,128]{3,2,1,0:T(8,128)(2,1)}, bf16[2,4,128,128]{3,2,1,0:T(8,128)(2,1)S(1)}, u32[]{:S(2)}, u32[]{:S(2)}) %collective-permute-start) | collective-permute-done | bytes 262176 | tf_op jit(solution)/shard_map/while/body/eval_jaxpr/ppermute | solution.py:18
  326.6 13.5 %collective-permute-done = bf16[2,4,128,128]{3,2,1,0:T(8,128)(2,1)S(1)} collective-permute-done((bf16[2,4,128,128]{3,2,1,0:T(8,128)(2,1)}, bf16[2,4,128,128]{3,2,1,0:T(8,128)(2,1)S(1)}, u32[]{:S(2)}, u32[]{:S(2)}) %collective-permute-start) | collective-permute-done | bytes 262176 | tf_op jit(solution)/shard_map/while/body/eval_jaxpr/ppermute | solution.py:18
  340.9 8.5 %conditional.6 = ((f32[4,8,128,128]{3,2,1,0:T(8,128)S(1)}, f32[2,4,128,128]{3,2,1,0:T(8,128)})) conditional(s32[]{:T(128)} %convert_element_type.112, (f32[4,8,128,128]{3,2,1,0:T(8,128)S(1)}, f32[2,4,128,128]{3,2,1,0:T(8,128)}) %tuple.91, (s32[2]{0:T(128)S(1)}, s32[2,64]{1,0:T(2,128)S(1)}, s32[2]{0:T(128)}, s32[2]{0:T(128)}, s32[2]{0:T(128)S(1)}, ...), branch_computations={%region_9.9_spmd, %region_10.10_spmd} | conditional | flops 675611008 | bytes 24586084 | solution.py:148
  355.4 10.1 %collective-permute-done = bf16[2,4,128,128]{3,2,1,0:T(8,128)(2,1)S(1)} collective-permute-done((bf16[2,4,128,128]{3,2,1,0:T(8,128)(2,1)}, bf16[2,4,128,128]{3,2,1,0:T(8,128)(2,1)S(1)}, u32[]{:S(2)}, u32[]{:S(2)}) %collective-permute-start) | collective-permute-done | bytes 262176 | tf_op jit(solution)/shard_map/while/body/eval_jaxpr/ppermute | solution.py:18
  366.3 8.5 %conditional.6 = ((f32[4,8,128,128]{3,2,1,0:T(8,128)S(1)}, f32[2,4,128,128]{3,2,1,0:T(8,128)})) conditional(s32[]{:T(128)} %convert_element_type.112, (f32[4,8,128,128]{3,2,1,0:T(8,128)S(1)}, f32[2,4,128,128]{3,2,1,0:T(8,128)}) %tuple.91, (s32[2]{0:T(128)S(1)}, s32[2,64]{1,0:T(2,128)S(1)}, s32[2]{0:T(128)}, s32[2]{0:T(128)}, s32[2]{0:T(128)S(1)}, ...), branch_computations={%region_9.9_spmd, %region_10.10_spmd} | conditional | flops 675611008 | bytes 24586084 | solution.py:148
  380.9 10.1 %collective-permute-done = bf16[2,4,128,128]{3,2,1,0:T(8,128)(2,1)S(1)} collective-permute-done((bf16[2,4,128,128]{3,2,1,0:T(8,128)(2,1)}, bf16[2,4,128,128]{3,2,1,0:T(8,128)(2,1)S(1)}, u32[]{:S(2)}, u32[]{:S(2)}) %collective-permute-start) | collective-permute-done | bytes 262176 | tf_op jit(solution)/shard_map/while/body/eval_jaxpr/ppermute | solution.py:18
  391.7 8.5 %conditional.6 = ((f32[4,8,128,128]{3,2,1,0:T(8,128)S(1)}, f32[2,4,128,128]{3,2,1,0:T(8,128)})) conditional(s32[]{:T(128)} %convert_element_type.112, (f32[4,8,128,128]{3,2,1,0:T(8,128)S(1)}, f32[2,4,128,128]{3,2,1,0:T(8,128)}) %tuple.91, (s32[2]{0:T(128)S(1)}, s32[2,64]{1,0:T(2,128)S(1)}, s32[2]{0:T(128)}, s32[2]{0:T(128)}, s32[2]{0:T(128)S(1)}, ...), branch_computations={%region_9.9_spmd, %region_10.10_spmd} | conditional | flops 675611008 | bytes 24586084 | solution.py:148
  406.3 10.1 %collective-permute-done = bf16[2,4,128,128]{3,2,1,0:T(8,128)(2,1)S(1)} collective-permute-done((bf16[2,4,128,128]{3,2,1,0:T(8,128)(2,1)}, bf16[2,4,128,128]{3,2,1,0:T(8,128)(2,1)S(1)}, u32[]{:S(2)}, u32[]{:S(2)}) %collective-permute-start) | collective-permute-done | bytes 262176 | tf_op jit(solution)/shard_map/while/body/eval_jaxpr/ppermute | solution.py:18
  417.1 8.5 %conditional.6 = ((f32[4,8,128,128]{3,2,1,0:T(8,128)S(1)}, f32[2,4,128,128]{3,2,1,0:T(8,128)})) conditional(s32[]{:T(128)} %convert_element_type.112, (f32[4,8,128,128]{3,2,1,0:T(8,128)S(1)}, f32[2,4,128,128]{3,2,1,0:T(8,128)}) %tuple.91, (s32[2]{0:T(128)S(1)}, s32[2,64]{1,0:T(2,128)S(1)}, s32[2]{0:T(128)}, s32[2]{0:T(128)}, s32[2]{0:T(128)S(1)}, ...), branch_computations={%region_9.9_spmd, %region_10.10_spmd} | conditional | flops 675611008 | bytes 24586084 | solution.py:148
  432.5 4.3 fusion.21
  436.8 2.2 collective-permute-done.2
  (482 shorter events, 233.5 us)
Async XLA Ops:
  0.6 7.8 %copy-start.10 = (bf16[128,512]{1,0:T(8,128)(2,1)S(1)}, bf16[128,512]{1,0:T(8,128)(2,1)}, u32[]{:S(2)}) copy-start(bf16[128,512]{1,0:T(8,128)(2,1)} %param.16) | copy-start | bytes 393220
  0.6 7.9 %copy-start.13 = (s32[3,128]{1,0:T(4,128)S(1)}, s32[3,128]{1,0:T(4,128)}, u32[]{:S(2)}) copy-start(s32[3,128]{1,0:T(4,128)} %param.21) | copy-start | bytes 4612
  3.0 6.3 %copy-start.6 = (bf16[128,4096]{1,0:T(8,128)(2,1)S(1)}, bf16[128,4096]{1,0:T(8,128)(2,1)}, u32[]{:S(2)}) copy-start(bf16[128,4096]{1,0:T(8,128)(2,1)} %param.15) | copy-start | bytes 3145732
  3.0 33.1 %all-to-all-start = ((bf16[64,2,4096]{2,0,1:T(8,128)(2,1)}), bf16[64,2,4096]{2,0,1:T(8,128)(2,1)S(1)}, u32[]{:S(2)}, u32[]{:S(2)}) async-start(bf16[64,2,4096]{2,0,1:T(8,128)(2,1)} %bitcast.149), calls=%async_computation | async-start | bytes 2097152 | tf_op jit(solution)/shard_map/all_to_all | solution.py:69
  11.9 1.5 copy-start.14
  15.5 1.7 copy-start.11
  19.3 4.9 %copy-start.12 = (s32[2]{0:T(128)}, s32[2]{0:T(128)S(1)}, u32[]{:S(2)}) copy-start(s32[2]{0:T(128)S(1)} %get-tuple-element.800) | copy-start | bytes 28
  33.0 2.3 copy-start.4
  36.6 1.6 copy-start.2
  45.0 2.2 copy-start.1
  47.2 1.6 copy-start.3
  50.7 15.5 %collective-permute-start.1 = (f32[2,4,128,128]{3,2,1,0:T(8,128)}, f32[2,4,128,128]{3,2,1,0:T(8,128)}, u32[]{:S(2)}, u32[]{:S(2)}) collective-permute-start(f32[2,4,128,128]{3,2,1,0:T(8,128)} %get-tuple-element.816), channel_id=1, source_target_pairs={{30,0},{0,2},{2,4},{4,6},{6,8},{8,10},{10,12},{12,14},{14,16},{16,... | collective-permute-start | bytes 1572872 | tf_op jit(solution)/shard_map/while/body/eval_jaxpr/ppermute | solution.py:18
  50.8 14.7 %collective-permute-start = (bf16[2,4,128,128]{3,2,1,0:T(8,128)(2,1)}, bf16[2,4,128,128]{3,2,1,0:T(8,128)(2,1)S(1)}, u32[]{:S(2)}, u32[]{:S(2)}) collective-permute-start(bf16[2,4,128,128]{3,2,1,0:T(8,128)(2,1)} %get-tuple-element.815), channel_id=1, source_target_pairs={{30,0},{0,2},{2,4},{4,6},{6,8},{8,10},{10,12},{12,14},{14,16},{16,... | collective-permute-start | bytes 786440 | tf_op jit(solution)/shard_map/while/body/eval_jaxpr/ppermute | solution.py:18
  70.0 1.2 copy-start
  76.6 15.1 %collective-permute-start.1 = (f32[2,4,128,128]{3,2,1,0:T(8,128)}, f32[2,4,128,128]{3,2,1,0:T(8,128)}, u32[]{:S(2)}, u32[]{:S(2)}) collective-permute-start(f32[2,4,128,128]{3,2,1,0:T(8,128)} %get-tuple-element.816), channel_id=1, source_target_pairs={{30,0},{0,2},{2,4},{4,6},{6,8},{8,10},{10,12},{12,14},{14,16},{16,... | collective-permute-start | bytes 1572872 | tf_op jit(solution)/shard_map/while/body/eval_jaxpr/ppermute | solution.py:18
  76.6 14.3 %collective-permute-start = (bf16[2,4,128,128]{3,2,1,0:T(8,128)(2,1)}, bf16[2,4,128,128]{3,2,1,0:T(8,128)(2,1)S(1)}, u32[]{:S(2)}, u32[]{:S(2)}) collective-permute-start(bf16[2,4,128,128]{3,2,1,0:T(8,128)(2,1)} %get-tuple-element.815), channel_id=1, source_target_pairs={{30,0},{0,2},{2,4},{4,6},{6,8},{8,10},{10,12},{12,14},{14,16},{16,... | collective-permute-start | bytes 786440 | tf_op jit(solution)/shard_map/while/body/eval_jaxpr/ppermute | solution.py:18
  95.5 1.2 copy-start
  102.0 15.1 %collective-permute-start.1 = (f32[2,4,128,128]{3,2,1,0:T(8,128)}, f32[2,4,128,128]{3,2,1,0:T(8,128)}, u32[]{:S(2)}, u32[]{:S(2)}) collective-permute-start(f32[2,4,128,128]{3,2,1,0:T(8,128)} %get-tuple-element.816), channel_id=1, source_target_pairs={{30,0},{0,2},{2,4},{4,6},{6,8},{8,10},{10,12},{12,14},{14,16},{16,... | collective-permute-start | bytes 1572872 | tf_op jit(solution)/shard_map/while/body/eval_jaxpr/ppermute | solution.py:18
  102.0 14.3 %collective-permute-start = (bf16[2,4,128,128]{3,2,1,0:T(8,128)(2,1)}, bf16[2,4,128,128]{3,2,1,0:T(8,128)(2,1)S(1)}, u32[]{:S(2)}, u32[]{:S(2)}) collective-permute-start(bf16[2,4,128,128]{3,2,1,0:T(8,128)(2,1)} %get-tuple-element.815), channel_id=1, source_target_pairs={{30,0},{0,2},{2,4},{4,6},{6,8},{8,10},{10,12},{12,14},{14,16},{16,... | collective-permute-start | bytes 786440 | tf_op jit(solution)/shard_map/while/body/eval_jaxpr/ppermute | solution.py:18
  120.9 1.2 copy-start
  127.4 15.1 %collective-permute-start.1 = (f32[2,4,128,128]{3,2,1,0:T(8,128)}, f32[2,4,128,128]{3,2,1,0:T(8,128)}, u32[]{:S(2)}, u32[]{:S(2)}) collective-permute-start(f32[2,4,128,128]{3,2,1,0:T(8,128)} %get-tuple-element.816), channel_id=1, source_target_pairs={{30,0},{0,2},{2,4},{4,6},{6,8},{8,10},{10,12},{12,14},{14,16},{16,... | collective-permute-start | bytes 1572872 | tf_op jit(solution)/shard_map/while/body/eval_jaxpr/ppermute | solution.py:18
  127.4 14.3 %collective-permute-start = (bf16[2,4,128,128]{3,2,1,0:T(8,128)(2,1)}, bf16[2,4,128,128]{3,2,1,0:T(8,128)(2,1)S(1)}, u32[]{:S(2)}, u32[]{:S(2)}) collective-permute-start(bf16[2,4,128,128]{3,2,1,0:T(8,128)(2,1)} %get-tuple-element.815), channel_id=1, source_target_pairs={{30,0},{0,2},{2,4},{4,6},{6,8},{8,10},{10,12},{12,14},{14,16},{16,... | collective-permute-start | bytes 786440 | tf_op jit(solution)/shard_map/while/body/eval_jaxpr/ppermute | solution.py:18
  152.9 15.1 %collective-permute-start.1 = (f32[2,4,128,128]{3,2,1,0:T(8,128)}, f32[2,4,128,128]{3,2,1,0:T(8,128)}, u32[]{:S(2)}, u32[]{:S(2)}) collective-permute-start(f32[2,4,128,128]{3,2,1,0:T(8,128)} %get-tuple-element.816), channel_id=1, source_target_pairs={{30,0},{0,2},{2,4},{4,6},{6,8},{8,10},{10,12},{12,14},{14,16},{16,... | collective-permute-start | bytes 1572872 | tf_op jit(solution)/shard_map/while/body/eval_jaxpr/ppermute | solution.py:18
  152.9 14.3 %collective-permute-start = (bf16[2,4,128,128]{3,2,1,0:T(8,128)(2,1)}, bf16[2,4,128,128]{3,2,1,0:T(8,128)(2,1)S(1)}, u32[]{:S(2)}, u32[]{:S(2)}) collective-permute-start(bf16[2,4,128,128]{3,2,1,0:T(8,128)(2,1)} %get-tuple-element.815), channel_id=1, source_target_pairs={{30,0},{0,2},{2,4},{4,6},{6,8},{8,10},{10,12},{12,14},{14,16},{16,... | collective-permute-start | bytes 786440 | tf_op jit(solution)/shard_map/while/body/eval_jaxpr/ppermute | solution.py:18
  178.3 15.1 %collective-permute-start.1 = (f32[2,4,128,128]{3,2,1,0:T(8,128)}, f32[2,4,128,128]{3,2,1,0:T(8,128)}, u32[]{:S(2)}, u32[]{:S(2)}) collective-permute-start(f32[2,4,128,128]{3,2,1,0:T(8,128)} %get-tuple-element.816), channel_id=1, source_target_pairs={{30,0},{0,2},{2,4},{4,6},{6,8},{8,10},{10,12},{12,14},{14,16},{16,... | collective-permute-start | bytes 1572872 | tf_op jit(solution)/shard_map/while/body/eval_jaxpr/ppermute | solution.py:18
  178.3 14.3 %collective-permute-start = (bf16[2,4,128,128]{3,2,1,0:T(8,128)(2,1)}, bf16[2,4,128,128]{3,2,1,0:T(8,128)(2,1)S(1)}, u32[]{:S(2)}, u32[]{:S(2)}) collective-permute-start(bf16[2,4,128,128]{3,2,1,0:T(8,128)(2,1)} %get-tuple-element.815), channel_id=1, source_target_pairs={{30,0},{0,2},{2,4},{4,6},{6,8},{8,10},{10,12},{12,14},{14,16},{16,... | collective-permute-start | bytes 786440 | tf_op jit(solution)/shard_map/while/body/eval_jaxpr/ppermute | solution.py:18
  197.2 1.2 copy-start
  203.7 15.1 %collective-permute-start.1 = (f32[2,4,128,128]{3,2,1,0:T(8,128)}, f32[2,4,128,128]{3,2,1,0:T(8,128)}, u32[]{:S(2)}, u32[]{:S(2)}) collective-permute-start(f32[2,4,128,128]{3,2,1,0:T(8,128)} %get-tuple-element.816), channel_id=1, source_target_pairs={{30,0},{0,2},{2,4},{4,6},{6,8},{8,10},{10,12},{12,14},{14,16},{16,... | collective-permute-start | bytes 1572872 | tf_op jit(solution)/shard_map/while/body/eval_jaxpr/ppermute | solution.py:18
  203.7 14.3 %collective-permute-start = (bf16[2,4,128,128]{3,2,1,0:T(8,128)(2,1)}, bf16[2,4,128,128]{3,2,1,0:T(8,128)(2,1)S(1)}, u32[]{:S(2)}, u32[]{:S(2)}) collective-permute-start(bf16[2,4,128,128]{3,2,1,0:T(8,128)(2,1)} %get-tuple-element.815), channel_id=1, source_target_pairs={{30,0},{0,2},{2,4},{4,6},{6,8},{8,10},{10,12},{12,14},{14,16},{16,... | collective-permute-start | bytes 786440 | tf_op jit(solution)/shard_map/while/body/eval_jaxpr/ppermute | solution.py:18
  222.6 1.2 copy-start
  229.1 15.1 %collective-permute-start.1 = (f32[2,4,128,128]{3,2,1,0:T(8,128)}, f32[2,4,128,128]{3,2,1,0:T(8,128)}, u32[]{:S(2)}, u32[]{:S(2)}) collective-permute-start(f32[2,4,128,128]{3,2,1,0:T(8,128)} %get-tuple-element.816), channel_id=1, source_target_pairs={{30,0},{0,2},{2,4},{4,6},{6,8},{8,10},{10,12},{12,14},{14,16},{16,... | collective-permute-start | bytes 1572872 | tf_op jit(solution)/shard_map/while/body/eval_jaxpr/ppermute | solution.py:18
  229.2 14.3 %collective-permute-start = (bf16[2,4,128,128]{3,2,1,0:T(8,128)(2,1)}, bf16[2,4,128,128]{3,2,1,0:T(8,128)(2,1)S(1)}, u32[]{:S(2)}, u32[]{:S(2)}) collective-permute-start(bf16[2,4,128,128]{3,2,1,0:T(8,128)(2,1)} %get-tuple-element.815), channel_id=1, source_target_pairs={{30,0},{0,2},{2,4},{4,6},{6,8},{8,10},{10,12},{12,14},{14,16},{16,... | collective-permute-start | bytes 786440 | tf_op jit(solution)/shard_map/while/body/eval_jaxpr/ppermute | solution.py:18
  248.0 1.2 copy-start
  254.6 15.1 %collective-permute-start.1 = (f32[2,4,128,128]{3,2,1,0:T(8,128)}, f32[2,4,128,128]{3,2,1,0:T(8,128)}, u32[]{:S(2)}, u32[]{:S(2)}) collective-permute-start(f32[2,4,128,128]{3,2,1,0:T(8,128)} %get-tuple-element.816), channel_id=1, source_target_pairs={{30,0},{0,2},{2,4},{4,6},{6,8},{8,10},{10,12},{12,14},{14,16},{16,... | collective-permute-start | bytes 1572872 | tf_op jit(solution)/shard_map/while/body/eval_jaxpr/ppermute | solution.py:18
  254.6 14.3 %collective-permute-start = (bf16[2,4,128,128]{3,2,1,0:T(8,128)(2,1)}, bf16[2,4,128,128]{3,2,1,0:T(8,128)(2,1)S(1)}, u32[]{:S(2)}, u32[]{:S(2)}) collective-permute-start(bf16[2,4,128,128]{3,2,1,0:T(8,128)(2,1)} %get-tuple-element.815), channel_id=1, source_target_pairs={{30,0},{0,2},{2,4},{4,6},{6,8},{8,10},{10,12},{12,14},{14,16},{16,... | collective-permute-start | bytes 786440 | tf_op jit(solution)/shard_map/while/body/eval_jaxpr/ppermute | solution.py:18
  280.0 15.1 %collective-permute-start.1 = (f32[2,4,128,128]{3,2,1,0:T(8,128)}, f32[2,4,128,128]{3,2,1,0:T(8,128)}, u32[]{:S(2)}, u32[]{:S(2)}) collective-permute-start(f32[2,4,128,128]{3,2,1,0:T(8,128)} %get-tuple-element.816), channel_id=1, source_target_pairs={{30,0},{0,2},{2,4},{4,6},{6,8},{8,10},{10,12},{12,14},{14,16},{16,... | collective-permute-start | bytes 1572872 | tf_op jit(solution)/shard_map/while/body/eval_jaxpr/ppermute | solution.py:18
  280.0 14.3 %collective-permute-start = (bf16[2,4,128,128]{3,2,1,0:T(8,128)(2,1)}, bf16[2,4,128,128]{3,2,1,0:T(8,128)(2,1)S(1)}, u32[]{:S(2)}, u32[]{:S(2)}) collective-permute-start(bf16[2,4,128,128]{3,2,1,0:T(8,128)(2,1)} %get-tuple-element.815), channel_id=1, source_target_pairs={{30,0},{0,2},{2,4},{4,6},{6,8},{8,10},{10,12},{12,14},{14,16},{16,... | collective-permute-start | bytes 786440 | tf_op jit(solution)/shard_map/while/body/eval_jaxpr/ppermute | solution.py:18
  305.4 15.1 %collective-permute-start.1 = (f32[2,4,128,128]{3,2,1,0:T(8,128)}, f32[2,4,128,128]{3,2,1,0:T(8,128)}, u32[]{:S(2)}, u32[]{:S(2)}) collective-permute-start(f32[2,4,128,128]{3,2,1,0:T(8,128)} %get-tuple-element.816), channel_id=1, source_target_pairs={{30,0},{0,2},{2,4},{4,6},{6,8},{8,10},{10,12},{12,14},{14,16},{16,... | collective-permute-start | bytes 1572872 | tf_op jit(solution)/shard_map/while/body/eval_jaxpr/ppermute | solution.py:18
  305.4 14.3 %collective-permute-start = (bf16[2,4,128,128]{3,2,1,0:T(8,128)(2,1)}, bf16[2,4,128,128]{3,2,1,0:T(8,128)(2,1)S(1)}, u32[]{:S(2)}, u32[]{:S(2)}) collective-permute-start(bf16[2,4,128,128]{3,2,1,0:T(8,128)(2,1)} %get-tuple-element.815), channel_id=1, source_target_pairs={{30,0},{0,2},{2,4},{4,6},{6,8},{8,10},{10,12},{12,14},{14,16},{16,... | collective-permute-start | bytes 786440 | tf_op jit(solution)/shard_map/while/body/eval_jaxpr/ppermute | solution.py:18
  322.4 18.5 %collective-permute-start.1 = (f32[2,4,128,128]{3,2,1,0:T(8,128)}, f32[2,4,128,128]{3,2,1,0:T(8,128)}, u32[]{:S(2)}, u32[]{:S(2)}) collective-permute-start(f32[2,4,128,128]{3,2,1,0:T(8,128)} %get-tuple-element.816), channel_id=1, source_target_pairs={{30,0},{0,2},{2,4},{4,6},{6,8},{8,10},{10,12},{12,14},{14,16},{16,... | collective-permute-start | bytes 1572872 | tf_op jit(solution)/shard_map/while/body/eval_jaxpr/ppermute | solution.py:18
  322.4 17.7 %collective-permute-start = (bf16[2,4,128,128]{3,2,1,0:T(8,128)(2,1)}, bf16[2,4,128,128]{3,2,1,0:T(8,128)(2,1)S(1)}, u32[]{:S(2)}, u32[]{:S(2)}) collective-permute-start(bf16[2,4,128,128]{3,2,1,0:T(8,128)(2,1)} %get-tuple-element.815), channel_id=1, source_target_pairs={{30,0},{0,2},{2,4},{4,6},{6,8},{8,10},{10,12},{12,14},{14,16},{16,... | collective-permute-start | bytes 786440 | tf_op jit(solution)/shard_map/while/body/eval_jaxpr/ppermute | solution.py:18
  351.2 15.1 %collective-permute-start.1 = (f32[2,4,128,128]{3,2,1,0:T(8,128)}, f32[2,4,128,128]{3,2,1,0:T(8,128)}, u32[]{:S(2)}, u32[]{:S(2)}) collective-permute-start(f32[2,4,128,128]{3,2,1,0:T(8,128)} %get-tuple-element.816), channel_id=1, source_target_pairs={{30,0},{0,2},{2,4},{4,6},{6,8},{8,10},{10,12},{12,14},{14,16},{16,... | collective-permute-start | bytes 1572872 | tf_op jit(solution)/shard_map/while/body/eval_jaxpr/ppermute | solution.py:18
  351.2 14.3 %collective-permute-start = (bf16[2,4,128,128]{3,2,1,0:T(8,128)(2,1)}, bf16[2,4,128,128]{3,2,1,0:T(8,128)(2,1)S(1)}, u32[]{:S(2)}, u32[]{:S(2)}) collective-permute-start(bf16[2,4,128,128]{3,2,1,0:T(8,128)(2,1)} %get-tuple-element.815), channel_id=1, source_target_pairs={{30,0},{0,2},{2,4},{4,6},{6,8},{8,10},{10,12},{12,14},{14,16},{16,... | collective-permute-start | bytes 786440 | tf_op jit(solution)/shard_map/while/body/eval_jaxpr/ppermute | solution.py:18
  376.6 15.1 %collective-permute-start.1 = (f32[2,4,128,128]{3,2,1,0:T(8,128)}, f32[2,4,128,128]{3,2,1,0:T(8,128)}, u32[]{:S(2)}, u32[]{:S(2)}) collective-permute-start(f32[2,4,128,128]{3,2,1,0:T(8,128)} %get-tuple-element.816), channel_id=1, source_target_pairs={{30,0},{0,2},{2,4},{4,6},{6,8},{8,10},{10,12},{12,14},{14,16},{16,... | collective-permute-start | bytes 1572872 | tf_op jit(solution)/shard_map/while/body/eval_jaxpr/ppermute | solution.py:18
  376.6 14.3 %collective-permute-start = (bf16[2,4,128,128]{3,2,1,0:T(8,128)(2,1)}, bf16[2,4,128,128]{3,2,1,0:T(8,128)(2,1)S(1)}, u32[]{:S(2)}, u32[]{:S(2)}) collective-permute-start(bf16[2,4,128,128]{3,2,1,0:T(8,128)(2,1)} %get-tuple-element.815), channel_id=1, source_target_pairs={{30,0},{0,2},{2,4},{4,6},{6,8},{8,10},{10,12},{12,14},{14,16},{16,... | collective-permute-start | bytes 786440 | tf_op jit(solution)/shard_map/while/body/eval_jaxpr/ppermute | solution.py:18
  402.1 15.1 %collective-permute-start.1 = (f32[2,4,128,128]{3,2,1,0:T(8,128)}, f32[2,4,128,128]{3,2,1,0:T(8,128)}, u32[]{:S(2)}, u32[]{:S(2)}) collective-permute-start(f32[2,4,128,128]{3,2,1,0:T(8,128)} %get-tuple-element.816), channel_id=1, source_target_pairs={{30,0},{0,2},{2,4},{4,6},{6,8},{8,10},{10,12},{12,14},{14,16},{16,... | collective-permute-start | bytes 1572872 | tf_op jit(solution)/shard_map/while/body/eval_jaxpr/ppermute | solution.py:18
  402.1 14.3 %collective-permute-start = (bf16[2,4,128,128]{3,2,1,0:T(8,128)(2,1)}, bf16[2,4,128,128]{3,2,1,0:T(8,128)(2,1)S(1)}, u32[]{:S(2)}, u32[]{:S(2)}) collective-permute-start(bf16[2,4,128,128]{3,2,1,0:T(8,128)(2,1)} %get-tuple-element.815), channel_id=1, source_target_pairs={{30,0},{0,2},{2,4},{4,6},{6,8},{8,10},{10,12},{12,14},{14,16},{16,... | collective-permute-start | bytes 786440 | tf_op jit(solution)/shard_map/while/body/eval_jaxpr/ppermute | solution.py:18
  427.5 11.5 %collective-permute-start.2 = (f32[2,4,128,128]{3,2,1,0:T(8,128)}, f32[2,4,128,128]{3,2,1,0:T(8,128)S(1)}, u32[]{:S(2)}, u32[]{:S(2)}) collective-permute-start(f32[2,4,128,128]{3,2,1,0:T(8,128)} %get-tuple-element.499), channel_id=1, source_target_pairs={{30,0},{0,2},{2,4},{4,6},{6,8},{8,10},{10,12},{12,14},{14,16},{16,... | collective-permute-start | bytes 1572872 | tf_op jit(solution)/shard_map/ppermute | solution.py:18
  (12 other events, 13.4 us)
where the time goes:
time: 447 us; the launch traced here: 441 us
  waiting for transfers between devices  155 us (35%)
  other arithmetic  110 us (25%)
  local copies, waits for them, and re-layouts  90.7 us (20%)
  matrix products  65.9 us (15%)
  loops' own time  10.8 us (2%)
  starting transfers between devices  6.93 us (2%)
    ppermute x31, waiting for transfers between devices, passed_along(): return lax.ppermute(block, axis, route)  155 us
    while x30, local copies, waits for them, and re-layouts  39.3 us
    dot_general x15, matrix products, compute(): jnp.einsum('kgqd,kcd->kgqc', q_rot, k_part, preferred_element_type=jnp.fl...  30.2 us
    add x14, other arithmetic, compute(): grads_total + jnp.stack([key_grad, value_grad])  26.9 us
    reduce_or x16, other arithmetic, visit_block(): jnp.any((their_blocks[None, :] <= my_blocks[:, None]) | block_shared)  21.8 us
    reduce_sum x16, other arithmetic, token_info(): spans_of = jnp.sum(jnp.where(matched, block_span[None, :], 0), axis=1)  14.2 us
    dot_general x15, matrix products, compute(): jnp.einsum('kgqd,kcd->kgqc', d_heads, v_part, preferred_element_type=jnp....  13.3 us
    unnamed x34, local copies, waits for them, and re-layouts  11.7 us
  transfers between devices with their start and end apart: 32, of which 16 were waited for; matrix products, arithmetic and copies ran while one was open for 23% of the time, Pallas kernels for 0%

commit v1 on v0

v1 whole, which is shorter than its diff:
```python
import functools
import math

import jax
import jax.numpy as jnp
from jax import lax
from jax.experimental import pallas as pl
from jax.experimental.pallas import tpu as pltpu
from jax.sharding import Mesh
from jax.sharding import PartitionSpec as P

HEAD_SIZE = 128
BLOCKS_DEV = 2
THETA = 1000000.0
CHUNK = 256
SCORE_SCALE = 1.0 / math.sqrt(HEAD_SIZE)
LOG2E = math.log2(math.e)
SWAP = [(0, 1), (1, 0)]


def turned_tables(ids, width):
    half = width // 2
    rows = ids.shape[1]
    pair = lax.broadcasted_iota(jnp.int32, (half, rows), 0)
    first_cut = width // 8
    second_cut = first_cut + 3 * width // 16
    inverse = jnp.exp(pair.astype(jnp.float32) * jnp.float32(-2.0 * math.log(THETA) / width))
    ids = ids.astype(jnp.float32)
    picked = jnp.where(
        pair < first_cut, ids[0:1, :], jnp.where(pair < second_cut, ids[1:2, :], ids[2:3, :])
    )
    angles = picked * inverse
    cosine = jnp.cos(angles)
    sine = jnp.sin(angles)
    return (
        jnp.concatenate([cosine, cosine], axis=0).T,
        jnp.concatenate([sine, sine], axis=0).T,
    )


def half_sign():
    lane = lax.broadcasted_iota(jnp.int32, (1, HEAD_SIZE), 1)
    return jnp.where(lane < HEAD_SIZE // 2, -1.0, 1.0).astype(jnp.float32)


def prep_kernel(
    split, heads, where_ref, ids_own, ids_other, k_own, k_other, v_own, v_other,
    kv_ref, cos_ref, sin_ref,
):
    core = where_ref[0]
    rows = k_own.shape[0]
    sign = half_sign()
    sources = [(ids_own, k_own, v_own, core)]
    if split == 2:
        sources.append((ids_other, k_other, v_other, 1 - core))
    else:
        sources = [(ids_own, k_own, v_own, 0)]
    for number, (ids, k_ref, v_ref, place) in enumerate(sources):
        cosine, sine = turned_tables(ids[...], HEAD_SIZE)
        cos_ref[pl.ds(number * rows, rows), :] = cosine
        sin_ref[pl.ds(number * rows, rows), :] = sine
        at = pl.multiple_of(place * rows, rows)
        for head in range(heads):
            columns = pl.ds(head * HEAD_SIZE, HEAD_SIZE)
            keys = k_ref[:, columns].astype(jnp.float32)
            turned = pltpu.roll(keys, HEAD_SIZE // 2, 1) * sign
            kv_ref[head, 0, pl.ds(at, rows), :] = (keys * cosine + turned * sine).astype(
                jnp.bfloat16
            )
            kv_ref[head, 1, pl.ds(at, rows), :] = v_ref[:, columns]


def row_vector(lse, upper, block_len):
    group, width = lse.shape
    rolled = pltpu.roll(lse, block_len, 1)
    low = jnp.where(upper == 0, lse, rolled)
    high = jnp.where(upper == 0, rolled, lse)
    lane = lax.broadcasted_iota(jnp.int32, (1, width), 1)
    pieces = [
        jnp.where(lane < block_len, low[h : h + 1, :], high[h + 1 : h + 2, :])
        for h in range(0, group, 2)
    ]
    return jnp.concatenate(pieces, axis=1)


def attend_kernel(split, group, block_len, where_ref, map_ref, span_ref, *refs):
    refs = list(refs)
    kv_ref = refs.pop(0)
    cos_ref = refs.pop(0)
    sin_ref = refs.pop(0)
    q_refs = [refs.pop(0) for _ in range(split)]
    a_refs = [refs.pop(0) for _ in range(split)]
    l_refs = [refs.pop(0) for _ in range(split)]
    g_refs = [refs.pop(0) for _ in range(4 if split == 2 else 1)]
    dq_refs = [refs.pop(0) for _ in range(split)]
    part_ref = refs.pop(0)
    k_sort, v_sort, k_turn, q_all, g_all, l_all, d_all, dk_sum, dv_sum, dq_sum = refs
    core, tp_index, device = where_ref[0], where_ref[1], where_ref[2]
    rows = q_refs[0].shape[0]
    units, _, unit_rows, _ = kv_ref.shape
    unit_blocks = unit_rows // block_len
    blocks = units * unit_blocks
    spans = span_ref.shape[0] // 2
    columns = group * block_len
    sign = half_sign()

    @pl.loop(0, blocks)
    def _(stored):
        unit = stored // unit_blocks
        at = pl.multiple_of((stored % unit_blocks) * block_len, block_len)
        to = pl.multiple_of(map_ref[stored] * block_len, block_len)
        k_sort[pl.ds(to, block_len), :] = kv_ref[unit, 0, pl.ds(at, block_len), :]
        v_sort[pl.ds(to, block_len), :] = kv_ref[unit, 1, pl.ds(at, block_len), :]

    @pl.loop(0, k_turn.shape[0])
    def _(chunk):
        at = pl.multiple_of(chunk * CHUNK, CHUNK)
        k_turn[chunk] = k_sort[pl.ds(at, CHUNK), :].T
        dk_sum[pl.ds(at, CHUNK), :] = jnp.zeros((CHUNK, HEAD_SIZE), jnp.float32)
        dv_sum[pl.ds(at, CHUNK), :] = jnp.zeros((CHUNK, HEAD_SIZE), jnp.float32)

    places = []
    for number in range(split):
        owner = device if number == 0 else device + 1 - 2 * core
        for step in range(BLOCKS_DEV):
            if split == 2:
                upper = tp_index if step == 0 else 1 - tp_index
                g_ref, g_row = g_refs[number * BLOCKS_DEV + step], 0
            else:
                upper = step
                g_ref, g_row = g_refs[0], step * block_len
            places.append((number, owner * BLOCKS_DEV + upper, upper, g_ref, g_row))

    for place, (number, stored, upper, g_ref, g_row) in enumerate(places):
        row = upper * block_len
        if not isinstance(row, int):
            row = pl.multiple_of(row, block_len)
        table_row = row + number * rows
        if not isinstance(table_row, int):
            table_row = pl.multiple_of(table_row, block_len)
        cosine = cos_ref[pl.ds(table_row, block_len), :]
        sine = sin_ref[pl.ds(table_row, block_len), :] * sign
        products = []
        for head in range(group):
            lanes = pl.ds(head * HEAD_SIZE, HEAD_SIZE)
            field = q_refs[number][pl.ds(row, block_len), lanes].astype(jnp.float32)
            turned = pltpu.roll(field, HEAD_SIZE // 2, 1)
            q_all[place, pl.ds(head * block_len, block_len), :] = (
                field * cosine + turned * sine
            ).astype(jnp.bfloat16)
            grad = g_ref[pl.ds(g_row, block_len), lanes]
            g_all[place, pl.ds(head * block_len, block_len), :] = grad
            products.append(
                grad.astype(jnp.float32)
                * a_refs[number][pl.ds(row, block_len), lanes].astype(jnp.float32)
            )
        product = jnp.concatenate(products, axis=0)
        d_all[place] = jnp.sum(product.T, axis=0, keepdims=True)
        l_all[place] = row_vector(l_refs[number][...], upper, block_len) * LOG2E

    lane = lax.broadcasted_iota(jnp.int32, (1, columns), 1)
    within = lax.rem(lane, block_len)
    key_row = lax.broadcasted_iota(jnp.int32, (CHUNK, 1), 0)

    for place, (number, stored, upper, g_ref, g_row) in enumerate(places):
        block = map_ref[stored]
        end = jnp.int32(0)
        for span in range(spans):
            inside = (block >= span_ref[2 * span]) & (block < span_ref[2 * span + 1])
            end = jnp.where(inside, span_ref[2 * span + 1], end)
        limit = jnp.where(end > 0, end * block_len, block * block_len + within + 1)
        last = jnp.maximum(end, block + 1) * block_len
        chunks = (last + CHUNK - 1) // CHUNK
        queries = q_all[place]
        grads = g_all[place]
        lse = l_all[place]
        delta = d_all[place]
        dq_sum[...] = jnp.zeros_like(dq_sum)

        @pl.loop(0, chunks)
        def _(chunk):
            at = pl.multiple_of(chunk * CHUNK, CHUNK)
            keys = k_sort[pl.ds(at, CHUNK), :]
            values = v_sort[pl.ds(at, CHUNK), :]
            scores = lax.dot_general(
                keys, queries, (((1,), (1,)), ((), ())), preferred_element_type=jnp.float32
            )
            raised = scores * (SCORE_SCALE * LOG2E) - lse
            raised = jnp.where(key_row + at < limit, raised, -jnp.inf)
            probs = jnp.exp2(raised)
            grad_p = lax.dot_general(
                values, grads, (((1,), (1,)), ((), ())), preferred_element_type=jnp.float32
            )
            grad_s = (probs * (grad_p - delta)).astype(jnp.bfloat16)
            dv_sum[pl.ds(at, CHUNK), :] += jnp.dot(
                probs.astype(jnp.bfloat16), grads, preferred_element_type=jnp.float32
            )
            dk_sum[pl.ds(at, CHUNK), :] += jnp.dot(
                grad_s, queries, preferred_element_type=jnp.float32
            )
            dq_sum[...] += jnp.dot(k_turn[chunk], grad_s, preferred_element_type=jnp.float32)

        row = upper * block_len
        if not isinstance(row, int):
            row = pl.multiple_of(row, block_len)
        table_row = row + number * rows
        if not isinstance(table_row, int):
            table_row = pl.multiple_of(table_row, block_len)
        cosine = cos_ref[pl.ds(table_row, block_len), :]
        sine = sin_ref[pl.ds(table_row, block_len), :]
        dq_rot = dq_sum[...].T * SCORE_SCALE
        for head in range(group):
            field = dq_rot[head * block_len : (head + 1) * block_len, :]
            turned = pltpu.roll(field * sine, HEAD_SIZE // 2, 1) * sign
            dq_refs[number][pl.ds(row, block_len), pl.ds(head * HEAD_SIZE, HEAD_SIZE)] = (
                field * cosine - turned
            ).astype(jnp.bfloat16)

    @pl.loop(0, blocks)
    def _(stored):
        unit = stored // unit_blocks
        to = pl.multiple_of((stored % unit_blocks) * block_len, block_len)
        at = pl.multiple_of(map_ref[stored] * block_len, block_len)
        part_ref[unit, 0, pl.ds(to, block_len), :] = (
            dk_sum[pl.ds(at, block_len), :] * SCORE_SCALE
        ).astype(part_ref.dtype)
        part_ref[unit, 1, pl.ds(to, block_len), :] = dv_sum[pl.ds(at, block_len), :].astype(
            part_ref.dtype
        )


def reverse_rotation(field, cosine, sine):
    half = field.shape[-1] // 2
    scaled = field * sine
    turned = jnp.concatenate([scaled[..., half:], -scaled[..., :half]], axis=-1)
    return field * cosine + turned


def whole(shape):
    return pl.BlockSpec(shape, lambda *_: (0,) * len(shape))


def shards(
    queries, keys, values, attn_out, out_grad, logsumexp, position_ids, block_map, span_blocks
):
    rows = queries.shape[0]
    kv_heads = keys.shape[1] // HEAD_SIZE
    q_heads = queries.shape[1] // HEAD_SIZE
    group = q_heads // kv_heads
    block_len = rows // BLOCKS_DEV
    tp_size = lax.axis_size("tp")
    split = 2 if kv_heads % 2 == 0 and tp_size == 2 else 1
    heads = kv_heads // split
    core = lax.axis_index("core")
    tp_index = lax.axis_index("tp")
    ring = lax.axis_size("z") * lax.axis_size("y")
    units = ring * 2 // split
    unit_rows = rows * split
    gather_axes = ("z", "y") if split == 2 else ("z", "y", "core")
    device = (lax.axis_index("z") * lax.axis_size("y") + lax.axis_index("y")) * 2 + core
    place = jnp.stack([core, tp_index, device]).astype(jnp.int32)
    spans = span_blocks.reshape(-1)
    width = group * HEAD_SIZE

    def other_half(array, axis):
        size = array.shape[axis] // 2
        return lax.dynamic_slice_in_dim(array, (1 - core) * size, size, axis)

    def own_half(array, axis):
        size = array.shape[axis] // 2
        return lax.dynamic_slice_in_dim(array, core * size, size, axis)

    def swap(array):
        return lax.ppermute(array, "core", SWAP)

    if split == 2:
        ids_other = swap(position_ids)
        k_other = swap(other_half(keys, 1))
        v_other = swap(other_half(values, 1))
        k_mine, v_mine = own_half(keys, 1), own_half(values, 1)
        lse_other = swap(other_half(logsumexp, 0))
    else:
        ids_other, k_other, v_other = position_ids, keys, values
        k_mine, v_mine = keys, values

    kv_block, cosine, sine = pl.pallas_call(
        functools.partial(prep_kernel, split, heads),
        grid_spec=pltpu.PrefetchScalarGridSpec(
            num_scalar_prefetch=1,
            grid=(1,),
            in_specs=[
                whole(a.shape)
                for a in (position_ids, ids_other, k_mine, k_other, v_mine, v_other)
            ],
            out_specs=[
                whole((heads, 2, unit_rows, HEAD_SIZE)),
                whole((unit_rows, HEAD_SIZE)),
                whole((unit_rows, HEAD_SIZE)),
            ],
        ),
        out_shape=[
            jax.ShapeDtypeStruct((heads, 2, unit_rows, HEAD_SIZE), jnp.bfloat16),
            jax.ShapeDtypeStruct((unit_rows, HEAD_SIZE), jnp.float32),
            jax.ShapeDtypeStruct((unit_rows, HEAD_SIZE), jnp.float32),
        ],
        name="prep",
    )(place, position_ids, ids_other, k_mine, k_other, v_mine, v_other)

    gathered = [
        lax.all_gather(kv_block[head], gather_axes, axis=0, tiled=False)
        for head in range(heads)
    ]

    if split == 1:
        grads_in = lax.all_to_all(out_grad, "tp", split_axis=1, concat_axis=0, tiled=True)

    tokens = units * unit_rows
    dq_parts = []
    finished = []
    for head in range(heads):
        own_column = core * heads + head if split == 2 else head

        def picked(array, block_rows):
            return pl.BlockSpec(
                (block_rows, width),
                lambda i, where, *_: (0, (where[0] * heads if split == 2 else 0) + head),
            )

        q_in, a_in, l_in = [queries], [attn_out], [logsumexp]
        q_spec, a_spec = [picked(queries, rows)], [picked(attn_out, rows)]
        l_spec = [
            pl.BlockSpec(
                (group, rows),
                lambda i, where, *_: ((where[0] * heads if split == 2 else 0) + head, 0),
            )
        ]
        if split == 2:
            away = ((1 - core) * heads + head) * width
            q_in.append(swap(lax.dynamic_slice_in_dim(queries, away, width, 1)))
            a_in.append(swap(lax.dynamic_slice_in_dim(attn_out, away, width, 1)))
            l_in.append(lse_other)
            q_spec.append(whole((rows, width)))
            a_spec.append(whole((rows, width)))
            l_spec.append(pl.BlockSpec((group, rows), lambda i, *_: (head, 0)))

            def grad_piece(to_tp, to_core):
                column = ((to_tp * 2 + to_core) * heads + head) * width
                return lax.dynamic_slice_in_dim(out_grad, column, width, 1)

            pairs = [(c, t) for c in range(2) for t in range(2)]

            def sent(piece, flip_core, flip_tp):
                route = [
                    (c * 2 + t, (c ^ flip_core) * 2 + (t ^ flip_tp)) for c, t in pairs
                ]
                return lax.ppermute(piece, ("core", "tp"), route)

            g_in = [
                grad_piece(tp_index, core),
                sent(grad_piece(1 - tp_index, core), 0, 1),
                sent(grad_piece(tp_index, 1 - core), 1, 0),
                sent(grad_piece(1 - tp_index, 1 - core), 1, 1),
            ]
            g_spec = [whole((block_len, width))] * 4
        else:
            g_in = [grads_in]
            g_spec = [picked(grads_in, rows)]

        inputs = [gathered[head], cosine, sine]
        specs = [whole(a.shape) for a in inputs]
        columns = group * block_len
        results = pl.pallas_call(
            functools.partial(attend_kernel, split, group, block_len),
            grid_spec=pltpu.PrefetchScalarGridSpec(
                num_scalar_prefetch=3,
                grid=(1,),
                in_specs=specs + q_spec + a_spec + l_spec + g_spec,
                out_specs=[whole((rows, width))] * split
                + [whole((units, 2, unit_rows, HEAD_SIZE))],
                scratch_shapes=[
                    pltpu.VMEM((tokens, HEAD_SIZE), jnp.bfloat16),
                    pltpu.VMEM((tokens, HEAD_SIZE), jnp.bfloat16),
                    pltpu.VMEM((tokens // CHUNK, HEAD_SIZE, CHUNK), jnp.bfloat16),
                    pltpu.VMEM((split * BLOCKS_DEV, columns, HEAD_SIZE), jnp.bfloat16),
                    pltpu.VMEM((split * BLOCKS_DEV, columns, HEAD_SIZE), jnp.bfloat16),
                    pltpu.VMEM((split * BLOCKS_DEV, 1, columns), jnp.float32),
                    pltpu.VMEM((split * BLOCKS_DEV, 1, columns), jnp.float32),
                    pltpu.VMEM((tokens, HEAD_SIZE), jnp.float32),
                    pltpu.VMEM((tokens, HEAD_SIZE), jnp.float32),
                    pltpu.VMEM((HEAD_SIZE, columns), jnp.float32),
                ],
            ),
            out_shape=[jax.ShapeDtypeStruct((rows, width), jnp.bfloat16)] * split
            + [jax.ShapeDtypeStruct((units, 2, unit_rows, HEAD_SIZE), jnp.bfloat16)],
            compiler_params=pltpu.CompilerParams(vmem_limit_bytes=40 * 1024 * 1024),
            cost_estimate=pl.CostEstimate(
                flops=6 * group * unit_rows * tokens * HEAD_SIZE,
                bytes_accessed=4 * 1024 * 1024,
                transcendentals=group * unit_rows * tokens // 2,
            ),
            name="attend",
        )(place, block_map, spans, *inputs, *q_in, *a_in, *l_in, *g_in)
        part = results[-1]
        total = lax.psum_scatter(part, gather_axes, scatter_dimension=0, tiled=True)[0]
        if split == 2:
            dq_parts.append((results[0], swap(results[1])))
            mine = own_half(total, 1)
            theirs = swap(other_half(total, 1))
            finished.append((mine, theirs))
        else:
            dq_parts.append((results[0],))
            finished.append((total,))

    def in_order(pairs):
        if split == 1:
            return jnp.concatenate([p[0] for p in pairs], axis=-1)
        mine = jnp.concatenate([p[0] for p in pairs], axis=-1)
        theirs = jnp.concatenate([p[1] for p in pairs], axis=-1)
        return jnp.where(
            core == 0,
            jnp.concatenate([mine, theirs], axis=-1),
            jnp.concatenate([theirs, mine], axis=-1),
        )

    grad_q = in_order(dq_parts)
    key_sums = in_order([tuple(p[0] for p in f) for f in finished]).astype(jnp.float32)
    key_gradient = (
        reverse_rotation(
            key_sums.reshape(rows, kv_heads, HEAD_SIZE),
            cosine[:rows, None, :],
            sine[:rows, None, :],
        )
        .astype(jnp.bfloat16)
        .reshape(rows, kv_heads * HEAD_SIZE)
    )
    value_gradient = in_order([tuple(p[1] for p in f) for f in finished])
    return (grad_q, key_gradient, value_gradient)


def solution(mesh):
    ctx, tp = mesh.shape["ctx"], mesh.shape["tp"]
    fine = Mesh(mesh.devices.reshape(ctx // 4, 2, 2, tp), ("z", "y", "core", "tp"))
    ctx_axes = ("z", "y", "core")
    return jax.shard_map(
        shards,
        mesh=fine,
        in_specs=(
            P(ctx_axes, "tp"),
            P(ctx_axes, "tp"),
            P(ctx_axes, "tp"),
            P(ctx_axes, "tp"),
            P((*ctx_axes, "tp"), None),
            P("tp", ctx_axes),
            P(None, ctx_axes),
            P(),
            P(),
        ),
        out_specs=(P(ctx_axes, "tp"), P(ctx_axes, "tp"), P(ctx_axes, "tp")),
        check_vma=False,
    )
```

time: 447 us -> 245 us (0.55); the launches traced: 441 us -> 244 us
  other arithmetic: 110 us -> 2.88 us
  matrix products: 65.9 us -> 0 us
  local copies, waits for them, and re-layouts: 90.7 us -> 25.9 us
  Pallas kernels: 0 us -> 34.7 us
  between operations: 1.53 us -> 13.9 us
  loops' own time: 10.8 us -> 0 us
    ppermute x31 -> x18, waiting for transfers between devices: 155 us -> 13.1 us  [the longest x6 11.3 us: sent(): return lax.ppermute(piece, ('core', 'tp'), route)]
    reduce_scatter x0 -> x2, waiting for transfers between devices: none -> 106 us  [shards(): lax.psum_scatter(part, gather_axes, scatter_dimension=0, tiled=True)[0]]
    dot_general x75 -> x0, matrix products: 65.9 us -> none  [the longest x15 30.2 us: compute(): jnp.einsum('kgqd,kcd->kgqc', q_rot, k_part, preferred_element_type=jnp.fl...]
    while x30 -> x0, local copies, waits for them, and re-layouts: 39.3 us -> none
    all_gather x0 -> x2, waiting for transfers between devices: none -> 38.5 us  [shards(): lax.all_gather(kv_block[head], gather_axes, axis=0, tiled=False)]
    add x30 -> x0, other arithmetic: 37.1 us -> none  [the longest x14 26.9 us: compute(): grads_total + jnp.stack([key_grad, value_grad])]
    pallas_call x0 -> x3, Pallas kernels: none -> 34.7 us  [the longest x2 31.8 us: shards(): pl.pallas_call(functools.partial(attend_kernel, split, group, block_len),...]
    reduce_or x16 -> x0, other arithmetic: 21.8 us -> none  [visit_block(): jnp.any((their_blocks[None, :] <= my_blocks[:, None]) | block_shared)]
  transfers between devices with their start and end apart: 32 -> 22, of which waited for: 16 -> 11; matrix products, arithmetic and copies ran while one was open for 23% -> 4% of each run, Pallas kernels for 0% -> 13%
where the time goes in v1:
time: 245 us; the launch traced here: 244 us
  waiting for transfers between devices  159 us (65%)
  Pallas kernels  34.7 us (14%)
  local copies, waits for them, and re-layouts  25.9 us (11%)
  between operations  13.9 us (6%)
  starting transfers between devices  8.02 us (3%)
  other arithmetic  2.88 us (1%)
    reduce_scatter x2, waiting for transfers between devices, shards(): lax.psum_scatter(part, gather_axes, scatter_dimension=0, tiled=True)[0]  106 us
    all_gather x2, waiting for transfers between devices, shards(): lax.all_gather(kv_block[head], gather_axes, axis=0, tiled=False)  38.5 us
    pallas_call x2, Pallas kernels, shards(): pl.pallas_call(functools.partial(attend_kernel, split, group, block_len),...  31.8 us
    unnamed x52, local copies, waits for them, and re-layouts  13.7 us
    ppermute x6, waiting for transfers between devices, sent(): return lax.ppermute(piece, ('core', 'tp'), route)  11.3 us
    ppermute x6, starting transfers between devices, sent(): return lax.ppermute(piece, ('core', 'tp'), route)  4.96 us
  transfers between devices with their start and end apart: 22, of which 11 were waited for; matrix products, arithmetic and copies ran while one was open for 4% of the time, Pallas kernels for 13%

profile of v1, /device:TPU:0, one launch (start us, length us, event | category | flops | bytes accessed | tf_op | source)
XLA Modules:
  0.0 244.1 jit_solution(4624291777121477479)
XLA Ops:
  7.2 1.6 constant_dynamic-slice_fusion.15
  8.8 0.5 collective-permute-start.1
  9.3 1.5 constant_dynamic-slice_fusion.13
  10.8 0.5 collective-permute-start
  11.3 0.7 pad_add_fusion.where_ref
  12.3 0.6 copy-done.23
  13.0 2.9 %prep.1 = (bf16[2,2,256,128]{3,2,1,0:T(8,128)(2,1)}, f32[256,128]{1,0:T(8,128)}, f32[256,128]{1,0:T(8,128)}) custom-call(s32[3]{0:T(128)} %pad_add_fusion.where_ref, s32[3,128]{1,0:T(4,128)} %ids_own.1, s32[3,128]{1,0:T(4,128)} %copy-done.23, bf16[128,256]{1,0:T(8,128)(2,1)} %get-tuple-element.50.k_own, bf16[128,256]{1,0:T(8,128)(2,1)} %copy-done.21, ...), custom_call_target="tpu_custom_call" | custom-call | tf_op jit(solution)/shard_map/prep/pallas_call | solution.py:286
  15.8 1.7 fusion.3
  17.6 0.7 all-gather.5.cloned.1.call-update
  18.4 0.9 constant_dynamic-slice_fusion.12
  19.6 0.8 constant_dynamic-slice_fusion.11
  21.0 2.3 constant_dynamic-slice_fusion.6
  23.2 2.7 %collective-permute-start.6 = (bf16[64,1024]{1,0:T(8,128)(2,1)}, bf16[64,1024]{1,0:T(8,128)(2,1)S(1)}, u32[]{:S(2)}, u32[]{:S(2)}) collective-permute-start(bf16[64,1024]{1,0:T(8,128)(2,1)} %get-tuple-element.31), channel_id=1, source_target_pairs={{0,1},{1,0},{2,3},{3,2},{4,5},{5,4},{6,7},{7,6},{8,9},{9,8},{10,11... | collective-permute-start | bytes 393224 | tf_op jit(solution)/shard_map/ppermute | solution.py:356
  26.3 4.1 %collective-permute-done.6.refs_10_ = bf16[64,1024]{1,0:T(8,128)(2,1)S(1)} collective-permute-done((bf16[64,1024]{1,0:T(8,128)(2,1)}, bf16[64,1024]{1,0:T(8,128)(2,1)S(1)}, u32[]{:S(2)}, u32[]{:S(2)}) %collective-permute-start.6) | collective-permute-done | bytes 131104 | tf_op jit(solution)/shard_map/ppermute | solution.py:356
  30.4 2.4 collective-permute-done.8.refs_12_
  32.8 0.7 copy-done.8
  33.5 27.0 %all-gather.3.cloned.1.call-done.refs_0_ = bf16[8,2,256,128]{3,2,1,0:T(8,128)(2,1)} async-done(((bf16[1,2,256,128]{3,2,1,0:T(8,128)(2,1)}), bf16[8,2,256,128]{3,2,1,0:T(8,128)(2,1)}) %all-gather.3.cloned.1.call-update) | async-done | bytes 1048592 | tf_op jit(solution)/shard_map/all_gather | solution.py:310
  60.5 1.2 copy-done.7
  61.7 0.9 copy-done.9
  62.7 16.3 %attend.2 = (bf16[128,1024]{1,0:T(8,128)(2,1)S(1)}, bf16[128,1024]{1,0:T(8,128)(2,1)S(1)}, bf16[8,2,256,128]{3,2,1,0:T(8,128)(2,1)}) custom-call(s32[3]{0:T(128)S(1)} %copy-done.5, s32[32]{0:T(128)S(1)} %copy-done.20, s32[8]{0:T(128)S(1)} %reshape.51.span_ref, bf16[8,2,256,128]{3,2,1,0:T(8,128)(2,1)S(1)} %copy-done.7, f32[256,128]{1,0:T(8,128)S(1)} %copy-done.2, ...), custom_call_target="tpu_custom_call" | custom-call | flops 3221225472 | bytes 4194304 | tf_op jit(solution)/shard_map/attend/pallas_call | solution.py:372
  79.0 0.7 copy-done.10
  79.8 0.5 collective-permute-start.9
  80.3 1.5 collective-permute-start.11
  81.8 0.7 collective-permute-start.13
  82.5 4.4 %collective-permute-done.11.refs_10_ = bf16[64,1024]{1,0:T(8,128)(2,1)S(1)} collective-permute-done((bf16[64,1024]{1,0:T(8,128)(2,1)}, bf16[64,1024]{1,0:T(8,128)(2,1)S(1)}, u32[]{:S(2)}, u32[]{:S(2)}) %collective-permute-start.11) | collective-permute-done | bytes 131104 | tf_op jit(solution)/shard_map/ppermute | solution.py:356
  86.9 0.7 copy-done.16
  88.0 0.7 copy-done.18
  88.6 0.7 copy-done.12
  89.3 0.7 copy-done.14
  90.0 11.5 %all-gather.5.cloned.1.call-done.refs_0_ = bf16[8,2,256,128]{3,2,1,0:T(8,128)(2,1)} async-done(((bf16[1,2,256,128]{3,2,1,0:T(8,128)(2,1)}), bf16[8,2,256,128]{3,2,1,0:T(8,128)(2,1)}) %all-gather.5.cloned.1.call-update) | async-done | bytes 1048592 | tf_op jit(solution)/shard_map/all_gather | solution.py:310
  101.6 1.2 copy-done.6
  102.8 0.9 copy-done.13
  103.7 0.9 copy-done.15
  104.7 0.9 copy-done.17
  105.6 0.9 copy-done.19
  106.5 15.5 %attend.3 = (bf16[128,1024]{1,0:T(8,128)(2,1)S(1)}, bf16[128,1024]{1,0:T(8,128)(2,1)S(1)}, bf16[8,2,256,128]{3,2,1,0:T(8,128)(2,1)}) custom-call(s32[3]{0:T(128)S(1)} %copy-done.5, s32[32]{0:T(128)S(1)} %copy-done.20, s32[8]{0:T(128)S(1)} %reshape.51.span_ref, bf16[8,2,256,128]{3,2,1,0:T(8,128)(2,1)S(1)} %copy-done.6, f32[256,128]{1,0:T(8,128)S(1)} %copy-done.2, ...), custom_call_target="tpu_custom_call" | custom-call | flops 3221225472 | bytes 4194304 | tf_op jit(solution)/shard_map/attend/pallas_call | solution.py:372
  122.0 0.9 copy-done.11
  123.0 0.5 collective-permute-start.15
  123.5 1.0 collective-permute-done.14
  124.9 1.2 maximum_select_fusion
  126.1 41.0 %reduce-scatter.3.cloned.1.call-done = bf16[1,2,256,128]{3,2,1,0:T(8,128)(2,1)} async-done(((bf16[8,2,256,128]{3,2,1,0:T(8,128)(2,1)}), bf16[1,2,256,128]{3,2,1,0:T(8,128)(2,1)}) %reduce-scatter.3.cloned.1.call-update) | async-done | bytes 131088 | tf_op jit(solution)/shard_map/reduce_scatter | solution.py:404
  167.1 0.8 dynamic-slice_bitcast_fusion.1
  168.0 65.2 %reduce-scatter.5.cloned.1.call-done = bf16[1,2,256,128]{3,2,1,0:T(8,128)(2,1)} async-done(((bf16[8,2,256,128]{3,2,1,0:T(8,128)(2,1)}), bf16[1,2,256,128]{3,2,1,0:T(8,128)(2,1)}) %reduce-scatter.5.cloned.1.call-update) | async-done | bytes 131088 | tf_op jit(solution)/shard_map/reduce_scatter | solution.py:404
  233.1 0.8 dynamic-slice_bitcast_fusion
  234.0 0.8 dynamic-slice_bitcast_fusion.3
  234.8 0.8 dynamic-slice_bitcast_fusion.2
  236.1 0.8 copy.18
  236.8 0.7 maximum_select_fusion.2
  (78 shorter events, 3.3 us)
Async XLA Ops:
  7.2 11.2 %copy-start = (bf16[128,4096]{1,0:T(8,128)(2,1)S(1)}, bf16[128,4096]{1,0:T(8,128)(2,1)}, u32[]{:S(2)}) copy-start(bf16[128,4096]{1,0:T(8,128)(2,1)} %refs_3_.3) | copy-start | bytes 3145732
  7.2 53.3 %all-gather.3.cloned.1.call-start = ((), (), s32[]{:S(2)}) async-start(), calls=%async_computation.2 | async-start | bytes 1179648 | tf_op jit(solution)/shard_map/all_gather | solution.py:310
  8.8 3.5 %collective-permute-start.1 = (bf16[128,256]{1,0:T(8,128)(2,1)S(1)}, bf16[128,256]{1,0:T(8,128)(2,1)S(1)}, u32[]{:S(2)}, u32[]{:S(2)}) collective-permute-start(bf16[128,256]{1,0:T(8,128)(2,1)S(1)} %get-tuple-element.49), channel_id=1, source_target_pairs={{0,2},{2,0},{1,3},{3,1},{4,6},{6,4},{5,7},{7,5},{8,10},{10,8},{9,1... | collective-permute-start | bytes 196616 | tf_op jit(solution)/shard_map/ppermute | solution.py:274
  10.8 1.6 collective-permute-start.2
  10.8 1.5 collective-permute-start
  12.3 0.6 copy-start.23
  12.3 0.6 copy-start.21
  12.3 0.6 copy-start.22
  13.0 6.6 %copy-start.1 = (bf16[128,4096]{1,0:T(8,128)(2,1)S(1)}, bf16[128,4096]{1,0:T(8,128)(2,1)}, u32[]{:S(2)}) copy-start(bf16[128,4096]{1,0:T(8,128)(2,1)} %refs_5_.3) | copy-start | bytes 3145732
  17.6 84.0 %all-gather.5.cloned.1.call-start = ((), (), s32[]{:S(2)}) async-start(), calls=%async_computation.3 | async-start | bytes 1179648 | tf_op jit(solution)/shard_map/all_gather | solution.py:310
  18.3 148.8 %reduce-scatter.3.cloned.1.call-start = ((), (), s32[]{:S(2)}) async-start(), calls=%async_computation.4 | async-start | bytes 1179648 | tf_op jit(solution)/shard_map/reduce_scatter | solution.py:404
  18.4 2.2 copy-start.4
  19.2 13.5 %collective-permute-start.3 = (bf16[128,1024]{1,0:T(8,128)(2,1)}, bf16[128,1024]{1,0:T(8,128)(2,1)S(1)}, u32[]{:S(2)}, u32[]{:S(2)}) collective-permute-start(bf16[128,1024]{1,0:T(8,128)(2,1)} %get-tuple-element.37), channel_id=1, source_target_pairs={{0,2},{2,0},{1,3},{3,1},{4,6},{6,4},{5,7},{7,5},{8,10},{10,8},{9,1... | collective-permute-start | bytes 786440 | tf_op jit(solution)/shard_map/ppermute | solution.py:274
  20.4 12.4 %collective-permute-start.4 = (bf16[128,1024]{1,0:T(8,128)(2,1)}, bf16[128,1024]{1,0:T(8,128)(2,1)S(1)}, u32[]{:S(2)}, u32[]{:S(2)}) collective-permute-start(bf16[128,1024]{1,0:T(8,128)(2,1)} %get-tuple-element.35), channel_id=1, source_target_pairs={{0,2},{2,0},{1,3},{3,1},{4,6},{6,4},{5,7},{7,5},{8,10},{10,8},{9,1... | collective-permute-start | bytes 786440 | tf_op jit(solution)/shard_map/ppermute | solution.py:274
  20.6 5.4 %collective-permute-start.5 = (f32[16,128]{1,0:T(8,128)S(1)}, f32[16,128]{1,0:T(8,128)S(1)}, u32[]{:S(2)}, u32[]{:S(2)}) collective-permute-start(f32[16,128]{1,0:T(8,128)S(1)} %constant_dynamic-slice_fusion.10), channel_id=1, source_target_pairs={{0,2},{2,0},{1,3},{3,1},{4,6},{6,4},{5,7},{7,5},{8,10},{10,8},{9,1... | collective-permute-start | bytes 24584 | tf_op jit(solution)/shard_map/ppermute | solution.py:274
  20.9 5.1 %copy-start.24 = (s32[4,2]{0,1:T(2,128)S(1)}, s32[4,2]{0,1:T(2,128)}, u32[]{:S(2)}) copy-start(s32[4,2]{0,1:T(2,128)} %param.17) | copy-start | bytes 100
  20.9 39.6 %copy-start.2 = (f32[256,128]{1,0:T(8,128)S(1)}, f32[256,128]{1,0:T(8,128)}, u32[]{:S(2)}) copy-start(f32[256,128]{1,0:T(8,128)} %get-tuple-element.13.refs_1_) | copy-start | bytes 393220
  20.9 39.6 %copy-start.3 = (f32[256,128]{1,0:T(8,128)S(1)}, f32[256,128]{1,0:T(8,128)}, u32[]{:S(2)}) copy-start(f32[256,128]{1,0:T(8,128)} %get-tuple-element.14.refs_2_) | copy-start | bytes 393220
  20.9 39.6 %copy-start.5 = (s32[3]{0:T(128)S(1)}, s32[3]{0:T(128)}, u32[]{:S(2)}) copy-start(s32[3]{0:T(128)} %pad_add_fusion.where_ref) | copy-start | bytes 40
  20.9 39.6 %copy-start.20 = (s32[32]{0:T(128)S(1)}, s32[32]{0:T(128)}, u32[]{:S(2)}) copy-start(s32[32]{0:T(128)} %map_ref.3) | copy-start | bytes 388
  23.2 7.1 %collective-permute-start.6 = (bf16[64,1024]{1,0:T(8,128)(2,1)}, bf16[64,1024]{1,0:T(8,128)(2,1)S(1)}, u32[]{:S(2)}, u32[]{:S(2)}) collective-permute-start(bf16[64,1024]{1,0:T(8,128)(2,1)} %get-tuple-element.31), channel_id=1, source_target_pairs={{0,1},{1,0},{2,3},{3,2},{4,5},{5,4},{6,7},{7,6},{8,9},{9,8},{10,11... | collective-permute-start | bytes 393224 | tf_op jit(solution)/shard_map/ppermute | solution.py:356
  25.9 4.5 %collective-permute-start.7 = (bf16[64,1024]{1,0:T(8,128)(2,1)}, bf16[64,1024]{1,0:T(8,128)(2,1)S(1)}, u32[]{:S(2)}, u32[]{:S(2)}) collective-permute-start(bf16[64,1024]{1,0:T(8,128)(2,1)} %get-tuple-element.30), channel_id=1, source_target_pairs={{0,2},{1,3},{2,0},{3,1},{4,6},{5,7},{6,4},{7,5},{8,10},{9,11},{10,... | collective-permute-start | bytes 393224 | tf_op jit(solution)/shard_map/ppermute | solution.py:356
  26.0 6.8 %collective-permute-start.8 = (bf16[64,1024]{1,0:T(8,128)(2,1)}, bf16[64,1024]{1,0:T(8,128)(2,1)}, u32[]{:S(2)}, u32[]{:S(2)}) collective-permute-start(bf16[64,1024]{1,0:T(8,128)(2,1)} %get-tuple-element.27), channel_id=1, source_target_pairs={{0,3},{1,2},{2,1},{3,0},{4,7},{5,6},{6,5},{7,4},{8,11},{9,10},{10,... | collective-permute-start | bytes 393224 | tf_op jit(solution)/shard_map/ppermute | solution.py:356
  32.8 0.7 copy-start.8
  60.5 1.2 copy-start.7
  61.7 0.9 copy-start.9
  79.0 0.7 copy-start.10
  79.7 153.4 %reduce-scatter.5.cloned.1.call-start = ((), (), s32[]{:S(2)}) async-start(), calls=%async_computation.5 | async-start | bytes 1179648 | tf_op jit(solution)/shard_map/reduce_scatter | solution.py:404
  79.8 8.9 %collective-permute-start.10 = (bf16[128,1024]{1,0:T(8,128)(2,1)}, bf16[128,1024]{1,0:T(8,128)(2,1)S(1)}, u32[]{:S(2)}, u32[]{:S(2)}) collective-permute-start(bf16[128,1024]{1,0:T(8,128)(2,1)} %get-tuple-element.36), channel_id=1, source_target_pairs={{0,2},{2,0},{1,3},{3,1},{4,6},{6,4},{5,7},{7,5},{8,10},{10,8},{9,1... | collective-permute-start | bytes 786440 | tf_op jit(solution)/shard_map/ppermute | solution.py:274
  79.8 9.5 %collective-permute-start.9 = (bf16[128,1024]{1,0:T(8,128)(2,1)}, bf16[128,1024]{1,0:T(8,128)(2,1)S(1)}, u32[]{:S(2)}, u32[]{:S(2)}) collective-permute-start(bf16[128,1024]{1,0:T(8,128)(2,1)} %get-tuple-element.38), channel_id=1, source_target_pairs={{0,2},{2,0},{1,3},{3,1},{4,6},{6,4},{5,7},{7,5},{8,10},{10,8},{9,1... | collective-permute-start | bytes 786440 | tf_op jit(solution)/shard_map/ppermute | solution.py:274
  80.3 6.6 %collective-permute-start.11 = (bf16[64,1024]{1,0:T(8,128)(2,1)}, bf16[64,1024]{1,0:T(8,128)(2,1)S(1)}, u32[]{:S(2)}, u32[]{:S(2)}) collective-permute-start(bf16[64,1024]{1,0:T(8,128)(2,1)} %get-tuple-element.28), channel_id=1, source_target_pairs={{0,1},{1,0},{2,3},{3,2},{4,5},{5,4},{6,7},{7,6},{8,9},{9,8},{10,11... | collective-permute-start | bytes 393224 | tf_op jit(solution)/shard_map/ppermute | solution.py:356
  81.8 5.1 %collective-permute-start.12 = (bf16[64,1024]{1,0:T(8,128)(2,1)}, bf16[64,1024]{1,0:T(8,128)(2,1)S(1)}, u32[]{:S(2)}, u32[]{:S(2)}) collective-permute-start(bf16[64,1024]{1,0:T(8,128)(2,1)} %get-tuple-element.34), channel_id=1, source_target_pairs={{0,2},{1,3},{2,0},{3,1},{4,6},{5,7},{6,4},{7,5},{8,10},{9,11},{10,... | collective-permute-start | bytes 393224 | tf_op jit(solution)/shard_map/ppermute | solution.py:356
  81.8 6.2 %collective-permute-start.13 = (bf16[64,1024]{1,0:T(8,128)(2,1)}, bf16[64,1024]{1,0:T(8,128)(2,1)S(1)}, u32[]{:S(2)}, u32[]{:S(2)}) collective-permute-start(bf16[64,1024]{1,0:T(8,128)(2,1)} %get-tuple-element.33), channel_id=1, source_target_pairs={{0,3},{1,2},{2,1},{3,0},{4,7},{5,6},{6,5},{7,4},{8,11},{9,10},{10,... | collective-permute-start | bytes 393224 | tf_op jit(solution)/shard_map/ppermute | solution.py:356
  86.9 0.7 copy-start.16
  88.0 0.7 copy-start.18
  88.6 0.7 copy-start.12
  89.3 0.7 copy-start.14
  101.6 1.2 copy-start.6
  102.8 0.9 copy-start.13
  103.7 0.9 copy-start.15
  104.7 0.9 copy-start.17
  105.6 0.9 copy-start.19
  122.0 1.0 copy-start.11
  123.0 1.5 collective-permute-start.14
  123.0 1.9 collective-permute-start.15
  168.0 67.6 %collective-permute-start.16 = (bf16[2,128,128]{2,1,0:T(8,128)(2,1)S(1)}, bf16[2,128,128]{2,1,0:T(8,128)(2,1)S(1)}, u32[]{:S(2)}, u32[]{:S(2)}) collective-permute-start(bf16[2,128,128]{2,1,0:T(8,128)(2,1)S(1)} %dynamic-slice_bitcast_fusion.1), channel_id=1, source_target_pairs={{0,2},{2,0},{1,3},{3,1},{4,6},{6,4},{5,7},{7,5},{8,10},{10,8},{9,1... | collective-permute-start | bytes 196616 | tf_op jit(solution)/shard_map/ppermute | solution.py:274
  234.0 1.6 collective-permute-start.17
Sparse Core Ops, SparseCore 0:
  17.7 42.7 all-gather.2
  62.6 38.8 all-gather.4
  105.0 62.0 reduce-scatter.2
  170.7 62.3 reduce-scatter.4

commit v2 on v0

v2 whole, which is shorter than its diff:
```python
import functools
import math

import jax
import jax.numpy as jnp
from jax import lax
from jax.experimental import pallas as pl
from jax.experimental.pallas import tpu as pltpu
from jax.sharding import Mesh
from jax.sharding import PartitionSpec as P

HEAD_SIZE = 128
BLOCKS_DEV = 2
THETA = 1000000.0
CHUNK = 256
SCORE_SCALE = 1.0 / math.sqrt(HEAD_SIZE)
LOG2E = math.log2(math.e)
MEMORY = 56 * 1024 * 1024


def turned_tables(ids, width):
    half = width // 2
    rows = ids.shape[1]
    pair = lax.broadcasted_iota(jnp.int32, (half, rows), 0)
    first_cut = width // 8
    second_cut = first_cut + 3 * width // 16
    inverse = jnp.exp(pair.astype(jnp.float32) * jnp.float32(-2.0 * math.log(THETA) / width))
    ids = ids.astype(jnp.float32)
    picked = jnp.where(
        pair < first_cut, ids[0:1, :], jnp.where(pair < second_cut, ids[1:2, :], ids[2:3, :])
    )
    angles = picked * inverse
    cosine = jnp.cos(angles)
    sine = jnp.sin(angles)
    return (
        jnp.concatenate([cosine, cosine], axis=0).T,
        jnp.concatenate([sine, sine], axis=0).T,
    )


def half_sign():
    lane = lax.broadcasted_iota(jnp.int32, (1, HEAD_SIZE), 1)
    return jnp.where(lane < HEAD_SIZE // 2, -1.0, 1.0).astype(jnp.float32)


def head_lanes(member, flip, heads, head):
    first = ((member ^ flip) * heads + head) * HEAD_SIZE
    return pl.ds(pl.multiple_of(first, HEAD_SIZE), HEAD_SIZE)


def first_kernel(members, with_piece, where_ref, ids_ref, k_ref, v_ref, *refs):
    refs = list(refs)
    if with_piece:
        grad_ref = refs.pop(0)
        copy_sem = refs.pop()
        piece_ref = refs.pop()
        width = piece_ref.shape[1]
        start = pl.multiple_of((1 - where_ref[1]) * width, width)
        copy = pltpu.make_async_copy(grad_ref.at[:, pl.ds(start, width)], piece_ref, copy_sem)
        copy.start()
    cos_ref, sin_ref = refs.pop(0), refs.pop(0)
    member = where_ref[0]
    cosine, sine = turned_tables(ids_ref[...], HEAD_SIZE)
    cos_ref[...] = cosine
    sin_ref[...] = sine
    signed = sine * half_sign()
    for flip in range(members):
        lanes = head_lanes(member, flip, 1, 0)
        keys = k_ref[:, lanes].astype(jnp.float32)
        refs[flip][0] = (keys * cosine + pltpu.roll(keys, HEAD_SIZE // 2, 1) * signed).astype(
            jnp.bfloat16
        )
        refs[flip][1] = v_ref[:, lanes]
    if with_piece:
        copy.wait()


def query_kernel(members, group, where_ref, cos_ref, sin_ref, q_ref, *out_refs):
    member = where_ref[0]
    cosine = cos_ref[...]
    signed = sin_ref[...] * half_sign()
    for flip in range(members):
        for head in range(group):
            field = q_ref[:, head_lanes(member, flip, group, head)].astype(jnp.float32)
            turned = pltpu.roll(field, HEAD_SIZE // 2, 1)
            out_refs[flip][:, head * HEAD_SIZE : (head + 1) * HEAD_SIZE] = (
                field * cosine + turned * signed
            ).astype(jnp.bfloat16)


def delta_kernel(members, group, where_ref, a_ref, l_ref, *refs):
    refs = list(refs)
    own_ref = refs.pop(0)
    other_ref = refs.pop(0) if members > 1 else None
    grad_refs, stat_refs = refs[:members], refs[members:]
    member, tp_index = where_ref[0], where_ref[1]
    rows = a_ref.shape[0]
    for flip in range(members):
        g_ref = grad_refs[flip]
        sums = []
        for head in range(group):
            lanes = head_lanes(member, flip, group, head)
            here = slice(head * HEAD_SIZE, (head + 1) * HEAD_SIZE)
            if members > 1:
                half = rows // 2
                mine = pl.multiple_of(tp_index * half, half)
                theirs = pl.multiple_of((1 - tp_index) * half, half)
                g_ref[pl.ds(mine, half), here] = own_ref[:, lanes]
                g_ref[pl.ds(theirs, half), here] = other_ref[:, lanes]
            else:
                g_ref[:, here] = own_ref[:, lanes]
            product = g_ref[:, here].astype(jnp.float32) * a_ref[:, lanes].astype(jnp.float32)
            sums.append(jnp.sum(product.T, axis=0, keepdims=True))
        first = pl.multiple_of((member ^ flip) * group, group)
        stat_refs[flip][0:group, :] = l_ref[pl.ds(first, group), :] * LOG2E
        stat_refs[flip][group : 2 * group, :] = jnp.concatenate(sums, axis=0)


def row_vector(table, upper, block_len):
    group, width = table.shape
    rolled = pltpu.roll(table, block_len, 1)
    low, high = (table, rolled) if upper == 0 else (rolled, table)
    lane = lax.broadcasted_iota(jnp.int32, (1, width), 1)
    pieces = [
        jnp.where(lane < block_len, low[h : h + 1, :], high[h + 1 : h + 2, :])
        for h in range(0, group, 2)
    ]
    return jnp.concatenate(pieces, axis=1)


def attend_kernel(members, group, block_len, slabs, where_ref, map_ref, span_ref, *refs):
    refs = list(refs)
    kv_refs = [refs.pop(0) for _ in range(slabs)]
    q_refs = [refs.pop(0) for _ in range(members)]
    g_refs = [refs.pop(0) for _ in range(members)]
    s_refs = [refs.pop(0) for _ in range(members)]
    dq_refs = [refs.pop(0) for _ in range(members)]
    part_refs = [refs.pop(0) for _ in range(slabs)]
    k_sort, v_sort, k_turn, q_all, g_all, l_all, d_all, dk_sum, dv_sum, dq_sum = refs
    member, layer, layers, device = where_ref[0], where_ref[2], where_ref[3], where_ref[4]
    rows = q_refs[0].shape[0]
    units = kv_refs[0].shape[0]
    spans = span_ref.shape[0] // 2
    columns = group * block_len

    def sequence_block(slab, unit, step):
        if members > 1:
            owner = lax.rem(layer - slab + layers, layers) * members + (member ^ unit)
        else:
            owner = unit
        return map_ref[owner * BLOCKS_DEV + step]

    def each_block(body):
        for slab in range(slabs):

            @pl.loop(0, units)
            def _(unit):
                for step in range(BLOCKS_DEV):
                    at = pl.multiple_of(sequence_block(slab, unit, step) * block_len, block_len)
                    body(slab, unit, step * block_len, pl.ds(at, block_len))

    def sort(slab, unit, row, to):
        k_sort[to, :] = kv_refs[slab][unit, 0, pl.ds(row, block_len), :]
        v_sort[to, :] = kv_refs[slab][unit, 1, pl.ds(row, block_len), :]

    each_block(sort)

    @pl.loop(0, k_turn.shape[0])
    def _(chunk):
        at = pl.multiple_of(chunk * CHUNK, CHUNK)
        k_turn[chunk] = k_sort[pl.ds(at, CHUNK), :].T
        dk_sum[pl.ds(at, CHUNK), :] = jnp.zeros((CHUNK, HEAD_SIZE), jnp.float32)
        dv_sum[pl.ds(at, CHUNK), :] = jnp.zeros((CHUNK, HEAD_SIZE), jnp.float32)

    for flip in range(members):
        lse, delta = s_refs[flip][0:group, :], s_refs[flip][group : 2 * group, :]
        for step in range(BLOCKS_DEV):
            place = flip * BLOCKS_DEV + step
            from_rows = slice(step * block_len, (step + 1) * block_len)
            for head in range(group):
                lanes = slice(head * HEAD_SIZE, (head + 1) * HEAD_SIZE)
                to_rows = slice(head * block_len, (head + 1) * block_len)
                q_all[place, to_rows, :] = q_refs[flip][from_rows, lanes]
                g_all[place, to_rows, :] = g_refs[flip][from_rows, lanes]
            l_all[place] = row_vector(lse, step, block_len)
            d_all[place] = row_vector(delta, step, block_len)

    lane = lax.broadcasted_iota(jnp.int32, (1, columns), 1)
    within = lax.rem(lane, block_len)
    key_row = lax.broadcasted_iota(jnp.int32, (CHUNK, 1), 0)

    for flip in range(members):
        for step in range(BLOCKS_DEV):
            place = flip * BLOCKS_DEV + step
            owner = device if members == 1 else layer * members + (member ^ flip)
            block = map_ref[owner * BLOCKS_DEV + step]
            end = jnp.int32(0)
            for span in range(spans):
                inside = (block >= span_ref[2 * span]) & (block < span_ref[2 * span + 1])
                end = jnp.where(inside, span_ref[2 * span + 1], end)
            limit = jnp.where(end > 0, end * block_len, block * block_len + within + 1)
            last = jnp.maximum(end, block + 1) * block_len
            chunks = (last + CHUNK - 1) // CHUNK
            queries = q_all[place]
            grads = g_all[place]
            lse = l_all[place]
            delta = d_all[place]
            dq_sum[...] = jnp.zeros_like(dq_sum)

            @pl.loop(0, chunks)
            def _(chunk):
                at = pl.multiple_of(chunk * CHUNK, CHUNK)
                keys = k_sort[pl.ds(at, CHUNK), :]
                values = v_sort[pl.ds(at, CHUNK), :]
                scores = lax.dot_general(
                    keys, queries, (((1,), (1,)), ((), ())), preferred_element_type=jnp.float32
                )
                raised = scores * (SCORE_SCALE * LOG2E) - lse
                raised = jnp.where(key_row + at < limit, raised, -jnp.inf)
                probs = jnp.exp2(raised)
                grad_p = lax.dot_general(
                    values, grads, (((1,), (1,)), ((), ())), preferred_element_type=jnp.float32
                )
                grad_s = (probs * (grad_p - delta)).astype(jnp.bfloat16)
                dv_sum[pl.ds(at, CHUNK), :] += jnp.dot(
                    probs.astype(jnp.bfloat16), grads, preferred_element_type=jnp.float32
                )
                dk_sum[pl.ds(at, CHUNK), :] += jnp.dot(
                    grad_s, queries, preferred_element_type=jnp.float32
                )
                dq_sum[...] += jnp.dot(k_turn[chunk], grad_s, preferred_element_type=jnp.float32)

            dq_rot = (dq_sum[...].T * SCORE_SCALE).astype(jnp.bfloat16)
            for head in range(group):
                dq_refs[flip][
                    step * block_len : (step + 1) * block_len,
                    head * HEAD_SIZE : (head + 1) * HEAD_SIZE,
                ] = dq_rot[head * block_len : (head + 1) * block_len, :]

    def unsort(slab, unit, row, at):
        kind = part_refs[slab].dtype
        here = pl.ds(row, block_len)
        part_refs[slab][unit, 0, here, :] = (dk_sum[at, :] * SCORE_SCALE).astype(kind)
        part_refs[slab][unit, 1, here, :] = dv_sum[at, :].astype(kind)

    each_block(unsort)


def turned_back(field, cosine, signed):
    return field * cosine - pltpu.roll(field, HEAD_SIZE // 2, 1) * signed


def query_gradient_kernel(members, group, where_ref, cos_ref, sin_ref, *refs):
    member = where_ref[0]
    cosine = cos_ref[...]
    signed = sin_ref[...] * half_sign()
    for flip in range(members):
        for head in range(group):
            field = refs[flip][:, head * HEAD_SIZE : (head + 1) * HEAD_SIZE].astype(jnp.float32)
            refs[members][:, head_lanes(member, flip, group, head)] = turned_back(
                field, cosine, signed
            ).astype(jnp.bfloat16)


def last_kernel(members, where_ref, cos_ref, sin_ref, *refs):
    member = where_ref[0]
    dk_ref, dv_ref = refs[members], refs[members + 1]
    cosine = cos_ref[...]
    signed = sin_ref[...] * half_sign()
    for flip in range(members):
        lanes = head_lanes(member, flip, 1, 0)
        field = refs[flip][0].astype(jnp.float32)
        dk_ref[:, lanes] = turned_back(field, cosine, signed).astype(jnp.bfloat16)
        dv_ref[:, lanes] = refs[flip][1].astype(jnp.bfloat16)


def whole(shape):
    return pl.BlockSpec(shape, lambda *_: (0,) * len(shape))


def call(kernel, name, scalars, inputs, outputs, in_specs=None, out_specs=None, scratch=(), cost=None):
    return pl.pallas_call(
        kernel,
        grid_spec=pltpu.PrefetchScalarGridSpec(
            num_scalar_prefetch=len(scalars),
            grid=(1,),
            in_specs=in_specs or [whole(a.shape) for a in inputs],
            out_specs=out_specs or [whole(shape) for shape, _ in outputs],
            scratch_shapes=list(scratch),
        ),
        out_shape=[jax.ShapeDtypeStruct(shape, kind) for shape, kind in outputs],
        compiler_params=pltpu.CompilerParams(vmem_limit_bytes=MEMORY),
        cost_estimate=cost,
        name=name,
    )(*scalars, *inputs)


def shards(
    queries, keys, values, attn_out, out_grad, logsumexp, position_ids, block_map, span_blocks
):
    rows = queries.shape[0]
    kv_heads = keys.shape[1] // HEAD_SIZE
    group = queries.shape[1] // keys.shape[1]
    block_len = rows // BLOCKS_DEV
    layers = lax.axis_size("z")
    members = 4 if kv_heads == 4 and lax.axis_size("tp") == 2 else 1
    tp_index = lax.axis_index("tp")
    layer = lax.axis_index("z")
    in_slab = lax.axis_index("y") * 2 + lax.axis_index("core")
    device = layer * 4 + in_slab
    member = in_slab if members > 1 else jnp.zeros_like(in_slab)
    place = jnp.stack([member, tp_index, layer, jnp.full_like(layer, layers), device])
    place = place.astype(jnp.int32)
    width = group * HEAD_SIZE
    bf16, f32 = jnp.bfloat16, jnp.float32

    def flipped(array, flip):
        if flip == 0:
            return array
        return lax.ppermute(array, ("y", "core"), [(i, i ^ flip) for i in range(4)])

    def climbed(array, steps):
        route = [(i, (i + steps) % layers) for i in range(layers)]
        return lax.ppermute(array, "z", route)

    every = range(members)
    table = ((rows, HEAD_SIZE), f32)
    pair = (2, rows, HEAD_SIZE)

    inputs = [position_ids, keys, values]
    outputs = [table, table] + [(pair, bf16)] * members
    in_specs = [whole(a.shape) for a in inputs]
    out_specs = [whole(shape) for shape, _ in outputs]
    scratch = []
    if members > 1:
        inputs.append(out_grad)
        in_specs.append(pl.BlockSpec(memory_space=pl.ANY))
        outputs.append(((out_grad.shape[0], members * width), bf16))
        out_specs.append(pl.BlockSpec(memory_space=pl.ANY))
        scratch = [pltpu.SemaphoreType.DMA]
    results = call(
        functools.partial(first_kernel, members, members > 1),
        "first", [place], inputs, outputs, in_specs, out_specs, scratch,
    )
    cosine, sine = results[:2]
    kv_pieces = results[2 : 2 + members]
    if members > 1:
        slab = jnp.stack([flipped(kv_pieces[f], f) for f in every])
        grads_other = lax.ppermute(results[-1], "tp", [(0, 1), (1, 0)])
        kv = [slab] + [climbed(slab, k) for k in range(1, layers)]
        slabs = layers
    else:
        kv = [lax.all_gather(kv_pieces[0], ("z", "y", "core"), axis=0, tiled=False)]
        slabs = 1
        grads_own = lax.all_to_all(out_grad, "tp", split_axis=1, concat_axis=0, tiled=True)

    q_pieces = call(
        functools.partial(query_kernel, members, group),
        "rotate", [place], [cosine, sine, queries], [((rows, width), bf16)] * members,
    )
    q_in = [flipped(q_pieces[f], f) for f in every]

    inputs = [attn_out, logsumexp]
    in_specs = [whole(a.shape) for a in inputs]
    if members > 1:
        inputs += [out_grad, grads_other]
        in_specs += [
            pl.BlockSpec(grads_other.shape, lambda i, where: (0, where[1])),
            whole(grads_other.shape),
        ]
    else:
        inputs += [grads_own]
        in_specs += [whole(grads_own.shape)]
    results = call(
        functools.partial(delta_kernel, members, group),
        "delta", [place], inputs,
        [((rows, width), bf16)] * members + [((2 * group, rows), f32)] * members,
        in_specs,
    )
    g_in = [flipped(results[f], f) for f in every]
    s_in = [flipped(results[members + f], f) for f in every]

    units = kv[0].shape[0]
    tokens = slabs * units * rows
    columns = group * block_len
    blocks = members * BLOCKS_DEV
    part = (units, 2, rows, HEAD_SIZE)
    kinds = [f32] + [bf16] * (slabs - 1) if members > 1 else [bf16]
    results = call(
        functools.partial(attend_kernel, members, group, block_len, slabs),
        "attend", [place, block_map, span_blocks.reshape(-1)],
        [*kv, *q_in, *g_in, *s_in],
        [((rows, width), bf16)] * members + [(part, kind) for kind in kinds],
        scratch=[
            pltpu.VMEM((tokens, HEAD_SIZE), bf16),
            pltpu.VMEM((tokens, HEAD_SIZE), bf16),
            pltpu.VMEM((tokens // CHUNK, HEAD_SIZE, CHUNK), bf16),
            pltpu.VMEM((blocks, columns, HEAD_SIZE), bf16),
            pltpu.VMEM((blocks, columns, HEAD_SIZE), bf16),
            pltpu.VMEM((blocks, 1, columns), f32),
            pltpu.VMEM((blocks, 1, columns), f32),
            pltpu.VMEM((tokens, HEAD_SIZE), f32),
            pltpu.VMEM((tokens, HEAD_SIZE), f32),
            pltpu.VMEM((HEAD_SIZE, columns), f32),
        ],
        cost=pl.CostEstimate(
            flops=6 * group * members * rows * tokens * HEAD_SIZE,
            bytes_accessed=6 * 1024 * 1024,
            transcendentals=group * members * rows * tokens // 2,
        ),
    )
    dq_pieces, parts = results[:members], results[members:]
    if members > 1:
        total = parts[0]
        for k in range(1, layers):
            total = total + climbed(parts[k], layers - k).astype(f32)
        sums = [flipped(total[f].astype(bf16), f) for f in every]
    else:
        sums = [
            lax.psum_scatter(parts[0], ("z", "y", "core"), scatter_dimension=0, tiled=True)[0]
        ]
    (grad_q,) = call(
        functools.partial(query_gradient_kernel, members, group),
        "turn_back", [place],
        [cosine, sine] + [flipped(dq_pieces[f], f) for f in every],
        [(queries.shape, bf16)],
    )
    key_gradient, value_gradient = call(
        functools.partial(last_kernel, members),
        "last", [place], [cosine, sine, *sums],
        [(keys.shape, bf16), (values.shape, bf16)],
    )
    return (grad_q, key_gradient, value_gradient)


def solution(mesh):
    ctx, tp = mesh.shape["ctx"], mesh.shape["tp"]
    fine = Mesh(mesh.devices.reshape(ctx // 4, 2, 2, tp), ("z", "y", "core", "tp"))
    ctx_axes = ("z", "y", "core")
    return jax.shard_map(
        shards,
        mesh=fine,
        in_specs=(
            P(ctx_axes, "tp"),
            P(ctx_axes, "tp"),
            P(ctx_axes, "tp"),
            P(ctx_axes, "tp"),
            P((*ctx_axes, "tp"), None),
            P("tp", ctx_axes),
            P(None, ctx_axes),
            P(),
            P(),
        ),
        out_specs=(P(ctx_axes, "tp"), P(ctx_axes, "tp"), P(ctx_axes, "tp")),
        check_vma=False,
    )
```

time: 447 us -> 129 us (0.29)
  waiting for transfers between devices: 155 us -> 36.5 us
  other arithmetic: 110 us -> 1.2 us
  local copies, waits for them, and re-layouts: 90.7 us -> 4.22 us
  matrix products: 65.9 us -> 0 us
  Pallas kernels: 0 us -> 60.4 us
  starting transfers between devices: 6.93 us -> 23.9 us
  loops' own time: 10.8 us -> 0 us
    ppermute x31 -> x25, waiting for transfers between devices: 155 us -> 36.5 us  [the longest x6 32.7 us: climbed(): return lax.ppermute(array, 'z', route)]
    dot_general x75 -> x0, matrix products: 65.9 us -> none  [the longest x15 30.2 us: compute(): jnp.einsum('kgqd,kcd->kgqc', q_rot, k_part, preferred_element_type=jnp.fl...]
    pallas_call x0 -> x6, Pallas kernels: none -> 60.4 us  [call(): pl.pallas_call(kernel, grid_spec=pltpu.PrefetchScalarGridSpec(num_scalar_...]
    while x30 -> x0, local copies, waits for them, and re-layouts: 39.3 us -> none
    add x30 -> x0, other arithmetic: 37.1 us -> none  [the longest x14 26.9 us: compute(): grads_total + jnp.stack([key_grad, value_grad])]
    reduce_or x16 -> x0, other arithmetic: 21.8 us -> none  [visit_block(): jnp.any((their_blocks[None, :] <= my_blocks[:, None]) | block_shared)]
    ppermute x31 -> x25, starting transfers between devices: 2.59 us -> 23.9 us  [the longest x18 11.2 us: flipped(): return lax.ppermute(array, ('y', 'core'), [(i, i ^ flip) for i in range(4)])]
    reduce_sum x18 -> x0, other arithmetic: 14.9 us -> none  [the longest x16 14.2 us: token_info(): spans_of = jnp.sum(jnp.where(matched, block_span[None, :], 0), axis=1)]
  transfers between devices with their start and end apart: 32 -> 25, of which waited for: 16 -> 7; matrix products, arithmetic and copies ran while one was open for 23% -> 2% of each run, Pallas kernels for 0% -> 8%
where the time goes in v2:
time: 129 us; the launch traced here: 127 us
  Pallas kernels  60.4 us (47%)
  waiting for transfers between devices  36.5 us (28%)
  starting transfers between devices  23.9 us (19%)
  local copies, waits for them, and re-layouts  4.22 us (3%)
    pallas_call x6, Pallas kernels, call(): pl.pallas_call(kernel, grid_spec=pltpu.PrefetchScalarGridSpec(num_scalar_...  60.4 us
    ppermute x6, waiting for transfers between devices, climbed(): return lax.ppermute(array, 'z', route)  32.7 us
    ppermute x18, starting transfers between devices, flipped(): return lax.ppermute(array, ('y', 'core'), [(i, i ^ flip) for i in range(4)])  11.2 us
    ppermute x6, starting transfers between devices, climbed(): return lax.ppermute(array, 'z', route)  9.7 us
    ppermute x1, starting transfers between devices, shards(): grads_other = lax.ppermute(results[-1], 'tp', [(0, 1), (1, 0)])  3 us
  transfers between devices with their start and end apart: 25, of which 7 were waited for; matrix products, arithmetic and copies ran while one was open for 2% of the time, Pallas kernels for 8%

profile of v2, /device:TPU:0, one launch (start us, length us, event | category | flops | bytes accessed | tf_op | source)
XLA Modules:
  0.0 127.1 jit_solution(2482115716910896100)
XLA Ops:
  0.6 0.6 stack.34.where_ref
  1.2 19.4 %first.1 = (f32[128,128]{1,0:T(8,128)}, f32[128,128]{1,0:T(8,128)}, bf16[2,128,128]{2,1,0:T(8,128)(2,1)}, bf16[2,128,128]{2,1,0:T(8,128)(2,1)}, bf16[2,128,128]{...) custom-call(s32[5]{0:T(128)} %stack.34.where_ref, s32[3,128]{1,0:T(4,128)} %ids_ref.1, ...), custom_call_target="tpu_custom_call" | custom-call | tf_op jit(solution)/shard_map/first/pallas_call | solution.py:282
  20.6 3.0 %collective-permute-start.9 = (bf16[64,4096]{1,0:T(8,128)(2,1)}, bf16[64,4096]{1,0:T(8,128)(2,1)S(1)}, u32[]{:S(2)}, u32[]{:S(2)}) collective-permute-start(bf16[64,4096]{1,0:T(8,128)(2,1)} %get-tuple-element.42), channel_id=1, source_target_pairs={{0,1},{1,0},{2,3},{3,2},{4,5},{5,4},{6,7},{7,6},{8,9},{9,8},{10,11... | collective-permute-start | bytes 1572872 | tf_op jit(solution)/shard_map/ppermute | solution.py:349
  23.6 1.5 %collective-permute-start.1 = (bf16[2,128,128]{2,1,0:T(8,128)(2,1)}, bf16[2,128,128]{2,1,0:T(8,128)(2,1)S(1)}, u32[]{:S(2)}, u32[]{:S(2)}) collective-permute-start(bf16[2,128,128]{2,1,0:T(8,128)(2,1)} %get-tuple-element.36), channel_id=1, source_target_pairs={{0,4},{2,6},{4,0},{6,2},{1,5},{3,7},{5,1},{7,3},{8,12},{10,14},{12... | collective-permute-start | bytes 196616 | tf_op jit(solution)/shard_map/ppermute | solution.py:320
  25.1 0.3 collective-permute-start.2
  25.5 3.4 %rotate.1 = (bf16[128,1024]{1,0:T(8,128)(2,1)}, bf16[128,1024]{1,0:T(8,128)(2,1)}, bf16[128,1024]{1,0:T(8,128)(2,1)}, bf16[128,1024]{1,0:T(8,128)(2,1)}) custom-call(s32[5]{0:T(128)} %stack.34.where_ref, f32[128,128]{1,0:T(8,128)} %get-tuple-element.32.cos_ref, f32[128,128]{1,0:T(8,128)} %get-tuple-element.33.sin_ref, bf16[128,4096]{1,0:T(8,128)(2,1)} %q_ref.1), custom_call_target="tpu_custom_call" | custom-call | tf_op jit(solution)/shard_map/rotate/pallas_call | solution.py:282
  28.9 0.3 collective-permute-start.6
  29.2 1.5 %collective-permute-start.7 = (bf16[128,1024]{1,0:T(8,128)(2,1)}, bf16[128,1024]{1,0:T(8,128)(2,1)S(1)}, u32[]{:S(2)}, u32[]{:S(2)}) collective-permute-start(bf16[128,1024]{1,0:T(8,128)(2,1)} %get-tuple-element.40), channel_id=1, source_target_pairs={{0,4},{2,6},{4,0},{6,2},{1,5},{3,7},{5,1},{7,3},{8,12},{10,14},{12... | collective-permute-start | bytes 786440 | tf_op jit(solution)/shard_map/ppermute | solution.py:320
  30.7 0.1 collective-permute-start.8
  30.9 3.7 %collective-permute-start.5 = (bf16[4,2,128,128]{3,2,1,0:T(8,128)(2,1)S(1)}, bf16[4,2,128,128]{3,2,1,0:T(8,128)(2,1)S(1)}, u32[]{:S(2)}, u32[]{:S(2)}) collective-permute-start(bf16[4,2,128,128]{3,2,1,0:T(8,128)(2,1)S(1)} %pad_maximum_fusion.refs_0_), channel_id=1, source_target_pairs={{0,24},{8,0},{16,8},{24,16},{1,25},{9,1},{17,9},{25,17},{2,26},{10... | collective-permute-start | bytes 786440 | tf_op jit(solution)/shard_map/ppermute | solution.py:324
  34.5 1.2 collective-permute-done.9.refs_1_
  35.8 1.8 %collective-permute-start.3 = (bf16[4,2,128,128]{3,2,1,0:T(8,128)(2,1)S(1)}, bf16[4,2,128,128]{3,2,1,0:T(8,128)(2,1)S(1)}, u32[]{:S(2)}, u32[]{:S(2)}) collective-permute-start(bf16[4,2,128,128]{3,2,1,0:T(8,128)(2,1)S(1)} %pad_maximum_fusion.refs_0_), channel_id=1, source_target_pairs={{0,8},{8,16},{16,24},{24,0},{1,9},{9,17},{17,25},{25,1},{2,10},{10... | collective-permute-start | bytes 786440 | tf_op jit(solution)/shard_map/ppermute | solution.py:324
  37.6 3.9 %delta.1 = (bf16[128,1024]{1,0:T(8,128)(2,1)}, bf16[128,1024]{1,0:T(8,128)(2,1)}, bf16[128,1024]{1,0:T(8,128)(2,1)}, bf16[128,1024]{1,0:T(8,128)(2,1)}, f32[16,1...) custom-call(s32[5]{0:T(128)} %stack.34.where_ref, bf16[128,4096]{1,0:T(8,128)(2,1)} %a_ref.1, ...), custom_call_target="tpu_custom_call" | custom-call | tf_op jit(solution)/shard_map/delta/pallas_call | solution.py:282
  41.5 0.1 collective-permute-start.10
  41.6 1.2 collective-permute-done.8.refs_7_
  42.8 1.5 %collective-permute-start.11 = (bf16[128,1024]{1,0:T(8,128)(2,1)}, bf16[128,1024]{1,0:T(8,128)(2,1)S(1)}, u32[]{:S(2)}, u32[]{:S(2)}) collective-permute-start(bf16[128,1024]{1,0:T(8,128)(2,1)} %get-tuple-element.45), channel_id=1, source_target_pairs={{0,4},{2,6},{4,0},{6,2},{1,5},{3,7},{5,1},{7,3},{8,12},{10,14},{12... | collective-permute-start | bytes 786440 | tf_op jit(solution)/shard_map/ppermute | solution.py:320
  44.3 0.7 collective-permute-start.12
  45.0 12.6 %collective-permute-done.4.refs_2_ = bf16[4,2,128,128]{3,2,1,0:T(8,128)(2,1)S(1)} collective-permute-done((bf16[4,2,128,128]{3,2,1,0:T(8,128)(2,1)S(1)}, bf16[4,2,128,128]{3,2,1,0:T(8,128)(2,1)S(1)}, u32[]{:S(2)}, u32[]{:S(2)}) %collective-permute-start.4) | collective-permute-done | bytes 262176 | tf_op jit(solution)/shard_map/ppermute | solution.py:324
  57.6 0.0 copy-start.9
  57.6 1.6 %collective-permute-start.14 = (f32[16,128]{1,0:T(8,128)}, f32[16,128]{1,0:T(8,128)S(1)}, u32[]{:S(2)}, u32[]{:S(2)}) collective-permute-start(f32[16,128]{1,0:T(8,128)} %get-tuple-element.49), channel_id=1, source_target_pairs={{0,4},{2,6},{4,0},{6,2},{1,5},{3,7},{5,1},{7,3},{8,12},{10,14},{12... | collective-permute-start | bytes 24584 | tf_op jit(solution)/shard_map/ppermute | solution.py:320
  59.2 1.1 collective-permute-start.15
  60.2 0.1 copy.13
  60.3 0.6 reshape.13.span_ref
  61.0 0.6 collective-permute-done.14.refs_14_
  61.5 0.8 collective-permute-done.15.refs_15_
  62.4 0.5 copy-done.22
  62.9 0.1 copy-done.16
  63.0 0.1 copy-done.17
  63.1 0.1 copy-done.18
  63.2 27.9 %attend.1 = (bf16[128,1024]{1,0:T(8,128)(2,1)}, bf16[128,1024]{1,0:T(8,128)(2,1)}, bf16[128,1024]{1,0:T(8,128)(2,1)}, bf16[128,1024]{1,0:T(8,128)(2,1)}, f32[4,2...) custom-call(s32[5]{0:T(128)} %stack.34.where_ref, ...), custom_call_target="tpu_custom_call" | custom-call | flops 6442450944 | bytes 6291456 | tf_op jit(solution)/shard_map/attend/pallas_call | solution.py:282
  91.1 2.3 %collective-permute-start.20 = (bf16[4,2,128,128]{3,2,1,0:T(8,128)(2,1)}, bf16[4,2,128,128]{3,2,1,0:T(8,128)(2,1)S(1)}, u32[]{:S(2)}, u32[]{:S(2)}) collective-permute-start(bf16[4,2,128,128]{3,2,1,0:T(8,128)(2,1)} %get-tuple-element.57), channel_id=1, source_target_pairs={{0,16},{8,24},{16,0},{24,8},{1,17},{9,25},{17,1},{25,9},{2,18},{10... | collective-permute-start | bytes 786440 | tf_op jit(solution)/shard_map/ppermute | solution.py:324
  93.3 1.9 %collective-permute-start.21 = (bf16[4,2,128,128]{3,2,1,0:T(8,128)(2,1)}, bf16[4,2,128,128]{3,2,1,0:T(8,128)(2,1)S(1)}, u32[]{:S(2)}, u32[]{:S(2)}) collective-permute-start(bf16[4,2,128,128]{3,2,1,0:T(8,128)(2,1)} %get-tuple-element.58), channel_id=1, source_target_pairs={{0,8},{8,16},{16,24},{24,0},{1,9},{9,17},{17,25},{25,1},{2,10},{10... | collective-permute-start | bytes 786440 | tf_op jit(solution)/shard_map/ppermute | solution.py:324
  95.3 0.7 collective-permute-start.17
  96.0 4.5 %collective-permute-done.19 = bf16[4,2,128,128]{3,2,1,0:T(8,128)(2,1)S(1)} collective-permute-done((bf16[4,2,128,128]{3,2,1,0:T(8,128)(2,1)}, bf16[4,2,128,128]{3,2,1,0:T(8,128)(2,1)S(1)}, u32[]{:S(2)}, u32[]{:S(2)}) %collective-permute-start.19) | collective-permute-done | bytes 262176 | tf_op jit(solution)/shard_map/ppermute | solution.py:324
  100.5 15.6 %collective-permute-done.20 = bf16[4,2,128,128]{3,2,1,0:T(8,128)(2,1)S(1)} collective-permute-done((bf16[4,2,128,128]{3,2,1,0:T(8,128)(2,1)}, bf16[4,2,128,128]{3,2,1,0:T(8,128)(2,1)S(1)}, u32[]{:S(2)}, u32[]{:S(2)}) %collective-permute-start.20) | collective-permute-done | bytes 262176 | tf_op jit(solution)/shard_map/ppermute | solution.py:324
  116.1 1.2 add_convert_fusion
  117.3 0.6 slice_bitcast_fusion
  117.9 0.7 collective-permute-start.24
  118.7 0.8 collective-permute-start.23
  119.5 0.3 collective-permute-start.22
  119.8 0.4 copy-done.1
  120.2 0.3 copy-done.2
  120.5 0.1 copy-done.3
  120.6 3.4 %turn_back.1 = bf16[128,4096]{1,0:T(8,128)(2,1)} custom-call(s32[5]{0:T(128)} %stack.34.where_ref, f32[128,128]{1,0:T(8,128)} %get-tuple-element.32.cos_ref, f32[128,128]{1,0:T(8,128)} %get-tuple-element.33.sin_ref, bf16[128,1024]{1,0:T(8,128)(2,1)} %get-tuple-element.51.refs_0_, bf16[128,1024]{1,0:T(8,128)(2,1)} %copy-done.1, bf16[128,1024]{1,0:T(8,128)(2,1)} %copy-done.2, ...), custom_call_target="tpu_custom_call" | custom-call | tf_op jit(solution)/shard_map/turn_back/pallas_call | solution.py:282
  124.1 0.6 copy-done.5
  124.7 0.0 copy-done.6
  124.7 0.0 copy-done.7
  124.7 2.4 %last.1 = (bf16[128,512]{1,0:T(8,128)(2,1)}, bf16[128,512]{1,0:T(8,128)(2,1)}) custom-call(s32[5]{0:T(128)} %stack.34.where_ref, f32[128,128]{1,0:T(8,128)} %get-tuple-element.32.cos_ref, f32[128,128]{1,0:T(8,128)} %get-tuple-element.33.sin_ref, bf16[2,128,128]{2,1,0:T(8,128)(2,1)} %get-tuple-element.64.refs_0_, bf16[2,128,128]{2,1,0:T(8,128)(2,1)} %copy-done.7, ...), custom_call_target="tpu_custom_call" | custom-call | tf_op jit(solution)/shard_map/last/pallas_call | solution.py:282
  (60 shorter events, 0.2 us)
Async XLA Ops:
  20.6 15.1 %collective-permute-start.9 = (bf16[64,4096]{1,0:T(8,128)(2,1)}, bf16[64,4096]{1,0:T(8,128)(2,1)S(1)}, u32[]{:S(2)}, u32[]{:S(2)}) collective-permute-start(bf16[64,4096]{1,0:T(8,128)(2,1)} %get-tuple-element.42), channel_id=1, source_target_pairs={{0,1},{1,0},{2,3},{3,2},{4,5},{5,4},{6,7},{7,6},{8,9},{9,8},{10,11... | collective-permute-start | bytes 1572872 | tf_op jit(solution)/shard_map/ppermute | solution.py:349
  23.6 5.6 %collective-permute-start = (bf16[2,128,128]{2,1,0:T(8,128)(2,1)}, bf16[2,128,128]{2,1,0:T(8,128)(2,1)S(1)}, u32[]{:S(2)}, u32[]{:S(2)}) collective-permute-start(bf16[2,128,128]{2,1,0:T(8,128)(2,1)} %get-tuple-element.35), channel_id=1, source_target_pairs={{0,2},{2,0},{4,6},{6,4},{1,3},{3,1},{5,7},{7,5},{8,10},{10,8},{12,... | collective-permute-start | bytes 196616 | tf_op jit(solution)/shard_map/ppermute | solution.py:320
  23.6 7.1 %collective-permute-start.1 = (bf16[2,128,128]{2,1,0:T(8,128)(2,1)}, bf16[2,128,128]{2,1,0:T(8,128)(2,1)S(1)}, u32[]{:S(2)}, u32[]{:S(2)}) collective-permute-start(bf16[2,128,128]{2,1,0:T(8,128)(2,1)} %get-tuple-element.36), channel_id=1, source_target_pairs={{0,4},{2,6},{4,0},{6,2},{1,5},{3,7},{5,1},{7,3},{8,12},{10,14},{12... | collective-permute-start | bytes 196616 | tf_op jit(solution)/shard_map/ppermute | solution.py:320
  25.1 5.7 %collective-permute-start.2 = (bf16[2,128,128]{2,1,0:T(8,128)(2,1)}, bf16[2,128,128]{2,1,0:T(8,128)(2,1)S(1)}, u32[]{:S(2)}, u32[]{:S(2)}) collective-permute-start(bf16[2,128,128]{2,1,0:T(8,128)(2,1)} %get-tuple-element.37), channel_id=1, source_target_pairs={{0,6},{2,4},{4,2},{6,0},{1,7},{3,5},{5,3},{7,1},{8,14},{10,12},{12... | collective-permute-start | bytes 196616 | tf_op jit(solution)/shard_map/ppermute | solution.py:320
  25.5 5.3 %copy-start.8 = (bf16[2,128,128]{2,1,0:T(8,128)(2,1)S(1)}, bf16[2,128,128]{2,1,0:T(8,128)(2,1)}, u32[]{:S(2)}) copy-start(bf16[2,128,128]{2,1,0:T(8,128)(2,1)} %get-tuple-element.34) | copy-start | bytes 196612
  28.9 5.6 %collective-permute-start.6 = (bf16[128,1024]{1,0:T(8,128)(2,1)}, bf16[128,1024]{1,0:T(8,128)(2,1)S(1)}, u32[]{:S(2)}, u32[]{:S(2)}) collective-permute-start(bf16[128,1024]{1,0:T(8,128)(2,1)} %get-tuple-element.39), channel_id=1, source_target_pairs={{0,2},{2,0},{4,6},{6,4},{1,3},{3,1},{5,7},{7,5},{8,10},{10,8},{12,... | collective-permute-start | bytes 786440 | tf_op jit(solution)/shard_map/ppermute | solution.py:320
  29.2 12.3 %collective-permute-start.7 = (bf16[128,1024]{1,0:T(8,128)(2,1)}, bf16[128,1024]{1,0:T(8,128)(2,1)S(1)}, u32[]{:S(2)}, u32[]{:S(2)}) collective-permute-start(bf16[128,1024]{1,0:T(8,128)(2,1)} %get-tuple-element.40), channel_id=1, source_target_pairs={{0,4},{2,6},{4,0},{6,2},{1,5},{3,7},{5,1},{7,3},{8,12},{10,14},{12... | collective-permute-start | bytes 786440 | tf_op jit(solution)/shard_map/ppermute | solution.py:320
  30.7 12.0 %collective-permute-start.8 = (bf16[128,1024]{1,0:T(8,128)(2,1)}, bf16[128,1024]{1,0:T(8,128)(2,1)S(1)}, u32[]{:S(2)}, u32[]{:S(2)}) collective-permute-start(bf16[128,1024]{1,0:T(8,128)(2,1)} %get-tuple-element.41), channel_id=1, source_target_pairs={{0,6},{2,4},{4,2},{6,0},{1,7},{3,5},{5,3},{7,1},{8,14},{10,12},{12... | collective-permute-start | bytes 786440 | tf_op jit(solution)/shard_map/ppermute | solution.py:320
  30.9 10.6 %copy-start.4 = (bf16[4,2,128,128]{3,2,1,0:T(8,128)(2,1)}, bf16[4,2,128,128]{3,2,1,0:T(8,128)(2,1)S(1)}, u32[]{:S(2)}) copy-start(bf16[4,2,128,128]{3,2,1,0:T(8,128)(2,1)S(1)} %pad_maximum_fusion.refs_0_) | copy-start | bytes 786436
  30.9 13.4 %collective-permute-start.5 = (bf16[4,2,128,128]{3,2,1,0:T(8,128)(2,1)S(1)}, bf16[4,2,128,128]{3,2,1,0:T(8,128)(2,1)S(1)}, u32[]{:S(2)}, u32[]{:S(2)}) collective-permute-start(bf16[4,2,128,128]{3,2,1,0:T(8,128)(2,1)S(1)} %pad_maximum_fusion.refs_0_), channel_id=1, source_target_pairs={{0,24},{8,0},{16,8},{24,16},{1,25},{9,1},{17,9},{25,17},{2,26},{10... | collective-permute-start | bytes 786440 | tf_op jit(solution)/shard_map/ppermute | solution.py:324
  34.5 7.0 %copy-start.10 = (bf16[128,1024]{1,0:T(8,128)(2,1)}, bf16[128,1024]{1,0:T(8,128)(2,1)S(1)}, u32[]{:S(2)}) copy-start(bf16[128,1024]{1,0:T(8,128)(2,1)S(1)} %collective-permute-done.6.refs_5_) | copy-start | bytes 786436
  34.5 23.0 %collective-permute-start.4 = (bf16[4,2,128,128]{3,2,1,0:T(8,128)(2,1)S(1)}, bf16[4,2,128,128]{3,2,1,0:T(8,128)(2,1)S(1)}, u32[]{:S(2)}, u32[]{:S(2)}) collective-permute-start(bf16[4,2,128,128]{3,2,1,0:T(8,128)(2,1)S(1)} %pad_maximum_fusion.refs_0_), channel_id=1, source_target_pairs={{0,16},{8,24},{16,0},{24,8},{1,17},{9,25},{17,1},{25,9},{2,18},{10... | collective-permute-start | bytes 786440 | tf_op jit(solution)/shard_map/ppermute | solution.py:324
  35.8 1.8 %copy-start = (bf16[64,4096]{1,0:T(8,128)(2,1)}, bf16[64,4096]{1,0:T(8,128)(2,1)S(1)}, u32[]{:S(2)}) copy-start(bf16[64,4096]{1,0:T(8,128)(2,1)S(1)} %collective-permute-done.9.refs_1_) | copy-start | bytes 1572868
  35.8 21.8 %collective-permute-start.3 = (bf16[4,2,128,128]{3,2,1,0:T(8,128)(2,1)S(1)}, bf16[4,2,128,128]{3,2,1,0:T(8,128)(2,1)S(1)}, u32[]{:S(2)}, u32[]{:S(2)}) collective-permute-start(bf16[4,2,128,128]{3,2,1,0:T(8,128)(2,1)S(1)} %pad_maximum_fusion.refs_0_), channel_id=1, source_target_pairs={{0,8},{8,16},{16,24},{24,0},{1,9},{9,17},{17,25},{25,1},{2,10},{10... | collective-permute-start | bytes 786440 | tf_op jit(solution)/shard_map/ppermute | solution.py:324
  41.5 17.7 %copy-start.20 = (f32[16,128]{1,0:T(8,128)S(1)}, f32[16,128]{1,0:T(8,128)}, u32[]{:S(2)}) copy-start(f32[16,128]{1,0:T(8,128)} %get-tuple-element.50) | copy-start | bytes 24580
  41.5 20.8 %copy-start.11 = (bf16[128,1024]{1,0:T(8,128)(2,1)}, bf16[128,1024]{1,0:T(8,128)(2,1)S(1)}, u32[]{:S(2)}) copy-start(bf16[128,1024]{1,0:T(8,128)(2,1)S(1)} %collective-permute-done.7.refs_6_) | copy-start | bytes 786436
  41.5 20.8 %collective-permute-start.10 = (bf16[128,1024]{1,0:T(8,128)(2,1)}, bf16[128,1024]{1,0:T(8,128)(2,1)S(1)}, u32[]{:S(2)}, u32[]{:S(2)}) collective-permute-start(bf16[128,1024]{1,0:T(8,128)(2,1)} %get-tuple-element.44), channel_id=1, source_target_pairs={{0,2},{2,0},{4,6},{6,4},{1,3},{3,1},{5,7},{7,5},{8,10},{10,8},{12,... | collective-permute-start | bytes 786440 | tf_op jit(solution)/shard_map/ppermute | solution.py:320
  42.8 19.6 %copy-start.12 = (bf16[128,1024]{1,0:T(8,128)(2,1)}, bf16[128,1024]{1,0:T(8,128)(2,1)S(1)}, u32[]{:S(2)}) copy-start(bf16[128,1024]{1,0:T(8,128)(2,1)S(1)} %collective-permute-done.8.refs_7_) | copy-start | bytes 786436
  42.8 19.5 %collective-permute-start.11 = (bf16[128,1024]{1,0:T(8,128)(2,1)}, bf16[128,1024]{1,0:T(8,128)(2,1)S(1)}, u32[]{:S(2)}, u32[]{:S(2)}) collective-permute-start(bf16[128,1024]{1,0:T(8,128)(2,1)} %get-tuple-element.45), channel_id=1, source_target_pairs={{0,4},{2,6},{4,0},{6,2},{1,5},{3,7},{5,1},{7,3},{8,12},{10,14},{12... | collective-permute-start | bytes 786440 | tf_op jit(solution)/shard_map/ppermute | solution.py:320
  44.3 18.1 %copy-start.13 = (bf16[4,2,128,128]{3,2,1,0:T(8,128)(2,1)}, bf16[4,2,128,128]{3,2,1,0:T(8,128)(2,1)S(1)}, u32[]{:S(2)}) copy-start(bf16[4,2,128,128]{3,2,1,0:T(8,128)(2,1)S(1)} %collective-permute-done.5.refs_3_) | copy-start | bytes 786436
  44.3 18.0 %collective-permute-start.12 = (bf16[128,1024]{1,0:T(8,128)(2,1)}, bf16[128,1024]{1,0:T(8,128)(2,1)S(1)}, u32[]{:S(2)}, u32[]{:S(2)}) collective-permute-start(bf16[128,1024]{1,0:T(8,128)(2,1)} %get-tuple-element.46), channel_id=1, source_target_pairs={{0,6},{2,4},{4,2},{6,0},{1,7},{3,5},{5,3},{7,1},{8,14},{10,12},{12... | collective-permute-start | bytes 786440 | tf_op jit(solution)/shard_map/ppermute | solution.py:320
  57.6 4.8 %copy-start.14 = (bf16[4,2,128,128]{3,2,1,0:T(8,128)(2,1)}, bf16[4,2,128,128]{3,2,1,0:T(8,128)(2,1)S(1)}, u32[]{:S(2)}) copy-start(bf16[4,2,128,128]{3,2,1,0:T(8,128)(2,1)S(1)} %collective-permute-done.4.refs_2_) | copy-start | bytes 786436
  57.6 1.6 %collective-permute-start.13 = (f32[16,128]{1,0:T(8,128)}, f32[16,128]{1,0:T(8,128)S(1)}, u32[]{:S(2)}, u32[]{:S(2)}) collective-permute-start(f32[16,128]{1,0:T(8,128)} %get-tuple-element.48), channel_id=1, source_target_pairs={{0,2},{2,0},{4,6},{6,4},{1,3},{3,1},{5,7},{7,5},{8,10},{10,8},{12,... | collective-permute-start | bytes 24584 | tf_op jit(solution)/shard_map/ppermute | solution.py:320
  57.6 4.8 %copy-start.15 = (bf16[4,2,128,128]{3,2,1,0:T(8,128)(2,1)}, bf16[4,2,128,128]{3,2,1,0:T(8,128)(2,1)S(1)}, u32[]{:S(2)}) copy-start(bf16[4,2,128,128]{3,2,1,0:T(8,128)(2,1)S(1)} %collective-permute-done.3.refs_1_) | copy-start | bytes 786436
  57.6 2.7 %copy-start.9 = (s32[4,2]{0,1:T(2,128)S(1)}, s32[4,2]{0,1:T(2,128)}, u32[]{:S(2)}) copy-start(s32[4,2]{0,1:T(2,128)} %param.17) | copy-start | bytes 100
  57.6 3.9 %collective-permute-start.14 = (f32[16,128]{1,0:T(8,128)}, f32[16,128]{1,0:T(8,128)S(1)}, u32[]{:S(2)}, u32[]{:S(2)}) collective-permute-start(f32[16,128]{1,0:T(8,128)} %get-tuple-element.49), channel_id=1, source_target_pairs={{0,4},{2,6},{4,0},{6,2},{1,5},{3,7},{5,1},{7,3},{8,12},{10,14},{12... | collective-permute-start | bytes 24584 | tf_op jit(solution)/shard_map/ppermute | solution.py:320
  59.2 3.2 %copy-start.19 = (f32[16,128]{1,0:T(8,128)}, f32[16,128]{1,0:T(8,128)S(1)}, u32[]{:S(2)}) copy-start(f32[16,128]{1,0:T(8,128)S(1)} %collective-permute-done.13.refs_13_) | copy-start | bytes 24580
  59.2 3.1 %collective-permute-start.15 = (f32[16,128]{1,0:T(8,128)S(1)}, f32[16,128]{1,0:T(8,128)S(1)}, u32[]{:S(2)}, u32[]{:S(2)}) collective-permute-start(f32[16,128]{1,0:T(8,128)S(1)} %copy-done.20), channel_id=1, source_target_pairs={{0,6},{2,4},{4,2},{6,0},{1,7},{3,5},{5,3},{7,1},{8,14},{10,12},{12... | collective-permute-start | bytes 24584 | tf_op jit(solution)/shard_map/ppermute | solution.py:320
  61.5 0.9 copy-start.21
  62.3 0.6 copy-start.22
  62.3 0.7 copy-start.16
  62.3 0.8 copy-start.17
  62.4 0.8 copy-start.18
  91.1 9.5 %collective-permute-start.19 = (bf16[4,2,128,128]{3,2,1,0:T(8,128)(2,1)}, bf16[4,2,128,128]{3,2,1,0:T(8,128)(2,1)S(1)}, u32[]{:S(2)}, u32[]{:S(2)}) collective-permute-start(bf16[4,2,128,128]{3,2,1,0:T(8,128)(2,1)} %get-tuple-element.56), channel_id=1, source_target_pairs={{0,24},{8,0},{16,8},{24,16},{1,25},{9,1},{17,9},{25,17},{2,26},{10... | collective-permute-start | bytes 786440 | tf_op jit(solution)/shard_map/ppermute | solution.py:324
  91.1 25.1 %collective-permute-start.20 = (bf16[4,2,128,128]{3,2,1,0:T(8,128)(2,1)}, bf16[4,2,128,128]{3,2,1,0:T(8,128)(2,1)S(1)}, u32[]{:S(2)}, u32[]{:S(2)}) collective-permute-start(bf16[4,2,128,128]{3,2,1,0:T(8,128)(2,1)} %get-tuple-element.57), channel_id=1, source_target_pairs={{0,16},{8,24},{16,0},{24,8},{1,17},{9,25},{17,1},{25,9},{2,18},{10... | collective-permute-start | bytes 786440 | tf_op jit(solution)/shard_map/ppermute | solution.py:324
  93.3 22.8 %collective-permute-start.21 = (bf16[4,2,128,128]{3,2,1,0:T(8,128)(2,1)}, bf16[4,2,128,128]{3,2,1,0:T(8,128)(2,1)S(1)}, u32[]{:S(2)}, u32[]{:S(2)}) collective-permute-start(bf16[4,2,128,128]{3,2,1,0:T(8,128)(2,1)} %get-tuple-element.58), channel_id=1, source_target_pairs={{0,8},{8,16},{16,24},{24,0},{1,9},{9,17},{17,25},{25,1},{2,10},{10... | collective-permute-start | bytes 786440 | tf_op jit(solution)/shard_map/ppermute | solution.py:324
  95.3 24.2 %collective-permute-start.16 = (bf16[128,1024]{1,0:T(8,128)(2,1)}, bf16[128,1024]{1,0:T(8,128)(2,1)S(1)}, u32[]{:S(2)}, u32[]{:S(2)}) collective-permute-start(bf16[128,1024]{1,0:T(8,128)(2,1)} %get-tuple-element.52), channel_id=1, source_target_pairs={{0,2},{2,0},{4,6},{6,4},{1,3},{3,1},{5,7},{7,5},{8,10},{10,8},{12,... | collective-permute-start | bytes 786440 | tf_op jit(solution)/shard_map/ppermute | solution.py:320
  95.3 24.5 %collective-permute-start.17 = (bf16[128,1024]{1,0:T(8,128)(2,1)}, bf16[128,1024]{1,0:T(8,128)(2,1)S(1)}, u32[]{:S(2)}, u32[]{:S(2)}) collective-permute-start(bf16[128,1024]{1,0:T(8,128)(2,1)} %get-tuple-element.53), channel_id=1, source_target_pairs={{0,4},{2,6},{4,0},{6,2},{1,5},{3,7},{5,1},{7,3},{8,12},{10,14},{12... | collective-permute-start | bytes 786440 | tf_op jit(solution)/shard_map/ppermute | solution.py:320
  100.5 19.3 %collective-permute-start.18 = (bf16[128,1024]{1,0:T(8,128)(2,1)}, bf16[128,1024]{1,0:T(8,128)(2,1)S(1)}, u32[]{:S(2)}, u32[]{:S(2)}) collective-permute-start(bf16[128,1024]{1,0:T(8,128)(2,1)} %get-tuple-element.54), channel_id=1, source_target_pairs={{0,6},{2,4},{4,2},{6,0},{1,7},{3,5},{5,3},{7,1},{8,14},{10,12},{12... | collective-permute-start | bytes 786440 | tf_op jit(solution)/shard_map/ppermute | solution.py:320
  117.9 6.1 %collective-permute-start.24 = (bf16[2,128,128]{2,1,0:T(8,128)(2,1)S(1)}, bf16[2,128,128]{2,1,0:T(8,128)(2,1)S(1)}, u32[]{:S(2)}, u32[]{:S(2)}) collective-permute-start(bf16[2,128,128]{2,1,0:T(8,128)(2,1)S(1)} %get-tuple-element.61), channel_id=1, source_target_pairs={{0,6},{2,4},{4,2},{6,0},{1,7},{3,5},{5,3},{7,1},{8,14},{10,12},{12... | collective-permute-start | bytes 196616 | tf_op jit(solution)/shard_map/ppermute | solution.py:320
  118.7 5.4 %collective-permute-start.23 = (bf16[2,128,128]{2,1,0:T(8,128)(2,1)S(1)}, bf16[2,128,128]{2,1,0:T(8,128)(2,1)S(1)}, u32[]{:S(2)}, u32[]{:S(2)}) collective-permute-start(bf16[2,128,128]{2,1,0:T(8,128)(2,1)S(1)} %get-tuple-element.62), channel_id=1, source_target_pairs={{0,4},{2,6},{4,0},{6,2},{1,5},{3,7},{5,1},{7,3},{8,12},{10,14},{12... | collective-permute-start | bytes 196616 | tf_op jit(solution)/shard_map/ppermute | solution.py:320
  119.5 0.7 copy-start.1
  119.5 4.6 %collective-permute-start.22 = (bf16[2,128,128]{2,1,0:T(8,128)(2,1)S(1)}, bf16[2,128,128]{2,1,0:T(8,128)(2,1)S(1)}, u32[]{:S(2)}, u32[]{:S(2)}) collective-permute-start(bf16[2,128,128]{2,1,0:T(8,128)(2,1)S(1)} %get-tuple-element.63), channel_id=1, source_target_pairs={{0,2},{2,0},{4,6},{6,4},{1,3},{3,1},{5,7},{7,5},{8,10},{10,8},{12,... | collective-permute-start | bytes 196616 | tf_op jit(solution)/shard_map/ppermute | solution.py:320
  119.8 0.7 copy-start.2
  119.8 0.8 copy-start.3
  124.0 0.6 copy-start.5
  124.0 0.6 copy-start.6
  124.1 0.6 copy-start.7

commit v3 on v2

v3 whole, which is shorter than its diff:
```python
import functools
import math

import jax
import jax.numpy as jnp
from jax import lax
from jax.experimental import pallas as pl
from jax.experimental.pallas import tpu as pltpu
from jax.sharding import Mesh
from jax.sharding import PartitionSpec as P

HEAD_SIZE = 128
BLOCKS_DEV = 2
THETA = 1000000.0
CHUNK = 256
SCORE_SCALE = 1.0 / math.sqrt(HEAD_SIZE)
LOG2E = math.log2(math.e)
MEMORY = 56 * 1024 * 1024


def turned_tables(ids, width):
    half = width // 2
    rows = ids.shape[1]
    pair = lax.broadcasted_iota(jnp.int32, (half, rows), 0)
    first_cut = width // 8
    second_cut = first_cut + 3 * width // 16
    inverse = jnp.exp(pair.astype(jnp.float32) * jnp.float32(-2.0 * math.log(THETA) / width))
    ids = ids.astype(jnp.float32)
    picked = jnp.where(
        pair < first_cut, ids[0:1, :], jnp.where(pair < second_cut, ids[1:2, :], ids[2:3, :])
    )
    angles = picked * inverse
    cosine = jnp.cos(angles)
    sine = jnp.sin(angles)
    return (
        jnp.concatenate([cosine, cosine], axis=0).T,
        jnp.concatenate([sine, sine], axis=0).T,
    )


def half_sign():
    lane = lax.broadcasted_iota(jnp.int32, (1, HEAD_SIZE), 1)
    return jnp.where(lane < HEAD_SIZE // 2, -1.0, 1.0).astype(jnp.float32)


def head_lanes(member, flip, heads, head):
    first = ((member ^ flip) * heads + head) * HEAD_SIZE
    return pl.ds(pl.multiple_of(first, HEAD_SIZE), HEAD_SIZE)


def first_kernel(members, with_piece, where_ref, ids_ref, k_ref, v_ref, *refs):
    refs = list(refs)
    if with_piece:
        grad_ref = refs.pop(0)
        refs.pop()[...] = grad_ref[...]
    cos_ref, sin_ref = refs.pop(0), refs.pop(0)
    member = where_ref[0]
    cosine, sine = turned_tables(ids_ref[...], HEAD_SIZE)
    cos_ref[...] = cosine
    sin_ref[...] = sine
    signed = sine * half_sign()
    for flip in range(members):
        lanes = head_lanes(member, flip, 1, 0)
        keys = k_ref[:, lanes].astype(jnp.float32)
        refs[flip][0] = (keys * cosine + pltpu.roll(keys, HEAD_SIZE // 2, 1) * signed).astype(
            jnp.bfloat16
        )
        refs[flip][1] = v_ref[:, lanes]


def stacked(head, block_len):
    return slice(head * block_len, (head + 1) * block_len)


def query_kernel(members, group, where_ref, cos_ref, sin_ref, q_ref, *out_refs):
    member = where_ref[0]
    cosine = cos_ref[...]
    signed = sin_ref[...] * half_sign()
    block_len = q_ref.shape[0] // BLOCKS_DEV
    for flip in range(members):
        for head in range(group):
            field = q_ref[:, head_lanes(member, flip, group, head)].astype(jnp.float32)
            turned = pltpu.roll(field, HEAD_SIZE // 2, 1)
            field = (field * cosine + turned * signed).astype(jnp.bfloat16)
            for step in range(BLOCKS_DEV):
                out_refs[flip][step, stacked(head, block_len), :] = field[
                    step * block_len : (step + 1) * block_len, :
                ]


def delta_kernel(members, group, where_ref, a_ref, l_ref, *refs):
    refs = list(refs)
    own_ref = refs.pop(0)
    other_ref = refs.pop(0) if members > 1 else None
    grad_refs, stat_refs = refs[:members], refs[members:]
    member, tp_index = where_ref[0], where_ref[1]
    block_len = a_ref.shape[0] // BLOCKS_DEV
    for flip in range(members):
        g_ref = grad_refs[flip]
        for head in range(group):
            lanes = head_lanes(member, flip, group, head)
            here = stacked(head, block_len)
            if members > 1:
                g_ref[tp_index, here, :] = own_ref[:, lanes]
                g_ref[1 - tp_index, here, :] = other_ref[:, lanes]
            else:
                for step in range(BLOCKS_DEV):
                    g_ref[step, here, :] = own_ref[stacked(step, block_len), lanes]
        first = pl.multiple_of((member ^ flip) * group, group)
        lse = l_ref[pl.ds(first, group), :] * LOG2E
        for step in range(BLOCKS_DEV):
            sums = []
            for head in range(group):
                lanes = head_lanes(member, flip, group, head)
                product = g_ref[step, stacked(head, block_len), :].astype(jnp.float32) * a_ref[
                    stacked(step, block_len), lanes
                ].astype(jnp.float32)
                sums.append(product)
            total = jnp.sum(jnp.concatenate(sums, axis=0).T, axis=0, keepdims=True)
            stat_refs[flip][2 * step : 2 * step + 1, :] = row_vector(lse, step, block_len)
            stat_refs[flip][2 * step + 1 : 2 * step + 2, :] = total


def row_vector(table, upper, block_len):
    group, width = table.shape
    rolled = pltpu.roll(table, block_len, 1)
    low, high = (table, rolled) if upper == 0 else (rolled, table)
    lane = lax.broadcasted_iota(jnp.int32, (1, width), 1)
    pieces = [
        jnp.where(lane < block_len, low[h : h + 1, :], high[h + 1 : h + 2, :])
        for h in range(0, group, 2)
    ]
    return jnp.concatenate(pieces, axis=1)


def attend_kernel(
    members, group, block_len, slabs, carried, carries, where_ref, map_ref, span_ref, *refs
):
    refs = list(refs)
    count = len(slabs)
    kv_refs = [refs.pop(0) for _ in range(count)]
    q_refs = [refs.pop(0) for _ in range(members)]
    g_refs = [refs.pop(0) for _ in range(members)]
    s_refs = [refs.pop(0) for _ in range(members)]
    in_ref = refs.pop(0) if carried else None
    dq_refs = [refs.pop(0) for _ in range(1 if carries else members)]
    part_refs = [refs.pop(0) for _ in range(count)]
    k_sort, v_sort, k_turn, q_all, g_all, l_all, d_all, dk_sum, dv_sum, dq_sum = refs[:10]
    dq_all, ranks, ordered = refs[10:]
    member, layer, layers, device = where_ref[0], where_ref[2], where_ref[3], where_ref[4]
    units = kv_refs[0].shape[0]
    spans = span_ref.shape[0] // 2
    columns = group * block_len
    blocks = count * units * BLOCKS_DEV
    complete = blocks == map_ref.shape[0]

    def sequence_block(slab, unit, step):
        if members > 1:
            owner = lax.rem(layer - slab + layers, layers) * members + (member ^ unit)
        else:
            owner = unit
        return map_ref[owner * BLOCKS_DEV + step]

    if complete:

        @pl.loop(0, blocks)
        def _(block):
            ordered[block] = block
            ranks[block] = map_ref[block]

        def blocks_before(bound):
            return bound
    else:
        present = [
            sequence_block(slab, unit, step)
            for slab in slabs
            for unit in range(units)
            for step in range(BLOCKS_DEV)
        ]

        def blocks_before(bound):
            return functools.reduce(jnp.add, [(b < bound).astype(jnp.int32) for b in present])

        for number, block in enumerate(present):
            rank = blocks_before(block)
            ranks[number] = rank
            ordered[rank] = block

    def each_block(body):
        for place in range(count):

            @pl.loop(0, units)
            def _(unit):
                for step in range(BLOCKS_DEV):
                    rank = ranks[(place * units + unit) * BLOCKS_DEV + step]
                    at = pl.multiple_of(rank * block_len, block_len)
                    body(place, unit, pl.ds(step * block_len, block_len), pl.ds(at, block_len))

    def sort(place, unit, row, to):
        k_sort[to, :] = kv_refs[place][unit, 0, row, :]
        v_sort[to, :] = kv_refs[place][unit, 1, row, :]

    each_block(sort)

    @pl.loop(0, k_turn.shape[0])
    def _(chunk):
        at = pl.multiple_of(chunk * CHUNK, CHUNK)
        k_turn[chunk] = k_sort[pl.ds(at, CHUNK), :].T
        dk_sum[pl.ds(at, CHUNK), :] = jnp.zeros((CHUNK, HEAD_SIZE), jnp.float32)
        dv_sum[pl.ds(at, CHUNK), :] = jnp.zeros((CHUNK, HEAD_SIZE), jnp.float32)

    for flip in range(members):
        for step in range(BLOCKS_DEV):
            place = flip * BLOCKS_DEV + step
            q_all[place] = q_refs[flip][step]
            g_all[place] = g_refs[flip][step]
            l_all[place] = s_refs[flip][2 * step : 2 * step + 1, :]
            d_all[place] = s_refs[flip][2 * step + 1 : 2 * step + 2, :]

    lane = lax.broadcasted_iota(jnp.int32, (1, columns), 1)
    within = lax.rem(lane, block_len)
    key_row = lax.broadcasted_iota(jnp.int32, (block_len, 1), 0)
    chunk_blocks = CHUNK // block_len

    @pl.loop(0, members * BLOCKS_DEV)
    def _(place):
        flip, step = place // BLOCKS_DEV, lax.rem(place, BLOCKS_DEV)
        owner = device if members == 1 else layer * members + (member ^ flip)
        block = map_ref[owner * BLOCKS_DEV + step]
        end = jnp.int32(0)
        for span in range(spans):
            inside = (block >= span_ref[2 * span]) & (block < span_ref[2 * span + 1])
            end = jnp.where(inside, span_ref[2 * span + 1], end)
        limit = jnp.where(end > 0, end * block_len, block * block_len + within + 1)
        full = blocks_before(jnp.where(end > 0, end, block)) // chunk_blocks
        seen = (blocks_before(jnp.maximum(end, block + 1)) + chunk_blocks - 1) // chunk_blocks
        dq_sum[...] = in_ref[place] if carried else jnp.zeros_like(dq_sum)

        def visit(chunk, masked):
            queries = q_all[place]
            grads = g_all[place]
            at = pl.multiple_of(chunk * CHUNK, CHUNK)
            keys = k_sort[pl.ds(at, CHUNK), :]
            values = v_sort[pl.ds(at, CHUNK), :]
            scores = lax.dot_general(
                keys, queries, (((1,), (1,)), ((), ())), preferred_element_type=jnp.float32
            )
            raised = scores * (SCORE_SCALE * LOG2E) - l_all[place]
            if masked:
                positions = jnp.concatenate(
                    [
                        key_row + ordered[chunk * chunk_blocks + i] * block_len
                        for i in range(chunk_blocks)
                    ],
                    axis=0,
                )
                raised = jnp.where(positions < limit, raised, -jnp.inf)
            probs = jnp.exp2(raised)
            grad_p = lax.dot_general(
                values, grads, (((1,), (1,)), ((), ())), preferred_element_type=jnp.float32
            )
            grad_s = (probs * (grad_p - d_all[place])).astype(jnp.bfloat16)
            dv_sum[pl.ds(at, CHUNK), :] += jnp.dot(
                probs.astype(jnp.bfloat16), grads, preferred_element_type=jnp.float32
            )
            dk_sum[pl.ds(at, CHUNK), :] += jnp.dot(
                grad_s, queries, preferred_element_type=jnp.float32
            )
            dq_sum[...] += jnp.dot(k_turn[chunk], grad_s, preferred_element_type=jnp.float32)

        pl.loop(0, full)(lambda chunk: visit(chunk, False))
        pl.loop(full, seen)(lambda chunk: visit(chunk, True))

        if carries:
            dq_refs[0][place] = dq_sum[...]
        else:
            dq_all[place] = (dq_sum[...].T * SCORE_SCALE).astype(jnp.bfloat16)

    if not carries:
        for flip in range(members):
            for step in range(BLOCKS_DEV):
                dq_refs[flip][step] = dq_all[flip * BLOCKS_DEV + step]

    def unsort(place, unit, here, at):
        kind = part_refs[place].dtype
        part_refs[place][unit, 0, here, :] = (dk_sum[at, :] * SCORE_SCALE).astype(kind)
        part_refs[place][unit, 1, here, :] = dv_sum[at, :].astype(kind)

    each_block(unsort)


def turned_back(field, cosine, signed):
    return field * cosine - pltpu.roll(field, HEAD_SIZE // 2, 1) * signed


def query_gradient_kernel(members, group, where_ref, cos_ref, sin_ref, *refs):
    member = where_ref[0]
    block_len = cos_ref.shape[0] // BLOCKS_DEV
    for step in range(BLOCKS_DEV):
        here = slice(step * block_len, (step + 1) * block_len)
        cosine = cos_ref[here, :]
        signed = sin_ref[here, :] * half_sign()
        for flip in range(members):
            for head in range(group):
                field = refs[flip][step, stacked(head, block_len), :].astype(jnp.float32)
                refs[members][here, head_lanes(member, flip, group, head)] = turned_back(
                    field, cosine, signed
                ).astype(jnp.bfloat16)


def last_kernel(members, where_ref, cos_ref, sin_ref, *refs):
    member = where_ref[0]
    dk_ref, dv_ref = refs[members], refs[members + 1]
    cosine = cos_ref[...]
    signed = sin_ref[...] * half_sign()
    for flip in range(members):
        lanes = head_lanes(member, flip, 1, 0)
        field = refs[flip][0].astype(jnp.float32)
        dk_ref[:, lanes] = turned_back(field, cosine, signed).astype(jnp.bfloat16)
        dv_ref[:, lanes] = refs[flip][1].astype(jnp.bfloat16)


def whole(shape):
    return pl.BlockSpec(shape, lambda *_: (0,) * len(shape))


def call(kernel, name, scalars, inputs, outputs, in_specs=None, out_specs=None, scratch=(), cost=None):
    return pl.pallas_call(
        kernel,
        grid_spec=pltpu.PrefetchScalarGridSpec(
            num_scalar_prefetch=len(scalars),
            grid=(1,),
            in_specs=in_specs or [whole(a.shape) for a in inputs],
            out_specs=out_specs or [whole(shape) for shape, _ in outputs],
            scratch_shapes=list(scratch),
        ),
        out_shape=[jax.ShapeDtypeStruct(shape, kind) for shape, kind in outputs],
        compiler_params=pltpu.CompilerParams(vmem_limit_bytes=MEMORY),
        cost_estimate=cost,
        name=name,
    )(*scalars, *inputs)


def shards(
    queries, keys, values, attn_out, out_grad, logsumexp, position_ids, block_map, span_blocks
):
    rows = queries.shape[0]
    kv_heads = keys.shape[1] // HEAD_SIZE
    group = queries.shape[1] // keys.shape[1]
    block_len = rows // BLOCKS_DEV
    layers = lax.axis_size("z")
    members = 4 if kv_heads == 4 and lax.axis_size("tp") == 2 else 1
    tp_index = lax.axis_index("tp")
    layer = lax.axis_index("z")
    in_slab = lax.axis_index("y") * 2 + lax.axis_index("core")
    device = layer * 4 + in_slab
    member = in_slab if members > 1 else jnp.zeros_like(in_slab)
    place = jnp.stack([member, tp_index, layer, jnp.full_like(layer, layers), device])
    place = place.astype(jnp.int32)
    width = group * HEAD_SIZE
    bf16, f32 = jnp.bfloat16, jnp.float32

    def flipped(array, flip):
        if flip == 0:
            return array
        return lax.ppermute(array, ("y", "core"), [(i, i ^ flip) for i in range(4)])

    def climbed(array, steps):
        route = [(i, (i + steps) % layers) for i in range(layers)]
        return lax.ppermute(array, "z", route)

    every = range(members)
    table = ((rows, HEAD_SIZE), f32)
    pair = (2, rows, HEAD_SIZE)

    inputs = [position_ids, keys, values]
    outputs = [table, table] + [(pair, bf16)] * members
    in_specs = [whole(a.shape) for a in inputs]
    if members > 1:
        other = (out_grad.shape[0], members * width)
        inputs.append(out_grad)
        in_specs.append(pl.BlockSpec(other, lambda i, where: (0, 1 - where[1])))
        outputs.append((other, bf16))
    results = call(
        functools.partial(first_kernel, members, members > 1),
        "first", [place], inputs, outputs, in_specs,
    )
    cosine, sine = results[:2]
    kv_pieces = results[2 : 2 + members]
    columns = group * block_len
    stack = (BLOCKS_DEV, columns, HEAD_SIZE)
    q_pieces = call(
        functools.partial(query_kernel, members, group),
        "rotate", [place], [cosine, sine, queries], [(stack, bf16)] * members,
    )
    if members > 1:
        slab = jnp.stack([flipped(kv_pieces[f], f) for f in every])
        grads_other = lax.ppermute(results[-1], "tp", [(0, 1), (1, 0)])
        far = sorted(range(1, layers), key=lambda k: abs(2 * k - layers))
        rounds = [far[: layers // 2], far[layers // 2 :] + [0]]
        slab, *q_pieces = lax.optimization_barrier((slab, *q_pieces))
        kv = {0: slab}
        for k in far:
            kv[k] = climbed(slab, k)
    else:
        kv = {0: lax.all_gather(kv_pieces[0], ("z", "y", "core"), axis=0, tiled=False)}
        rounds = [[0]]
        grads_own = lax.all_to_all(out_grad, "tp", split_axis=1, concat_axis=0, tiled=True)
    q_in = [flipped(q_pieces[f], f) for f in every]

    inputs = [attn_out, logsumexp]
    in_specs = [whole(a.shape) for a in inputs]
    if members > 1:
        inputs += [out_grad, grads_other]
        in_specs += [
            pl.BlockSpec(grads_other.shape, lambda i, where: (0, where[1])),
            whole(grads_other.shape),
        ]
    else:
        inputs += [grads_own]
        in_specs += [whole(grads_own.shape)]
    results = call(
        functools.partial(delta_kernel, members, group),
        "delta", [place], inputs,
        [(stack, bf16)] * members + [((2 * BLOCKS_DEV, columns), f32)] * members,
        in_specs,
    )
    g_in = [flipped(results[f], f) for f in every]
    s_in = [flipped(results[members + f], f) for f in every]

    units = kv[0].shape[0]
    blocks = members * BLOCKS_DEV
    part = (units, 2, rows, HEAD_SIZE)
    sums = (blocks, HEAD_SIZE, columns)
    parts = {}
    carry = []
    for number, slabs in enumerate(rounds):
        tokens = len(slabs) * units * rows
        carries = number < len(rounds) - 1
        results = call(
            functools.partial(
                attend_kernel, members, group, block_len, slabs, number > 0, carries
            ),
            "attend", [place, block_map, span_blocks.reshape(-1)],
            [*[kv[k] for k in slabs], *q_in, *g_in, *s_in, *carry],
            ([(sums, f32)] if carries else [(stack, bf16)] * members)
            + [(part, f32 if k == 0 and members > 1 else bf16) for k in slabs],
            scratch=[
                pltpu.VMEM((tokens, HEAD_SIZE), bf16),
                pltpu.VMEM((tokens, HEAD_SIZE), bf16),
                pltpu.VMEM((tokens // CHUNK, HEAD_SIZE, CHUNK), bf16),
                pltpu.VMEM((blocks, columns, HEAD_SIZE), bf16),
                pltpu.VMEM((blocks, columns, HEAD_SIZE), bf16),
                pltpu.VMEM((blocks, 1, columns), f32),
                pltpu.VMEM((blocks, 1, columns), f32),
                pltpu.VMEM((tokens, HEAD_SIZE), f32),
                pltpu.VMEM((tokens, HEAD_SIZE), f32),
                pltpu.VMEM((HEAD_SIZE, columns), f32),
                pltpu.VMEM((blocks, columns, HEAD_SIZE), bf16),
                pltpu.SMEM((tokens // block_len,), jnp.int32),
                pltpu.SMEM((tokens // block_len,), jnp.int32),
            ],
            cost=pl.CostEstimate(
                flops=6 * group * members * rows * tokens * HEAD_SIZE,
                bytes_accessed=6 * 1024 * 1024,
                transcendentals=group * members * rows * tokens // 2,
            ),
        )
        outs = 1 if carries else members
        carry = results[:outs]
        parts.update(zip(slabs, results[outs:]))
    dq_pieces = carry
    if members > 1:
        total = parts[0]
        for k in far:
            total = total + climbed(parts[k], layers - k).astype(f32)
        sums = [flipped(total[f].astype(bf16), f) for f in every]
    else:
        sums = [
            lax.psum_scatter(parts[0], ("z", "y", "core"), scatter_dimension=0, tiled=True)[0]
        ]
    (grad_q,) = call(
        functools.partial(query_gradient_kernel, members, group),
        "turn_back", [place],
        [cosine, sine] + [flipped(dq_pieces[f], f) for f in every],
        [(queries.shape, bf16)],
    )
    key_gradient, value_gradient = call(
        functools.partial(last_kernel, members),
        "last", [place], [cosine, sine, *sums],
        [(keys.shape, bf16), (values.shape, bf16)],
    )
    return (grad_q, key_gradient, value_gradient)


def solution(mesh):
    ctx, tp = mesh.shape["ctx"], mesh.shape["tp"]
    fine = Mesh(mesh.devices.reshape(ctx // 4, 2, 2, tp), ("z", "y", "core", "tp"))
    ctx_axes = ("z", "y", "core")
    return jax.shard_map(
        shards,
        mesh=fine,
        in_specs=(
            P(ctx_axes, "tp"),
            P(ctx_axes, "tp"),
            P(ctx_axes, "tp"),
            P(ctx_axes, "tp"),
            P((*ctx_axes, "tp"), None),
            P("tp", ctx_axes),
            P(None, ctx_axes),
            P(),
            P(),
        ),
        out_specs=(P(ctx_axes, "tp"), P(ctx_axes, "tp"), P(ctx_axes, "tp")),
        check_vma=False,
    )
```

time: 129 us -> 112 us (0.87)
  the two profiles are of different devices: /device:TPU:0 before, /device:TPU:9 now
where the time goes in v3:
time: 112 us; the launch traced here: 111 us
  Pallas kernels  47.9 us (43%)
  starting transfers between devices  42.3 us (38%)
  waiting for transfers between devices  12.8 us (11%)
  local copies, waits for them, and re-layouts  5.01 us (4%)
  other arithmetic  2.04 us (2%)
    pallas_call x7, Pallas kernels, call(): pl.pallas_call(kernel, grid_spec=pltpu.PrefetchScalarGridSpec(num_scalar_...  47.9 us
    ppermute x18, starting transfers between devices, flipped(): return lax.ppermute(array, ('y', 'core'), [(i, i ^ flip) for i in range(4)])  33.2 us
    ppermute x6, waiting for transfers between devices, climbed(): return lax.ppermute(array, 'z', route)  8.15 us
    ppermute x6, starting transfers between devices, climbed(): return lax.ppermute(array, 'z', route)  7.87 us
    ppermute x18, waiting for transfers between devices, flipped(): return lax.ppermute(array, ('y', 'core'), [(i, i ^ flip) for i in range(4)])  3.95 us
    unnamed x47, local copies, waits for them, and re-layouts  3.09 us
  transfers between devices with their start and end apart: 25, of which 8 were waited for; matrix products, arithmetic and copies ran while one was open for 3% of the time, Pallas kernels for 23%

profile of v3, /device:TPU:9, one launch (start us, length us, event | category | flops | bytes accessed | tf_op | source)
XLA Modules:
  0.0 110.9 jit_solution(13753296643102652155)
XLA Ops:
  0.6 0.7 stack.34.where_ref
  1.3 3.0 %first.1 = (f32[128,128]{1,0:T(8,128)}, f32[128,128]{1,0:T(8,128)}, bf16[2,128,128]{2,1,0:T(8,128)(2,1)}, bf16[2,128,128]{2,1,0:T(8,128)(2,1)}, bf16[2,128,128]{...) custom-call(s32[5]{0:T(128)} %stack.34.where_ref, s32[3,128]{1,0:T(4,128)} %ids_ref.1, ...), custom_call_target="tpu_custom_call" | custom-call | tf_op jit(solution)/shard_map/first/pallas_call | solution.py:328
  4.3 1.2 %collective-permute-start.7 = (bf16[64,4096]{1,0:T(8,128)(2,1)}, bf16[64,4096]{1,0:T(8,128)(2,1)S(1)}, u32[]{:S(2)}, u32[]{:S(2)}) collective-permute-start(bf16[64,4096]{1,0:T(8,128)(2,1)} %get-tuple-element.53), channel_id=1, source_target_pairs={{0,1},{1,0},{2,3},{3,2},{4,5},{5,4},{6,7},{7,6},{8,9},{9,8},{10,11... | collective-permute-start | bytes 1572872 | tf_op jit(solution)/shard_map/ppermute | solution.py:398
  5.5 1.0 collective-permute-start
  6.5 1.2 %collective-permute-start.1 = (bf16[2,128,128]{2,1,0:T(8,128)(2,1)}, bf16[2,128,128]{2,1,0:T(8,128)(2,1)S(1)}, u32[]{:S(2)}, u32[]{:S(2)}) collective-permute-start(bf16[2,128,128]{2,1,0:T(8,128)(2,1)} %get-tuple-element.42), channel_id=1, source_target_pairs={{0,4},{2,6},{4,0},{6,2},{1,5},{3,7},{5,1},{7,3},{8,12},{10,14},{12... | collective-permute-start | bytes 196616 | tf_op jit(solution)/shard_map/ppermute | solution.py:366
  7.7 0.4 collective-permute-start.2
  8.1 3.4 %rotate.1 = (bf16[2,512,128]{2,1,0:T(8,128)(2,1)}, bf16[2,512,128]{2,1,0:T(8,128)(2,1)}, bf16[2,512,128]{2,1,0:T(8,128)(2,1)}, bf16[2,512,128]{2,1,0:T(8,128)(2,1)}) custom-call(s32[5]{0:T(128)} %stack.34.where_ref, f32[128,128]{1,0:T(8,128)} %get-tuple-element.38.cos_ref, f32[128,128]{1,0:T(8,128)} %get-tuple-element.39.sin_ref, bf16[128,4096]{1,0:T(8,128)(2,1)} %q_ref.1), custom_call_target="tpu_custom_call" | custom-call | tf_op jit(solution)/shard_map/rotate/pallas_call | solution.py:328
  11.5 0.7 collective-permute-done.2
  12.2 0.9 pad_maximum_fusion.refs_1_
  13.1 0.1 collective-permute-start.4
  13.3 1.2 %collective-permute-start.5 = (bf16[2,512,128]{2,1,0:T(8,128)(2,1)}, bf16[2,512,128]{2,1,0:T(8,128)(2,1)S(1)}, u32[]{:S(2)}, u32[]{:S(2)}) collective-permute-start(bf16[2,512,128]{2,1,0:T(8,128)(2,1)} %get-tuple-element.51), channel_id=1, source_target_pairs={{0,4},{2,6},{4,0},{6,2},{1,5},{3,7},{5,1},{7,3},{8,12},{10,14},{12... | collective-permute-start | bytes 786440 | tf_op jit(solution)/shard_map/ppermute | solution.py:366
  14.5 0.8 collective-permute-start.6
  15.3 1.3 %collective-permute-start.15 = (bf16[4,2,128,128]{3,2,1,0:T(8,128)(2,1)S(1)}, bf16[4,2,128,128]{3,2,1,0:T(8,128)(2,1)S(1)}, u32[]{:S(2)}, u32[]{:S(2)}) collective-permute-start(bf16[4,2,128,128]{3,2,1,0:T(8,128)(2,1)S(1)} %pad_maximum_fusion.refs_1_), channel_id=1, source_target_pairs={{0,8},{8,16},{16,24},{24,0},{1,9},{9,17},{17,25},{25,1},{2,10},{10... | collective-permute-start | bytes 786440 | tf_op jit(solution)/shard_map/ppermute | solution.py:370
  16.6 0.7 collective-permute-done.7.refs_1_
  17.3 2.3 %collective-permute-start.14 = (bf16[4,2,128,128]{3,2,1,0:T(8,128)(2,1)S(1)}, bf16[4,2,128,128]{3,2,1,0:T(8,128)(2,1)S(1)}, u32[]{:S(2)}, u32[]{:S(2)}) collective-permute-start(bf16[4,2,128,128]{3,2,1,0:T(8,128)(2,1)S(1)} %pad_maximum_fusion.refs_1_), channel_id=1, source_target_pairs={{0,16},{8,24},{16,0},{24,8},{1,17},{9,25},{17,1},{25,9},{2,18},{10... | collective-permute-start | bytes 786440 | tf_op jit(solution)/shard_map/ppermute | solution.py:370
  19.6 3.8 %delta.1 = (bf16[2,512,128]{2,1,0:T(8,128)(2,1)}, bf16[2,512,128]{2,1,0:T(8,128)(2,1)}, bf16[2,512,128]{2,1,0:T(8,128)(2,1)}, bf16[2,512,128]{2,1,0:T(8,128)(2,1...) custom-call(s32[5]{0:T(128)} %stack.34.where_ref, bf16[128,4096]{1,0:T(8,128)(2,1)} %a_ref.1, ...), custom_call_target="tpu_custom_call" | custom-call | tf_op jit(solution)/shard_map/delta/pallas_call | solution.py:328
  23.4 1.9 %collective-permute-start.8 = (bf16[2,512,128]{2,1,0:T(8,128)(2,1)}, bf16[2,512,128]{2,1,0:T(8,128)(2,1)S(1)}, u32[]{:S(2)}, u32[]{:S(2)}) collective-permute-start(bf16[2,512,128]{2,1,0:T(8,128)(2,1)} %get-tuple-element.55), channel_id=1, source_target_pairs={{0,2},{2,0},{4,6},{6,4},{1,3},{3,1},{5,7},{7,5},{8,10},{10,8},{12,... | collective-permute-start | bytes 786440 | tf_op jit(solution)/shard_map/ppermute | solution.py:366
  25.3 1.3 %collective-permute-start.9 = (bf16[2,512,128]{2,1,0:T(8,128)(2,1)}, bf16[2,512,128]{2,1,0:T(8,128)(2,1)S(1)}, u32[]{:S(2)}, u32[]{:S(2)}) collective-permute-start(bf16[2,512,128]{2,1,0:T(8,128)(2,1)} %get-tuple-element.56), channel_id=1, source_target_pairs={{0,4},{2,6},{4,0},{6,2},{1,5},{3,7},{5,1},{7,3},{8,12},{10,14},{12... | collective-permute-start | bytes 786440 | tf_op jit(solution)/shard_map/ppermute | solution.py:366
  26.6 0.8 collective-permute-done.6.refs_5_
  27.4 0.6 collective-permute-start.10
  28.1 1.0 collective-permute-start.11
  29.1 4.7 %collective-permute-done.14.refs_0_ = bf16[4,2,128,128]{3,2,1,0:T(8,128)(2,1)S(1)} collective-permute-done((bf16[4,2,128,128]{3,2,1,0:T(8,128)(2,1)S(1)}, bf16[4,2,128,128]{3,2,1,0:T(8,128)(2,1)S(1)}, u32[]{:S(2)}, u32[]{:S(2)}) %collective-permute-start.14) | collective-permute-done | bytes 262176 | tf_op jit(solution)/shard_map/ppermute | solution.py:370
  33.7 1.2 %collective-permute-start.12 = (f32[4,512]{1,0:T(4,128)}, f32[4,512]{1,0:T(4,128)S(1)}, u32[]{:S(2)}, u32[]{:S(2)}) collective-permute-start(f32[4,512]{1,0:T(4,128)} %get-tuple-element.60), channel_id=1, source_target_pairs={{0,4},{2,6},{4,0},{6,2},{1,5},{3,7},{5,1},{7,3},{8,12},{10,14},{12... | collective-permute-start | bytes 24584 | tf_op jit(solution)/shard_map/ppermute | solution.py:366
  35.0 1.0 collective-permute-start.13
  36.1 0.6 reshape.14.span_ref
  36.7 2.3 %collective-permute-done.12.refs_12_ = f32[4,512]{1,0:T(4,128)S(1)} collective-permute-done((f32[4,512]{1,0:T(4,128)}, f32[4,512]{1,0:T(4,128)S(1)}, u32[]{:S(2)}, u32[]{:S(2)}) %collective-permute-start.12) | collective-permute-done | bytes 8224 | tf_op jit(solution)/shard_map/ppermute | solution.py:366
  39.0 0.6 collective-permute-start.3
  39.9 0.5 copy-done.22
  40.4 0.1 copy-done.14
  40.5 0.1 copy-done.15
  40.7 15.2 %attend.2 = (f32[8,128,512]{2,1,0:T(8,128)}, bf16[4,2,128,128]{3,2,1,0:T(8,128)(2,1)}, bf16[4,2,128,128]{3,2,1,0:T(8,128)(2,1)}) custom-call(s32[5]{0:T(128)} %stack.34.where_ref, s32[32]{0:T(128)} %map_ref.3, s32[8]{0:T(128)} %reshape.14.span_ref, bf16[4,2,128,128]{3,2,1,0:T(8,128)(2,1)} %copy-done.13, bf16[4,2,128,128]{3,2,1,0:T(8,128)(2,1)} %copy-done.12, ...), custom_call_target="tpu_custom_call" | custom-call | flops 3221225472 | bytes 6291456 | tf_op jit(solution)/shard_map/attend/pallas_call | solution.py:328
  55.9 0.7 copy-done.19
  56.6 16.8 %attend.3 = (bf16[2,512,128]{2,1,0:T(8,128)(2,1)}, bf16[2,512,128]{2,1,0:T(8,128)(2,1)}, bf16[2,512,128]{2,1,0:T(8,128)(2,1)}, bf16[2,512,128]{2,1,0:T(8,128)(2,...) custom-call(s32[5]{0:T(128)} %stack.34.where_ref, s32[32]{0:T(128)} %map_ref.3, s32[8]{0:T(128)} %reshape.14.span_ref, ...), custom_call_target="tpu_custom_call" | custom-call | flops 3221225472 | bytes 6291456 | tf_op jit(solution)/shard_map/attend/pallas_call | solution.py:328
  73.4 0.7 collective-permute-start.21
  74.1 2.9 %collective-permute-start.19 = (bf16[4,2,128,128]{3,2,1,0:T(8,128)(2,1)S(1)}, bf16[4,2,128,128]{3,2,1,0:T(8,128)(2,1)S(1)}, u32[]{:S(2)}, u32[]{:S(2)}) collective-permute-start(bf16[4,2,128,128]{3,2,1,0:T(8,128)(2,1)S(1)} %copy-done.18), channel_id=1, source_target_pairs={{0,16},{8,24},{16,0},{24,8},{1,17},{9,25},{17,1},{25,9},{2,18},{10... | collective-permute-start | bytes 786440 | tf_op jit(solution)/shard_map/ppermute | solution.py:370
  77.0 2.2 %collective-permute-start.16 = (bf16[2,512,128]{2,1,0:T(8,128)(2,1)}, bf16[2,512,128]{2,1,0:T(8,128)(2,1)S(1)}, u32[]{:S(2)}, u32[]{:S(2)}) collective-permute-start(bf16[2,512,128]{2,1,0:T(8,128)(2,1)} %get-tuple-element.64), channel_id=1, source_target_pairs={{0,2},{2,0},{4,6},{6,4},{1,3},{3,1},{5,7},{7,5},{8,10},{10,8},{12,... | collective-permute-start | bytes 786440 | tf_op jit(solution)/shard_map/ppermute | solution.py:366
  79.2 1.3 %collective-permute-start.17 = (bf16[2,512,128]{2,1,0:T(8,128)(2,1)}, bf16[2,512,128]{2,1,0:T(8,128)(2,1)S(1)}, u32[]{:S(2)}, u32[]{:S(2)}) collective-permute-start(bf16[2,512,128]{2,1,0:T(8,128)(2,1)} %get-tuple-element.65), channel_id=1, source_target_pairs={{0,4},{2,6},{4,0},{6,2},{1,5},{3,7},{5,1},{7,3},{8,12},{10,14},{12... | collective-permute-start | bytes 786440 | tf_op jit(solution)/shard_map/ppermute | solution.py:366
  80.5 14.7 %collective-permute-start.18 = (bf16[2,512,128]{2,1,0:T(8,128)(2,1)}, bf16[2,512,128]{2,1,0:T(8,128)(2,1)S(1)}, u32[]{:S(2)}, u32[]{:S(2)}) collective-permute-start(bf16[2,512,128]{2,1,0:T(8,128)(2,1)} %get-tuple-element.66), channel_id=1, source_target_pairs={{0,6},{2,4},{4,2},{6,0},{1,7},{3,5},{5,3},{7,1},{8,14},{10,12},{12... | collective-permute-start | bytes 786440 | tf_op jit(solution)/shard_map/ppermute | solution.py:366
  95.3 3.4 %collective-permute-done.20 = bf16[4,2,128,128]{3,2,1,0:T(8,128)(2,1)S(1)} collective-permute-done((bf16[4,2,128,128]{3,2,1,0:T(8,128)(2,1)S(1)}, bf16[4,2,128,128]{3,2,1,0:T(8,128)(2,1)S(1)}, u32[]{:S(2)}, u32[]{:S(2)}) %collective-permute-start.20) | collective-permute-done | bytes 262176 | tf_op jit(solution)/shard_map/ppermute | solution.py:370
  98.7 1.2 %add_convert_fusion = bf16[4,2,128,128]{3,2,1,0:T(8,128)(2,1)S(1)} fusion(bf16[4,2,128,128]{3,2,1,0:T(8,128)(2,1)S(1)} %collective-permute-done.21, bf16[4,2,128,128]{3,2,1,0:T(8,128)(2,1)S(1)} %collective-permute-done.20, f32[4,2,128,128]{3,2,1,0:T(8,128)} %get-tuple-element.67, bf16[4,2,128,128]{3,2,1,0:T(8,128)(2,1)S(1)} %collective-permute-done.19), kind=kLoop, calls=%fused_computation | loop fusion | flops 917504 | bytes 1572864 | tf_op jit(solution)/shard_map/convert.3
  99.9 0.6 slice_bitcast_fusion
  100.5 2.6 %collective-permute-start.24 = (bf16[2,128,128]{2,1,0:T(8,128)(2,1)S(1)}, bf16[2,128,128]{2,1,0:T(8,128)(2,1)S(1)}, u32[]{:S(2)}, u32[]{:S(2)}) collective-permute-start(bf16[2,128,128]{2,1,0:T(8,128)(2,1)S(1)} %get-tuple-element.73), channel_id=1, source_target_pairs={{0,6},{2,4},{4,2},{6,0},{1,7},{3,5},{5,3},{7,1},{8,14},{10,12},{12... | collective-permute-start | bytes 196616 | tf_op jit(solution)/shard_map/ppermute | solution.py:366
  103.2 0.3 collective-permute-start.23
  103.5 0.1 collective-permute-start.22
  103.6 0.6 copy-done.1
  104.4 3.4 %turn_back.1 = bf16[128,4096]{1,0:T(8,128)(2,1)} custom-call(s32[5]{0:T(128)} %stack.34.where_ref, f32[128,128]{1,0:T(8,128)} %get-tuple-element.38.cos_ref, f32[128,128]{1,0:T(8,128)} %get-tuple-element.39.sin_ref, bf16[2,512,128]{2,1,0:T(8,128)(2,1)} %get-tuple-element.63.refs_0_, bf16[2,512,128]{2,1,0:T(8,128)(2,1)} %copy-done.1, ...), custom_call_target="tpu_custom_call" | custom-call | tf_op jit(solution)/shard_map/turn_back/pallas_call | solution.py:328
  107.8 0.6 copy-done.5
  108.5 2.4 %last.1 = (bf16[128,512]{1,0:T(8,128)(2,1)}, bf16[128,512]{1,0:T(8,128)(2,1)}) custom-call(s32[5]{0:T(128)} %stack.34.where_ref, f32[128,128]{1,0:T(8,128)} %get-tuple-element.38.cos_ref, f32[128,128]{1,0:T(8,128)} %get-tuple-element.39.sin_ref, bf16[2,128,128]{2,1,0:T(8,128)(2,1)} %get-tuple-element.76.refs_0_, bf16[2,128,128]{2,1,0:T(8,128)(2,1)} %copy-done.7, ...), custom_call_target="tpu_custom_call" | custom-call | tf_op jit(solution)/shard_map/last/pallas_call | solution.py:328
  (61 shorter events, 0.7 us)
Async XLA Ops:
  4.3 13.0 %collective-permute-start.7 = (bf16[64,4096]{1,0:T(8,128)(2,1)}, bf16[64,4096]{1,0:T(8,128)(2,1)S(1)}, u32[]{:S(2)}, u32[]{:S(2)}) collective-permute-start(bf16[64,4096]{1,0:T(8,128)(2,1)} %get-tuple-element.53), channel_id=1, source_target_pairs={{0,1},{1,0},{2,3},{3,2},{4,5},{5,4},{6,7},{7,6},{8,9},{9,8},{10,11... | collective-permute-start | bytes 1572872 | tf_op jit(solution)/shard_map/ppermute | solution.py:398
  5.5 6.0 %collective-permute-start = (bf16[2,128,128]{2,1,0:T(8,128)(2,1)}, bf16[2,128,128]{2,1,0:T(8,128)(2,1)S(1)}, u32[]{:S(2)}, u32[]{:S(2)}) collective-permute-start(bf16[2,128,128]{2,1,0:T(8,128)(2,1)} %get-tuple-element.41), channel_id=1, source_target_pairs={{0,2},{2,0},{4,6},{6,4},{1,3},{3,1},{5,7},{7,5},{8,10},{10,8},{12,... | collective-permute-start | bytes 196616 | tf_op jit(solution)/shard_map/ppermute | solution.py:366
  6.5 5.0 %collective-permute-start.1 = (bf16[2,128,128]{2,1,0:T(8,128)(2,1)}, bf16[2,128,128]{2,1,0:T(8,128)(2,1)S(1)}, u32[]{:S(2)}, u32[]{:S(2)}) collective-permute-start(bf16[2,128,128]{2,1,0:T(8,128)(2,1)} %get-tuple-element.42), channel_id=1, source_target_pairs={{0,4},{2,6},{4,0},{6,2},{1,5},{3,7},{5,1},{7,3},{8,12},{10,14},{12... | collective-permute-start | bytes 196616 | tf_op jit(solution)/shard_map/ppermute | solution.py:366
  7.7 4.5 %collective-permute-start.2 = (bf16[2,128,128]{2,1,0:T(8,128)(2,1)}, bf16[2,128,128]{2,1,0:T(8,128)(2,1)S(1)}, u32[]{:S(2)}, u32[]{:S(2)}) collective-permute-start(bf16[2,128,128]{2,1,0:T(8,128)(2,1)} %get-tuple-element.43), channel_id=1, source_target_pairs={{0,6},{2,4},{4,2},{6,0},{1,7},{3,5},{5,3},{7,1},{8,14},{10,12},{12... | collective-permute-start | bytes 196616 | tf_op jit(solution)/shard_map/ppermute | solution.py:366
  8.1 27.9 %copy-start.8 = (s32[4,2]{0,1:T(2,128)S(1)}, s32[4,2]{0,1:T(2,128)}, u32[]{:S(2)}) copy-start(s32[4,2]{0,1:T(2,128)} %param.17) | copy-start | bytes 100
  13.1 42.8 %copy-start.4 = (bf16[4,2,128,128]{3,2,1,0:T(8,128)(2,1)}, bf16[4,2,128,128]{3,2,1,0:T(8,128)(2,1)S(1)}, u32[]{:S(2)}) copy-start(bf16[4,2,128,128]{3,2,1,0:T(8,128)(2,1)S(1)} %pad_maximum_fusion.refs_1_) | copy-start | bytes 786436
  13.1 10.3 %collective-permute-start.4 = (bf16[2,512,128]{2,1,0:T(8,128)(2,1)}, bf16[2,512,128]{2,1,0:T(8,128)(2,1)S(1)}, u32[]{:S(2)}, u32[]{:S(2)}) collective-permute-start(bf16[2,512,128]{2,1,0:T(8,128)(2,1)} %get-tuple-element.50), channel_id=1, source_target_pairs={{0,2},{2,0},{4,6},{6,4},{1,3},{3,1},{5,7},{7,5},{8,10},{10,8},{12,... | collective-permute-start | bytes 786440 | tf_op jit(solution)/shard_map/ppermute | solution.py:366
  13.3 12.1 %collective-permute-start.5 = (bf16[2,512,128]{2,1,0:T(8,128)(2,1)}, bf16[2,512,128]{2,1,0:T(8,128)(2,1)S(1)}, u32[]{:S(2)}, u32[]{:S(2)}) collective-permute-start(bf16[2,512,128]{2,1,0:T(8,128)(2,1)} %get-tuple-element.51), channel_id=1, source_target_pairs={{0,4},{2,6},{4,0},{6,2},{1,5},{3,7},{5,1},{7,3},{8,12},{10,14},{12... | collective-permute-start | bytes 786440 | tf_op jit(solution)/shard_map/ppermute | solution.py:366
  14.5 12.9 %collective-permute-start.6 = (bf16[2,512,128]{2,1,0:T(8,128)(2,1)}, bf16[2,512,128]{2,1,0:T(8,128)(2,1)S(1)}, u32[]{:S(2)}, u32[]{:S(2)}) collective-permute-start(bf16[2,512,128]{2,1,0:T(8,128)(2,1)} %get-tuple-element.52), channel_id=1, source_target_pairs={{0,6},{2,4},{4,2},{6,0},{1,7},{3,5},{5,3},{7,1},{8,14},{10,12},{12... | collective-permute-start | bytes 786440 | tf_op jit(solution)/shard_map/ppermute | solution.py:366
  15.3 12.7 %collective-permute-start.15 = (bf16[4,2,128,128]{3,2,1,0:T(8,128)(2,1)S(1)}, bf16[4,2,128,128]{3,2,1,0:T(8,128)(2,1)S(1)}, u32[]{:S(2)}, u32[]{:S(2)}) collective-permute-start(bf16[4,2,128,128]{3,2,1,0:T(8,128)(2,1)S(1)} %pad_maximum_fusion.refs_1_), channel_id=1, source_target_pairs={{0,8},{8,16},{16,24},{24,0},{1,9},{9,17},{17,25},{25,1},{2,10},{10... | collective-permute-start | bytes 786440 | tf_op jit(solution)/shard_map/ppermute | solution.py:370
  17.3 2.3 %copy-start = (bf16[64,4096]{1,0:T(8,128)(2,1)}, bf16[64,4096]{1,0:T(8,128)(2,1)S(1)}, u32[]{:S(2)}) copy-start(bf16[64,4096]{1,0:T(8,128)(2,1)S(1)} %collective-permute-done.7.refs_1_) | copy-start | bytes 1572868
  17.3 16.4 %collective-permute-start.14 = (bf16[4,2,128,128]{3,2,1,0:T(8,128)(2,1)S(1)}, bf16[4,2,128,128]{3,2,1,0:T(8,128)(2,1)S(1)}, u32[]{:S(2)}, u32[]{:S(2)}) collective-permute-start(bf16[4,2,128,128]{3,2,1,0:T(8,128)(2,1)S(1)} %pad_maximum_fusion.refs_1_), channel_id=1, source_target_pairs={{0,16},{8,24},{16,0},{24,8},{1,17},{9,25},{17,1},{25,9},{2,18},{10... | collective-permute-start | bytes 786440 | tf_op jit(solution)/shard_map/ppermute | solution.py:370
  23.4 16.4 %copy-start.9 = (bf16[2,512,128]{2,1,0:T(8,128)(2,1)}, bf16[2,512,128]{2,1,0:T(8,128)(2,1)S(1)}, u32[]{:S(2)}) copy-start(bf16[2,512,128]{2,1,0:T(8,128)(2,1)S(1)} %collective-permute-done.4.refs_3_) | copy-start | bytes 786436
  23.4 16.3 %collective-permute-start.8 = (bf16[2,512,128]{2,1,0:T(8,128)(2,1)}, bf16[2,512,128]{2,1,0:T(8,128)(2,1)S(1)}, u32[]{:S(2)}, u32[]{:S(2)}) collective-permute-start(bf16[2,512,128]{2,1,0:T(8,128)(2,1)} %get-tuple-element.55), channel_id=1, source_target_pairs={{0,2},{2,0},{4,6},{6,4},{1,3},{3,1},{5,7},{7,5},{8,10},{10,8},{12,... | collective-permute-start | bytes 786440 | tf_op jit(solution)/shard_map/ppermute | solution.py:366
  25.3 14.5 %copy-start.10 = (bf16[2,512,128]{2,1,0:T(8,128)(2,1)}, bf16[2,512,128]{2,1,0:T(8,128)(2,1)S(1)}, u32[]{:S(2)}) copy-start(bf16[2,512,128]{2,1,0:T(8,128)(2,1)S(1)} %collective-permute-done.5.refs_4_) | copy-start | bytes 786436
  25.3 14.4 %collective-permute-start.9 = (bf16[2,512,128]{2,1,0:T(8,128)(2,1)}, bf16[2,512,128]{2,1,0:T(8,128)(2,1)S(1)}, u32[]{:S(2)}, u32[]{:S(2)}) collective-permute-start(bf16[2,512,128]{2,1,0:T(8,128)(2,1)} %get-tuple-element.56), channel_id=1, source_target_pairs={{0,4},{2,6},{4,0},{6,2},{1,5},{3,7},{5,1},{7,3},{8,12},{10,14},{12... | collective-permute-start | bytes 786440 | tf_op jit(solution)/shard_map/ppermute | solution.py:366
  27.4 12.4 %copy-start.11 = (bf16[2,512,128]{2,1,0:T(8,128)(2,1)}, bf16[2,512,128]{2,1,0:T(8,128)(2,1)S(1)}, u32[]{:S(2)}) copy-start(bf16[2,512,128]{2,1,0:T(8,128)(2,1)S(1)} %collective-permute-done.6.refs_5_) | copy-start | bytes 786436
  27.4 12.4 %collective-permute-start.10 = (bf16[2,512,128]{2,1,0:T(8,128)(2,1)}, bf16[2,512,128]{2,1,0:T(8,128)(2,1)S(1)}, u32[]{:S(2)}, u32[]{:S(2)}) collective-permute-start(bf16[2,512,128]{2,1,0:T(8,128)(2,1)} %get-tuple-element.57), channel_id=1, source_target_pairs={{0,6},{2,4},{4,2},{6,0},{1,7},{3,5},{5,3},{7,1},{8,14},{10,12},{12... | collective-permute-start | bytes 786440 | tf_op jit(solution)/shard_map/ppermute | solution.py:366
  28.1 11.8 %copy-start.12 = (bf16[4,2,128,128]{3,2,1,0:T(8,128)(2,1)}, bf16[4,2,128,128]{3,2,1,0:T(8,128)(2,1)S(1)}, u32[]{:S(2)}) copy-start(bf16[4,2,128,128]{3,2,1,0:T(8,128)(2,1)S(1)} %collective-permute-done.15.refs_1_) | copy-start | bytes 786436
  28.1 6.9 %collective-permute-start.11 = (f32[4,512]{1,0:T(4,128)}, f32[4,512]{1,0:T(4,128)S(1)}, u32[]{:S(2)}, u32[]{:S(2)}) collective-permute-start(f32[4,512]{1,0:T(4,128)} %get-tuple-element.59), channel_id=1, source_target_pairs={{0,2},{2,0},{4,6},{6,4},{1,3},{3,1},{5,7},{7,5},{8,10},{10,8},{12,... | collective-permute-start | bytes 24584 | tf_op jit(solution)/shard_map/ppermute | solution.py:366
  33.7 6.1 %copy-start.13 = (bf16[4,2,128,128]{3,2,1,0:T(8,128)(2,1)}, bf16[4,2,128,128]{3,2,1,0:T(8,128)(2,1)S(1)}, u32[]{:S(2)}) copy-start(bf16[4,2,128,128]{3,2,1,0:T(8,128)(2,1)S(1)} %collective-permute-done.14.refs_0_) | copy-start | bytes 786436
  33.7 5.3 %collective-permute-start.12 = (f32[4,512]{1,0:T(4,128)}, f32[4,512]{1,0:T(4,128)S(1)}, u32[]{:S(2)}, u32[]{:S(2)}) collective-permute-start(f32[4,512]{1,0:T(4,128)} %get-tuple-element.60), channel_id=1, source_target_pairs={{0,4},{2,6},{4,0},{6,2},{1,5},{3,7},{5,1},{7,3},{8,12},{10,14},{12... | collective-permute-start | bytes 24584 | tf_op jit(solution)/shard_map/ppermute | solution.py:366
  35.0 4.9 %copy-start.20 = (f32[4,512]{1,0:T(4,128)}, f32[4,512]{1,0:T(4,128)S(1)}, u32[]{:S(2)}) copy-start(f32[4,512]{1,0:T(4,128)S(1)} %collective-permute-done.11.refs_11_) | copy-start | bytes 24580
  35.0 4.8 %collective-permute-start.13 = (f32[4,512]{1,0:T(4,128)}, f32[4,512]{1,0:T(4,128)S(1)}, u32[]{:S(2)}, u32[]{:S(2)}) collective-permute-start(f32[4,512]{1,0:T(4,128)} %get-tuple-element.61), channel_id=1, source_target_pairs={{0,6},{2,4},{4,2},{6,0},{1,7},{3,5},{5,3},{7,1},{8,14},{10,12},{12... | collective-permute-start | bytes 24584 | tf_op jit(solution)/shard_map/ppermute | solution.py:366
  39.0 0.8 copy-start.21
  39.0 16.9 %collective-permute-start.3 = (bf16[4,2,128,128]{3,2,1,0:T(8,128)(2,1)S(1)}, bf16[4,2,128,128]{3,2,1,0:T(8,128)(2,1)S(1)}, u32[]{:S(2)}, u32[]{:S(2)}) collective-permute-start(bf16[4,2,128,128]{3,2,1,0:T(8,128)(2,1)S(1)} %pad_maximum_fusion.refs_1_), channel_id=1, source_target_pairs={{0,24},{8,0},{16,8},{24,16},{1,25},{9,1},{17,9},{25,17},{2,26},{10... | collective-permute-start | bytes 786440 | tf_op jit(solution)/shard_map/ppermute | solution.py:370
  39.8 0.6 copy-start.22
  39.8 0.7 copy-start.14
  39.8 0.8 copy-start.15
  39.8 0.9 copy-start.16
  55.9 0.7 copy-start.19
  56.6 17.5 %copy-start.18 = (bf16[4,2,128,128]{3,2,1,0:T(8,128)(2,1)S(1)}, bf16[4,2,128,128]{3,2,1,0:T(8,128)(2,1)}, u32[]{:S(2)}) copy-start(bf16[4,2,128,128]{3,2,1,0:T(8,128)(2,1)} %get-tuple-element.68) | copy-start | bytes 786436
  56.6 20.4 %copy-start.17 = (bf16[4,2,128,128]{3,2,1,0:T(8,128)(2,1)S(1)}, bf16[4,2,128,128]{3,2,1,0:T(8,128)(2,1)}, u32[]{:S(2)}) copy-start(bf16[4,2,128,128]{3,2,1,0:T(8,128)(2,1)} %get-tuple-element.69) | copy-start | bytes 786436
  73.4 7.2 %collective-permute-start.21 = (bf16[4,2,128,128]{3,2,1,0:T(8,128)(2,1)}, bf16[4,2,128,128]{3,2,1,0:T(8,128)(2,1)S(1)}, u32[]{:S(2)}, u32[]{:S(2)}) collective-permute-start(bf16[4,2,128,128]{3,2,1,0:T(8,128)(2,1)} %get-tuple-element.70), channel_id=1, source_target_pairs={{0,8},{8,16},{16,24},{24,0},{1,9},{9,17},{17,25},{25,1},{2,10},{10... | collective-permute-start | bytes 786440 | tf_op jit(solution)/shard_map/ppermute | solution.py:370
  74.1 21.2 %collective-permute-start.19 = (bf16[4,2,128,128]{3,2,1,0:T(8,128)(2,1)S(1)}, bf16[4,2,128,128]{3,2,1,0:T(8,128)(2,1)S(1)}, u32[]{:S(2)}, u32[]{:S(2)}) collective-permute-start(bf16[4,2,128,128]{3,2,1,0:T(8,128)(2,1)S(1)} %copy-done.18), channel_id=1, source_target_pairs={{0,16},{8,24},{16,0},{24,8},{1,17},{9,25},{17,1},{25,9},{2,18},{10... | collective-permute-start | bytes 786440 | tf_op jit(solution)/shard_map/ppermute | solution.py:370
  77.0 21.7 %collective-permute-start.20 = (bf16[4,2,128,128]{3,2,1,0:T(8,128)(2,1)S(1)}, bf16[4,2,128,128]{3,2,1,0:T(8,128)(2,1)S(1)}, u32[]{:S(2)}, u32[]{:S(2)}) collective-permute-start(bf16[4,2,128,128]{3,2,1,0:T(8,128)(2,1)S(1)} %copy-done.17), channel_id=1, source_target_pairs={{0,24},{8,0},{16,8},{24,16},{1,25},{9,1},{17,9},{25,17},{2,26},{10... | collective-permute-start | bytes 786440 | tf_op jit(solution)/shard_map/ppermute | solution.py:370
  77.0 26.5 %collective-permute-start.16 = (bf16[2,512,128]{2,1,0:T(8,128)(2,1)}, bf16[2,512,128]{2,1,0:T(8,128)(2,1)S(1)}, u32[]{:S(2)}, u32[]{:S(2)}) collective-permute-start(bf16[2,512,128]{2,1,0:T(8,128)(2,1)} %get-tuple-element.64), channel_id=1, source_target_pairs={{0,2},{2,0},{4,6},{6,4},{1,3},{3,1},{5,7},{7,5},{8,10},{10,8},{12,... | collective-permute-start | bytes 786440 | tf_op jit(solution)/shard_map/ppermute | solution.py:366
  79.2 24.4 %collective-permute-start.17 = (bf16[2,512,128]{2,1,0:T(8,128)(2,1)}, bf16[2,512,128]{2,1,0:T(8,128)(2,1)S(1)}, u32[]{:S(2)}, u32[]{:S(2)}) collective-permute-start(bf16[2,512,128]{2,1,0:T(8,128)(2,1)} %get-tuple-element.65), channel_id=1, source_target_pairs={{0,4},{2,6},{4,0},{6,2},{1,5},{3,7},{5,1},{7,3},{8,12},{10,14},{12... | collective-permute-start | bytes 786440 | tf_op jit(solution)/shard_map/ppermute | solution.py:366
  80.5 23.1 %collective-permute-start.18 = (bf16[2,512,128]{2,1,0:T(8,128)(2,1)}, bf16[2,512,128]{2,1,0:T(8,128)(2,1)S(1)}, u32[]{:S(2)}, u32[]{:S(2)}) collective-permute-start(bf16[2,512,128]{2,1,0:T(8,128)(2,1)} %get-tuple-element.66), channel_id=1, source_target_pairs={{0,6},{2,4},{4,2},{6,0},{1,7},{3,5},{5,3},{7,1},{8,14},{10,12},{12... | collective-permute-start | bytes 786440 | tf_op jit(solution)/shard_map/ppermute | solution.py:366
  100.5 7.2 %collective-permute-start.24 = (bf16[2,128,128]{2,1,0:T(8,128)(2,1)S(1)}, bf16[2,128,128]{2,1,0:T(8,128)(2,1)S(1)}, u32[]{:S(2)}, u32[]{:S(2)}) collective-permute-start(bf16[2,128,128]{2,1,0:T(8,128)(2,1)S(1)} %get-tuple-element.73), channel_id=1, source_target_pairs={{0,6},{2,4},{4,2},{6,0},{1,7},{3,5},{5,3},{7,1},{8,14},{10,12},{12... | collective-permute-start | bytes 196616 | tf_op jit(solution)/shard_map/ppermute | solution.py:366
  103.2 4.6 %collective-permute-start.23 = (bf16[2,128,128]{2,1,0:T(8,128)(2,1)S(1)}, bf16[2,128,128]{2,1,0:T(8,128)(2,1)S(1)}, u32[]{:S(2)}, u32[]{:S(2)}) collective-permute-start(bf16[2,128,128]{2,1,0:T(8,128)(2,1)S(1)} %get-tuple-element.74), channel_id=1, source_target_pairs={{0,4},{2,6},{4,0},{6,2},{1,5},{3,7},{5,1},{7,3},{8,12},{10,14},{12... | collective-permute-start | bytes 196616 | tf_op jit(solution)/shard_map/ppermute | solution.py:366
  103.5 0.7 copy-start.1
  103.5 4.3 %collective-permute-start.22 = (bf16[2,128,128]{2,1,0:T(8,128)(2,1)S(1)}, bf16[2,128,128]{2,1,0:T(8,128)(2,1)S(1)}, u32[]{:S(2)}, u32[]{:S(2)}) collective-permute-start(bf16[2,128,128]{2,1,0:T(8,128)(2,1)S(1)} %get-tuple-element.75), channel_id=1, source_target_pairs={{0,2},{2,0},{4,6},{6,4},{1,3},{3,1},{5,7},{7,5},{8,10},{10,8},{12,... | collective-permute-start | bytes 196616 | tf_op jit(solution)/shard_map/ppermute | solution.py:366
  103.6 0.7 copy-start.2
  103.6 0.8 copy-start.3
  107.8 0.6 copy-start.5
  107.8 0.6 copy-start.6
  107.8 0.6 copy-start.7

commit v4 on v3

--- a/solution.py
+++ b/solution.py
@@ -13,6 +13,8 @@
 BLOCKS_DEV = 2
 THETA = 1000000.0
 CHUNK = 256
+WIDE = 512
+STAT_ROWS = 32
 SCORE_SCALE = 1.0 / math.sqrt(HEAD_SIZE)
 LOG2E = math.log2(math.e)
 MEMORY = 56 * 1024 * 1024
@@ -72,27 +74,44 @@
     return slice(head * block_len, (head + 1) * block_len)
 
 
-def query_kernel(members, group, where_ref, cos_ref, sin_ref, q_ref, *out_refs):
-    member = where_ref[0]
+def query_kernel(members, group, cos_ref, sin_ref, q_ref, out_ref):
     cosine = cos_ref[...]
     signed = sin_ref[...] * half_sign()
     block_len = q_ref.shape[0] // BLOCKS_DEV
-    for flip in range(members):
+    for member in range(members):
         for head in range(group):
-            field = q_ref[:, head_lanes(member, flip, group, head)].astype(jnp.float32)
+            first = (member * group + head) * HEAD_SIZE
+            field = q_ref[:, first : first + HEAD_SIZE].astype(jnp.float32)
             turned = pltpu.roll(field, HEAD_SIZE // 2, 1)
             field = (field * cosine + turned * signed).astype(jnp.bfloat16)
             for step in range(BLOCKS_DEV):
-                out_refs[flip][step, stacked(head, block_len), :] = field[
+                out_ref[member, step, stacked(head, block_len), :] = field[
                     step * block_len : (step + 1) * block_len, :
                 ]
+
+
+def split_rows(vector):
+    pieces = []
+    for _ in range(3):
+        addend = vector.astype(jnp.bfloat16).astype(jnp.float32)
+        vector = vector - addend
+        pieces += [
+            addend[:, i : i + HEAD_SIZE] for i in range(0, addend.shape[1], HEAD_SIZE)
+        ]
+    return pieces
+
+
+def joined_row(rows):
+    count = rows.shape[0] // 3
+    total = rows[:count] + rows[count : 2 * count] + rows[2 * count :]
+    return jnp.concatenate([total[i : i + 1] for i in range(count)], axis=1)
 
 
 def delta_kernel(members, group, where_ref, a_ref, l_ref, *refs):
     refs = list(refs)
     own_ref = refs.pop(0)
     other_ref = refs.pop(0) if members > 1 else None
-    grad_refs, stat_refs = refs[:members], refs[members:]
+    grad_refs = refs
     member, tp_index = where_ref[0], where_ref[1]
     block_len = a_ref.shape[0] // BLOCKS_DEV
     for flip in range(members):
@@ -117,8 +136,12 @@
                 ].astype(jnp.float32)
                 sums.append(product)
             total = jnp.sum(jnp.concatenate(sums, axis=0).T, axis=0, keepdims=True)
-            stat_refs[flip][2 * step : 2 * step + 1, :] = row_vector(lse, step, block_len)
-            stat_refs[flip][2 * step + 1 : 2 * step + 2, :] = total
+            pieces = split_rows(row_vector(lse, step, block_len)) + split_rows(total)
+            pieces.append(jnp.zeros((STAT_ROWS - len(pieces), HEAD_SIZE), jnp.float32))
+            below = group * block_len
+            g_ref[step, below : below + STAT_ROWS, :] = jnp.concatenate(pieces, axis=0).astype(
+                jnp.bfloat16
+            )
 
 
 def row_vector(table, upper, block_len):
@@ -139,9 +162,8 @@
     refs = list(refs)
     count = len(slabs)
     kv_refs = [refs.pop(0) for _ in range(count)]
-    q_refs = [refs.pop(0) for _ in range(members)]
+    q_ref = refs.pop(0)
     g_refs = [refs.pop(0) for _ in range(members)]
-    s_refs = [refs.pop(0) for _ in range(members)]
     in_ref = refs.pop(0) if carried else None
     dq_refs = [refs.pop(0) for _ in range(1 if carries else members)]
     part_refs = [refs.pop(0) for _ in range(count)]
@@ -212,10 +234,12 @@
     for flip in range(members):
         for step in range(BLOCKS_DEV):
             place = flip * BLOCKS_DEV + step
-            q_all[place] = q_refs[flip][step]
-            g_all[place] = g_refs[flip][step]
-            l_all[place] = s_refs[flip][2 * step : 2 * step + 1, :]
-            d_all[place] = s_refs[flip][2 * step + 1 : 2 * step + 2, :]
+            q_all[place] = q_ref[member ^ flip, step]
+            g_all[place] = g_refs[flip][step, :columns, :]
+            stats = g_refs[flip][step, columns:, :].astype(jnp.float32)
+            half = 3 * columns // HEAD_SIZE
+            l_all[place] = joined_row(stats[:half])
+            d_all[place] = joined_row(stats[half : 2 * half])
 
     lane = lax.broadcasted_iota(jnp.int32, (1, columns), 1)
     within = lax.rem(lane, block_len)
@@ -236,12 +260,12 @@
         seen = (blocks_before(jnp.maximum(end, block + 1)) + chunk_blocks - 1) // chunk_blocks
         dq_sum[...] = in_ref[place] if carried else jnp.zeros_like(dq_sum)
 
-        def visit(chunk, masked):
+        def visit(chunk, size, masked):
             queries = q_all[place]
             grads = g_all[place]
             at = pl.multiple_of(chunk * CHUNK, CHUNK)
-            keys = k_sort[pl.ds(at, CHUNK), :]
-            values = v_sort[pl.ds(at, CHUNK), :]
+            keys = k_sort[pl.ds(at, size), :]
+            values = v_sort[pl.ds(at, size), :]
             scores = lax.dot_general(
                 keys, queries, (((1,), (1,)), ((), ())), preferred_element_type=jnp.float32
             )
@@ -260,16 +284,21 @@
                 values, grads, (((1,), (1,)), ((), ())), preferred_element_type=jnp.float32
             )
             grad_s = (probs * (grad_p - d_all[place])).astype(jnp.bfloat16)
-            dv_sum[pl.ds(at, CHUNK), :] += jnp.dot(
+            dv_sum[pl.ds(at, size), :] += jnp.dot(
                 probs.astype(jnp.bfloat16), grads, preferred_element_type=jnp.float32
             )
-            dk_sum[pl.ds(at, CHUNK), :] += jnp.dot(
+            dk_sum[pl.ds(at, size), :] += jnp.dot(
                 grad_s, queries, preferred_element_type=jnp.float32
             )
-            dq_sum[...] += jnp.dot(k_turn[chunk], grad_s, preferred_element_type=jnp.float32)
-
-        pl.loop(0, full)(lambda chunk: visit(chunk, False))
-        pl.loop(full, seen)(lambda chunk: visit(chunk, True))
+            turned = [k_turn[chunk + i] for i in range(size // CHUNK)]
+            dq_sum[...] += jnp.dot(
+                jnp.concatenate(turned, axis=1), grad_s, preferred_element_type=jnp.float32
+            )
+
+        pairs = full // 2
+        pl.loop(0, pairs)(lambda pair: visit(2 * pair, WIDE, False))
+        pl.loop(2 * pairs, full)(lambda chunk: visit(chunk, CHUNK, False))
+        pl.loop(full, seen)(lambda chunk: visit(chunk, CHUNK, True))
 
         if carries:
             dq_refs[0][place] = dq_sum[...]
@@ -389,16 +418,16 @@
     kv_pieces = results[2 : 2 + members]
     columns = group * block_len
     stack = (BLOCKS_DEV, columns, HEAD_SIZE)
-    q_pieces = call(
+    (q_stack,) = call(
         functools.partial(query_kernel, members, group),
-        "rotate", [place], [cosine, sine, queries], [(stack, bf16)] * members,
+        "rotate", [], [cosine, sine, queries], [((members, *stack), bf16)],
     )
     if members > 1:
         slab = jnp.stack([flipped(kv_pieces[f], f) for f in every])
         grads_other = lax.ppermute(results[-1], "tp", [(0, 1), (1, 0)])
         far = sorted(range(1, layers), key=lambda k: abs(2 * k - layers))
         rounds = [far[: layers // 2], far[layers // 2 :] + [0]]
-        slab, *q_pieces = lax.optimization_barrier((slab, *q_pieces))
+        q_stack = lax.all_to_all(q_stack, ("y", "core"), 0, 0, tiled=True)
         kv = {0: slab}
         for k in far:
             kv[k] = climbed(slab, k)
@@ -406,7 +435,6 @@
         kv = {0: lax.all_gather(kv_pieces[0], ("z", "y", "core"), axis=0, tiled=False)}
         rounds = [[0]]
         grads_own = lax.all_to_all(out_grad, "tp", split_axis=1, concat_axis=0, tiled=True)
-    q_in = [flipped(q_pieces[f], f) for f in every]
 
     inputs = [attn_out, logsumexp]
     in_specs = [whole(a.shape) for a in inputs]
@@ -422,11 +450,10 @@
     results = call(
         functools.partial(delta_kernel, members, group),
         "delta", [place], inputs,
-        [(stack, bf16)] * members + [((2 * BLOCKS_DEV, columns), f32)] * members,
+        [((BLOCKS_DEV, columns + STAT_ROWS, HEAD_SIZE), bf16)] * members,
         in_specs,
     )
     g_in = [flipped(results[f], f) for f in every]
-    s_in = [flipped(results[members + f], f) for f in every]
 
     units = kv[0].shape[0]
     blocks = members * BLOCKS_DEV
@@ -442,7 +469,7 @@
                 attend_kernel, members, group, block_len, slabs, number > 0, carries
             ),
             "attend", [place, block_map, span_blocks.reshape(-1)],
-            [*[kv[k] for k in slabs], *q_in, *g_in, *s_in, *carry],
+            [*[kv[k] for k in slabs], q_stack, *g_in, *carry],
             ([(sums, f32)] if carries else [(stack, bf16)] * members)
             + [(part, f32 if k == 0 and members > 1 else bf16) for k in slabs],
             scratch=[
@@ -469,11 +496,17 @@
         outs = 1 if carries else members
         carry = results[:outs]
         parts.update(zip(slabs, results[outs:]))
+        if carries:
+            home = {k: climbed(parts[k], layers - k) for k in slabs}
     dq_pieces = carry
     if members > 1:
-        total = parts[0]
+        carry, home, late = lax.optimization_barrier(
+            (carry, home, {k: parts[k] for k in rounds[-1]})
+        )
+        dq_pieces, total = carry, late.pop(0)
+        home.update({k: climbed(late[k], layers - k) for k in late})
         for k in far:
-            total = total + climbed(parts[k], layers - k).astype(f32)
+            total = total + home[k].astype(f32)
         sums = [flipped(total[f].astype(bf16), f) for f in every]
     else:
         sums = [

time: 112 us -> 114 us (1.018)
  the two profiles are of different devices: /device:TPU:9 before, /device:TPU:0 now
where the time goes in v4:
time: 114 us; the launch traced here: 113 us
  Pallas kernels  47.3 us (41%)
  waiting for transfers between devices  32.5 us (29%)
  starting transfers between devices  24.8 us (22%)
  local copies, waits for them, and re-layouts  6.16 us (5%)
  other arithmetic  1.2 us (1%)
    pallas_call x7, Pallas kernels, call(): pl.pallas_call(kernel, grid_spec=pltpu.PrefetchScalarGridSpec(num_scalar_...  47.3 us
    ppermute x6, waiting for transfers between devices, climbed(): return lax.ppermute(array, 'z', route)  23.5 us
    ppermute x6, starting transfers between devices, climbed(): return lax.ppermute(array, 'z', route)  10.4 us
    ppermute x12, starting transfers between devices, flipped(): return lax.ppermute(array, ('y', 'core'), [(i, i ^ flip) for i in range(4)])  7.78 us
    ppermute x12, waiting for transfers between devices, flipped(): return lax.ppermute(array, ('y', 'core'), [(i, i ^ flip) for i in range(4)])  5.48 us
    unnamed x41, local copies, waits for them, and re-layouts  4.26 us
    all_to_all x1, starting transfers between devices, shards(): q_stack = lax.all_to_all(q_stack, ('y', 'core'), 0, 0, tiled=True)  3.65 us
    ppermute x1, waiting for transfers between devices, shards(): grads_other = lax.ppermute(results[-1], 'tp', [(0, 1), (1, 0)])  3.5 us
  transfers between devices with their start and end apart: 20, of which 8 were waited for; matrix products, arithmetic and copies ran while one was open for 2% of the time, Pallas kernels for 37%

profile of v4, /device:TPU:0, one launch (start us, length us, event | category | flops | bytes accessed | tf_op | source)
XLA Modules:
  0.0 112.7 jit_solution(16278848822512223838)
XLA Ops:
  0.6 0.7 stack.34.where_ref
  1.3 3.0 %first.1 = (f32[128,128]{1,0:T(8,128)}, f32[128,128]{1,0:T(8,128)}, bf16[2,128,128]{2,1,0:T(8,128)(2,1)}, bf16[2,128,128]{2,1,0:T(8,128)(2,1)}, bf16[2,128,128]{...) custom-call(s32[5]{0:T(128)} %stack.34.where_ref, s32[3,128]{1,0:T(4,128)} %ids_ref.1, ...), custom_call_target="tpu_custom_call" | custom-call | tf_op jit(solution)/shard_map/first/pallas_call | solution.py:357
  4.3 2.9 %collective-permute-start.4 = (bf16[64,4096]{1,0:T(8,128)(2,1)}, bf16[64,4096]{1,0:T(8,128)(2,1)S(1)}, u32[]{:S(2)}, u32[]{:S(2)}) collective-permute-start(bf16[64,4096]{1,0:T(8,128)(2,1)} %get-tuple-element.39), channel_id=1, source_target_pairs={{0,1},{1,0},{2,3},{3,2},{4,5},{5,4},{6,7},{7,6},{8,9},{9,8},{10,11... | collective-permute-start | bytes 1572872 | tf_op jit(solution)/shard_map/ppermute | solution.py:427
  7.3 2.8 %rotate.1 = bf16[4,2,512,128]{3,2,1,0:T(8,128)(2,1)} custom-call(f32[128,128]{1,0:T(8,128)} %get-tuple-element.33.cos_ref, f32[128,128]{1,0:T(8,128)} %get-tuple-element.34.sin_ref, bf16[128,4096]{1,0:T(8,128)(2,1)} %q_ref.1), custom_call_target="tpu_custom_call" | custom-call | tf_op jit(solution)/shard_map/rotate/pallas_call | solution.py:357
  10.1 3.6 %all-to-all-start = ((bf16[4,2,512,128]{3,2,1,0:T(8,128)(2,1)}), bf16[4,2,512,128]{3,2,1,0:T(8,128)(2,1)S(1)}, u32[]{:S(2)}, u32[]{:S(2)}) async-start(bf16[4,2,512,128]{3,2,1,0:T(8,128)(2,1)} %rotate.1), calls=%async_computation | async-start | bytes 2097152 | tf_op jit(solution)/shard_map/all_to_all | solution.py:430
  13.7 0.0 copy-start.10
  13.7 0.5 collective-permute-start
  14.2 1.7 %collective-permute-start.1 = (bf16[2,128,128]{2,1,0:T(8,128)(2,1)S(1)}, bf16[2,128,128]{2,1,0:T(8,128)(2,1)S(1)}, u32[]{:S(2)}, u32[]{:S(2)}) collective-permute-start(bf16[2,128,128]{2,1,0:T(8,128)(2,1)S(1)} %copy-done.18), channel_id=1, source_target_pairs={{0,4},{2,6},{4,0},{6,2},{1,5},{3,7},{5,1},{7,3},{8,12},{10,14},{12... | collective-permute-start | bytes 196616 | tf_op jit(solution)/shard_map/ppermute | solution.py:395
  15.9 0.0 collective-permute-start.2
  15.9 3.5 %collective-permute-done.4.refs_1_ = bf16[64,4096]{1,0:T(8,128)(2,1)S(1)} collective-permute-done((bf16[64,4096]{1,0:T(8,128)(2,1)}, bf16[64,4096]{1,0:T(8,128)(2,1)S(1)}, u32[]{:S(2)}, u32[]{:S(2)}) %collective-permute-start.4) | collective-permute-done | bytes 524320 | tf_op jit(solution)/shard_map/ppermute | solution.py:427
  19.4 0.8 copy-done.1
  20.2 3.9 %delta.1 = (bf16[2,544,128]{2,1,0:T(8,128)(2,1)}, bf16[2,544,128]{2,1,0:T(8,128)(2,1)}, bf16[2,544,128]{2,1,0:T(8,128)(2,1)}, bf16[2,544,128]{2,1,0:T(8,128)(2,1)}) custom-call(s32[5]{0:T(128)} %stack.34.where_ref, bf16[128,4096]{1,0:T(8,128)(2,1)} %a_ref.1, f32[32,128]{1,0:T(8,128)} %l_ref.1, bf16[64,8192]{1,0:T(8,128)(2,1)} %refs_0_.3, ...), custom_call_target="tpu_custom_call" | custom-call | tf_op jit(solution)/shard_map/delta/pallas_call | solution.py:357
  24.1 0.0 collective-permute-start.5
  24.1 1.8 %collective-permute-start.6 = (bf16[2,544,128]{2,1,0:T(8,128)(2,1)}, bf16[2,544,128]{2,1,0:T(8,128)(2,1)S(1)}, u32[]{:S(2)}, u32[]{:S(2)}) collective-permute-start(bf16[2,544,128]{2,1,0:T(8,128)(2,1)} %get-tuple-element.42), channel_id=1, source_target_pairs={{0,4},{2,6},{4,0},{6,2},{1,5},{3,7},{5,1},{7,3},{8,12},{10,14},{12... | collective-permute-start | bytes 835592 | tf_op jit(solution)/shard_map/ppermute | solution.py:395
  25.9 0.1 collective-permute-start.7
  26.0 4.0 %collective-permute-done.1 = bf16[2,128,128]{2,1,0:T(8,128)(2,1)S(1)} collective-permute-done((bf16[2,128,128]{2,1,0:T(8,128)(2,1)S(1)}, bf16[2,128,128]{2,1,0:T(8,128)(2,1)S(1)}, u32[]{:S(2)}, u32[]{:S(2)}) %collective-permute-start.1) | collective-permute-done | bytes 65568 | tf_op jit(solution)/shard_map/ppermute | solution.py:395
  30.0 0.5 collective-permute-done.2
  30.5 1.6 %collective-permute-start.9 = (bf16[4,2,128,128]{3,2,1,0:T(8,128)(2,1)S(1)}, bf16[4,2,128,128]{3,2,1,0:T(8,128)(2,1)S(1)}, u32[]{:S(2)}, u32[]{:S(2)}) collective-permute-start(bf16[4,2,128,128]{3,2,1,0:T(8,128)(2,1)S(1)} %pad_maximum_fusion.refs_1_), channel_id=1, source_target_pairs={{0,8},{8,16},{16,24},{24,0},{1,9},{9,17},{17,25},{25,1},{2,10},{10... | collective-permute-start | bytes 786440 | tf_op jit(solution)/shard_map/ppermute | solution.py:399
  32.2 2.6 %collective-permute-start.8 = (bf16[4,2,128,128]{3,2,1,0:T(8,128)(2,1)S(1)}, bf16[4,2,128,128]{3,2,1,0:T(8,128)(2,1)S(1)}, u32[]{:S(2)}, u32[]{:S(2)}) collective-permute-start(bf16[4,2,128,128]{3,2,1,0:T(8,128)(2,1)S(1)} %pad_maximum_fusion.refs_1_), channel_id=1, source_target_pairs={{0,16},{8,24},{16,0},{24,8},{1,17},{9,25},{17,1},{25,9},{2,18},{10... | collective-permute-start | bytes 786440 | tf_op jit(solution)/shard_map/ppermute | solution.py:399
  34.8 0.1 copy.13
  34.9 0.6 reshape.14.span_ref
  35.4 6.2 %collective-permute-done.9.refs_1_ = bf16[4,2,128,128]{3,2,1,0:T(8,128)(2,1)S(1)} collective-permute-done((bf16[4,2,128,128]{3,2,1,0:T(8,128)(2,1)S(1)}, bf16[4,2,128,128]{3,2,1,0:T(8,128)(2,1)S(1)}, u32[]{:S(2)}, u32[]{:S(2)}) %collective-permute-start.9) | collective-permute-done | bytes 262176 | tf_op jit(solution)/shard_map/ppermute | solution.py:399
  41.7 1.6 %collective-permute-start.3 = (bf16[4,2,128,128]{3,2,1,0:T(8,128)(2,1)S(1)}, bf16[4,2,128,128]{3,2,1,0:T(8,128)(2,1)S(1)}, u32[]{:S(2)}, u32[]{:S(2)}) collective-permute-start(bf16[4,2,128,128]{3,2,1,0:T(8,128)(2,1)S(1)} %pad_maximum_fusion.refs_1_), channel_id=1, source_target_pairs={{0,24},{8,0},{16,8},{24,16},{1,25},{9,1},{17,9},{25,17},{2,26},{10... | collective-permute-start | bytes 786440 | tf_op jit(solution)/shard_map/ppermute | solution.py:399
  43.3 9.5 %collective-permute-done.8.refs_0_ = bf16[4,2,128,128]{3,2,1,0:T(8,128)(2,1)S(1)} collective-permute-done((bf16[4,2,128,128]{3,2,1,0:T(8,128)(2,1)S(1)}, bf16[4,2,128,128]{3,2,1,0:T(8,128)(2,1)S(1)}, u32[]{:S(2)}, u32[]{:S(2)}) %collective-permute-start.8) | collective-permute-done | bytes 262176 | tf_op jit(solution)/shard_map/ppermute | solution.py:399
  52.8 0.6 copy-done.16
  53.5 0.4 copy-done
  53.8 0.1 copy-done.11
  53.9 0.1 copy-done.12
  54.0 0.1 copy-done.13
  54.1 15.2 %attend.2 = (f32[8,128,512]{2,1,0:T(8,128)}, bf16[4,2,128,128]{3,2,1,0:T(8,128)(2,1)}, bf16[4,2,128,128]{3,2,1,0:T(8,128)(2,1)}) custom-call(s32[5]{0:T(128)} %stack.34.where_ref, s32[32]{0:T(128)} %map_ref.3, s32[8]{0:T(128)} %reshape.14.span_ref, bf16[4,2,128,128]{3,2,1,0:T(8,128)(2,1)} %copy-done.16, bf16[4,2,128,128]{3,2,1,0:T(8,128)(2,1)} %copy-done.15, ...), custom_call_target="tpu_custom_call" | custom-call | flops 3221225472 | bytes 6291456 | tf_op jit(solution)/shard_map/attend/pallas_call | solution.py:357
  69.2 3.0 %collective-permute-start.10 = (bf16[4,2,128,128]{3,2,1,0:T(8,128)(2,1)}, bf16[4,2,128,128]{3,2,1,0:T(8,128)(2,1)S(1)}, u32[]{:S(2)}, u32[]{:S(2)}) collective-permute-start(bf16[4,2,128,128]{3,2,1,0:T(8,128)(2,1)} %get-tuple-element.49), channel_id=1, source_target_pairs={{0,24},{8,0},{16,8},{24,16},{1,25},{9,1},{17,9},{25,17},{2,26},{10... | collective-permute-start | bytes 786440 | tf_op jit(solution)/shard_map/ppermute | solution.py:399
  72.2 1.6 %collective-permute-start.11 = (bf16[4,2,128,128]{3,2,1,0:T(8,128)(2,1)}, bf16[4,2,128,128]{3,2,1,0:T(8,128)(2,1)S(1)}, u32[]{:S(2)}, u32[]{:S(2)}) collective-permute-start(bf16[4,2,128,128]{3,2,1,0:T(8,128)(2,1)} %get-tuple-element.50), channel_id=1, source_target_pairs={{0,16},{8,24},{16,0},{24,8},{1,17},{9,25},{17,1},{25,9},{2,18},{10... | collective-permute-start | bytes 786440 | tf_op jit(solution)/shard_map/ppermute | solution.py:399
  73.8 0.7 copy-done.14
  74.5 16.6 %attend.3 = (bf16[2,512,128]{2,1,0:T(8,128)(2,1)}, bf16[2,512,128]{2,1,0:T(8,128)(2,1)}, bf16[2,512,128]{2,1,0:T(8,128)(2,1)}, bf16[2,512,128]{2,1,0:T(8,128)(2,...) custom-call(s32[5]{0:T(128)} %stack.34.where_ref, s32[32]{0:T(128)} %map_ref.3, s32[8]{0:T(128)} %reshape.14.span_ref, ...), custom_call_target="tpu_custom_call" | custom-call | flops 3221225472 | bytes 6291456 | tf_op jit(solution)/shard_map/attend/pallas_call | solution.py:357
  91.2 0.2 collective-permute-done.11
  91.4 0.1 collective-permute-start.13
  91.5 1.7 %collective-permute-start.14 = (bf16[2,512,128]{2,1,0:T(8,128)(2,1)}, bf16[2,512,128]{2,1,0:T(8,128)(2,1)S(1)}, u32[]{:S(2)}, u32[]{:S(2)}) collective-permute-start(bf16[2,512,128]{2,1,0:T(8,128)(2,1)} %get-tuple-element.56), channel_id=1, source_target_pairs={{0,6},{2,4},{4,2},{6,0},{1,7},{3,5},{5,3},{7,1},{8,14},{10,12},{12... | collective-permute-start | bytes 786440 | tf_op jit(solution)/shard_map/ppermute | solution.py:395
  93.2 7.6 %collective-permute-done.15 = bf16[4,2,128,128]{3,2,1,0:T(8,128)(2,1)S(1)} collective-permute-done((bf16[4,2,128,128]{3,2,1,0:T(8,128)(2,1)}, bf16[4,2,128,128]{3,2,1,0:T(8,128)(2,1)S(1)}, u32[]{:S(2)}, u32[]{:S(2)}) %collective-permute-start.15) | collective-permute-done | bytes 262176 | tf_op jit(solution)/shard_map/ppermute | solution.py:399
  100.8 1.2 %add_convert_fusion = bf16[4,2,128,128]{3,2,1,0:T(8,128)(2,1)S(1)} fusion(bf16[4,2,128,128]{3,2,1,0:T(8,128)(2,1)S(1)} %collective-permute-done.15, bf16[4,2,128,128]{3,2,1,0:T(8,128)(2,1)S(1)} %collective-permute-done.10, f32[4,2,128,128]{3,2,1,0:T(8,128)} %get-tuple-element.57, bf16[4,2,128,128]{3,2,1,0:T(8,128)(2,1)S(1)} %collective-permute-done.11), kind=kLoop, calls=%fused_computation | loop fusion | flops 917504 | bytes 1572864 | tf_op jit(solution)/shard_map/convert.3
  102.0 0.6 slice_bitcast_fusion
  102.7 1.8 %collective-permute-start.16 = (bf16[2,128,128]{2,1,0:T(8,128)(2,1)S(1)}, bf16[2,128,128]{2,1,0:T(8,128)(2,1)S(1)}, u32[]{:S(2)}, u32[]{:S(2)}) collective-permute-start(bf16[2,128,128]{2,1,0:T(8,128)(2,1)S(1)} %get-tuple-element.65), channel_id=1, source_target_pairs={{0,2},{2,0},{4,6},{6,4},{1,3},{3,1},{5,7},{7,5},{8,10},{10,8},{12,... | collective-permute-start | bytes 196616 | tf_op jit(solution)/shard_map/ppermute | solution.py:395
  104.5 1.0 collective-permute-done.14.refs_3_
  105.5 0.7 copy-done.4
  106.2 3.4 %turn_back.1 = bf16[128,4096]{1,0:T(8,128)(2,1)} custom-call(s32[5]{0:T(128)} %stack.34.where_ref, f32[128,128]{1,0:T(8,128)} %get-tuple-element.33.cos_ref, f32[128,128]{1,0:T(8,128)} %get-tuple-element.34.sin_ref, bf16[2,512,128]{2,1,0:T(8,128)(2,1)} %get-tuple-element.53.refs_0_, bf16[2,512,128]{2,1,0:T(8,128)(2,1)} %copy-done.2, ...), custom_call_target="tpu_custom_call" | custom-call | tf_op jit(solution)/shard_map/turn_back/pallas_call | solution.py:357
  109.6 0.6 copy-done.6
  110.2 0.0 copy-done.7
  110.2 0.0 copy-done.8
  110.3 2.4 %last.1 = (bf16[128,512]{1,0:T(8,128)(2,1)}, bf16[128,512]{1,0:T(8,128)(2,1)}) custom-call(s32[5]{0:T(128)} %stack.34.where_ref, f32[128,128]{1,0:T(8,128)} %get-tuple-element.33.cos_ref, f32[128,128]{1,0:T(8,128)} %get-tuple-element.34.sin_ref, bf16[2,128,128]{2,1,0:T(8,128)(2,1)} %get-tuple-element.66.refs_0_, bf16[2,128,128]{2,1,0:T(8,128)(2,1)} %copy-done.8, ...), custom_call_target="tpu_custom_call" | custom-call | tf_op jit(solution)/shard_map/last/pallas_call | solution.py:357
  (45 shorter events, 0.1 us)
Async XLA Ops:
  4.3 15.1 %collective-permute-start.4 = (bf16[64,4096]{1,0:T(8,128)(2,1)}, bf16[64,4096]{1,0:T(8,128)(2,1)S(1)}, u32[]{:S(2)}, u32[]{:S(2)}) collective-permute-start(bf16[64,4096]{1,0:T(8,128)(2,1)} %get-tuple-element.39), channel_id=1, source_target_pairs={{0,1},{1,0},{2,3},{3,2},{4,5},{5,4},{6,7},{7,6},{8,9},{9,8},{10,11... | collective-permute-start | bytes 1572872 | tf_op jit(solution)/shard_map/ppermute | solution.py:427
  7.3 6.5 %copy-start.19 = (bf16[2,128,128]{2,1,0:T(8,128)(2,1)S(1)}, bf16[2,128,128]{2,1,0:T(8,128)(2,1)}, u32[]{:S(2)}) copy-start(bf16[2,128,128]{2,1,0:T(8,128)(2,1)} %get-tuple-element.36) | copy-start | bytes 196612
  7.3 6.9 %copy-start.18 = (bf16[2,128,128]{2,1,0:T(8,128)(2,1)S(1)}, bf16[2,128,128]{2,1,0:T(8,128)(2,1)}, u32[]{:S(2)}) copy-start(bf16[2,128,128]{2,1,0:T(8,128)(2,1)} %get-tuple-element.37) | copy-start | bytes 196612
  7.3 8.6 %copy-start.17 = (bf16[2,128,128]{2,1,0:T(8,128)(2,1)S(1)}, bf16[2,128,128]{2,1,0:T(8,128)(2,1)}, u32[]{:S(2)}) copy-start(bf16[2,128,128]{2,1,0:T(8,128)(2,1)} %get-tuple-element.38) | copy-start | bytes 196612
  10.1 20.4 %copy-start.9 = (bf16[2,128,128]{2,1,0:T(8,128)(2,1)S(1)}, bf16[2,128,128]{2,1,0:T(8,128)(2,1)}, u32[]{:S(2)}) copy-start(bf16[2,128,128]{2,1,0:T(8,128)(2,1)} %get-tuple-element.35) | copy-start | bytes 196612
  10.1 42.7 %all-to-all-start = ((bf16[4,2,512,128]{3,2,1,0:T(8,128)(2,1)}), bf16[4,2,512,128]{3,2,1,0:T(8,128)(2,1)S(1)}, u32[]{:S(2)}, u32[]{:S(2)}) async-start(bf16[4,2,512,128]{3,2,1,0:T(8,128)(2,1)} %rotate.1), calls=%async_computation | async-start | bytes 2097152 | tf_op jit(solution)/shard_map/all_to_all | solution.py:430
  13.7 21.0 %copy-start.10 = (s32[4,2]{0,1:T(2,128)S(1)}, s32[4,2]{0,1:T(2,128)}, u32[]{:S(2)}) copy-start(s32[4,2]{0,1:T(2,128)} %param.17) | copy-start | bytes 100
  13.7 12.1 %collective-permute-start = (bf16[2,128,128]{2,1,0:T(8,128)(2,1)S(1)}, bf16[2,128,128]{2,1,0:T(8,128)(2,1)S(1)}, u32[]{:S(2)}, u32[]{:S(2)}) collective-permute-start(bf16[2,128,128]{2,1,0:T(8,128)(2,1)S(1)} %copy-done.19), channel_id=1, source_target_pairs={{0,2},{2,0},{4,6},{6,4},{1,3},{3,1},{5,7},{7,5},{8,10},{10,8},{12,... | collective-permute-start | bytes 196616 | tf_op jit(solution)/shard_map/ppermute | solution.py:395
  14.2 15.8 %collective-permute-start.1 = (bf16[2,128,128]{2,1,0:T(8,128)(2,1)S(1)}, bf16[2,128,128]{2,1,0:T(8,128)(2,1)S(1)}, u32[]{:S(2)}, u32[]{:S(2)}) collective-permute-start(bf16[2,128,128]{2,1,0:T(8,128)(2,1)S(1)} %copy-done.18), channel_id=1, source_target_pairs={{0,4},{2,6},{4,0},{6,2},{1,5},{3,7},{5,1},{7,3},{8,12},{10,14},{12... | collective-permute-start | bytes 196616 | tf_op jit(solution)/shard_map/ppermute | solution.py:395
  15.9 14.6 %collective-permute-start.2 = (bf16[2,128,128]{2,1,0:T(8,128)(2,1)S(1)}, bf16[2,128,128]{2,1,0:T(8,128)(2,1)S(1)}, u32[]{:S(2)}, u32[]{:S(2)}) collective-permute-start(bf16[2,128,128]{2,1,0:T(8,128)(2,1)S(1)} %copy-done.17), channel_id=1, source_target_pairs={{0,6},{2,4},{4,2},{6,0},{1,7},{3,5},{5,3},{7,1},{8,14},{10,12},{12... | collective-permute-start | bytes 196616 | tf_op jit(solution)/shard_map/ppermute | solution.py:395
  19.4 0.8 copy-start.1
  24.1 28.7 %collective-permute-start.5 = (bf16[2,544,128]{2,1,0:T(8,128)(2,1)}, bf16[2,544,128]{2,1,0:T(8,128)(2,1)S(1)}, u32[]{:S(2)}, u32[]{:S(2)}) collective-permute-start(bf16[2,544,128]{2,1,0:T(8,128)(2,1)} %get-tuple-element.41), channel_id=1, source_target_pairs={{0,2},{2,0},{4,6},{6,4},{1,3},{3,1},{5,7},{7,5},{8,10},{10,8},{12,... | collective-permute-start | bytes 835592 | tf_op jit(solution)/shard_map/ppermute | solution.py:395
  24.1 28.7 %collective-permute-start.6 = (bf16[2,544,128]{2,1,0:T(8,128)(2,1)}, bf16[2,544,128]{2,1,0:T(8,128)(2,1)S(1)}, u32[]{:S(2)}, u32[]{:S(2)}) collective-permute-start(bf16[2,544,128]{2,1,0:T(8,128)(2,1)} %get-tuple-element.42), channel_id=1, source_target_pairs={{0,4},{2,6},{4,0},{6,2},{1,5},{3,7},{5,1},{7,3},{8,12},{10,14},{12... | collective-permute-start | bytes 835592 | tf_op jit(solution)/shard_map/ppermute | solution.py:395
  25.9 27.0 %collective-permute-start.7 = (bf16[2,544,128]{2,1,0:T(8,128)(2,1)}, bf16[2,544,128]{2,1,0:T(8,128)(2,1)S(1)}, u32[]{:S(2)}, u32[]{:S(2)}) collective-permute-start(bf16[2,544,128]{2,1,0:T(8,128)(2,1)} %get-tuple-element.43), channel_id=1, source_target_pairs={{0,6},{2,4},{4,2},{6,0},{1,7},{3,5},{5,3},{7,1},{8,14},{10,12},{12... | collective-permute-start | bytes 835592 | tf_op jit(solution)/shard_map/ppermute | solution.py:395
  30.5 43.3 %copy-start.5 = (bf16[4,2,128,128]{3,2,1,0:T(8,128)(2,1)}, bf16[4,2,128,128]{3,2,1,0:T(8,128)(2,1)S(1)}, u32[]{:S(2)}) copy-start(bf16[4,2,128,128]{3,2,1,0:T(8,128)(2,1)S(1)} %pad_maximum_fusion.refs_1_) | copy-start | bytes 786436
  30.5 11.1 %collective-permute-start.9 = (bf16[4,2,128,128]{3,2,1,0:T(8,128)(2,1)S(1)}, bf16[4,2,128,128]{3,2,1,0:T(8,128)(2,1)S(1)}, u32[]{:S(2)}, u32[]{:S(2)}) collective-permute-start(bf16[4,2,128,128]{3,2,1,0:T(8,128)(2,1)S(1)} %pad_maximum_fusion.refs_1_), channel_id=1, source_target_pairs={{0,8},{8,16},{16,24},{24,0},{1,9},{9,17},{17,25},{25,1},{2,10},{10... | collective-permute-start | bytes 786440 | tf_op jit(solution)/shard_map/ppermute | solution.py:399
  32.2 20.6 %collective-permute-start.8 = (bf16[4,2,128,128]{3,2,1,0:T(8,128)(2,1)S(1)}, bf16[4,2,128,128]{3,2,1,0:T(8,128)(2,1)S(1)}, u32[]{:S(2)}, u32[]{:S(2)}) collective-permute-start(bf16[4,2,128,128]{3,2,1,0:T(8,128)(2,1)S(1)} %pad_maximum_fusion.refs_1_), channel_id=1, source_target_pairs={{0,16},{8,24},{16,0},{24,8},{1,17},{9,25},{17,1},{25,9},{2,18},{10... | collective-permute-start | bytes 786440 | tf_op jit(solution)/shard_map/ppermute | solution.py:399
  41.7 11.2 %copy-start.15 = (bf16[4,2,128,128]{3,2,1,0:T(8,128)(2,1)}, bf16[4,2,128,128]{3,2,1,0:T(8,128)(2,1)S(1)}, u32[]{:S(2)}) copy-start(bf16[4,2,128,128]{3,2,1,0:T(8,128)(2,1)S(1)} %collective-permute-done.9.refs_1_) | copy-start | bytes 786436
  41.7 32.2 %collective-permute-start.3 = (bf16[4,2,128,128]{3,2,1,0:T(8,128)(2,1)S(1)}, bf16[4,2,128,128]{3,2,1,0:T(8,128)(2,1)S(1)}, u32[]{:S(2)}, u32[]{:S(2)}) collective-permute-start(bf16[4,2,128,128]{3,2,1,0:T(8,128)(2,1)S(1)} %pad_maximum_fusion.refs_1_), channel_id=1, source_target_pairs={{0,24},{8,0},{16,8},{24,16},{1,25},{9,1},{17,9},{25,17},{2,26},{10... | collective-permute-start | bytes 786440 | tf_op jit(solution)/shard_map/ppermute | solution.py:399
  52.8 0.7 copy-start.16
  52.8 1.1 copy-start
  52.8 1.1 copy-start.11
  52.8 1.2 %copy-start.12 = (bf16[2,544,128]{2,1,0:T(8,128)(2,1)}, bf16[2,544,128]{2,1,0:T(8,128)(2,1)S(1)}, u32[]{:S(2)}) copy-start(bf16[2,544,128]{2,1,0:T(8,128)(2,1)S(1)} %collective-permute-done.6.refs_5_) | copy-start | bytes 835588
  52.8 1.3 %copy-start.13 = (bf16[2,544,128]{2,1,0:T(8,128)(2,1)}, bf16[2,544,128]{2,1,0:T(8,128)(2,1)S(1)}, u32[]{:S(2)}) copy-start(bf16[2,544,128]{2,1,0:T(8,128)(2,1)S(1)} %collective-permute-done.7.refs_6_) | copy-start | bytes 835588
  69.2 21.9 %collective-permute-start.10 = (bf16[4,2,128,128]{3,2,1,0:T(8,128)(2,1)}, bf16[4,2,128,128]{3,2,1,0:T(8,128)(2,1)S(1)}, u32[]{:S(2)}, u32[]{:S(2)}) collective-permute-start(bf16[4,2,128,128]{3,2,1,0:T(8,128)(2,1)} %get-tuple-element.49), channel_id=1, source_target_pairs={{0,24},{8,0},{16,8},{24,16},{1,25},{9,1},{17,9},{25,17},{2,26},{10... | collective-permute-start | bytes 786440 | tf_op jit(solution)/shard_map/ppermute | solution.py:399
  72.2 19.2 %collective-permute-start.11 = (bf16[4,2,128,128]{3,2,1,0:T(8,128)(2,1)}, bf16[4,2,128,128]{3,2,1,0:T(8,128)(2,1)S(1)}, u32[]{:S(2)}, u32[]{:S(2)}) collective-permute-start(bf16[4,2,128,128]{3,2,1,0:T(8,128)(2,1)} %get-tuple-element.50), channel_id=1, source_target_pairs={{0,16},{8,24},{16,0},{24,8},{1,17},{9,25},{17,1},{25,9},{2,18},{10... | collective-permute-start | bytes 786440 | tf_op jit(solution)/shard_map/ppermute | solution.py:399
  73.8 0.7 copy-start.14
  91.4 9.4 %collective-permute-start.15 = (bf16[4,2,128,128]{3,2,1,0:T(8,128)(2,1)}, bf16[4,2,128,128]{3,2,1,0:T(8,128)(2,1)S(1)}, u32[]{:S(2)}, u32[]{:S(2)}) collective-permute-start(bf16[4,2,128,128]{3,2,1,0:T(8,128)(2,1)} %get-tuple-element.60), channel_id=1, source_target_pairs={{0,8},{8,16},{16,24},{24,0},{1,9},{9,17},{17,25},{25,1},{2,10},{10... | collective-permute-start | bytes 786440 | tf_op jit(solution)/shard_map/ppermute | solution.py:399
  91.4 11.3 %collective-permute-start.12 = (bf16[2,512,128]{2,1,0:T(8,128)(2,1)}, bf16[2,512,128]{2,1,0:T(8,128)(2,1)S(1)}, u32[]{:S(2)}, u32[]{:S(2)}) collective-permute-start(bf16[2,512,128]{2,1,0:T(8,128)(2,1)} %get-tuple-element.54), channel_id=1, source_target_pairs={{0,2},{2,0},{4,6},{6,4},{1,3},{3,1},{5,7},{7,5},{8,10},{10,8},{12,... | collective-permute-start | bytes 786440 | tf_op jit(solution)/shard_map/ppermute | solution.py:395
  91.4 13.1 %collective-permute-start.13 = (bf16[2,512,128]{2,1,0:T(8,128)(2,1)}, bf16[2,512,128]{2,1,0:T(8,128)(2,1)S(1)}, u32[]{:S(2)}, u32[]{:S(2)}) collective-permute-start(bf16[2,512,128]{2,1,0:T(8,128)(2,1)} %get-tuple-element.55), channel_id=1, source_target_pairs={{0,4},{2,6},{4,0},{6,2},{1,5},{3,7},{5,1},{7,3},{8,12},{10,14},{12... | collective-permute-start | bytes 786440 | tf_op jit(solution)/shard_map/ppermute | solution.py:395
  91.5 14.0 %collective-permute-start.14 = (bf16[2,512,128]{2,1,0:T(8,128)(2,1)}, bf16[2,512,128]{2,1,0:T(8,128)(2,1)S(1)}, u32[]{:S(2)}, u32[]{:S(2)}) collective-permute-start(bf16[2,512,128]{2,1,0:T(8,128)(2,1)} %get-tuple-element.56), channel_id=1, source_target_pairs={{0,6},{2,4},{4,2},{6,0},{1,7},{3,5},{5,3},{7,1},{8,14},{10,12},{12... | collective-permute-start | bytes 786440 | tf_op jit(solution)/shard_map/ppermute | solution.py:395
  102.6 6.9 %collective-permute-start.18 = (bf16[2,128,128]{2,1,0:T(8,128)(2,1)S(1)}, bf16[2,128,128]{2,1,0:T(8,128)(2,1)S(1)}, u32[]{:S(2)}, u32[]{:S(2)}) collective-permute-start(bf16[2,128,128]{2,1,0:T(8,128)(2,1)S(1)} %get-tuple-element.63), channel_id=1, source_target_pairs={{0,6},{2,4},{4,2},{6,0},{1,7},{3,5},{5,3},{7,1},{8,14},{10,12},{12... | collective-permute-start | bytes 196616 | tf_op jit(solution)/shard_map/ppermute | solution.py:395
  102.6 6.9 %collective-permute-start.17 = (bf16[2,128,128]{2,1,0:T(8,128)(2,1)S(1)}, bf16[2,128,128]{2,1,0:T(8,128)(2,1)S(1)}, u32[]{:S(2)}, u32[]{:S(2)}) collective-permute-start(bf16[2,128,128]{2,1,0:T(8,128)(2,1)S(1)} %get-tuple-element.64), channel_id=1, source_target_pairs={{0,4},{2,6},{4,0},{6,2},{1,5},{3,7},{5,1},{7,3},{8,12},{10,14},{12... | collective-permute-start | bytes 196616 | tf_op jit(solution)/shard_map/ppermute | solution.py:395
  102.6 2.8 %copy-start.2 = (bf16[2,512,128]{2,1,0:T(8,128)(2,1)}, bf16[2,512,128]{2,1,0:T(8,128)(2,1)S(1)}, u32[]{:S(2)}) copy-start(bf16[2,512,128]{2,1,0:T(8,128)(2,1)S(1)} %collective-permute-done.12.refs_1_) | copy-start | bytes 786436
  102.7 6.9 %collective-permute-start.16 = (bf16[2,128,128]{2,1,0:T(8,128)(2,1)S(1)}, bf16[2,128,128]{2,1,0:T(8,128)(2,1)S(1)}, u32[]{:S(2)}, u32[]{:S(2)}) collective-permute-start(bf16[2,128,128]{2,1,0:T(8,128)(2,1)S(1)} %get-tuple-element.65), channel_id=1, source_target_pairs={{0,2},{2,0},{4,6},{6,4},{1,3},{3,1},{5,7},{7,5},{8,10},{10,8},{12,... | collective-permute-start | bytes 196616 | tf_op jit(solution)/shard_map/ppermute | solution.py:395
  104.5 1.0 copy-start.3
  105.5 0.7 copy-start.4
  109.6 0.6 copy-start.6
  109.6 0.6 copy-start.7
  109.6 0.7 copy-start.8

commit v5 on v4

--- a/solution.py
+++ b/solution.py
@@ -50,44 +50,43 @@
     return pl.ds(pl.multiple_of(first, HEAD_SIZE), HEAD_SIZE)
 
 
-def first_kernel(members, with_piece, where_ref, ids_ref, k_ref, v_ref, *refs):
+def first_kernel(members, group, where_ref, ids_ref, k_ref, v_ref, q_ref, *refs):
     refs = list(refs)
-    if with_piece:
-        grad_ref = refs.pop(0)
-        refs.pop()[...] = grad_ref[...]
+    if members > 1:
+        own_ref, other_ref = refs.pop(0), refs.pop(0)
+        refs.pop()[...] = other_ref[...]
+    pack_ref = refs.pop()
     cos_ref, sin_ref = refs.pop(0), refs.pop(0)
-    member = where_ref[0]
+    this = where_ref[0]
     cosine, sine = turned_tables(ids_ref[...], HEAD_SIZE)
     cos_ref[...] = cosine
     sin_ref[...] = sine
     signed = sine * half_sign()
+    block_len = q_ref.shape[0] // BLOCKS_DEV
     for flip in range(members):
-        lanes = head_lanes(member, flip, 1, 0)
+        lanes = head_lanes(this, flip, 1, 0)
         keys = k_ref[:, lanes].astype(jnp.float32)
         refs[flip][0] = (keys * cosine + pltpu.roll(keys, HEAD_SIZE // 2, 1) * signed).astype(
             jnp.bfloat16
         )
         refs[flip][1] = v_ref[:, lanes]
-
-
-def stacked(head, block_len):
-    return slice(head * block_len, (head + 1) * block_len)
-
-
-def query_kernel(members, group, cos_ref, sin_ref, q_ref, out_ref):
-    cosine = cos_ref[...]
-    signed = sin_ref[...] * half_sign()
-    block_len = q_ref.shape[0] // BLOCKS_DEV
     for member in range(members):
         for head in range(group):
-            first = (member * group + head) * HEAD_SIZE
-            field = q_ref[:, first : first + HEAD_SIZE].astype(jnp.float32)
+            start = (member * group + head) * HEAD_SIZE
+            lanes = slice(start, start + HEAD_SIZE)
+            field = q_ref[:, lanes].astype(jnp.float32)
             turned = pltpu.roll(field, HEAD_SIZE // 2, 1)
             field = (field * cosine + turned * signed).astype(jnp.bfloat16)
             for step in range(BLOCKS_DEV):
-                out_ref[member, step, stacked(head, block_len), :] = field[
+                pack_ref[member, step, stacked(head, block_len), :] = field[
                     step * block_len : (step + 1) * block_len, :
                 ]
+            if members > 1:
+                pack_ref[member, BLOCKS_DEV, stacked(head, block_len), :] = own_ref[:, lanes]
+
+
+def stacked(head, block_len):
+    return slice(head * block_len, (head + 1) * block_len)
 
 
 def split_rows(vector):
@@ -108,46 +107,50 @@
 
 
 def delta_kernel(members, group, where_ref, a_ref, l_ref, *refs):
-    refs = list(refs)
-    own_ref = refs.pop(0)
-    other_ref = refs.pop(0) if members > 1 else None
-    grad_refs = refs
-    member, tp_index = where_ref[0], where_ref[1]
+    late_ref = refs[-1]
     block_len = a_ref.shape[0] // BLOCKS_DEV
-    for flip in range(members):
-        g_ref = grad_refs[flip]
-        for head in range(group):
-            lanes = head_lanes(member, flip, group, head)
-            here = stacked(head, block_len)
+    columns = group * block_len
+    for member in range(members):
+        for number in range(BLOCKS_DEV):
             if members > 1:
-                g_ref[tp_index, here, :] = own_ref[:, lanes]
-                g_ref[1 - tp_index, here, :] = other_ref[:, lanes]
+                step = where_ref[1] if number == 0 else 1 - where_ref[1]
+                source, from_rows = refs[number], slice(None)
             else:
-                for step in range(BLOCKS_DEV):
-                    g_ref[step, here, :] = own_ref[stacked(step, block_len), lanes]
-        first = pl.multiple_of((member ^ flip) * group, group)
-        lse = l_ref[pl.ds(first, group), :] * LOG2E
-        for step in range(BLOCKS_DEV):
-            sums = []
+                step = number
+                source, from_rows = refs[0], stacked(step, block_len)
+            row = step * block_len
+            if members > 1:
+                row = pl.multiple_of(row, block_len)
+            products = []
             for head in range(group):
-                lanes = head_lanes(member, flip, group, head)
-                product = g_ref[step, stacked(head, block_len), :].astype(jnp.float32) * a_ref[
-                    stacked(step, block_len), lanes
-                ].astype(jnp.float32)
-                sums.append(product)
-            total = jnp.sum(jnp.concatenate(sums, axis=0).T, axis=0, keepdims=True)
+                start = (member * group + head) * HEAD_SIZE
+                lanes = slice(start, start + HEAD_SIZE)
+                grad = source[from_rows, lanes]
+                if members == 1:
+                    late_ref[0, stacked(step * group + head, block_len), :] = grad
+                elif number == 1:
+                    late_ref[member, stacked(head, block_len), :] = grad
+                products.append(
+                    grad.astype(jnp.float32)
+                    * a_ref[pl.ds(row, block_len), lanes].astype(jnp.float32)
+                )
+            total = jnp.sum(jnp.concatenate(products, axis=0).T, axis=0, keepdims=True)
+            lse = l_ref[member * group : (member + 1) * group, :] * LOG2E
             pieces = split_rows(row_vector(lse, step, block_len)) + split_rows(total)
             pieces.append(jnp.zeros((STAT_ROWS - len(pieces), HEAD_SIZE), jnp.float32))
-            below = group * block_len
-            g_ref[step, below : below + STAT_ROWS, :] = jnp.concatenate(pieces, axis=0).astype(
-                jnp.bfloat16
-            )
+            below = late_ref.shape[1] - BLOCKS_DEV * STAT_ROWS + step * STAT_ROWS
+            if members > 1:
+                below = pl.multiple_of(below, STAT_ROWS)
+            late_ref[member, pl.ds(below, STAT_ROWS), :] = jnp.concatenate(
+                pieces, axis=0
+            ).astype(jnp.bfloat16)
 
 
 def row_vector(table, upper, block_len):
     group, width = table.shape
     rolled = pltpu.roll(table, block_len, 1)
-    low, high = (table, rolled) if upper == 0 else (rolled, table)
+    low = jnp.where(upper == 0, table, rolled)
+    high = jnp.where(upper == 0, rolled, table)
     lane = lax.broadcasted_iota(jnp.int32, (1, width), 1)
     pieces = [
         jnp.where(lane < block_len, low[h : h + 1, :], high[h + 1 : h + 2, :])
@@ -162,8 +165,7 @@
     refs = list(refs)
     count = len(slabs)
     kv_refs = [refs.pop(0) for _ in range(count)]
-    q_ref = refs.pop(0)
-    g_refs = [refs.pop(0) for _ in range(members)]
+    pack_ref, late_ref = refs.pop(0), refs.pop(0)
     in_ref = refs.pop(0) if carried else None
     dq_refs = [refs.pop(0) for _ in range(1 if carries else members)]
     part_refs = [refs.pop(0) for _ in range(count)]
@@ -234,10 +236,17 @@
     for flip in range(members):
         for step in range(BLOCKS_DEV):
             place = flip * BLOCKS_DEV + step
-            q_all[place] = q_ref[member ^ flip, step]
-            g_all[place] = g_refs[flip][step, :columns, :]
-            stats = g_refs[flip][step, columns:, :].astype(jnp.float32)
+            source = member ^ flip
+            q_all[place] = pack_ref[source, step]
+            if members == 1:
+                g_all[place] = late_ref[0, step * columns : (step + 1) * columns, :]
+            elif step == 0:
+                tp_index = where_ref[1]
+                g_all[flip * BLOCKS_DEV + tp_index] = pack_ref[source, BLOCKS_DEV]
+                g_all[flip * BLOCKS_DEV + 1 - tp_index] = late_ref[source, :columns, :]
             half = 3 * columns // HEAD_SIZE
+            below = late_ref.shape[1] - (BLOCKS_DEV - step) * STAT_ROWS
+            stats = late_ref[source, below : below + STAT_ROWS, :].astype(jnp.float32)
             l_all[place] = joined_row(stats[:half])
             d_all[place] = joined_row(stats[half : 2 * half])
 
@@ -322,7 +331,9 @@
     return field * cosine - pltpu.roll(field, HEAD_SIZE // 2, 1) * signed
 
 
-def query_gradient_kernel(members, group, where_ref, cos_ref, sin_ref, *refs):
+def last_kernel(members, group, where_ref, cos_ref, sin_ref, *refs):
+    dq_refs, sum_refs = refs[:members], refs[members : 2 * members]
+    grad_ref, dk_ref, dv_ref = refs[2 * members :]
     member = where_ref[0]
     block_len = cos_ref.shape[0] // BLOCKS_DEV
     for step in range(BLOCKS_DEV):
@@ -330,23 +341,15 @@
         cosine = cos_ref[here, :]
         signed = sin_ref[here, :] * half_sign()
         for flip in range(members):
+            lanes = head_lanes(member, flip, 1, 0)
+            field = sum_refs[flip][0, here, :].astype(jnp.float32)
+            dk_ref[here, lanes] = turned_back(field, cosine, signed).astype(jnp.bfloat16)
+            dv_ref[here, lanes] = sum_refs[flip][1, here, :].astype(jnp.bfloat16)
             for head in range(group):
-                field = refs[flip][step, stacked(head, block_len), :].astype(jnp.float32)
-                refs[members][here, head_lanes(member, flip, group, head)] = turned_back(
+                field = dq_refs[flip][step, stacked(head, block_len), :].astype(jnp.float32)
+                grad_ref[here, head_lanes(member, flip, group, head)] = turned_back(
                     field, cosine, signed
                 ).astype(jnp.bfloat16)
-
-
-def last_kernel(members, where_ref, cos_ref, sin_ref, *refs):
-    member = where_ref[0]
-    dk_ref, dv_ref = refs[members], refs[members + 1]
-    cosine = cos_ref[...]
-    signed = sin_ref[...] * half_sign()
-    for flip in range(members):
-        lanes = head_lanes(member, flip, 1, 0)
-        field = refs[flip][0].astype(jnp.float32)
-        dk_ref[:, lanes] = turned_back(field, cosine, signed).astype(jnp.bfloat16)
-        dv_ref[:, lanes] = refs[flip][1].astype(jnp.bfloat16)
 
 
 def whole(shape):
@@ -402,32 +405,39 @@
     table = ((rows, HEAD_SIZE), f32)
     pair = (2, rows, HEAD_SIZE)
 
-    inputs = [position_ids, keys, values]
+    columns = group * block_len
+    stack = (BLOCKS_DEV, columns, HEAD_SIZE)
+    inputs = [position_ids, keys, values, queries]
+    in_specs = [whole(a.shape) for a in inputs]
     outputs = [table, table] + [(pair, bf16)] * members
-    in_specs = [whole(a.shape) for a in inputs]
+    late_rows = columns + BLOCKS_DEV * STAT_ROWS
     if members > 1:
-        other = (out_grad.shape[0], members * width)
-        inputs.append(out_grad)
-        in_specs.append(pl.BlockSpec(other, lambda i, where: (0, 1 - where[1])))
-        outputs.append((other, bf16))
+        half = (out_grad.shape[0], members * width)
+        own_half = pl.BlockSpec(half, lambda i, where: (0, where[1]))
+        inputs += [out_grad, out_grad]
+        in_specs += [own_half, pl.BlockSpec(half, lambda i, where: (0, 1 - where[1]))]
+        outputs += [((members, BLOCKS_DEV + 1, columns, HEAD_SIZE), bf16), (half, bf16)]
+    else:
+        outputs.append(((members, *stack), bf16))
+        late_rows += columns
     results = call(
-        functools.partial(first_kernel, members, members > 1),
+        functools.partial(first_kernel, members, group),
         "first", [place], inputs, outputs, in_specs,
     )
     cosine, sine = results[:2]
-    kv_pieces = results[2 : 2 + members]
-    columns = group * block_len
-    stack = (BLOCKS_DEV, columns, HEAD_SIZE)
-    (q_stack,) = call(
-        functools.partial(query_kernel, members, group),
-        "rotate", [], [cosine, sine, queries], [((members, *stack), bf16)],
-    )
+    kv_pieces, pack = results[2 : 2 + members], results[2 + members]
+
+    def shared(array):
+        if members == 1:
+            return array
+        return lax.all_to_all(array, ("y", "core"), 0, 0, tiled=True)
+
     if members > 1:
+        grads_other = lax.ppermute(results[-1], "tp", [(0, 1), (1, 0)])
         slab = jnp.stack([flipped(kv_pieces[f], f) for f in every])
-        grads_other = lax.ppermute(results[-1], "tp", [(0, 1), (1, 0)])
         far = sorted(range(1, layers), key=lambda k: abs(2 * k - layers))
         rounds = [far[: layers // 2], far[layers // 2 :] + [0]]
-        q_stack = lax.all_to_all(q_stack, ("y", "core"), 0, 0, tiled=True)
+        slab, grads_other = lax.optimization_barrier((slab, grads_other))
         kv = {0: slab}
         for k in far:
             kv[k] = climbed(slab, k)
@@ -435,25 +445,21 @@
         kv = {0: lax.all_gather(kv_pieces[0], ("z", "y", "core"), axis=0, tiled=False)}
         rounds = [[0]]
         grads_own = lax.all_to_all(out_grad, "tp", split_axis=1, concat_axis=0, tiled=True)
+    pack = shared(pack)
 
     inputs = [attn_out, logsumexp]
     in_specs = [whole(a.shape) for a in inputs]
     if members > 1:
         inputs += [out_grad, grads_other]
-        in_specs += [
-            pl.BlockSpec(grads_other.shape, lambda i, where: (0, where[1])),
-            whole(grads_other.shape),
-        ]
+        in_specs += [own_half, whole(grads_other.shape)]
     else:
         inputs += [grads_own]
         in_specs += [whole(grads_own.shape)]
-    results = call(
+    (late,) = call(
         functools.partial(delta_kernel, members, group),
-        "delta", [place], inputs,
-        [((BLOCKS_DEV, columns + STAT_ROWS, HEAD_SIZE), bf16)] * members,
-        in_specs,
+        "delta", [place], inputs, [((members, late_rows, HEAD_SIZE), bf16)], in_specs,
     )
-    g_in = [flipped(results[f], f) for f in every]
+    late = shared(late)
 
     units = kv[0].shape[0]
     blocks = members * BLOCKS_DEV
@@ -469,7 +475,7 @@
                 attend_kernel, members, group, block_len, slabs, number > 0, carries
             ),
             "attend", [place, block_map, span_blocks.reshape(-1)],
-            [*[kv[k] for k in slabs], q_stack, *g_in, *carry],
+            [*[kv[k] for k in slabs], pack, late, *carry],
             ([(sums, f32)] if carries else [(stack, bf16)] * members)
             + [(part, f32 if k == 0 and members > 1 else bf16) for k in slabs],
             scratch=[
@@ -512,18 +518,14 @@
         sums = [
             lax.psum_scatter(parts[0], ("z", "y", "core"), scatter_dimension=0, tiled=True)[0]
         ]
-    (grad_q,) = call(
-        functools.partial(query_gradient_kernel, members, group),
-        "turn_back", [place],
-        [cosine, sine] + [flipped(dq_pieces[f], f) for f in every],
-        [(queries.shape, bf16)],
+    return tuple(
+        call(
+            functools.partial(last_kernel, members, group),
+            "last", [place],
+            [cosine, sine, *[flipped(dq_pieces[f], f) for f in every], *sums],
+            [(queries.shape, bf16), (keys.shape, bf16), (values.shape, bf16)],
+        )
     )
-    key_gradient, value_gradient = call(
-        functools.partial(last_kernel, members),
-        "last", [place], [cosine, sine, *sums],
-        [(keys.shape, bf16), (values.shape, bf16)],
-    )
-    return (grad_q, key_gradient, value_gradient)
 
 
 def solution(mesh):

time: 114 us -> 127 us (1.11)
  blocking collectives: 0 us -> 13.8 us
  Pallas kernels: 47.3 us -> 39.1 us
  waiting for transfers between devices: 32.5 us -> 38.5 us
  starting transfers between devices: 24.8 us -> 26.3 us
    all_to_all x0 -> x1, blocking collectives: none -> 13.8 us  [shared(): return lax.all_to_all(array, ('y', 'core'), 0, 0, tiled=True)]
    pallas_call x7 -> x5, Pallas kernels: 47.3 us -> 39.1 us  [call(): pl.pallas_call(kernel, grid_spec=pltpu.PrefetchScalarGridSpec(num_scalar_...]
    ppermute x6, starting transfers between devices: 10.4 us -> 14 us  [climbed(): return lax.ppermute(array, 'z', route)]
    ppermute x12 -> x9, waiting for transfers between devices: 5.48 us -> 8.66 us  [flipped(): return lax.ppermute(array, ('y', 'core'), [(i, i ^ flip) for i in range(4)])]
    ppermute x12 -> x9, starting transfers between devices: 7.78 us -> 5.58 us  [flipped(): return lax.ppermute(array, ('y', 'core'), [(i, i ^ flip) for i in range(4)])]
    ppermute x1, waiting for transfers between devices: 3.5 us -> 5.44 us  [shards(): grads_other = lax.ppermute(results[-1], 'tp', [(0, 1), (1, 0)])]
    unnamed x41 -> x27, local copies, waits for them, and re-layouts: 4.26 us -> 4.05 us
  transfers between devices with their start and end apart: 20 -> 17, of which waited for: 8 -> 10; matrix products, arithmetic and copies ran while one was open for 2% -> 3% of each run, Pallas kernels for 37% -> 22%
where the time goes in v5:
time: 127 us; the launch traced here: 126 us
  Pallas kernels  39.1 us (31%)
  waiting for transfers between devices  38.5 us (30%)
  starting transfers between devices  26.3 us (21%)
  blocking collectives  13.8 us (11%)
  local copies, waits for them, and re-layouts  5.87 us (5%)
  other arithmetic  2.04 us (2%)
    pallas_call x5, Pallas kernels, call(): pl.pallas_call(kernel, grid_spec=pltpu.PrefetchScalarGridSpec(num_scalar_...  39.1 us
    ppermute x6, waiting for transfers between devices, climbed(): return lax.ppermute(array, 'z', route)  24.4 us
    ppermute x6, starting transfers between devices, climbed(): return lax.ppermute(array, 'z', route)  14 us
    all_to_all x1, blocking collectives, shared(): return lax.all_to_all(array, ('y', 'core'), 0, 0, tiled=True)  13.8 us
    ppermute x9, waiting for transfers between devices, flipped(): return lax.ppermute(array, ('y', 'core'), [(i, i ^ flip) for i in range(4)])  8.66 us
    ppermute x9, starting transfers between devices, flipped(): return lax.ppermute(array, ('y', 'core'), [(i, i ^ flip) for i in range(4)])  5.58 us
    ppermute x1, waiting for transfers between devices, shards(): grads_other = lax.ppermute(results[-1], 'tp', [(0, 1), (1, 0)])  5.44 us
    unnamed x27, local copies, waits for them, and re-layouts  4.05 us
  transfers between devices with their start and end apart: 17, of which 10 were waited for; matrix products, arithmetic and copies ran while one was open for 3% of the time, Pallas kernels for 22%

profile of v5, /device:TPU:0, one launch (start us, length us, event | category | flops | bytes accessed | tf_op | source)
XLA Modules:
  0.0 126.2 jit_solution(16104370875370393503)
XLA Ops:
  0.6 0.6 stack.34.where_ref
  1.2 4.5 %first.1 = (f32[128,128]{1,0:T(8,128)}, f32[128,128]{1,0:T(8,128)}, bf16[2,128,128]{2,1,0:T(8,128)(2,1)}, bf16[2,128,128]{2,1,0:T(8,128)(2,1)}, bf16[2,128,128]{...) custom-call(s32[5]{0:T(128)} %stack.34.where_ref, ...), custom_call_target="tpu_custom_call" | custom-call | tf_op jit(solution)/shard_map/first/pallas_call | solution.py:360
  5.7 2.9 %collective-permute-start.3 = (bf16[64,4096]{1,0:T(8,128)(2,1)}, bf16[64,4096]{1,0:T(8,128)(2,1)S(1)}, u32[]{:S(2)}, u32[]{:S(2)}) collective-permute-start(bf16[64,4096]{1,0:T(8,128)(2,1)} %get-tuple-element.36), channel_id=1, source_target_pairs={{0,1},{1,0},{2,3},{3,2},{4,5},{5,4},{6,7},{7,6},{8,9},{9,8},{10,11... | collective-permute-start | bytes 1572872 | tf_op jit(solution)/shard_map/ppermute | solution.py:436
  8.6 0.0 collective-permute-start
  8.6 1.5 %collective-permute-start.1 = (bf16[2,128,128]{2,1,0:T(8,128)(2,1)}, bf16[2,128,128]{2,1,0:T(8,128)(2,1)S(1)}, u32[]{:S(2)}, u32[]{:S(2)}) collective-permute-start(bf16[2,128,128]{2,1,0:T(8,128)(2,1)} %get-tuple-element.34), channel_id=1, source_target_pairs={{0,4},{2,6},{4,0},{6,2},{1,5},{3,7},{5,1},{7,3},{8,12},{10,14},{12... | collective-permute-start | bytes 196616 | tf_op jit(solution)/shard_map/ppermute | solution.py:398
  10.2 0.3 collective-permute-start.2
  10.5 0.0 collective-permute-done
  10.5 2.9 %collective-permute-done.1 = bf16[2,128,128]{2,1,0:T(8,128)(2,1)S(1)} collective-permute-done((bf16[2,128,128]{2,1,0:T(8,128)(2,1)}, bf16[2,128,128]{2,1,0:T(8,128)(2,1)S(1)}, u32[]{:S(2)}, u32[]{:S(2)}) %collective-permute-start.1) | collective-permute-done | bytes 65568 | tf_op jit(solution)/shard_map/ppermute | solution.py:398
  13.4 1.1 collective-permute-done.2
  14.4 0.9 pad_maximum_fusion.refs_1_
  15.3 5.4 %collective-permute-done.3.refs_1_ = bf16[64,4096]{1,0:T(8,128)(2,1)S(1)} collective-permute-done((bf16[64,4096]{1,0:T(8,128)(2,1)}, bf16[64,4096]{1,0:T(8,128)(2,1)S(1)}, u32[]{:S(2)}, u32[]{:S(2)}) %collective-permute-start.3) | collective-permute-done | bytes 524320 | tf_op jit(solution)/shard_map/ppermute | solution.py:436
  20.8 0.8 copy-done.1
  21.6 3.8 %delta.1 = bf16[4,576,128]{2,1,0:T(8,128)(2,1)} custom-call(s32[5]{0:T(128)} %stack.34.where_ref, bf16[128,4096]{1,0:T(8,128)(2,1)} %a_ref.1, f32[32,128]{1,0:T(8,128)} %l_ref.1, bf16[64,8192]{1,0:T(8,128)(2,1)} %refs_0_.3, bf16[64,4096]{1,0:T(8,128)(2,1)} %copy-done.1), custom_call_target="tpu_custom_call" | custom-call | tf_op jit(solution)/shard_map/delta/pallas_call | solution.py:360
  25.3 13.8 %all_to_all.10.refs_3_ = bf16[4,576,128]{2,1,0:T(8,128)(2,1)} all-to-all(bf16[4,576,128]{2,1,0:T(8,128)(2,1)} %delta.1), channel_id=1, replica_groups=mesh['z'=4,'y'=2,'core'=2,'tp'=2] {'y','core'}, dimensions={0} | all-to-all | bytes 1179648 | tf_op jit(solution)/shard_map/all_to_all | solution.py:433
  39.1 3.7 %all-to-all-start = ((bf16[4,3,512,128]{3,2,1,0:T(8,128)(2,1)}), bf16[4,3,512,128]{3,2,1,0:T(8,128)(2,1)S(1)}, u32[]{:S(2)}, u32[]{:S(2)}) async-start(bf16[4,3,512,128]{3,2,1,0:T(8,128)(2,1)} %get-tuple-element.38), calls=%async_computation | async-start | bytes 3145728 | tf_op jit(solution)/shard_map/all_to_all | solution.py:433
  42.8 1.9 %collective-permute-start.6 = (bf16[4,2,128,128]{3,2,1,0:T(8,128)(2,1)S(1)}, bf16[4,2,128,128]{3,2,1,0:T(8,128)(2,1)S(1)}, u32[]{:S(2)}, u32[]{:S(2)}) collective-permute-start(bf16[4,2,128,128]{3,2,1,0:T(8,128)(2,1)S(1)} %pad_maximum_fusion.refs_1_), channel_id=1, source_target_pairs={{0,8},{8,16},{16,24},{24,0},{1,9},{9,17},{17,25},{25,1},{2,10},{10... | collective-permute-start | bytes 786440 | tf_op jit(solution)/shard_map/ppermute | solution.py:402
  44.7 2.6 %collective-permute-start.5 = (bf16[4,2,128,128]{3,2,1,0:T(8,128)(2,1)S(1)}, bf16[4,2,128,128]{3,2,1,0:T(8,128)(2,1)S(1)}, u32[]{:S(2)}, u32[]{:S(2)}) collective-permute-start(bf16[4,2,128,128]{3,2,1,0:T(8,128)(2,1)S(1)} %pad_maximum_fusion.refs_1_), channel_id=1, source_target_pairs={{0,16},{8,24},{16,0},{24,8},{1,17},{9,25},{17,1},{25,9},{2,18},{10... | collective-permute-start | bytes 786440 | tf_op jit(solution)/shard_map/ppermute | solution.py:402
  47.2 0.1 copy.13
  47.3 0.6 reshape.14.span_ref
  47.9 1.3 %collective-permute-start.4 = (bf16[4,2,128,128]{3,2,1,0:T(8,128)(2,1)S(1)}, bf16[4,2,128,128]{3,2,1,0:T(8,128)(2,1)S(1)}, u32[]{:S(2)}, u32[]{:S(2)}) collective-permute-start(bf16[4,2,128,128]{3,2,1,0:T(8,128)(2,1)S(1)} %pad_maximum_fusion.refs_1_), channel_id=1, source_target_pairs={{0,24},{8,0},{16,8},{24,16},{1,25},{9,1},{17,9},{25,17},{2,26},{10... | collective-permute-start | bytes 786440 | tf_op jit(solution)/shard_map/ppermute | solution.py:402
  49.3 4.7 %collective-permute-done.6.refs_1_ = bf16[4,2,128,128]{3,2,1,0:T(8,128)(2,1)S(1)} collective-permute-done((bf16[4,2,128,128]{3,2,1,0:T(8,128)(2,1)S(1)}, bf16[4,2,128,128]{3,2,1,0:T(8,128)(2,1)S(1)}, u32[]{:S(2)}, u32[]{:S(2)}) %collective-permute-start.6) | collective-permute-done | bytes 262176 | tf_op jit(solution)/shard_map/ppermute | solution.py:402
  54.0 10.9 %collective-permute-done.5.refs_0_ = bf16[4,2,128,128]{3,2,1,0:T(8,128)(2,1)S(1)} collective-permute-done((bf16[4,2,128,128]{3,2,1,0:T(8,128)(2,1)S(1)}, bf16[4,2,128,128]{3,2,1,0:T(8,128)(2,1)S(1)}, u32[]{:S(2)}, u32[]{:S(2)}) %collective-permute-start.5) | collective-permute-done | bytes 262176 | tf_op jit(solution)/shard_map/ppermute | solution.py:402
  64.9 0.0 all-to-all-done.refs_2_
  64.9 0.7 copy-done.12
  65.6 1.1 copy-done
  66.8 12.5 %attend.2 = (f32[8,128,512]{2,1,0:T(8,128)}, bf16[4,2,128,128]{3,2,1,0:T(8,128)(2,1)}, bf16[4,2,128,128]{3,2,1,0:T(8,128)(2,1)}) custom-call(s32[5]{0:T(128)} %stack.34.where_ref, s32[32]{0:T(128)} %map_ref.3, s32[8]{0:T(128)} %reshape.14.span_ref, bf16[4,2,128,128]{3,2,1,0:T(8,128)(2,1)} %copy-done.12, bf16[4,2,128,128]{3,2,1,0:T(8,128)(2,1)} %copy-done.11, ...), custom_call_target="tpu_custom_call" | custom-call | flops 3221225472 | bytes 6291456 | tf_op jit(solution)/shard_map/attend/pallas_call | solution.py:360
  79.2 7.1 %collective-permute-start.7 = (bf16[4,2,128,128]{3,2,1,0:T(8,128)(2,1)}, bf16[4,2,128,128]{3,2,1,0:T(8,128)(2,1)S(1)}, u32[]{:S(2)}, u32[]{:S(2)}) collective-permute-start(bf16[4,2,128,128]{3,2,1,0:T(8,128)(2,1)} %get-tuple-element.45), channel_id=1, source_target_pairs={{0,24},{8,0},{16,8},{24,16},{1,25},{9,1},{17,9},{25,17},{2,26},{10... | collective-permute-start | bytes 786440 | tf_op jit(solution)/shard_map/ppermute | solution.py:402
  86.4 1.1 collective-permute-start.8
  87.5 0.0 collective-permute-done.4.refs_0_
  87.5 0.7 copy-done.10
  88.2 14.9 %attend.3 = (bf16[2,512,128]{2,1,0:T(8,128)(2,1)}, bf16[2,512,128]{2,1,0:T(8,128)(2,1)}, bf16[2,512,128]{2,1,0:T(8,128)(2,1)}, bf16[2,512,128]{2,1,0:T(8,128)(2,...) custom-call(s32[5]{0:T(128)} %stack.34.where_ref, s32[32]{0:T(128)} %map_ref.3, s32[8]{0:T(128)} %reshape.14.span_ref, ...), custom_call_target="tpu_custom_call" | custom-call | flops 3221225472 | bytes 6291456 | tf_op jit(solution)/shard_map/attend/pallas_call | solution.py:360
  103.1 1.6 %collective-permute-done.8 = bf16[4,2,128,128]{3,2,1,0:T(8,128)(2,1)S(1)} collective-permute-done((bf16[4,2,128,128]{3,2,1,0:T(8,128)(2,1)}, bf16[4,2,128,128]{3,2,1,0:T(8,128)(2,1)S(1)}, u32[]{:S(2)}, u32[]{:S(2)}) %collective-permute-start.8) | collective-permute-done | bytes 262176 | tf_op jit(solution)/shard_map/ppermute | solution.py:402
  104.7 1.3 %collective-permute-start.10 = (bf16[2,512,128]{2,1,0:T(8,128)(2,1)}, bf16[2,512,128]{2,1,0:T(8,128)(2,1)S(1)}, u32[]{:S(2)}, u32[]{:S(2)}) collective-permute-start(bf16[2,512,128]{2,1,0:T(8,128)(2,1)} %get-tuple-element.51), channel_id=1, source_target_pairs={{0,4},{2,6},{4,0},{6,2},{1,5},{3,7},{5,1},{7,3},{8,12},{10,14},{12... | collective-permute-start | bytes 786440 | tf_op jit(solution)/shard_map/ppermute | solution.py:398
  106.1 0.5 collective-permute-start.11
  106.6 7.1 %collective-permute-done.12 = bf16[4,2,128,128]{3,2,1,0:T(8,128)(2,1)S(1)} collective-permute-done((bf16[4,2,128,128]{3,2,1,0:T(8,128)(2,1)}, bf16[4,2,128,128]{3,2,1,0:T(8,128)(2,1)S(1)}, u32[]{:S(2)}, u32[]{:S(2)}) %collective-permute-start.12) | collective-permute-done | bytes 262176 | tf_op jit(solution)/shard_map/ppermute | solution.py:402
  113.7 1.2 add_convert_fusion
  114.9 0.6 slice_bitcast_fusion
  115.5 0.0 collective-permute-start.15
  115.5 1.1 collective-permute-start.14
  116.6 0.8 collective-permute-start.13
  117.4 0.0 collective-permute-done.10.refs_2_
  117.4 1.5 %collective-permute-done.11.refs_3_ = bf16[2,512,128]{2,1,0:T(8,128)(2,1)S(1)} collective-permute-done((bf16[2,512,128]{2,1,0:T(8,128)(2,1)}, bf16[2,512,128]{2,1,0:T(8,128)(2,1)S(1)}, u32[]{:S(2)}, u32[]{:S(2)}) %collective-permute-start.11) | collective-permute-done | bytes 262176 | tf_op jit(solution)/shard_map/ppermute | solution.py:398
  118.9 1.4 %collective-permute-done.15.refs_7_ = bf16[2,128,128]{2,1,0:T(8,128)(2,1)S(1)} collective-permute-done((bf16[2,128,128]{2,1,0:T(8,128)(2,1)S(1)}, bf16[2,128,128]{2,1,0:T(8,128)(2,1)S(1)}, u32[]{:S(2)}, u32[]{:S(2)}) %collective-permute-start.15) | collective-permute-done | bytes 65568 | tf_op jit(solution)/shard_map/ppermute | solution.py:398
  120.3 1.8 %collective-permute-done.14.refs_6_ = bf16[2,128,128]{2,1,0:T(8,128)(2,1)S(1)} collective-permute-done((bf16[2,128,128]{2,1,0:T(8,128)(2,1)S(1)}, bf16[2,128,128]{2,1,0:T(8,128)(2,1)S(1)}, u32[]{:S(2)}, u32[]{:S(2)}) %collective-permute-start.14) | collective-permute-done | bytes 65568 | tf_op jit(solution)/shard_map/ppermute | solution.py:398
  122.1 0.0 collective-permute-done.13.refs_5_
  122.1 0.6 copy-done.7
  122.7 0.0 copy-done.8
  122.7 3.5 %last.1 = (bf16[128,4096]{1,0:T(8,128)(2,1)}, bf16[128,512]{1,0:T(8,128)(2,1)}, bf16[128,512]{1,0:T(8,128)(2,1)}) custom-call(s32[5]{0:T(128)} %stack.34.where_ref, f32[128,128]{1,0:T(8,128)} %get-tuple-element.30.cos_ref, f32[128,128]{1,0:T(8,128)} %get-tuple-element.31.sin_ref, bf16[2,512,128]{2,1,0:T(8,128)(2,1)} %get-tuple-element.49.refs_0_, ...), custom_call_target="tpu_custom_call" | custom-call | tf_op jit(solution)/shard_map/last/pallas_call | solution.py:360
  (24 shorter events, 0.0 us)
Async XLA Ops:
  5.7 15.1 %collective-permute-start.3 = (bf16[64,4096]{1,0:T(8,128)(2,1)}, bf16[64,4096]{1,0:T(8,128)(2,1)S(1)}, u32[]{:S(2)}, u32[]{:S(2)}) collective-permute-start(bf16[64,4096]{1,0:T(8,128)(2,1)} %get-tuple-element.36), channel_id=1, source_target_pairs={{0,1},{1,0},{2,3},{3,2},{4,5},{5,4},{6,7},{7,6},{8,9},{9,8},{10,11... | collective-permute-start | bytes 1572872 | tf_op jit(solution)/shard_map/ppermute | solution.py:436
  8.6 1.9 %collective-permute-start = (bf16[2,128,128]{2,1,0:T(8,128)(2,1)}, bf16[2,128,128]{2,1,0:T(8,128)(2,1)S(1)}, u32[]{:S(2)}, u32[]{:S(2)}) collective-permute-start(bf16[2,128,128]{2,1,0:T(8,128)(2,1)} %get-tuple-element.33), channel_id=1, source_target_pairs={{0,2},{2,0},{4,6},{6,4},{1,3},{3,1},{5,7},{7,5},{8,10},{10,8},{12,... | collective-permute-start | bytes 196616 | tf_op jit(solution)/shard_map/ppermute | solution.py:398
  8.6 4.7 %collective-permute-start.1 = (bf16[2,128,128]{2,1,0:T(8,128)(2,1)}, bf16[2,128,128]{2,1,0:T(8,128)(2,1)S(1)}, u32[]{:S(2)}, u32[]{:S(2)}) collective-permute-start(bf16[2,128,128]{2,1,0:T(8,128)(2,1)} %get-tuple-element.34), channel_id=1, source_target_pairs={{0,4},{2,6},{4,0},{6,2},{1,5},{3,7},{5,1},{7,3},{8,12},{10,14},{12... | collective-permute-start | bytes 196616 | tf_op jit(solution)/shard_map/ppermute | solution.py:398
  10.2 4.3 %collective-permute-start.2 = (bf16[2,128,128]{2,1,0:T(8,128)(2,1)}, bf16[2,128,128]{2,1,0:T(8,128)(2,1)S(1)}, u32[]{:S(2)}, u32[]{:S(2)}) collective-permute-start(bf16[2,128,128]{2,1,0:T(8,128)(2,1)} %get-tuple-element.35), channel_id=1, source_target_pairs={{0,6},{2,4},{4,2},{6,0},{1,7},{3,5},{5,3},{7,1},{8,14},{10,12},{12... | collective-permute-start | bytes 196616 | tf_op jit(solution)/shard_map/ppermute | solution.py:398
  15.3 63.9 %copy-start.2 = (bf16[4,2,128,128]{3,2,1,0:T(8,128)(2,1)}, bf16[4,2,128,128]{3,2,1,0:T(8,128)(2,1)S(1)}, u32[]{:S(2)}) copy-start(bf16[4,2,128,128]{3,2,1,0:T(8,128)(2,1)S(1)} %pad_maximum_fusion.refs_1_) | copy-start | bytes 786436
  20.8 0.8 copy-start.1
  39.1 8.2 %copy-start.9 = (s32[4,2]{0,1:T(2,128)S(1)}, s32[4,2]{0,1:T(2,128)}, u32[]{:S(2)}) copy-start(s32[4,2]{0,1:T(2,128)} %param.17) | copy-start | bytes 100
  39.1 25.8 %all-to-all-start = ((bf16[4,3,512,128]{3,2,1,0:T(8,128)(2,1)}), bf16[4,3,512,128]{3,2,1,0:T(8,128)(2,1)S(1)}, u32[]{:S(2)}, u32[]{:S(2)}) async-start(bf16[4,3,512,128]{3,2,1,0:T(8,128)(2,1)} %get-tuple-element.38), calls=%async_computation | async-start | bytes 3145728 | tf_op jit(solution)/shard_map/all_to_all | solution.py:433
  42.8 11.2 %collective-permute-start.6 = (bf16[4,2,128,128]{3,2,1,0:T(8,128)(2,1)S(1)}, bf16[4,2,128,128]{3,2,1,0:T(8,128)(2,1)S(1)}, u32[]{:S(2)}, u32[]{:S(2)}) collective-permute-start(bf16[4,2,128,128]{3,2,1,0:T(8,128)(2,1)S(1)} %pad_maximum_fusion.refs_1_), channel_id=1, source_target_pairs={{0,8},{8,16},{16,24},{24,0},{1,9},{9,17},{17,25},{25,1},{2,10},{10... | collective-permute-start | bytes 786440 | tf_op jit(solution)/shard_map/ppermute | solution.py:402
  44.7 20.3 %collective-permute-start.5 = (bf16[4,2,128,128]{3,2,1,0:T(8,128)(2,1)S(1)}, bf16[4,2,128,128]{3,2,1,0:T(8,128)(2,1)S(1)}, u32[]{:S(2)}, u32[]{:S(2)}) collective-permute-start(bf16[4,2,128,128]{3,2,1,0:T(8,128)(2,1)S(1)} %pad_maximum_fusion.refs_1_), channel_id=1, source_target_pairs={{0,16},{8,24},{16,0},{24,8},{1,17},{9,25},{17,1},{25,9},{2,18},{10... | collective-permute-start | bytes 786440 | tf_op jit(solution)/shard_map/ppermute | solution.py:402
  47.9 39.5 %collective-permute-start.4 = (bf16[4,2,128,128]{3,2,1,0:T(8,128)(2,1)S(1)}, bf16[4,2,128,128]{3,2,1,0:T(8,128)(2,1)S(1)}, u32[]{:S(2)}, u32[]{:S(2)}) collective-permute-start(bf16[4,2,128,128]{3,2,1,0:T(8,128)(2,1)S(1)} %pad_maximum_fusion.refs_1_), channel_id=1, source_target_pairs={{0,24},{8,0},{16,8},{24,16},{1,25},{9,1},{17,9},{25,17},{2,26},{10... | collective-permute-start | bytes 786440 | tf_op jit(solution)/shard_map/ppermute | solution.py:402
  54.0 10.9 %copy-start.11 = (bf16[4,2,128,128]{3,2,1,0:T(8,128)(2,1)}, bf16[4,2,128,128]{3,2,1,0:T(8,128)(2,1)S(1)}, u32[]{:S(2)}) copy-start(bf16[4,2,128,128]{3,2,1,0:T(8,128)(2,1)S(1)} %collective-permute-done.6.refs_1_) | copy-start | bytes 786436
  64.9 0.7 copy-start.12
  65.6 1.2 copy-start
  79.2 23.8 %collective-permute-start.7 = (bf16[4,2,128,128]{3,2,1,0:T(8,128)(2,1)}, bf16[4,2,128,128]{3,2,1,0:T(8,128)(2,1)S(1)}, u32[]{:S(2)}, u32[]{:S(2)}) collective-permute-start(bf16[4,2,128,128]{3,2,1,0:T(8,128)(2,1)} %get-tuple-element.45), channel_id=1, source_target_pairs={{0,24},{8,0},{16,8},{24,16},{1,25},{9,1},{17,9},{25,17},{2,26},{10... | collective-permute-start | bytes 786440 | tf_op jit(solution)/shard_map/ppermute | solution.py:402
  86.4 18.3 %collective-permute-start.8 = (bf16[4,2,128,128]{3,2,1,0:T(8,128)(2,1)}, bf16[4,2,128,128]{3,2,1,0:T(8,128)(2,1)S(1)}, u32[]{:S(2)}, u32[]{:S(2)}) collective-permute-start(bf16[4,2,128,128]{3,2,1,0:T(8,128)(2,1)} %get-tuple-element.46), channel_id=1, source_target_pairs={{0,16},{8,24},{16,0},{24,8},{1,17},{9,25},{17,1},{25,9},{2,18},{10... | collective-permute-start | bytes 786440 | tf_op jit(solution)/shard_map/ppermute | solution.py:402
  87.5 0.7 copy-start.10
  104.7 9.0 %collective-permute-start.12 = (bf16[4,2,128,128]{3,2,1,0:T(8,128)(2,1)}, bf16[4,2,128,128]{3,2,1,0:T(8,128)(2,1)S(1)}, u32[]{:S(2)}, u32[]{:S(2)}) collective-permute-start(bf16[4,2,128,128]{3,2,1,0:T(8,128)(2,1)} %get-tuple-element.56), channel_id=1, source_target_pairs={{0,8},{8,16},{16,24},{24,0},{1,9},{9,17},{17,25},{25,1},{2,10},{10... | collective-permute-start | bytes 786440 | tf_op jit(solution)/shard_map/ppermute | solution.py:402
  104.7 11.8 %collective-permute-start.9 = (bf16[2,512,128]{2,1,0:T(8,128)(2,1)}, bf16[2,512,128]{2,1,0:T(8,128)(2,1)S(1)}, u32[]{:S(2)}, u32[]{:S(2)}) collective-permute-start(bf16[2,512,128]{2,1,0:T(8,128)(2,1)} %get-tuple-element.50), channel_id=1, source_target_pairs={{0,2},{2,0},{4,6},{6,4},{1,3},{3,1},{5,7},{7,5},{8,10},{10,8},{12,... | collective-permute-start | bytes 786440 | tf_op jit(solution)/shard_map/ppermute | solution.py:398
  104.7 12.6 %collective-permute-start.10 = (bf16[2,512,128]{2,1,0:T(8,128)(2,1)}, bf16[2,512,128]{2,1,0:T(8,128)(2,1)S(1)}, u32[]{:S(2)}, u32[]{:S(2)}) collective-permute-start(bf16[2,512,128]{2,1,0:T(8,128)(2,1)} %get-tuple-element.51), channel_id=1, source_target_pairs={{0,4},{2,6},{4,0},{6,2},{1,5},{3,7},{5,1},{7,3},{8,12},{10,14},{12... | collective-permute-start | bytes 786440 | tf_op jit(solution)/shard_map/ppermute | solution.py:398
  106.1 12.8 %collective-permute-start.11 = (bf16[2,512,128]{2,1,0:T(8,128)(2,1)}, bf16[2,512,128]{2,1,0:T(8,128)(2,1)S(1)}, u32[]{:S(2)}, u32[]{:S(2)}) collective-permute-start(bf16[2,512,128]{2,1,0:T(8,128)(2,1)} %get-tuple-element.52), channel_id=1, source_target_pairs={{0,6},{2,4},{4,2},{6,0},{1,7},{3,5},{5,3},{7,1},{8,14},{10,12},{12... | collective-permute-start | bytes 786440 | tf_op jit(solution)/shard_map/ppermute | solution.py:398
  115.5 4.8 %collective-permute-start.15 = (bf16[2,128,128]{2,1,0:T(8,128)(2,1)S(1)}, bf16[2,128,128]{2,1,0:T(8,128)(2,1)S(1)}, u32[]{:S(2)}, u32[]{:S(2)}) collective-permute-start(bf16[2,128,128]{2,1,0:T(8,128)(2,1)S(1)} %get-tuple-element.57), channel_id=1, source_target_pairs={{0,6},{2,4},{4,2},{6,0},{1,7},{3,5},{5,3},{7,1},{8,14},{10,12},{12... | collective-permute-start | bytes 196616 | tf_op jit(solution)/shard_map/ppermute | solution.py:398
  115.5 6.6 %collective-permute-start.14 = (bf16[2,128,128]{2,1,0:T(8,128)(2,1)S(1)}, bf16[2,128,128]{2,1,0:T(8,128)(2,1)S(1)}, u32[]{:S(2)}, u32[]{:S(2)}) collective-permute-start(bf16[2,128,128]{2,1,0:T(8,128)(2,1)S(1)} %get-tuple-element.58), channel_id=1, source_target_pairs={{0,4},{2,6},{4,0},{6,2},{1,5},{3,7},{5,1},{7,3},{8,12},{10,14},{12... | collective-permute-start | bytes 196616 | tf_op jit(solution)/shard_map/ppermute | solution.py:398
  116.6 5.5 %copy-start.3 = (bf16[2,512,128]{2,1,0:T(8,128)(2,1)}, bf16[2,512,128]{2,1,0:T(8,128)(2,1)S(1)}, u32[]{:S(2)}) copy-start(bf16[2,512,128]{2,1,0:T(8,128)(2,1)S(1)} %collective-permute-done.9.refs_1_) | copy-start | bytes 786436
  116.6 5.5 %collective-permute-start.13 = (bf16[2,128,128]{2,1,0:T(8,128)(2,1)S(1)}, bf16[2,128,128]{2,1,0:T(8,128)(2,1)S(1)}, u32[]{:S(2)}, u32[]{:S(2)}) collective-permute-start(bf16[2,128,128]{2,1,0:T(8,128)(2,1)S(1)} %get-tuple-element.59), channel_id=1, source_target_pairs={{0,2},{2,0},{4,6},{6,4},{1,3},{3,1},{5,7},{7,5},{8,10},{10,8},{12,... | collective-permute-start | bytes 196616 | tf_op jit(solution)/shard_map/ppermute | solution.py:398
  117.4 4.7 %copy-start.4 = (bf16[2,512,128]{2,1,0:T(8,128)(2,1)}, bf16[2,512,128]{2,1,0:T(8,128)(2,1)S(1)}, u32[]{:S(2)}) copy-start(bf16[2,512,128]{2,1,0:T(8,128)(2,1)S(1)} %collective-permute-done.10.refs_2_) | copy-start | bytes 786436
  118.9 3.2 %copy-start.5 = (bf16[2,512,128]{2,1,0:T(8,128)(2,1)}, bf16[2,512,128]{2,1,0:T(8,128)(2,1)S(1)}, u32[]{:S(2)}) copy-start(bf16[2,512,128]{2,1,0:T(8,128)(2,1)S(1)} %collective-permute-done.11.refs_3_) | copy-start | bytes 786436
  120.3 1.8 %copy-start.6 = (bf16[2,128,128]{2,1,0:T(8,128)(2,1)}, bf16[2,128,128]{2,1,0:T(8,128)(2,1)S(1)}, u32[]{:S(2)}) copy-start(bf16[2,128,128]{2,1,0:T(8,128)(2,1)S(1)} %collective-permute-done.15.refs_7_) | copy-start | bytes 196612
  122.1 0.6 copy-start.7
  122.1 0.6 copy-start.8

commit v6 on v4

--- a/solution.py
+++ b/solution.py
@@ -74,18 +74,18 @@
     return slice(head * block_len, (head + 1) * block_len)
 
 
-def query_kernel(members, group, cos_ref, sin_ref, q_ref, out_ref):
+def query_kernel(members, group, where_ref, cos_ref, sin_ref, q_ref, *out_refs):
+    member = where_ref[0]
     cosine = cos_ref[...]
     signed = sin_ref[...] * half_sign()
     block_len = q_ref.shape[0] // BLOCKS_DEV
-    for member in range(members):
+    for flip in range(members):
         for head in range(group):
-            first = (member * group + head) * HEAD_SIZE
-            field = q_ref[:, first : first + HEAD_SIZE].astype(jnp.float32)
+            field = q_ref[:, head_lanes(member, flip, group, head)].astype(jnp.float32)
             turned = pltpu.roll(field, HEAD_SIZE // 2, 1)
             field = (field * cosine + turned * signed).astype(jnp.bfloat16)
             for step in range(BLOCKS_DEV):
-                out_ref[member, step, stacked(head, block_len), :] = field[
+                out_refs[flip][step, stacked(head, block_len), :] = field[
                     step * block_len : (step + 1) * block_len, :
                 ]
 
@@ -107,47 +107,39 @@
     return jnp.concatenate([total[i : i + 1] for i in range(count)], axis=1)
 
 
-def delta_kernel(members, group, where_ref, a_ref, l_ref, *refs):
-    refs = list(refs)
-    own_ref = refs.pop(0)
-    other_ref = refs.pop(0) if members > 1 else None
-    grad_refs = refs
-    member, tp_index = where_ref[0], where_ref[1]
-    block_len = a_ref.shape[0] // BLOCKS_DEV
+def block_half(members, number, where):
+    if members == 1:
+        return number
+    return where[1] if number == 0 else 1 - where[1]
+
+
+def delta_kernel(members, group, number, where_ref, a_ref, l_ref, source_ref, *grad_refs):
+    member = where_ref[0]
+    upper = block_half(members, number, where_ref)
+    block_len = a_ref.shape[0]
+    columns = group * block_len
     for flip in range(members):
-        g_ref = grad_refs[flip]
+        products = []
         for head in range(group):
             lanes = head_lanes(member, flip, group, head)
-            here = stacked(head, block_len)
-            if members > 1:
-                g_ref[tp_index, here, :] = own_ref[:, lanes]
-                g_ref[1 - tp_index, here, :] = other_ref[:, lanes]
-            else:
-                for step in range(BLOCKS_DEV):
-                    g_ref[step, here, :] = own_ref[stacked(step, block_len), lanes]
+            grad = source_ref[:, lanes]
+            grad_refs[flip][stacked(head, block_len), :] = grad
+            products.append(grad.astype(jnp.float32) * a_ref[:, lanes].astype(jnp.float32))
+        total = jnp.sum(jnp.concatenate(products, axis=0).T, axis=0, keepdims=True)
         first = pl.multiple_of((member ^ flip) * group, group)
         lse = l_ref[pl.ds(first, group), :] * LOG2E
-        for step in range(BLOCKS_DEV):
-            sums = []
-            for head in range(group):
-                lanes = head_lanes(member, flip, group, head)
-                product = g_ref[step, stacked(head, block_len), :].astype(jnp.float32) * a_ref[
-                    stacked(step, block_len), lanes
-                ].astype(jnp.float32)
-                sums.append(product)
-            total = jnp.sum(jnp.concatenate(sums, axis=0).T, axis=0, keepdims=True)
-            pieces = split_rows(row_vector(lse, step, block_len)) + split_rows(total)
-            pieces.append(jnp.zeros((STAT_ROWS - len(pieces), HEAD_SIZE), jnp.float32))
-            below = group * block_len
-            g_ref[step, below : below + STAT_ROWS, :] = jnp.concatenate(pieces, axis=0).astype(
-                jnp.bfloat16
-            )
+        pieces = split_rows(row_vector(lse, upper, block_len)) + split_rows(total)
+        pieces.append(jnp.zeros((STAT_ROWS - len(pieces), HEAD_SIZE), jnp.float32))
+        grad_refs[flip][columns : columns + STAT_ROWS, :] = jnp.concatenate(
+            pieces, axis=0
+        ).astype(jnp.bfloat16)
 
 
 def row_vector(table, upper, block_len):
     group, width = table.shape
     rolled = pltpu.roll(table, block_len, 1)
-    low, high = (table, rolled) if upper == 0 else (rolled, table)
+    low = jnp.where(upper == 0, table, rolled)
+    high = jnp.where(upper == 0, rolled, table)
     lane = lax.broadcasted_iota(jnp.int32, (1, width), 1)
     pieces = [
         jnp.where(lane < block_len, low[h : h + 1, :], high[h + 1 : h + 2, :])
@@ -162,8 +154,8 @@
     refs = list(refs)
     count = len(slabs)
     kv_refs = [refs.pop(0) for _ in range(count)]
-    q_ref = refs.pop(0)
-    g_refs = [refs.pop(0) for _ in range(members)]
+    q_refs = [refs.pop(0) for _ in range(members)]
+    g_refs = [[refs.pop(0) for _ in range(members)] for _ in range(BLOCKS_DEV)]
     in_ref = refs.pop(0) if carried else None
     dq_refs = [refs.pop(0) for _ in range(1 if carries else members)]
     part_refs = [refs.pop(0) for _ in range(count)]
@@ -234,9 +226,10 @@
     for flip in range(members):
         for step in range(BLOCKS_DEV):
             place = flip * BLOCKS_DEV + step
-            q_all[place] = q_ref[member ^ flip, step]
-            g_all[place] = g_refs[flip][step, :columns, :]
-            stats = g_refs[flip][step, columns:, :].astype(jnp.float32)
+            q_all[place] = q_refs[flip][step]
+            place = flip * BLOCKS_DEV + block_half(members, step, where_ref)
+            g_all[place] = g_refs[step][flip][:columns, :]
+            stats = g_refs[step][flip][columns:, :].astype(jnp.float32)
             half = 3 * columns // HEAD_SIZE
             l_all[place] = joined_row(stats[:half])
             d_all[place] = joined_row(stats[half : 2 * half])
@@ -322,7 +315,9 @@
     return field * cosine - pltpu.roll(field, HEAD_SIZE // 2, 1) * signed
 
 
-def query_gradient_kernel(members, group, where_ref, cos_ref, sin_ref, *refs):
+def last_kernel(members, group, where_ref, cos_ref, sin_ref, *refs):
+    dq_refs, sum_refs = refs[:members], refs[members : 2 * members]
+    grad_ref, dk_ref, dv_ref = refs[2 * members :]
     member = where_ref[0]
     block_len = cos_ref.shape[0] // BLOCKS_DEV
     for step in range(BLOCKS_DEV):
@@ -330,23 +325,15 @@
         cosine = cos_ref[here, :]
         signed = sin_ref[here, :] * half_sign()
         for flip in range(members):
+            lanes = head_lanes(member, flip, 1, 0)
+            field = sum_refs[flip][0, here, :].astype(jnp.float32)
+            dk_ref[here, lanes] = turned_back(field, cosine, signed).astype(jnp.bfloat16)
+            dv_ref[here, lanes] = sum_refs[flip][1, here, :].astype(jnp.bfloat16)
             for head in range(group):
-                field = refs[flip][step, stacked(head, block_len), :].astype(jnp.float32)
-                refs[members][here, head_lanes(member, flip, group, head)] = turned_back(
+                field = dq_refs[flip][step, stacked(head, block_len), :].astype(jnp.float32)
+                grad_ref[here, head_lanes(member, flip, group, head)] = turned_back(
                     field, cosine, signed
                 ).astype(jnp.bfloat16)
-
-
-def last_kernel(members, where_ref, cos_ref, sin_ref, *refs):
-    member = where_ref[0]
-    dk_ref, dv_ref = refs[members], refs[members + 1]
-    cosine = cos_ref[...]
-    signed = sin_ref[...] * half_sign()
-    for flip in range(members):
-        lanes = head_lanes(member, flip, 1, 0)
-        field = refs[flip][0].astype(jnp.float32)
-        dk_ref[:, lanes] = turned_back(field, cosine, signed).astype(jnp.bfloat16)
-        dv_ref[:, lanes] = refs[flip][1].astype(jnp.bfloat16)
 
 
 def whole(shape):
@@ -418,16 +405,16 @@
     kv_pieces = results[2 : 2 + members]
     columns = group * block_len
     stack = (BLOCKS_DEV, columns, HEAD_SIZE)
-    (q_stack,) = call(
+    q_pieces = call(
         functools.partial(query_kernel, members, group),
-        "rotate", [], [cosine, sine, queries], [((members, *stack), bf16)],
+        "rotate", [place], [cosine, sine, queries], [(stack, bf16)] * members,
     )
     if members > 1:
         slab = jnp.stack([flipped(kv_pieces[f], f) for f in every])
         grads_other = lax.ppermute(results[-1], "tp", [(0, 1), (1, 0)])
         far = sorted(range(1, layers), key=lambda k: abs(2 * k - layers))
         rounds = [far[: layers // 2], far[layers // 2 :] + [0]]
-        q_stack = lax.all_to_all(q_stack, ("y", "core"), 0, 0, tiled=True)
+        slab, *q_pieces = lax.optimization_barrier((slab, *q_pieces))
         kv = {0: slab}
         for k in far:
             kv[k] = climbed(slab, k)
@@ -435,25 +422,29 @@
         kv = {0: lax.all_gather(kv_pieces[0], ("z", "y", "core"), axis=0, tiled=False)}
         rounds = [[0]]
         grads_own = lax.all_to_all(out_grad, "tp", split_axis=1, concat_axis=0, tiled=True)
-
-    inputs = [attn_out, logsumexp]
-    in_specs = [whole(a.shape) for a in inputs]
-    if members > 1:
-        inputs += [out_grad, grads_other]
-        in_specs += [
-            pl.BlockSpec(grads_other.shape, lambda i, where: (0, where[1])),
-            whole(grads_other.shape),
-        ]
-    else:
-        inputs += [grads_own]
-        in_specs += [whole(grads_own.shape)]
-    results = call(
-        functools.partial(delta_kernel, members, group),
-        "delta", [place], inputs,
-        [((BLOCKS_DEV, columns + STAT_ROWS, HEAD_SIZE), bf16)] * members,
-        in_specs,
-    )
-    g_in = [flipped(results[f], f) for f in every]
+    q_in = [flipped(q_pieces[f], f) for f in every]
+
+    g_in = []
+    for number in range(BLOCKS_DEV):
+
+        def half_rows(i, where, number=number):
+            return (block_half(members, number, where), 0)
+
+        own_rows = pl.BlockSpec((block_len, members * width), half_rows)
+        if members == 1:
+            source, spec = grads_own, own_rows
+        elif number == 0:
+            source = out_grad
+            spec = pl.BlockSpec(grads_other.shape, lambda i, where: (0, where[1]))
+        else:
+            source, spec = grads_other, whole(grads_other.shape)
+        pieces = call(
+            functools.partial(delta_kernel, members, group, number),
+            "delta", [place], [attn_out, logsumexp, source],
+            [((columns + STAT_ROWS, HEAD_SIZE), bf16)] * members,
+            [own_rows, whole(logsumexp.shape), spec],
+        )
+        g_in += [flipped(pieces[f], f) for f in every]
 
     units = kv[0].shape[0]
     blocks = members * BLOCKS_DEV
@@ -469,7 +460,7 @@
                 attend_kernel, members, group, block_len, slabs, number > 0, carries
             ),
             "attend", [place, block_map, span_blocks.reshape(-1)],
-            [*[kv[k] for k in slabs], q_stack, *g_in, *carry],
+            [*[kv[k] for k in slabs], *q_in, *g_in, *carry],
             ([(sums, f32)] if carries else [(stack, bf16)] * members)
             + [(part, f32 if k == 0 and members > 1 else bf16) for k in slabs],
             scratch=[
@@ -512,18 +503,14 @@
         sums = [
             lax.psum_scatter(parts[0], ("z", "y", "core"), scatter_dimension=0, tiled=True)[0]
         ]
-    (grad_q,) = call(
-        functools.partial(query_gradient_kernel, members, group),
-        "turn_back", [place],
-        [cosine, sine] + [flipped(dq_pieces[f], f) for f in every],
-        [(queries.shape, bf16)],
+    return tuple(
+        call(
+            functools.partial(last_kernel, members, group),
+            "last", [place],
+            [cosine, sine, *[flipped(dq_pieces[f], f) for f in every], *sums],
+            [(queries.shape, bf16), (keys.shape, bf16), (values.shape, bf16)],
+        )
     )
-    key_gradient, value_gradient = call(
-        functools.partial(last_kernel, members),
-        "last", [place], [cosine, sine, *sums],
-        [(keys.shape, bf16), (values.shape, bf16)],
-    )
-    return (grad_q, key_gradient, value_gradient)
 
 
 def solution(mesh):

time: 114 us -> 106 us (0.930)
  waiting for transfers between devices: 32.5 us -> 25 us
  starting transfers between devices: 24.8 us -> 27.9 us
  local copies, waits for them, and re-layouts: 6.16 us -> 3.98 us
    ppermute x6, waiting for transfers between devices: 23.5 us -> 12.9 us  [climbed(): return lax.ppermute(array, 'z', route)]
    ppermute x12 -> x18, waiting for transfers between devices: 5.48 us -> 12 us  [flipped(): return lax.ppermute(array, ('y', 'core'), [(i, i ^ flip) for i in range(4)])]
    ppermute x6, starting transfers between devices: 10.4 us -> 14.5 us  [climbed(): return lax.ppermute(array, 'z', route)]
    all_to_all x1 -> x0, starting transfers between devices: 3.65 us -> none  [shards(): q_stack = lax.all_to_all(q_stack, ('y', 'core'), 0, 0, tiled=True)]
    ppermute x1, waiting for transfers between devices: 3.5 us -> 0.01 us  [shards(): grads_other = lax.ppermute(results[-1], 'tp', [(0, 1), (1, 0)])]
    ppermute x12 -> x18, starting transfers between devices: 7.78 us -> 10.5 us  [flipped(): return lax.ppermute(array, ('y', 'core'), [(i, i ^ flip) for i in range(4)])]
    unnamed x41 -> x45, local copies, waits for them, and re-layouts: 4.26 us -> 2.15 us
  transfers between devices with their start and end apart: 20 -> 25, of which waited for: 8 -> 8; matrix products, arithmetic and copies ran while one was open for 2% -> 2% of each run, Pallas kernels for 37% -> 38%
where the time goes in v6:
time: 106 us
  Pallas kernels  46.8 us (44%)
  starting transfers between devices  27.9 us (26%)
  waiting for transfers between devices  25 us (24%)
  local copies, waits for them, and re-layouts  3.98 us (4%)
  other arithmetic  1.2 us (1%)
    pallas_call x7, Pallas kernels, call(): pl.pallas_call(kernel, grid_spec=pltpu.PrefetchScalarGridSpec(num_scalar_...  46.8 us
    ppermute x6, starting transfers between devices, climbed(): return lax.ppermute(array, 'z', route)  14.5 us
    ppermute x6, waiting for transfers between devices, climbed(): return lax.ppermute(array, 'z', route)  12.9 us
    ppermute x18, waiting for transfers between devices, flipped(): return lax.ppermute(array, ('y', 'core'), [(i, i ^ flip) for i in range(4)])  12 us
    ppermute x18, starting transfers between devices, flipped(): return lax.ppermute(array, ('y', 'core'), [(i, i ^ flip) for i in range(4)])  10.5 us
    ppermute x1, starting transfers between devices, shards(): grads_other = lax.ppermute(results[-1], 'tp', [(0, 1), (1, 0)])  2.94 us
    unnamed x45, local copies, waits for them, and re-layouts  2.15 us
  transfers between devices with their start and end apart: 25, of which 8 were waited for; matrix products, arithmetic and copies ran while one was open for 2% of the time, Pallas kernels for 38%

profile of v6, /device:TPU:0, one launch (start us, length us, event | category | flops | bytes accessed | tf_op | source)
XLA Modules:
  0.0 105.8 jit_solution(3942030431647680732)
XLA Ops:
  0.6 0.6 stack.34.where_ref
  1.2 3.0 %first.1 = (f32[128,128]{1,0:T(8,128)}, f32[128,128]{1,0:T(8,128)}, bf16[2,128,128]{2,1,0:T(8,128)(2,1)}, bf16[2,128,128]{2,1,0:T(8,128)(2,1)}, bf16[2,128,128]{...) custom-call(s32[5]{0:T(128)} %stack.34.where_ref, s32[3,128]{1,0:T(4,128)} %ids_ref.1, ...), custom_call_target="tpu_custom_call" | custom-call | tf_op jit(solution)/shard_map/first/pallas_call | solution.py:344
  4.3 2.9 %collective-permute-start.10 = (bf16[64,4096]{1,0:T(8,128)(2,1)}, bf16[64,4096]{1,0:T(8,128)(2,1)S(1)}, u32[]{:S(2)}, u32[]{:S(2)}) collective-permute-start(bf16[64,4096]{1,0:T(8,128)(2,1)} %get-tuple-element.63), channel_id=1, source_target_pairs={{0,1},{1,0},{2,3},{3,2},{4,5},{5,4},{6,7},{7,6},{8,9},{9,8},{10,11... | collective-permute-start | bytes 1572872 | tf_op jit(solution)/shard_map/ppermute | solution.py:414
  7.2 1.5 %collective-permute-start.1 = (bf16[2,128,128]{2,1,0:T(8,128)(2,1)}, bf16[2,128,128]{2,1,0:T(8,128)(2,1)S(1)}, u32[]{:S(2)}, u32[]{:S(2)}) collective-permute-start(bf16[2,128,128]{2,1,0:T(8,128)(2,1)} %get-tuple-element.48), channel_id=1, source_target_pairs={{0,4},{2,6},{4,0},{6,2},{1,5},{3,7},{5,1},{7,3},{8,12},{10,14},{12... | collective-permute-start | bytes 196616 | tf_op jit(solution)/shard_map/ppermute | solution.py:382
  8.7 0.3 collective-permute-start.2
  9.1 3.0 %delta.2 = (bf16[544,128]{1,0:T(8,128)(2,1)}, bf16[544,128]{1,0:T(8,128)(2,1)}, bf16[544,128]{1,0:T(8,128)(2,1)}, bf16[544,128]{1,0:T(8,128)(2,1)}) custom-call(s32[5]{0:T(128)} %stack.34.where_ref, bf16[128,4096]{1,0:T(8,128)(2,1)} %a_ref.3, f32[32,128]{1,0:T(8,128)} %l_ref.3, bf16[64,8192]{1,0:T(8,128)(2,1)} %source_ref.1), custom_call_target="tpu_custom_call" | custom-call | tf_op jit(solution)/shard_map/delta/pallas_call | solution.py:344
  12.1 0.3 collective-permute-start.7
  12.4 1.5 %collective-permute-start.8 = (bf16[544,128]{1,0:T(8,128)(2,1)}, bf16[544,128]{1,0:T(8,128)(2,1)S(1)}, u32[]{:S(2)}, u32[]{:S(2)}) collective-permute-start(bf16[544,128]{1,0:T(8,128)(2,1)} %get-tuple-element.61), channel_id=1, source_target_pairs={{0,4},{2,6},{4,0},{6,2},{1,5},{3,7},{5,1},{7,3},{8,12},{10,14},{12... | collective-permute-start | bytes 417800 | tf_op jit(solution)/shard_map/ppermute | solution.py:382
  13.9 3.3 %rotate.1 = (bf16[2,512,128]{2,1,0:T(8,128)(2,1)}, bf16[2,512,128]{2,1,0:T(8,128)(2,1)}, bf16[2,512,128]{2,1,0:T(8,128)(2,1)}, bf16[2,512,128]{2,1,0:T(8,128)(2,1)}) custom-call(s32[5]{0:T(128)} %stack.34.where_ref, f32[128,128]{1,0:T(8,128)} %get-tuple-element.44.cos_ref, f32[128,128]{1,0:T(8,128)} %get-tuple-element.45.sin_ref, bf16[128,4096]{1,0:T(8,128)(2,1)} %q_ref.1), custom_call_target="tpu_custom_call" | custom-call | tf_op jit(solution)/shard_map/rotate/pallas_call | solution.py:344
  17.2 0.1 collective-permute-start.9
  17.3 0.6 collective-permute-start.4
  17.9 1.5 %collective-permute-start.5 = (bf16[2,512,128]{2,1,0:T(8,128)(2,1)}, bf16[2,512,128]{2,1,0:T(8,128)(2,1)S(1)}, u32[]{:S(2)}, u32[]{:S(2)}) collective-permute-start(bf16[2,512,128]{2,1,0:T(8,128)(2,1)} %get-tuple-element.57), channel_id=1, source_target_pairs={{0,4},{2,6},{4,0},{6,2},{1,5},{3,7},{5,1},{7,3},{8,12},{10,14},{12... | collective-permute-start | bytes 786440 | tf_op jit(solution)/shard_map/ppermute | solution.py:382
  19.5 3.8 %collective-permute-done.9.refs_9_ = bf16[544,128]{1,0:T(8,128)(2,1)S(1)} collective-permute-done((bf16[544,128]{1,0:T(8,128)(2,1)}, bf16[544,128]{1,0:T(8,128)(2,1)S(1)}, u32[]{:S(2)}, u32[]{:S(2)}) %collective-permute-start.9) | collective-permute-done | bytes 139296 | tf_op jit(solution)/shard_map/ppermute | solution.py:382
  23.2 1.6 %collective-permute-start.15 = (bf16[4,2,128,128]{3,2,1,0:T(8,128)(2,1)S(1)}, bf16[4,2,128,128]{3,2,1,0:T(8,128)(2,1)S(1)}, u32[]{:S(2)}, u32[]{:S(2)}) collective-permute-start(bf16[4,2,128,128]{3,2,1,0:T(8,128)(2,1)S(1)} %pad_maximum_fusion.refs_1_), channel_id=1, source_target_pairs={{0,8},{8,16},{16,24},{24,0},{1,9},{9,17},{17,25},{25,1},{2,10},{10... | collective-permute-start | bytes 786440 | tf_op jit(solution)/shard_map/ppermute | solution.py:386
  24.8 2.6 %collective-permute-start.14 = (bf16[4,2,128,128]{3,2,1,0:T(8,128)(2,1)S(1)}, bf16[4,2,128,128]{3,2,1,0:T(8,128)(2,1)S(1)}, u32[]{:S(2)}, u32[]{:S(2)}) collective-permute-start(bf16[4,2,128,128]{3,2,1,0:T(8,128)(2,1)S(1)} %pad_maximum_fusion.refs_1_), channel_id=1, source_target_pairs={{0,16},{8,24},{16,0},{24,8},{1,17},{9,25},{17,1},{25,9},{2,18},{10... | collective-permute-start | bytes 786440 | tf_op jit(solution)/shard_map/ppermute | solution.py:386
  27.4 3.0 %delta.3 = (bf16[544,128]{1,0:T(8,128)(2,1)}, bf16[544,128]{1,0:T(8,128)(2,1)}, bf16[544,128]{1,0:T(8,128)(2,1)}, bf16[544,128]{1,0:T(8,128)(2,1)}) custom-call(s32[5]{0:T(128)} %stack.34.where_ref, bf16[128,4096]{1,0:T(8,128)(2,1)} %a_ref.3, f32[32,128]{1,0:T(8,128)} %l_ref.3, bf16[64,4096]{1,0:T(8,128)(2,1)} %copy-done), custom_call_target="tpu_custom_call" | custom-call | tf_op jit(solution)/shard_map/delta/pallas_call | solution.py:344
  30.4 0.1 collective-permute-start.11
  30.5 0.6 collective-permute-start.12
  31.1 3.4 %collective-permute-done.6.refs_5_ = bf16[2,512,128]{2,1,0:T(8,128)(2,1)S(1)} collective-permute-done((bf16[2,512,128]{2,1,0:T(8,128)(2,1)}, bf16[2,512,128]{2,1,0:T(8,128)(2,1)S(1)}, u32[]{:S(2)}, u32[]{:S(2)}) %collective-permute-start.6) | collective-permute-done | bytes 262176 | tf_op jit(solution)/shard_map/ppermute | solution.py:382
  34.5 0.2 collective-permute-start.13
  34.7 0.1 copy.13
  34.8 0.6 reshape.14.span_ref
  35.4 3.6 %collective-permute-start.3 = (bf16[4,2,128,128]{3,2,1,0:T(8,128)(2,1)S(1)}, bf16[4,2,128,128]{3,2,1,0:T(8,128)(2,1)S(1)}, u32[]{:S(2)}, u32[]{:S(2)}) collective-permute-start(bf16[4,2,128,128]{3,2,1,0:T(8,128)(2,1)S(1)} %pad_maximum_fusion.refs_1_), channel_id=1, source_target_pairs={{0,24},{8,0},{16,8},{24,16},{1,25},{9,1},{17,9},{25,17},{2,26},{10... | collective-permute-start | bytes 786440 | tf_op jit(solution)/shard_map/ppermute | solution.py:386
  39.0 5.8 %collective-permute-done.14.refs_0_ = bf16[4,2,128,128]{3,2,1,0:T(8,128)(2,1)S(1)} collective-permute-done((bf16[4,2,128,128]{3,2,1,0:T(8,128)(2,1)S(1)}, bf16[4,2,128,128]{3,2,1,0:T(8,128)(2,1)S(1)}, u32[]{:S(2)}, u32[]{:S(2)}) %collective-permute-start.14) | collective-permute-done | bytes 262176 | tf_op jit(solution)/shard_map/ppermute | solution.py:386
  44.9 0.6 copy-done.14
  45.5 0.0 copy-done.19
  45.5 0.0 copy-done.20
  45.6 0.0 copy-done.21
  45.6 15.0 %attend.2 = (f32[8,128,512]{2,1,0:T(8,128)}, bf16[4,2,128,128]{3,2,1,0:T(8,128)(2,1)}, bf16[4,2,128,128]{3,2,1,0:T(8,128)(2,1)}) custom-call(s32[5]{0:T(128)} %stack.34.where_ref, s32[32]{0:T(128)} %map_ref.3, s32[8]{0:T(128)} %reshape.14.span_ref, bf16[4,2,128,128]{3,2,1,0:T(8,128)(2,1)} %copy-done.14, bf16[4,2,128,128]{3,2,1,0:T(8,128)(2,1)} %copy-done.13, ...), custom_call_target="tpu_custom_call" | custom-call | flops 3221225472 | bytes 6291456 | tf_op jit(solution)/shard_map/attend/pallas_call | solution.py:344
  60.6 5.5 %collective-permute-start.16 = (bf16[4,2,128,128]{3,2,1,0:T(8,128)(2,1)}, bf16[4,2,128,128]{3,2,1,0:T(8,128)(2,1)S(1)}, u32[]{:S(2)}, u32[]{:S(2)}) collective-permute-start(bf16[4,2,128,128]{3,2,1,0:T(8,128)(2,1)} %get-tuple-element.73), channel_id=1, source_target_pairs={{0,24},{8,0},{16,8},{24,16},{1,25},{9,1},{17,9},{25,17},{2,26},{10... | collective-permute-start | bytes 786440 | tf_op jit(solution)/shard_map/ppermute | solution.py:386
  66.1 1.3 %collective-permute-start.17 = (bf16[4,2,128,128]{3,2,1,0:T(8,128)(2,1)}, bf16[4,2,128,128]{3,2,1,0:T(8,128)(2,1)S(1)}, u32[]{:S(2)}, u32[]{:S(2)}) collective-permute-start(bf16[4,2,128,128]{3,2,1,0:T(8,128)(2,1)} %get-tuple-element.74), channel_id=1, source_target_pairs={{0,16},{8,24},{16,0},{24,8},{1,17},{9,25},{17,1},{25,9},{2,18},{10... | collective-permute-start | bytes 786440 | tf_op jit(solution)/shard_map/ppermute | solution.py:386
  67.4 0.7 copy-done.15
  68.1 16.1 %attend.3 = (bf16[2,512,128]{2,1,0:T(8,128)(2,1)}, bf16[2,512,128]{2,1,0:T(8,128)(2,1)}, bf16[2,512,128]{2,1,0:T(8,128)(2,1)}, bf16[2,512,128]{2,1,0:T(8,128)(2,...) custom-call(s32[5]{0:T(128)} %stack.34.where_ref, s32[32]{0:T(128)} %map_ref.3, s32[8]{0:T(128)} %reshape.14.span_ref, ...), custom_call_target="tpu_custom_call" | custom-call | flops 3221225472 | bytes 6291456 | tf_op jit(solution)/shard_map/attend/pallas_call | solution.py:344
  84.1 0.1 collective-permute-done.17
  84.3 0.0 collective-permute-start.18
  84.3 0.6 collective-permute-start.19
  84.9 1.3 %collective-permute-start.20 = (bf16[2,512,128]{2,1,0:T(8,128)(2,1)}, bf16[2,512,128]{2,1,0:T(8,128)(2,1)S(1)}, u32[]{:S(2)}, u32[]{:S(2)}) collective-permute-start(bf16[2,512,128]{2,1,0:T(8,128)(2,1)} %get-tuple-element.80), channel_id=1, source_target_pairs={{0,6},{2,4},{4,2},{6,0},{1,7},{3,5},{5,3},{7,1},{8,14},{10,12},{12... | collective-permute-start | bytes 786440 | tf_op jit(solution)/shard_map/ppermute | solution.py:382
  86.1 7.0 %collective-permute-done.21 = bf16[4,2,128,128]{3,2,1,0:T(8,128)(2,1)S(1)} collective-permute-done((bf16[4,2,128,128]{3,2,1,0:T(8,128)(2,1)}, bf16[4,2,128,128]{3,2,1,0:T(8,128)(2,1)S(1)}, u32[]{:S(2)}, u32[]{:S(2)}) %collective-permute-start.21) | collective-permute-done | bytes 262176 | tf_op jit(solution)/shard_map/ppermute | solution.py:386
  93.1 1.2 %add_convert_fusion = bf16[4,2,128,128]{3,2,1,0:T(8,128)(2,1)S(1)} fusion(bf16[4,2,128,128]{3,2,1,0:T(8,128)(2,1)S(1)} %collective-permute-done.21, bf16[4,2,128,128]{3,2,1,0:T(8,128)(2,1)S(1)} %collective-permute-done.16, f32[4,2,128,128]{3,2,1,0:T(8,128)} %get-tuple-element.81, bf16[4,2,128,128]{3,2,1,0:T(8,128)(2,1)S(1)} %collective-permute-done.17), kind=kLoop, calls=%fused_computation | loop fusion | flops 917504 | bytes 1572864 | tf_op jit(solution)/shard_map/convert.3
  94.3 0.6 slice_bitcast_fusion
  94.9 0.4 collective-permute-start.23
  95.3 1.4 %collective-permute-start.22 = (bf16[2,128,128]{2,1,0:T(8,128)(2,1)S(1)}, bf16[2,128,128]{2,1,0:T(8,128)(2,1)S(1)}, u32[]{:S(2)}, u32[]{:S(2)}) collective-permute-start(bf16[2,128,128]{2,1,0:T(8,128)(2,1)S(1)} %get-tuple-element.87), channel_id=1, source_target_pairs={{0,2},{2,0},{4,6},{6,4},{1,3},{3,1},{5,7},{7,5},{8,10},{10,8},{12,... | collective-permute-start | bytes 196616 | tf_op jit(solution)/shard_map/ppermute | solution.py:382
  96.8 1.6 %collective-permute-done.20.refs_3_ = bf16[2,512,128]{2,1,0:T(8,128)(2,1)S(1)} collective-permute-done((bf16[2,512,128]{2,1,0:T(8,128)(2,1)}, bf16[2,512,128]{2,1,0:T(8,128)(2,1)S(1)}, u32[]{:S(2)}, u32[]{:S(2)}) %collective-permute-start.20) | collective-permute-done | bytes 262176 | tf_op jit(solution)/shard_map/ppermute | solution.py:382
  98.4 1.4 %collective-permute-done.24.refs_7_ = bf16[2,128,128]{2,1,0:T(8,128)(2,1)S(1)} collective-permute-done((bf16[2,128,128]{2,1,0:T(8,128)(2,1)S(1)}, bf16[2,128,128]{2,1,0:T(8,128)(2,1)S(1)}, u32[]{:S(2)}, u32[]{:S(2)}) %collective-permute-start.24) | collective-permute-done | bytes 65568 | tf_op jit(solution)/shard_map/ppermute | solution.py:382
  99.8 1.9 %collective-permute-done.23.refs_6_ = bf16[2,128,128]{2,1,0:T(8,128)(2,1)S(1)} collective-permute-done((bf16[2,128,128]{2,1,0:T(8,128)(2,1)S(1)}, bf16[2,128,128]{2,1,0:T(8,128)(2,1)S(1)}, u32[]{:S(2)}, u32[]{:S(2)}) %collective-permute-start.23) | collective-permute-done | bytes 65568 | tf_op jit(solution)/shard_map/ppermute | solution.py:382
  101.7 0.6 copy-done.7
  102.3 0.0 copy-done.8
  102.3 3.5 %last.1 = (bf16[128,4096]{1,0:T(8,128)(2,1)}, bf16[128,512]{1,0:T(8,128)(2,1)}, bf16[128,512]{1,0:T(8,128)(2,1)}) custom-call(s32[5]{0:T(128)} %stack.34.where_ref, f32[128,128]{1,0:T(8,128)} %get-tuple-element.44.cos_ref, f32[128,128]{1,0:T(8,128)} %get-tuple-element.45.sin_ref, bf16[2,512,128]{2,1,0:T(8,128)(2,1)} %get-tuple-element.77.refs_0_, ...), custom_call_target="tpu_custom_call" | custom-call | tf_op jit(solution)/shard_map/last/pallas_call | solution.py:344
  (59 shorter events, 0.2 us)
Async XLA Ops:
  4.3 13.0 %copy-start.5 = (bf16[2,128,128]{2,1,0:T(8,128)(2,1)S(1)}, bf16[2,128,128]{2,1,0:T(8,128)(2,1)}, u32[]{:S(2)}) copy-start(bf16[2,128,128]{2,1,0:T(8,128)(2,1)} %get-tuple-element.46) | copy-start | bytes 196612
  4.3 20.5 %collective-permute-start.10 = (bf16[64,4096]{1,0:T(8,128)(2,1)}, bf16[64,4096]{1,0:T(8,128)(2,1)S(1)}, u32[]{:S(2)}, u32[]{:S(2)}) collective-permute-start(bf16[64,4096]{1,0:T(8,128)(2,1)} %get-tuple-element.63), channel_id=1, source_target_pairs={{0,1},{1,0},{2,3},{3,2},{4,5},{5,4},{6,7},{7,6},{8,9},{9,8},{10,11... | collective-permute-start | bytes 1572872 | tf_op jit(solution)/shard_map/ppermute | solution.py:414
  7.2 5.2 %collective-permute-start = (bf16[2,128,128]{2,1,0:T(8,128)(2,1)}, bf16[2,128,128]{2,1,0:T(8,128)(2,1)S(1)}, u32[]{:S(2)}, u32[]{:S(2)}) collective-permute-start(bf16[2,128,128]{2,1,0:T(8,128)(2,1)} %get-tuple-element.47), channel_id=1, source_target_pairs={{0,2},{2,0},{4,6},{6,4},{1,3},{3,1},{5,7},{7,5},{8,10},{10,8},{12,... | collective-permute-start | bytes 196616 | tf_op jit(solution)/shard_map/ppermute | solution.py:382
  7.2 10.0 %collective-permute-start.1 = (bf16[2,128,128]{2,1,0:T(8,128)(2,1)}, bf16[2,128,128]{2,1,0:T(8,128)(2,1)S(1)}, u32[]{:S(2)}, u32[]{:S(2)}) collective-permute-start(bf16[2,128,128]{2,1,0:T(8,128)(2,1)} %get-tuple-element.48), channel_id=1, source_target_pairs={{0,4},{2,6},{4,0},{6,2},{1,5},{3,7},{5,1},{7,3},{8,12},{10,14},{12... | collective-permute-start | bytes 196616 | tf_op jit(solution)/shard_map/ppermute | solution.py:382
  8.7 8.5 %collective-permute-start.2 = (bf16[2,128,128]{2,1,0:T(8,128)(2,1)}, bf16[2,128,128]{2,1,0:T(8,128)(2,1)S(1)}, u32[]{:S(2)}, u32[]{:S(2)}) collective-permute-start(bf16[2,128,128]{2,1,0:T(8,128)(2,1)} %get-tuple-element.49), channel_id=1, source_target_pairs={{0,6},{2,4},{4,2},{6,0},{1,7},{3,5},{5,3},{7,1},{8,14},{10,12},{12... | collective-permute-start | bytes 196616 | tf_op jit(solution)/shard_map/ppermute | solution.py:382
  12.1 22.6 %copy-start.9 = (s32[4,2]{0,1:T(2,128)S(1)}, s32[4,2]{0,1:T(2,128)}, u32[]{:S(2)}) copy-start(s32[4,2]{0,1:T(2,128)} %param.17) | copy-start | bytes 100
  12.1 5.8 %collective-permute-start.7 = (bf16[544,128]{1,0:T(8,128)(2,1)}, bf16[544,128]{1,0:T(8,128)(2,1)S(1)}, u32[]{:S(2)}, u32[]{:S(2)}) collective-permute-start(bf16[544,128]{1,0:T(8,128)(2,1)} %get-tuple-element.60), channel_id=1, source_target_pairs={{0,2},{2,0},{4,6},{6,4},{1,3},{3,1},{5,7},{7,5},{8,10},{10,8},{12,... | collective-permute-start | bytes 417800 | tf_op jit(solution)/shard_map/ppermute | solution.py:382
  12.4 7.1 %collective-permute-start.8 = (bf16[544,128]{1,0:T(8,128)(2,1)}, bf16[544,128]{1,0:T(8,128)(2,1)S(1)}, u32[]{:S(2)}, u32[]{:S(2)}) collective-permute-start(bf16[544,128]{1,0:T(8,128)(2,1)} %get-tuple-element.61), channel_id=1, source_target_pairs={{0,4},{2,6},{4,0},{6,2},{1,5},{3,7},{5,1},{7,3},{8,12},{10,14},{12... | collective-permute-start | bytes 417800 | tf_op jit(solution)/shard_map/ppermute | solution.py:382
  17.2 6.1 %collective-permute-start.9 = (bf16[544,128]{1,0:T(8,128)(2,1)}, bf16[544,128]{1,0:T(8,128)(2,1)S(1)}, u32[]{:S(2)}, u32[]{:S(2)}) collective-permute-start(bf16[544,128]{1,0:T(8,128)(2,1)} %get-tuple-element.62), channel_id=1, source_target_pairs={{0,6},{2,4},{4,2},{6,0},{1,7},{3,5},{5,3},{7,1},{8,14},{10,12},{12... | collective-permute-start | bytes 417800 | tf_op jit(solution)/shard_map/ppermute | solution.py:382
  17.3 43.3 %copy-start.1 = (bf16[4,2,128,128]{3,2,1,0:T(8,128)(2,1)}, bf16[4,2,128,128]{3,2,1,0:T(8,128)(2,1)S(1)}, u32[]{:S(2)}) copy-start(bf16[4,2,128,128]{3,2,1,0:T(8,128)(2,1)S(1)} %pad_maximum_fusion.refs_1_) | copy-start | bytes 786436
  17.3 13.1 %collective-permute-start.4 = (bf16[2,512,128]{2,1,0:T(8,128)(2,1)}, bf16[2,512,128]{2,1,0:T(8,128)(2,1)S(1)}, u32[]{:S(2)}, u32[]{:S(2)}) collective-permute-start(bf16[2,512,128]{2,1,0:T(8,128)(2,1)} %get-tuple-element.56), channel_id=1, source_target_pairs={{0,2},{2,0},{4,6},{6,4},{1,3},{3,1},{5,7},{7,5},{8,10},{10,8},{12,... | collective-permute-start | bytes 786440 | tf_op jit(solution)/shard_map/ppermute | solution.py:382
  17.9 26.9 %copy-start.16 = (bf16[544,128]{1,0:T(8,128)(2,1)}, bf16[544,128]{1,0:T(8,128)(2,1)S(1)}, u32[]{:S(2)}) copy-start(bf16[544,128]{1,0:T(8,128)(2,1)S(1)} %collective-permute-done.7.refs_7_) | copy-start | bytes 417796
  17.9 12.6 %collective-permute-start.5 = (bf16[2,512,128]{2,1,0:T(8,128)(2,1)}, bf16[2,512,128]{2,1,0:T(8,128)(2,1)S(1)}, u32[]{:S(2)}, u32[]{:S(2)}) collective-permute-start(bf16[2,512,128]{2,1,0:T(8,128)(2,1)} %get-tuple-element.57), channel_id=1, source_target_pairs={{0,4},{2,6},{4,0},{6,2},{1,5},{3,7},{5,1},{7,3},{8,12},{10,14},{12... | collective-permute-start | bytes 786440 | tf_op jit(solution)/shard_map/ppermute | solution.py:382
  19.4 25.4 %copy-start.17 = (bf16[544,128]{1,0:T(8,128)(2,1)}, bf16[544,128]{1,0:T(8,128)(2,1)S(1)}, u32[]{:S(2)}) copy-start(bf16[544,128]{1,0:T(8,128)(2,1)S(1)} %collective-permute-done.8.refs_8_) | copy-start | bytes 417796
  19.4 15.0 %collective-permute-start.6 = (bf16[2,512,128]{2,1,0:T(8,128)(2,1)}, bf16[2,512,128]{2,1,0:T(8,128)(2,1)S(1)}, u32[]{:S(2)}, u32[]{:S(2)}) collective-permute-start(bf16[2,512,128]{2,1,0:T(8,128)(2,1)} %get-tuple-element.58), channel_id=1, source_target_pairs={{0,6},{2,4},{4,2},{6,0},{1,7},{3,5},{5,3},{7,1},{8,14},{10,12},{12... | collective-permute-start | bytes 786440 | tf_op jit(solution)/shard_map/ppermute | solution.py:382
  23.2 21.6 %copy-start.18 = (bf16[544,128]{1,0:T(8,128)(2,1)}, bf16[544,128]{1,0:T(8,128)(2,1)S(1)}, u32[]{:S(2)}) copy-start(bf16[544,128]{1,0:T(8,128)(2,1)S(1)} %collective-permute-done.9.refs_9_) | copy-start | bytes 417796
  23.2 12.2 %collective-permute-start.15 = (bf16[4,2,128,128]{3,2,1,0:T(8,128)(2,1)S(1)}, bf16[4,2,128,128]{3,2,1,0:T(8,128)(2,1)S(1)}, u32[]{:S(2)}, u32[]{:S(2)}) collective-permute-start(bf16[4,2,128,128]{3,2,1,0:T(8,128)(2,1)S(1)} %pad_maximum_fusion.refs_1_), channel_id=1, source_target_pairs={{0,8},{8,16},{16,24},{24,0},{1,9},{9,17},{17,25},{25,1},{2,10},{10... | collective-permute-start | bytes 786440 | tf_op jit(solution)/shard_map/ppermute | solution.py:386
  24.8 2.6 %copy-start = (bf16[64,4096]{1,0:T(8,128)(2,1)}, bf16[64,4096]{1,0:T(8,128)(2,1)S(1)}, u32[]{:S(2)}) copy-start(bf16[64,4096]{1,0:T(8,128)(2,1)S(1)} %collective-permute-done.10.source_ref) | copy-start | bytes 1572868
  24.8 20.0 %collective-permute-start.14 = (bf16[4,2,128,128]{3,2,1,0:T(8,128)(2,1)S(1)}, bf16[4,2,128,128]{3,2,1,0:T(8,128)(2,1)S(1)}, u32[]{:S(2)}, u32[]{:S(2)}) collective-permute-start(bf16[4,2,128,128]{3,2,1,0:T(8,128)(2,1)S(1)} %pad_maximum_fusion.refs_1_), channel_id=1, source_target_pairs={{0,16},{8,24},{16,0},{24,8},{1,17},{9,25},{17,1},{25,9},{2,18},{10... | collective-permute-start | bytes 786440 | tf_op jit(solution)/shard_map/ppermute | solution.py:386
  30.4 14.5 %copy-start.10 = (bf16[2,512,128]{2,1,0:T(8,128)(2,1)}, bf16[2,512,128]{2,1,0:T(8,128)(2,1)S(1)}, u32[]{:S(2)}) copy-start(bf16[2,512,128]{2,1,0:T(8,128)(2,1)S(1)} %collective-permute-done.4.refs_3_) | copy-start | bytes 786436
  30.4 14.4 %collective-permute-start.11 = (bf16[544,128]{1,0:T(8,128)(2,1)}, bf16[544,128]{1,0:T(8,128)(2,1)S(1)}, u32[]{:S(2)}, u32[]{:S(2)}) collective-permute-start(bf16[544,128]{1,0:T(8,128)(2,1)} %get-tuple-element.65), channel_id=1, source_target_pairs={{0,2},{2,0},{4,6},{6,4},{1,3},{3,1},{5,7},{7,5},{8,10},{10,8},{12,... | collective-permute-start | bytes 417800 | tf_op jit(solution)/shard_map/ppermute | solution.py:382
  30.5 14.4 %copy-start.11 = (bf16[2,512,128]{2,1,0:T(8,128)(2,1)}, bf16[2,512,128]{2,1,0:T(8,128)(2,1)S(1)}, u32[]{:S(2)}) copy-start(bf16[2,512,128]{2,1,0:T(8,128)(2,1)S(1)} %collective-permute-done.5.refs_4_) | copy-start | bytes 786436
  30.5 14.3 %collective-permute-start.12 = (bf16[544,128]{1,0:T(8,128)(2,1)}, bf16[544,128]{1,0:T(8,128)(2,1)S(1)}, u32[]{:S(2)}, u32[]{:S(2)}) collective-permute-start(bf16[544,128]{1,0:T(8,128)(2,1)} %get-tuple-element.66), channel_id=1, source_target_pairs={{0,4},{2,6},{4,0},{6,2},{1,5},{3,7},{5,1},{7,3},{8,12},{10,14},{12... | collective-permute-start | bytes 417800 | tf_op jit(solution)/shard_map/ppermute | solution.py:382
  34.5 10.4 %copy-start.12 = (bf16[2,512,128]{2,1,0:T(8,128)(2,1)}, bf16[2,512,128]{2,1,0:T(8,128)(2,1)S(1)}, u32[]{:S(2)}) copy-start(bf16[2,512,128]{2,1,0:T(8,128)(2,1)S(1)} %collective-permute-done.6.refs_5_) | copy-start | bytes 786436
  34.5 10.4 %collective-permute-start.13 = (bf16[544,128]{1,0:T(8,128)(2,1)}, bf16[544,128]{1,0:T(8,128)(2,1)S(1)}, u32[]{:S(2)}, u32[]{:S(2)}) collective-permute-start(bf16[544,128]{1,0:T(8,128)(2,1)} %get-tuple-element.67), channel_id=1, source_target_pairs={{0,6},{2,4},{4,2},{6,0},{1,7},{3,5},{5,3},{7,1},{8,14},{10,12},{12... | collective-permute-start | bytes 417800 | tf_op jit(solution)/shard_map/ppermute | solution.py:382
  35.4 9.5 %copy-start.13 = (bf16[4,2,128,128]{3,2,1,0:T(8,128)(2,1)}, bf16[4,2,128,128]{3,2,1,0:T(8,128)(2,1)S(1)}, u32[]{:S(2)}) copy-start(bf16[4,2,128,128]{3,2,1,0:T(8,128)(2,1)S(1)} %collective-permute-done.15.refs_1_) | copy-start | bytes 786436
  35.4 32.0 %collective-permute-start.3 = (bf16[4,2,128,128]{3,2,1,0:T(8,128)(2,1)S(1)}, bf16[4,2,128,128]{3,2,1,0:T(8,128)(2,1)S(1)}, u32[]{:S(2)}, u32[]{:S(2)}) collective-permute-start(bf16[4,2,128,128]{3,2,1,0:T(8,128)(2,1)S(1)} %pad_maximum_fusion.refs_1_), channel_id=1, source_target_pairs={{0,24},{8,0},{16,8},{24,16},{1,25},{9,1},{17,9},{25,17},{2,26},{10... | collective-permute-start | bytes 786440 | tf_op jit(solution)/shard_map/ppermute | solution.py:386
  44.8 0.7 copy-start.14
  44.8 0.7 copy-start.19
  44.8 0.8 copy-start.20
  44.8 0.8 copy-start.21
  60.6 23.5 %collective-permute-start.16 = (bf16[4,2,128,128]{3,2,1,0:T(8,128)(2,1)}, bf16[4,2,128,128]{3,2,1,0:T(8,128)(2,1)S(1)}, u32[]{:S(2)}, u32[]{:S(2)}) collective-permute-start(bf16[4,2,128,128]{3,2,1,0:T(8,128)(2,1)} %get-tuple-element.73), channel_id=1, source_target_pairs={{0,24},{8,0},{16,8},{24,16},{1,25},{9,1},{17,9},{25,17},{2,26},{10... | collective-permute-start | bytes 786440 | tf_op jit(solution)/shard_map/ppermute | solution.py:386
  66.1 18.1 %collective-permute-start.17 = (bf16[4,2,128,128]{3,2,1,0:T(8,128)(2,1)}, bf16[4,2,128,128]{3,2,1,0:T(8,128)(2,1)S(1)}, u32[]{:S(2)}, u32[]{:S(2)}) collective-permute-start(bf16[4,2,128,128]{3,2,1,0:T(8,128)(2,1)} %get-tuple-element.74), channel_id=1, source_target_pairs={{0,16},{8,24},{16,0},{24,8},{1,17},{9,25},{17,1},{25,9},{2,18},{10... | collective-permute-start | bytes 786440 | tf_op jit(solution)/shard_map/ppermute | solution.py:386
  67.4 0.7 copy-start.15
  84.3 8.8 %collective-permute-start.21 = (bf16[4,2,128,128]{3,2,1,0:T(8,128)(2,1)}, bf16[4,2,128,128]{3,2,1,0:T(8,128)(2,1)S(1)}, u32[]{:S(2)}, u32[]{:S(2)}) collective-permute-start(bf16[4,2,128,128]{3,2,1,0:T(8,128)(2,1)} %get-tuple-element.84), channel_id=1, source_target_pairs={{0,8},{8,16},{16,24},{24,0},{1,9},{9,17},{17,25},{25,1},{2,10},{10... | collective-permute-start | bytes 786440 | tf_op jit(solution)/shard_map/ppermute | solution.py:386
  84.3 11.1 %collective-permute-start.18 = (bf16[2,512,128]{2,1,0:T(8,128)(2,1)}, bf16[2,512,128]{2,1,0:T(8,128)(2,1)S(1)}, u32[]{:S(2)}, u32[]{:S(2)}) collective-permute-start(bf16[2,512,128]{2,1,0:T(8,128)(2,1)} %get-tuple-element.78), channel_id=1, source_target_pairs={{0,2},{2,0},{4,6},{6,4},{1,3},{3,1},{5,7},{7,5},{8,10},{10,8},{12,... | collective-permute-start | bytes 786440 | tf_op jit(solution)/shard_map/ppermute | solution.py:382
  84.3 12.5 %collective-permute-start.19 = (bf16[2,512,128]{2,1,0:T(8,128)(2,1)}, bf16[2,512,128]{2,1,0:T(8,128)(2,1)S(1)}, u32[]{:S(2)}, u32[]{:S(2)}) collective-permute-start(bf16[2,512,128]{2,1,0:T(8,128)(2,1)} %get-tuple-element.79), channel_id=1, source_target_pairs={{0,4},{2,6},{4,0},{6,2},{1,5},{3,7},{5,1},{7,3},{8,12},{10,14},{12... | collective-permute-start | bytes 786440 | tf_op jit(solution)/shard_map/ppermute | solution.py:382
  84.9 13.5 %collective-permute-start.20 = (bf16[2,512,128]{2,1,0:T(8,128)(2,1)}, bf16[2,512,128]{2,1,0:T(8,128)(2,1)S(1)}, u32[]{:S(2)}, u32[]{:S(2)}) collective-permute-start(bf16[2,512,128]{2,1,0:T(8,128)(2,1)} %get-tuple-element.80), channel_id=1, source_target_pairs={{0,6},{2,4},{4,2},{6,0},{1,7},{3,5},{5,3},{7,1},{8,14},{10,12},{12... | collective-permute-start | bytes 786440 | tf_op jit(solution)/shard_map/ppermute | solution.py:382
  94.9 4.9 %collective-permute-start.24 = (bf16[2,128,128]{2,1,0:T(8,128)(2,1)S(1)}, bf16[2,128,128]{2,1,0:T(8,128)(2,1)S(1)}, u32[]{:S(2)}, u32[]{:S(2)}) collective-permute-start(bf16[2,128,128]{2,1,0:T(8,128)(2,1)S(1)} %get-tuple-element.85), channel_id=1, source_target_pairs={{0,6},{2,4},{4,2},{6,0},{1,7},{3,5},{5,3},{7,1},{8,14},{10,12},{12... | collective-permute-start | bytes 196616 | tf_op jit(solution)/shard_map/ppermute | solution.py:382
  94.9 6.7 %collective-permute-start.23 = (bf16[2,128,128]{2,1,0:T(8,128)(2,1)S(1)}, bf16[2,128,128]{2,1,0:T(8,128)(2,1)S(1)}, u32[]{:S(2)}, u32[]{:S(2)}) collective-permute-start(bf16[2,128,128]{2,1,0:T(8,128)(2,1)S(1)} %get-tuple-element.86), channel_id=1, source_target_pairs={{0,4},{2,6},{4,0},{6,2},{1,5},{3,7},{5,1},{7,3},{8,12},{10,14},{12... | collective-permute-start | bytes 196616 | tf_op jit(solution)/shard_map/ppermute | solution.py:382
  95.3 6.3 %copy-start.2 = (bf16[2,512,128]{2,1,0:T(8,128)(2,1)}, bf16[2,512,128]{2,1,0:T(8,128)(2,1)S(1)}, u32[]{:S(2)}) copy-start(bf16[2,512,128]{2,1,0:T(8,128)(2,1)S(1)} %collective-permute-done.18.refs_1_) | copy-start | bytes 786436
  95.3 6.3 %collective-permute-start.22 = (bf16[2,128,128]{2,1,0:T(8,128)(2,1)S(1)}, bf16[2,128,128]{2,1,0:T(8,128)(2,1)S(1)}, u32[]{:S(2)}, u32[]{:S(2)}) collective-permute-start(bf16[2,128,128]{2,1,0:T(8,128)(2,1)S(1)} %get-tuple-element.87), channel_id=1, source_target_pairs={{0,2},{2,0},{4,6},{6,4},{1,3},{3,1},{5,7},{7,5},{8,10},{10,8},{12,... | collective-permute-start | bytes 196616 | tf_op jit(solution)/shard_map/ppermute | solution.py:382
  96.8 4.9 %copy-start.3 = (bf16[2,512,128]{2,1,0:T(8,128)(2,1)}, bf16[2,512,128]{2,1,0:T(8,128)(2,1)S(1)}, u32[]{:S(2)}) copy-start(bf16[2,512,128]{2,1,0:T(8,128)(2,1)S(1)} %collective-permute-done.19.refs_2_) | copy-start | bytes 786436
  98.4 3.3 %copy-start.4 = (bf16[2,512,128]{2,1,0:T(8,128)(2,1)}, bf16[2,512,128]{2,1,0:T(8,128)(2,1)S(1)}, u32[]{:S(2)}) copy-start(bf16[2,512,128]{2,1,0:T(8,128)(2,1)S(1)} %collective-permute-done.20.refs_3_) | copy-start | bytes 786436
  99.8 1.9 %copy-start.6 = (bf16[2,128,128]{2,1,0:T(8,128)(2,1)}, bf16[2,128,128]{2,1,0:T(8,128)(2,1)S(1)}, u32[]{:S(2)}) copy-start(bf16[2,128,128]{2,1,0:T(8,128)(2,1)S(1)} %collective-permute-done.24.refs_7_) | copy-start | bytes 196612
  101.6 0.6 copy-start.7
  101.6 0.6 copy-start.8

commit v7 on v6

--- a/solution.py
+++ b/solution.py
@@ -405,23 +405,25 @@
     kv_pieces = results[2 : 2 + members]
     columns = group * block_len
     stack = (BLOCKS_DEV, columns, HEAD_SIZE)
-    q_pieces = call(
-        functools.partial(query_kernel, members, group),
-        "rotate", [place], [cosine, sine, queries], [(stack, bf16)] * members,
-    )
+    cosine_now = cosine
     if members > 1:
         slab = jnp.stack([flipped(kv_pieces[f], f) for f in every])
         grads_other = lax.ppermute(results[-1], "tp", [(0, 1), (1, 0)])
         far = sorted(range(1, layers), key=lambda k: abs(2 * k - layers))
         rounds = [far[: layers // 2], far[layers // 2 :] + [0]]
-        slab, *q_pieces = lax.optimization_barrier((slab, *q_pieces))
+        slab, cosine_now = lax.optimization_barrier((slab, cosine))
         kv = {0: slab}
         for k in far:
             kv[k] = climbed(slab, k)
+        kv[far[0]], grads_other = lax.optimization_barrier((kv[far[0]], grads_other))
     else:
         kv = {0: lax.all_gather(kv_pieces[0], ("z", "y", "core"), axis=0, tiled=False)}
         rounds = [[0]]
         grads_own = lax.all_to_all(out_grad, "tp", split_axis=1, concat_axis=0, tiled=True)
+    q_pieces = call(
+        functools.partial(query_kernel, members, group),
+        "rotate", [place], [cosine_now, sine, queries], [(stack, bf16)] * members,
+    )
     q_in = [flipped(q_pieces[f], f) for f in every]
 
     g_in = []

time: 106 us -> 109 us (1.028)
  waiting for transfers between devices: 25 us -> 36.9 us
  starting transfers between devices: 27.9 us -> 19.8 us
  Pallas kernels: 46.8 us -> 45.1 us
    ppermute x6, starting transfers between devices: 14.5 us -> 5.42 us  [climbed(): return lax.ppermute(array, 'z', route)]
    ppermute x6, waiting for transfers between devices: 12.9 us -> 21.1 us  [climbed(): return lax.ppermute(array, 'z', route)]
    ppermute x18, waiting for transfers between devices: 12 us -> 15.8 us  [flipped(): return lax.ppermute(array, ('y', 'core'), [(i, i ^ flip) for i in range(4)])]
    pallas_call x7, Pallas kernels: 46.8 us -> 45.1 us  [call(): pl.pallas_call(kernel, grid_spec=pltpu.PrefetchScalarGridSpec(num_scalar_...]
  transfers between devices with their start and end apart: 25 -> 25, of which waited for: 8 -> 11; matrix products, arithmetic and copies ran while one was open for 2% -> 2% of each run, Pallas kernels for 38% -> 36%
where the time goes in v7:
time: 109 us
  Pallas kernels  45.1 us (41%)
  waiting for transfers between devices  36.9 us (34%)
  starting transfers between devices  19.8 us (18%)
  local copies, waits for them, and re-layouts  4.63 us (4%)
  other arithmetic  1.2 us (1%)
    pallas_call x7, Pallas kernels, call(): pl.pallas_call(kernel, grid_spec=pltpu.PrefetchScalarGridSpec(num_scalar_...  45.1 us
    ppermute x6, waiting for transfers between devices, climbed(): return lax.ppermute(array, 'z', route)  21.1 us
    ppermute x18, waiting for transfers between devices, flipped(): return lax.ppermute(array, ('y', 'core'), [(i, i ^ flip) for i in range(4)])  15.8 us
    ppermute x18, starting transfers between devices, flipped(): return lax.ppermute(array, ('y', 'core'), [(i, i ^ flip) for i in range(4)])  11.4 us
    ppermute x6, starting transfers between devices, climbed(): return lax.ppermute(array, 'z', route)  5.42 us
    ppermute x1, starting transfers between devices, shards(): grads_other = lax.ppermute(results[-1], 'tp', [(0, 1), (1, 0)])  2.94 us
    unnamed x45, local copies, waits for them, and re-layouts  2.8 us
  transfers between devices with their start and end apart: 25, of which 11 were waited for; matrix products, arithmetic and copies ran while one was open for 2% of the time, Pallas kernels for 36%

profile of v7, /device:TPU:0, one launch (start us, length us, event | category | flops | bytes accessed | tf_op | source)
XLA Modules:
  0.0 108.5 jit_solution(13836664248169409882)
XLA Ops:
  0.6 0.6 stack.34.where_ref
  1.2 3.0 %first.1 = (f32[128,128]{1,0:T(8,128)}, f32[128,128]{1,0:T(8,128)}, bf16[2,128,128]{2,1,0:T(8,128)(2,1)}, bf16[2,128,128]{2,1,0:T(8,128)(2,1)}, bf16[2,128,128]{...) custom-call(s32[5]{0:T(128)} %stack.34.where_ref, s32[3,128]{1,0:T(4,128)} %ids_ref.1, ...), custom_call_target="tpu_custom_call" | custom-call | tf_op jit(solution)/shard_map/first/pallas_call | solution.py:344
  4.3 2.9 %collective-permute-start.11 = (bf16[64,4096]{1,0:T(8,128)(2,1)}, bf16[64,4096]{1,0:T(8,128)(2,1)S(1)}, u32[]{:S(2)}, u32[]{:S(2)}) collective-permute-start(bf16[64,4096]{1,0:T(8,128)(2,1)} %get-tuple-element.59), channel_id=1, source_target_pairs={{0,1},{1,0},{2,3},{3,2},{4,5},{5,4},{6,7},{7,6},{8,9},{9,8},{10,11... | collective-permute-start | bytes 1572872 | tf_op jit(solution)/shard_map/ppermute | solution.py:411
  7.2 1.5 %collective-permute-start.1 = (bf16[2,128,128]{2,1,0:T(8,128)(2,1)}, bf16[2,128,128]{2,1,0:T(8,128)(2,1)S(1)}, u32[]{:S(2)}, u32[]{:S(2)}) collective-permute-start(bf16[2,128,128]{2,1,0:T(8,128)(2,1)} %get-tuple-element.47), channel_id=1, source_target_pairs={{0,4},{2,6},{4,0},{6,2},{1,5},{3,7},{5,1},{7,3},{8,12},{10,14},{12... | collective-permute-start | bytes 196616 | tf_op jit(solution)/shard_map/ppermute | solution.py:382
  8.7 0.3 collective-permute-start.2
  9.1 3.0 %delta.2 = (bf16[544,128]{1,0:T(8,128)(2,1)}, bf16[544,128]{1,0:T(8,128)(2,1)}, bf16[544,128]{1,0:T(8,128)(2,1)}, bf16[544,128]{1,0:T(8,128)(2,1)}) custom-call(s32[5]{0:T(128)} %stack.34.where_ref, bf16[128,4096]{1,0:T(8,128)(2,1)} %a_ref.3, f32[32,128]{1,0:T(8,128)} %l_ref.3, bf16[64,8192]{1,0:T(8,128)(2,1)} %source_ref.1), custom_call_target="tpu_custom_call" | custom-call | tf_op jit(solution)/shard_map/delta/pallas_call | solution.py:344
  12.1 0.3 collective-permute-start.7
  12.4 0.6 collective-permute-done.2
  13.1 2.7 %collective-permute-start.10 = (bf16[4,2,128,128]{3,2,1,0:T(8,128)(2,1)S(1)}, bf16[4,2,128,128]{3,2,1,0:T(8,128)(2,1)S(1)}, u32[]{:S(2)}, u32[]{:S(2)}) collective-permute-start(bf16[4,2,128,128]{3,2,1,0:T(8,128)(2,1)S(1)} %pad_maximum_fusion.refs_1_), channel_id=1, source_target_pairs={{0,16},{8,24},{16,0},{24,8},{1,17},{9,25},{17,1},{25,9},{2,18},{10... | collective-permute-start | bytes 786440 | tf_op jit(solution)/shard_map/ppermute | solution.py:386
  15.7 1.4 %collective-permute-start.8 = (bf16[544,128]{1,0:T(8,128)(2,1)}, bf16[544,128]{1,0:T(8,128)(2,1)S(1)}, u32[]{:S(2)}, u32[]{:S(2)}) collective-permute-start(bf16[544,128]{1,0:T(8,128)(2,1)} %get-tuple-element.57), channel_id=1, source_target_pairs={{0,4},{2,6},{4,0},{6,2},{1,5},{3,7},{5,1},{7,3},{8,12},{10,14},{12... | collective-permute-start | bytes 417800 | tf_op jit(solution)/shard_map/ppermute | solution.py:382
  17.2 1.6 %collective-permute-start.15 = (bf16[4,2,128,128]{3,2,1,0:T(8,128)(2,1)S(1)}, bf16[4,2,128,128]{3,2,1,0:T(8,128)(2,1)S(1)}, u32[]{:S(2)}, u32[]{:S(2)}) collective-permute-start(bf16[4,2,128,128]{3,2,1,0:T(8,128)(2,1)S(1)} %pad_maximum_fusion.refs_1_), channel_id=1, source_target_pairs={{0,8},{8,16},{16,24},{24,0},{1,9},{9,17},{17,25},{25,1},{2,10},{10... | collective-permute-start | bytes 786440 | tf_op jit(solution)/shard_map/ppermute | solution.py:386
  18.7 3.3 %rotate.1 = (bf16[2,512,128]{2,1,0:T(8,128)(2,1)}, bf16[2,512,128]{2,1,0:T(8,128)(2,1)}, bf16[2,512,128]{2,1,0:T(8,128)(2,1)}, bf16[2,512,128]{2,1,0:T(8,128)(2,1)}) custom-call(s32[5]{0:T(128)} %stack.34.where_ref, f32[128,128]{1,0:T(8,128)} %get-tuple-element.50.cos_ref, f32[128,128]{1,0:T(8,128)} %get-tuple-element.44.sin_ref, bf16[128,4096]{1,0:T(8,128)(2,1)} %q_ref.1), custom_call_target="tpu_custom_call" | custom-call | tf_op jit(solution)/shard_map/rotate/pallas_call | solution.py:344
  22.0 0.0 collective-permute-start.4
  22.1 0.7 collective-permute-start.9
  22.8 11.1 %collective-permute-done.10.refs_0_ = bf16[4,2,128,128]{3,2,1,0:T(8,128)(2,1)S(1)} collective-permute-done((bf16[4,2,128,128]{3,2,1,0:T(8,128)(2,1)S(1)}, bf16[4,2,128,128]{3,2,1,0:T(8,128)(2,1)S(1)}, u32[]{:S(2)}, u32[]{:S(2)}) %collective-permute-start.10) | collective-permute-done | bytes 262176 | tf_op jit(solution)/shard_map/ppermute | solution.py:386
  33.9 1.5 %collective-permute-start.5 = (bf16[2,512,128]{2,1,0:T(8,128)(2,1)}, bf16[2,512,128]{2,1,0:T(8,128)(2,1)S(1)}, u32[]{:S(2)}, u32[]{:S(2)}) collective-permute-start(bf16[2,512,128]{2,1,0:T(8,128)(2,1)} %get-tuple-element.53), channel_id=1, source_target_pairs={{0,4},{2,6},{4,0},{6,2},{1,5},{3,7},{5,1},{7,3},{8,12},{10,14},{12... | collective-permute-start | bytes 786440 | tf_op jit(solution)/shard_map/ppermute | solution.py:382
  35.4 0.8 copy-done
  36.2 3.0 %delta.3 = (bf16[544,128]{1,0:T(8,128)(2,1)}, bf16[544,128]{1,0:T(8,128)(2,1)}, bf16[544,128]{1,0:T(8,128)(2,1)}, bf16[544,128]{1,0:T(8,128)(2,1)}) custom-call(s32[5]{0:T(128)} %stack.34.where_ref, bf16[128,4096]{1,0:T(8,128)(2,1)} %a_ref.3, f32[32,128]{1,0:T(8,128)} %l_ref.3, bf16[64,4096]{1,0:T(8,128)(2,1)} %copy-done), custom_call_target="tpu_custom_call" | custom-call | tf_op jit(solution)/shard_map/delta/pallas_call | solution.py:344
  39.2 0.1 collective-permute-start.12
  39.3 1.3 %collective-permute-start.13 = (bf16[544,128]{1,0:T(8,128)(2,1)}, bf16[544,128]{1,0:T(8,128)(2,1)S(1)}, u32[]{:S(2)}, u32[]{:S(2)}) collective-permute-start(bf16[544,128]{1,0:T(8,128)(2,1)} %get-tuple-element.63), channel_id=1, source_target_pairs={{0,4},{2,6},{4,0},{6,2},{1,5},{3,7},{5,1},{7,3},{8,12},{10,14},{12... | collective-permute-start | bytes 417800 | tf_op jit(solution)/shard_map/ppermute | solution.py:382
  40.6 0.5 collective-permute-start.14
  41.2 0.1 copy.13
  41.3 0.6 reshape.14.span_ref
  41.9 1.5 %collective-permute-done.5.refs_4_ = bf16[2,512,128]{2,1,0:T(8,128)(2,1)S(1)} collective-permute-done((bf16[2,512,128]{2,1,0:T(8,128)(2,1)}, bf16[2,512,128]{2,1,0:T(8,128)(2,1)S(1)}, u32[]{:S(2)}, u32[]{:S(2)}) %collective-permute-start.5) | collective-permute-done | bytes 262176 | tf_op jit(solution)/shard_map/ppermute | solution.py:382
  43.3 4.7 %collective-permute-done.6.refs_5_ = bf16[2,512,128]{2,1,0:T(8,128)(2,1)S(1)} collective-permute-done((bf16[2,512,128]{2,1,0:T(8,128)(2,1)}, bf16[2,512,128]{2,1,0:T(8,128)(2,1)S(1)}, u32[]{:S(2)}, u32[]{:S(2)}) %collective-permute-start.6) | collective-permute-done | bytes 262176 | tf_op jit(solution)/shard_map/ppermute | solution.py:382
  48.1 3.8 %collective-permute-done.13.refs_12_ = bf16[544,128]{1,0:T(8,128)(2,1)S(1)} collective-permute-done((bf16[544,128]{1,0:T(8,128)(2,1)}, bf16[544,128]{1,0:T(8,128)(2,1)S(1)}, u32[]{:S(2)}, u32[]{:S(2)}) %collective-permute-start.13) | collective-permute-done | bytes 139296 | tf_op jit(solution)/shard_map/ppermute | solution.py:382
  51.9 0.8 collective-permute-done.14.refs_13_
  52.9 0.6 copy-done.21
  53.4 13.9 %attend.2 = (f32[8,128,512]{2,1,0:T(8,128)}, bf16[4,2,128,128]{3,2,1,0:T(8,128)(2,1)}, bf16[4,2,128,128]{3,2,1,0:T(8,128)(2,1)}) custom-call(s32[5]{0:T(128)} %stack.34.where_ref, s32[32]{0:T(128)} %map_ref.3, s32[8]{0:T(128)} %reshape.14.span_ref, bf16[4,2,128,128]{3,2,1,0:T(8,128)(2,1)} %copy-done.11, bf16[4,2,128,128]{3,2,1,0:T(8,128)(2,1)} %copy-done.12, ...), custom_call_target="tpu_custom_call" | custom-call | flops 3221225472 | bytes 6291456 | tf_op jit(solution)/shard_map/attend/pallas_call | solution.py:344
  67.4 0.0 collective-permute-start.16
  67.4 0.1 collective-permute-start.17
  67.5 0.7 copy-done.15
  68.2 15.4 %attend.3 = (bf16[2,512,128]{2,1,0:T(8,128)(2,1)}, bf16[2,512,128]{2,1,0:T(8,128)(2,1)}, bf16[2,512,128]{2,1,0:T(8,128)(2,1)}, bf16[2,512,128]{2,1,0:T(8,128)(2,...) custom-call(s32[5]{0:T(128)} %stack.34.where_ref, s32[32]{0:T(128)} %map_ref.3, s32[8]{0:T(128)} %reshape.14.span_ref, ...), custom_call_target="tpu_custom_call" | custom-call | flops 3221225472 | bytes 6291456 | tf_op jit(solution)/shard_map/attend/pallas_call | solution.py:344
  83.6 2.4 %collective-permute-done.17 = bf16[4,2,128,128]{3,2,1,0:T(8,128)(2,1)S(1)} collective-permute-done((bf16[4,2,128,128]{3,2,1,0:T(8,128)(2,1)}, bf16[4,2,128,128]{3,2,1,0:T(8,128)(2,1)S(1)}, u32[]{:S(2)}, u32[]{:S(2)}) %collective-permute-start.17) | collective-permute-done | bytes 262176 | tf_op jit(solution)/shard_map/ppermute | solution.py:386
  86.0 1.1 collective-permute-start.21
  87.0 1.2 %collective-permute-start.19 = (bf16[2,512,128]{2,1,0:T(8,128)(2,1)}, bf16[2,512,128]{2,1,0:T(8,128)(2,1)S(1)}, u32[]{:S(2)}, u32[]{:S(2)}) collective-permute-start(bf16[2,512,128]{2,1,0:T(8,128)(2,1)} %get-tuple-element.77), channel_id=1, source_target_pairs={{0,4},{2,6},{4,0},{6,2},{1,5},{3,7},{5,1},{7,3},{8,12},{10,14},{12... | collective-permute-start | bytes 786440 | tf_op jit(solution)/shard_map/ppermute | solution.py:382
  88.2 0.7 collective-permute-start.20
  88.9 7.6 %collective-permute-done.21 = bf16[4,2,128,128]{3,2,1,0:T(8,128)(2,1)S(1)} collective-permute-done((bf16[4,2,128,128]{3,2,1,0:T(8,128)(2,1)}, bf16[4,2,128,128]{3,2,1,0:T(8,128)(2,1)S(1)}, u32[]{:S(2)}, u32[]{:S(2)}) %collective-permute-start.21) | collective-permute-done | bytes 262176 | tf_op jit(solution)/shard_map/ppermute | solution.py:386
  96.5 1.2 %add_convert_fusion = bf16[4,2,128,128]{3,2,1,0:T(8,128)(2,1)S(1)} fusion(bf16[4,2,128,128]{3,2,1,0:T(8,128)(2,1)S(1)} %collective-permute-done.21, bf16[4,2,128,128]{3,2,1,0:T(8,128)(2,1)S(1)} %collective-permute-done.16, f32[4,2,128,128]{3,2,1,0:T(8,128)} %get-tuple-element.79, bf16[4,2,128,128]{3,2,1,0:T(8,128)(2,1)S(1)} %collective-permute-done.17), kind=kLoop, calls=%fused_computation | loop fusion | flops 917504 | bytes 1572864 | tf_op jit(solution)/shard_map/convert.3
  97.7 0.6 slice_bitcast_fusion
  98.3 0.4 collective-permute-start.24
  98.7 0.8 collective-permute-start.23
  99.6 0.6 collective-permute-start.22
  100.2 1.0 collective-permute-done.20.refs_3_
  101.2 1.6 %collective-permute-done.24.refs_7_ = bf16[2,128,128]{2,1,0:T(8,128)(2,1)S(1)} collective-permute-done((bf16[2,128,128]{2,1,0:T(8,128)(2,1)S(1)}, bf16[2,128,128]{2,1,0:T(8,128)(2,1)S(1)}, u32[]{:S(2)}, u32[]{:S(2)}) %collective-permute-start.24) | collective-permute-done | bytes 65568 | tf_op jit(solution)/shard_map/ppermute | solution.py:382
  102.8 1.6 %collective-permute-done.23.refs_6_ = bf16[2,128,128]{2,1,0:T(8,128)(2,1)S(1)} collective-permute-done((bf16[2,128,128]{2,1,0:T(8,128)(2,1)S(1)}, bf16[2,128,128]{2,1,0:T(8,128)(2,1)S(1)}, u32[]{:S(2)}, u32[]{:S(2)}) %collective-permute-start.23) | collective-permute-done | bytes 65568 | tf_op jit(solution)/shard_map/ppermute | solution.py:382
  104.4 0.6 copy-done.7
  105.0 3.5 %last.1 = (bf16[128,4096]{1,0:T(8,128)(2,1)}, bf16[128,512]{1,0:T(8,128)(2,1)}, bf16[128,512]{1,0:T(8,128)(2,1)}) custom-call(s32[5]{0:T(128)} %stack.34.where_ref, f32[128,128]{1,0:T(8,128)} %get-tuple-element.50.cos_ref, f32[128,128]{1,0:T(8,128)} %get-tuple-element.44.sin_ref, bf16[2,512,128]{2,1,0:T(8,128)(2,1)} %get-tuple-element.75.refs_0_, ...), custom_call_target="tpu_custom_call" | custom-call | tf_op jit(solution)/shard_map/last/pallas_call | solution.py:344
  (59 shorter events, 0.2 us)
Async XLA Ops:
  4.3 8.7 %copy-start.5 = (bf16[2,128,128]{2,1,0:T(8,128)(2,1)S(1)}, bf16[2,128,128]{2,1,0:T(8,128)(2,1)}, u32[]{:S(2)}) copy-start(bf16[2,128,128]{2,1,0:T(8,128)(2,1)} %get-tuple-element.45) | copy-start | bytes 196612
  4.3 31.2 %collective-permute-start.11 = (bf16[64,4096]{1,0:T(8,128)(2,1)}, bf16[64,4096]{1,0:T(8,128)(2,1)S(1)}, u32[]{:S(2)}, u32[]{:S(2)}) collective-permute-start(bf16[64,4096]{1,0:T(8,128)(2,1)} %get-tuple-element.59), channel_id=1, source_target_pairs={{0,1},{1,0},{2,3},{3,2},{4,5},{5,4},{6,7},{7,6},{8,9},{9,8},{10,11... | collective-permute-start | bytes 1572872 | tf_op jit(solution)/shard_map/ppermute | solution.py:411
  7.2 5.2 %collective-permute-start = (bf16[2,128,128]{2,1,0:T(8,128)(2,1)}, bf16[2,128,128]{2,1,0:T(8,128)(2,1)S(1)}, u32[]{:S(2)}, u32[]{:S(2)}) collective-permute-start(bf16[2,128,128]{2,1,0:T(8,128)(2,1)} %get-tuple-element.46), channel_id=1, source_target_pairs={{0,2},{2,0},{4,6},{6,4},{1,3},{3,1},{5,7},{7,5},{8,10},{10,8},{12,... | collective-permute-start | bytes 196616 | tf_op jit(solution)/shard_map/ppermute | solution.py:382
  7.2 5.2 %collective-permute-start.1 = (bf16[2,128,128]{2,1,0:T(8,128)(2,1)}, bf16[2,128,128]{2,1,0:T(8,128)(2,1)S(1)}, u32[]{:S(2)}, u32[]{:S(2)}) collective-permute-start(bf16[2,128,128]{2,1,0:T(8,128)(2,1)} %get-tuple-element.47), channel_id=1, source_target_pairs={{0,4},{2,6},{4,0},{6,2},{1,5},{3,7},{5,1},{7,3},{8,12},{10,14},{12... | collective-permute-start | bytes 196616 | tf_op jit(solution)/shard_map/ppermute | solution.py:382
  8.7 4.3 %collective-permute-start.2 = (bf16[2,128,128]{2,1,0:T(8,128)(2,1)}, bf16[2,128,128]{2,1,0:T(8,128)(2,1)S(1)}, u32[]{:S(2)}, u32[]{:S(2)}) collective-permute-start(bf16[2,128,128]{2,1,0:T(8,128)(2,1)} %get-tuple-element.48), channel_id=1, source_target_pairs={{0,6},{2,4},{4,2},{6,0},{1,7},{3,5},{5,3},{7,1},{8,14},{10,12},{12... | collective-permute-start | bytes 196616 | tf_op jit(solution)/shard_map/ppermute | solution.py:382
  12.1 29.1 %copy-start.9 = (s32[4,2]{0,1:T(2,128)S(1)}, s32[4,2]{0,1:T(2,128)}, u32[]{:S(2)}) copy-start(s32[4,2]{0,1:T(2,128)} %param.17) | copy-start | bytes 100
  12.1 10.0 %collective-permute-start.7 = (bf16[544,128]{1,0:T(8,128)(2,1)}, bf16[544,128]{1,0:T(8,128)(2,1)S(1)}, u32[]{:S(2)}, u32[]{:S(2)}) collective-permute-start(bf16[544,128]{1,0:T(8,128)(2,1)} %get-tuple-element.56), channel_id=1, source_target_pairs={{0,2},{2,0},{4,6},{6,4},{1,3},{3,1},{5,7},{7,5},{8,10},{10,8},{12,... | collective-permute-start | bytes 417800 | tf_op jit(solution)/shard_map/ppermute | solution.py:382
  13.0 54.3 %copy-start.1 = (bf16[4,2,128,128]{3,2,1,0:T(8,128)(2,1)}, bf16[4,2,128,128]{3,2,1,0:T(8,128)(2,1)S(1)}, u32[]{:S(2)}) copy-start(bf16[4,2,128,128]{3,2,1,0:T(8,128)(2,1)S(1)} %pad_maximum_fusion.refs_1_) | copy-start | bytes 786436
  13.1 20.8 %collective-permute-start.10 = (bf16[4,2,128,128]{3,2,1,0:T(8,128)(2,1)S(1)}, bf16[4,2,128,128]{3,2,1,0:T(8,128)(2,1)S(1)}, u32[]{:S(2)}, u32[]{:S(2)}) collective-permute-start(bf16[4,2,128,128]{3,2,1,0:T(8,128)(2,1)S(1)} %pad_maximum_fusion.refs_1_), channel_id=1, source_target_pairs={{0,16},{8,24},{16,0},{24,8},{1,17},{9,25},{17,1},{25,9},{2,18},{10... | collective-permute-start | bytes 786440 | tf_op jit(solution)/shard_map/ppermute | solution.py:386
  15.7 6.4 %collective-permute-start.8 = (bf16[544,128]{1,0:T(8,128)(2,1)}, bf16[544,128]{1,0:T(8,128)(2,1)S(1)}, u32[]{:S(2)}, u32[]{:S(2)}) collective-permute-start(bf16[544,128]{1,0:T(8,128)(2,1)} %get-tuple-element.57), channel_id=1, source_target_pairs={{0,4},{2,6},{4,0},{6,2},{1,5},{3,7},{5,1},{7,3},{8,12},{10,14},{12... | collective-permute-start | bytes 417800 | tf_op jit(solution)/shard_map/ppermute | solution.py:382
  17.2 22.1 %collective-permute-start.15 = (bf16[4,2,128,128]{3,2,1,0:T(8,128)(2,1)S(1)}, bf16[4,2,128,128]{3,2,1,0:T(8,128)(2,1)S(1)}, u32[]{:S(2)}, u32[]{:S(2)}) collective-permute-start(bf16[4,2,128,128]{3,2,1,0:T(8,128)(2,1)S(1)} %pad_maximum_fusion.refs_1_), channel_id=1, source_target_pairs={{0,8},{8,16},{16,24},{24,0},{1,9},{9,17},{17,25},{25,1},{2,10},{10... | collective-permute-start | bytes 786440 | tf_op jit(solution)/shard_map/ppermute | solution.py:386
  22.0 30.8 %copy-start.16 = (bf16[544,128]{1,0:T(8,128)(2,1)}, bf16[544,128]{1,0:T(8,128)(2,1)S(1)}, u32[]{:S(2)}) copy-start(bf16[544,128]{1,0:T(8,128)(2,1)S(1)} %collective-permute-done.7.refs_7_) | copy-start | bytes 417796
  22.0 18.6 %collective-permute-start.4 = (bf16[2,512,128]{2,1,0:T(8,128)(2,1)}, bf16[2,512,128]{2,1,0:T(8,128)(2,1)S(1)}, u32[]{:S(2)}, u32[]{:S(2)}) collective-permute-start(bf16[2,512,128]{2,1,0:T(8,128)(2,1)} %get-tuple-element.52), channel_id=1, source_target_pairs={{0,2},{2,0},{4,6},{6,4},{1,3},{3,1},{5,7},{7,5},{8,10},{10,8},{12,... | collective-permute-start | bytes 786440 | tf_op jit(solution)/shard_map/ppermute | solution.py:382
  22.1 30.7 %copy-start.17 = (bf16[544,128]{1,0:T(8,128)(2,1)}, bf16[544,128]{1,0:T(8,128)(2,1)S(1)}, u32[]{:S(2)}) copy-start(bf16[544,128]{1,0:T(8,128)(2,1)S(1)} %collective-permute-done.8.refs_8_) | copy-start | bytes 417796
  22.1 17.1 %collective-permute-start.9 = (bf16[544,128]{1,0:T(8,128)(2,1)}, bf16[544,128]{1,0:T(8,128)(2,1)S(1)}, u32[]{:S(2)}, u32[]{:S(2)}) collective-permute-start(bf16[544,128]{1,0:T(8,128)(2,1)} %get-tuple-element.58), channel_id=1, source_target_pairs={{0,6},{2,4},{4,2},{6,0},{1,7},{3,5},{5,3},{7,1},{8,14},{10,12},{12... | collective-permute-start | bytes 417800 | tf_op jit(solution)/shard_map/ppermute | solution.py:382
  33.9 18.9 %copy-start.11 = (bf16[4,2,128,128]{3,2,1,0:T(8,128)(2,1)}, bf16[4,2,128,128]{3,2,1,0:T(8,128)(2,1)S(1)}, u32[]{:S(2)}) copy-start(bf16[4,2,128,128]{3,2,1,0:T(8,128)(2,1)S(1)} %collective-permute-done.10.refs_0_) | copy-start | bytes 786436
  33.9 9.4 %collective-permute-start.5 = (bf16[2,512,128]{2,1,0:T(8,128)(2,1)}, bf16[2,512,128]{2,1,0:T(8,128)(2,1)S(1)}, u32[]{:S(2)}, u32[]{:S(2)}) collective-permute-start(bf16[2,512,128]{2,1,0:T(8,128)(2,1)} %get-tuple-element.53), channel_id=1, source_target_pairs={{0,4},{2,6},{4,0},{6,2},{1,5},{3,7},{5,1},{7,3},{8,12},{10,14},{12... | collective-permute-start | bytes 786440 | tf_op jit(solution)/shard_map/ppermute | solution.py:382
  35.4 0.8 copy-start
  35.4 12.7 %collective-permute-start.6 = (bf16[2,512,128]{2,1,0:T(8,128)(2,1)}, bf16[2,512,128]{2,1,0:T(8,128)(2,1)S(1)}, u32[]{:S(2)}, u32[]{:S(2)}) collective-permute-start(bf16[2,512,128]{2,1,0:T(8,128)(2,1)} %get-tuple-element.54), channel_id=1, source_target_pairs={{0,6},{2,4},{4,2},{6,0},{1,7},{3,5},{5,3},{7,1},{8,14},{10,12},{12... | collective-permute-start | bytes 786440 | tf_op jit(solution)/shard_map/ppermute | solution.py:382
  39.2 13.6 %copy-start.18 = (bf16[544,128]{1,0:T(8,128)(2,1)}, bf16[544,128]{1,0:T(8,128)(2,1)S(1)}, u32[]{:S(2)}) copy-start(bf16[544,128]{1,0:T(8,128)(2,1)S(1)} %collective-permute-done.9.refs_9_) | copy-start | bytes 417796
  39.2 8.9 %collective-permute-start.12 = (bf16[544,128]{1,0:T(8,128)(2,1)}, bf16[544,128]{1,0:T(8,128)(2,1)S(1)}, u32[]{:S(2)}, u32[]{:S(2)}) collective-permute-start(bf16[544,128]{1,0:T(8,128)(2,1)} %get-tuple-element.62), channel_id=1, source_target_pairs={{0,2},{2,0},{4,6},{6,4},{1,3},{3,1},{5,7},{7,5},{8,10},{10,8},{12,... | collective-permute-start | bytes 417800 | tf_op jit(solution)/shard_map/ppermute | solution.py:382
  39.3 13.5 %copy-start.12 = (bf16[4,2,128,128]{3,2,1,0:T(8,128)(2,1)}, bf16[4,2,128,128]{3,2,1,0:T(8,128)(2,1)S(1)}, u32[]{:S(2)}) copy-start(bf16[4,2,128,128]{3,2,1,0:T(8,128)(2,1)S(1)} %collective-permute-done.15.refs_1_) | copy-start | bytes 786436
  39.3 12.6 %collective-permute-start.13 = (bf16[544,128]{1,0:T(8,128)(2,1)}, bf16[544,128]{1,0:T(8,128)(2,1)S(1)}, u32[]{:S(2)}, u32[]{:S(2)}) collective-permute-start(bf16[544,128]{1,0:T(8,128)(2,1)} %get-tuple-element.63), channel_id=1, source_target_pairs={{0,4},{2,6},{4,0},{6,2},{1,5},{3,7},{5,1},{7,3},{8,12},{10,14},{12... | collective-permute-start | bytes 417800 | tf_op jit(solution)/shard_map/ppermute | solution.py:382
  40.6 12.2 %copy-start.10 = (bf16[2,512,128]{2,1,0:T(8,128)(2,1)}, bf16[2,512,128]{2,1,0:T(8,128)(2,1)S(1)}, u32[]{:S(2)}) copy-start(bf16[2,512,128]{2,1,0:T(8,128)(2,1)S(1)} %collective-permute-done.4.refs_3_) | copy-start | bytes 786436
  40.6 12.1 %collective-permute-start.14 = (bf16[544,128]{1,0:T(8,128)(2,1)}, bf16[544,128]{1,0:T(8,128)(2,1)S(1)}, u32[]{:S(2)}, u32[]{:S(2)}) collective-permute-start(bf16[544,128]{1,0:T(8,128)(2,1)} %get-tuple-element.64), channel_id=1, source_target_pairs={{0,6},{2,4},{4,2},{6,0},{1,7},{3,5},{5,3},{7,1},{8,14},{10,12},{12... | collective-permute-start | bytes 417800 | tf_op jit(solution)/shard_map/ppermute | solution.py:382
  43.3 9.5 %copy-start.13 = (bf16[2,512,128]{2,1,0:T(8,128)(2,1)}, bf16[2,512,128]{2,1,0:T(8,128)(2,1)S(1)}, u32[]{:S(2)}) copy-start(bf16[2,512,128]{2,1,0:T(8,128)(2,1)S(1)} %collective-permute-done.5.refs_4_) | copy-start | bytes 786436
  43.3 24.2 %collective-permute-start.3 = (bf16[4,2,128,128]{3,2,1,0:T(8,128)(2,1)S(1)}, bf16[4,2,128,128]{3,2,1,0:T(8,128)(2,1)S(1)}, u32[]{:S(2)}, u32[]{:S(2)}) collective-permute-start(bf16[4,2,128,128]{3,2,1,0:T(8,128)(2,1)S(1)} %pad_maximum_fusion.refs_1_), channel_id=1, source_target_pairs={{0,24},{8,0},{16,8},{24,16},{1,25},{9,1},{17,9},{25,17},{2,26},{10... | collective-permute-start | bytes 786440 | tf_op jit(solution)/shard_map/ppermute | solution.py:386
  48.1 4.8 %copy-start.14 = (bf16[2,512,128]{2,1,0:T(8,128)(2,1)}, bf16[2,512,128]{2,1,0:T(8,128)(2,1)S(1)}, u32[]{:S(2)}) copy-start(bf16[2,512,128]{2,1,0:T(8,128)(2,1)S(1)} %collective-permute-done.6.refs_5_) | copy-start | bytes 786436
  48.1 4.8 %copy-start.19 = (bf16[544,128]{1,0:T(8,128)(2,1)}, bf16[544,128]{1,0:T(8,128)(2,1)S(1)}, u32[]{:S(2)}) copy-start(bf16[544,128]{1,0:T(8,128)(2,1)S(1)} %collective-permute-done.12.refs_11_) | copy-start | bytes 417796
  51.9 0.9 copy-start.20
  52.8 0.7 copy-start.21
  67.4 16.2 %collective-permute-start.16 = (bf16[4,2,128,128]{3,2,1,0:T(8,128)(2,1)}, bf16[4,2,128,128]{3,2,1,0:T(8,128)(2,1)S(1)}, u32[]{:S(2)}, u32[]{:S(2)}) collective-permute-start(bf16[4,2,128,128]{3,2,1,0:T(8,128)(2,1)} %get-tuple-element.71), channel_id=1, source_target_pairs={{0,24},{8,0},{16,8},{24,16},{1,25},{9,1},{17,9},{25,17},{2,26},{10... | collective-permute-start | bytes 786440 | tf_op jit(solution)/shard_map/ppermute | solution.py:386
  67.4 18.6 %collective-permute-start.17 = (bf16[4,2,128,128]{3,2,1,0:T(8,128)(2,1)}, bf16[4,2,128,128]{3,2,1,0:T(8,128)(2,1)S(1)}, u32[]{:S(2)}, u32[]{:S(2)}) collective-permute-start(bf16[4,2,128,128]{3,2,1,0:T(8,128)(2,1)} %get-tuple-element.72), channel_id=1, source_target_pairs={{0,16},{8,24},{16,0},{24,8},{1,17},{9,25},{17,1},{25,9},{2,18},{10... | collective-permute-start | bytes 786440 | tf_op jit(solution)/shard_map/ppermute | solution.py:386
  67.5 0.7 copy-start.15
  86.0 10.5 %collective-permute-start.21 = (bf16[4,2,128,128]{3,2,1,0:T(8,128)(2,1)}, bf16[4,2,128,128]{3,2,1,0:T(8,128)(2,1)S(1)}, u32[]{:S(2)}, u32[]{:S(2)}) collective-permute-start(bf16[4,2,128,128]{3,2,1,0:T(8,128)(2,1)} %get-tuple-element.82), channel_id=1, source_target_pairs={{0,8},{8,16},{16,24},{24,0},{1,9},{9,17},{17,25},{25,1},{2,10},{10... | collective-permute-start | bytes 786440 | tf_op jit(solution)/shard_map/ppermute | solution.py:386
  87.0 12.5 %collective-permute-start.18 = (bf16[2,512,128]{2,1,0:T(8,128)(2,1)}, bf16[2,512,128]{2,1,0:T(8,128)(2,1)S(1)}, u32[]{:S(2)}, u32[]{:S(2)}) collective-permute-start(bf16[2,512,128]{2,1,0:T(8,128)(2,1)} %get-tuple-element.76), channel_id=1, source_target_pairs={{0,2},{2,0},{4,6},{6,4},{1,3},{3,1},{5,7},{7,5},{8,10},{10,8},{12,... | collective-permute-start | bytes 786440 | tf_op jit(solution)/shard_map/ppermute | solution.py:382
  87.0 13.1 %collective-permute-start.19 = (bf16[2,512,128]{2,1,0:T(8,128)(2,1)}, bf16[2,512,128]{2,1,0:T(8,128)(2,1)S(1)}, u32[]{:S(2)}, u32[]{:S(2)}) collective-permute-start(bf16[2,512,128]{2,1,0:T(8,128)(2,1)} %get-tuple-element.77), channel_id=1, source_target_pairs={{0,4},{2,6},{4,0},{6,2},{1,5},{3,7},{5,1},{7,3},{8,12},{10,14},{12... | collective-permute-start | bytes 786440 | tf_op jit(solution)/shard_map/ppermute | solution.py:382
  88.2 13.0 %collective-permute-start.20 = (bf16[2,512,128]{2,1,0:T(8,128)(2,1)}, bf16[2,512,128]{2,1,0:T(8,128)(2,1)S(1)}, u32[]{:S(2)}, u32[]{:S(2)}) collective-permute-start(bf16[2,512,128]{2,1,0:T(8,128)(2,1)} %get-tuple-element.78), channel_id=1, source_target_pairs={{0,6},{2,4},{4,2},{6,0},{1,7},{3,5},{5,3},{7,1},{8,14},{10,12},{12... | collective-permute-start | bytes 786440 | tf_op jit(solution)/shard_map/ppermute | solution.py:382
  98.3 4.5 %collective-permute-start.24 = (bf16[2,128,128]{2,1,0:T(8,128)(2,1)S(1)}, bf16[2,128,128]{2,1,0:T(8,128)(2,1)S(1)}, u32[]{:S(2)}, u32[]{:S(2)}) collective-permute-start(bf16[2,128,128]{2,1,0:T(8,128)(2,1)S(1)} %get-tuple-element.83), channel_id=1, source_target_pairs={{0,6},{2,4},{4,2},{6,0},{1,7},{3,5},{5,3},{7,1},{8,14},{10,12},{12... | collective-permute-start | bytes 196616 | tf_op jit(solution)/shard_map/ppermute | solution.py:382
  98.7 5.7 %collective-permute-start.23 = (bf16[2,128,128]{2,1,0:T(8,128)(2,1)S(1)}, bf16[2,128,128]{2,1,0:T(8,128)(2,1)S(1)}, u32[]{:S(2)}, u32[]{:S(2)}) collective-permute-start(bf16[2,128,128]{2,1,0:T(8,128)(2,1)S(1)} %get-tuple-element.84), channel_id=1, source_target_pairs={{0,4},{2,6},{4,0},{6,2},{1,5},{3,7},{5,1},{7,3},{8,12},{10,14},{12... | collective-permute-start | bytes 196616 | tf_op jit(solution)/shard_map/ppermute | solution.py:382
  99.6 4.8 %copy-start.2 = (bf16[2,512,128]{2,1,0:T(8,128)(2,1)}, bf16[2,512,128]{2,1,0:T(8,128)(2,1)S(1)}, u32[]{:S(2)}) copy-start(bf16[2,512,128]{2,1,0:T(8,128)(2,1)S(1)} %collective-permute-done.18.refs_1_) | copy-start | bytes 786436
  99.6 4.8 %collective-permute-start.22 = (bf16[2,128,128]{2,1,0:T(8,128)(2,1)S(1)}, bf16[2,128,128]{2,1,0:T(8,128)(2,1)S(1)}, u32[]{:S(2)}, u32[]{:S(2)}) collective-permute-start(bf16[2,128,128]{2,1,0:T(8,128)(2,1)S(1)} %get-tuple-element.85), channel_id=1, source_target_pairs={{0,2},{2,0},{4,6},{6,4},{1,3},{3,1},{5,7},{7,5},{8,10},{10,8},{12,... | collective-permute-start | bytes 196616 | tf_op jit(solution)/shard_map/ppermute | solution.py:382
  100.2 4.2 %copy-start.3 = (bf16[2,512,128]{2,1,0:T(8,128)(2,1)}, bf16[2,512,128]{2,1,0:T(8,128)(2,1)S(1)}, u32[]{:S(2)}) copy-start(bf16[2,512,128]{2,1,0:T(8,128)(2,1)S(1)} %collective-permute-done.19.refs_2_) | copy-start | bytes 786436
  101.2 3.2 %copy-start.4 = (bf16[2,512,128]{2,1,0:T(8,128)(2,1)}, bf16[2,512,128]{2,1,0:T(8,128)(2,1)S(1)}, u32[]{:S(2)}) copy-start(bf16[2,512,128]{2,1,0:T(8,128)(2,1)S(1)} %collective-permute-done.20.refs_3_) | copy-start | bytes 786436
  102.8 1.7 %copy-start.6 = (bf16[2,128,128]{2,1,0:T(8,128)(2,1)}, bf16[2,128,128]{2,1,0:T(8,128)(2,1)S(1)}, u32[]{:S(2)}) copy-start(bf16[2,128,128]{2,1,0:T(8,128)(2,1)S(1)} %collective-permute-done.24.refs_7_) | copy-start | bytes 196612
  104.4 0.6 copy-start.7
  104.4 0.6 copy-start.8

commit v8 on v7

--- a/solution.py
+++ b/solution.py
@@ -415,7 +415,7 @@
         kv = {0: slab}
         for k in far:
             kv[k] = climbed(slab, k)
-        kv[far[0]], grads_other = lax.optimization_barrier((kv[far[0]], grads_other))
+        kv[far[1]], grads_other = lax.optimization_barrier((kv[far[1]], grads_other))
     else:
         kv = {0: lax.all_gather(kv_pieces[0], ("z", "y", "core"), axis=0, tiled=False)}
         rounds = [[0]]

time: 109 us -> 103 us (0.945)
  waiting for transfers between devices: 36.9 us -> 27 us
  starting transfers between devices: 19.8 us -> 25.8 us
  Pallas kernels: 45.1 us -> 44 us
    ppermute x6, starting transfers between devices: 5.42 us -> 11.8 us  [climbed(): return lax.ppermute(array, 'z', route)]
    ppermute x18, waiting for transfers between devices: 15.8 us -> 9.98 us  [flipped(): return lax.ppermute(array, ('y', 'core'), [(i, i ^ flip) for i in range(4)])]
    ppermute x6, waiting for transfers between devices: 21.1 us -> 17 us  [climbed(): return lax.ppermute(array, 'z', route)]
    pallas_call x7, Pallas kernels: 45.1 us -> 44 us  [call(): pl.pallas_call(kernel, grid_spec=pltpu.PrefetchScalarGridSpec(num_scalar_...]
  transfers between devices with their start and end apart: 25 -> 25, of which waited for: 11 -> 10; matrix products, arithmetic and copies ran while one was open for 2% -> 2% of each run, Pallas kernels for 36% -> 36%
where the time goes in v8:
time: 103 us
  Pallas kernels  44 us (43%)
  waiting for transfers between devices  27 us (26%)
  starting transfers between devices  25.8 us (25%)
  local copies, waits for them, and re-layouts  4.62 us (4%)
  other arithmetic  1.2 us (1%)
    pallas_call x7, Pallas kernels, call(): pl.pallas_call(kernel, grid_spec=pltpu.PrefetchScalarGridSpec(num_scalar_...  44 us
    ppermute x6, waiting for transfers between devices, climbed(): return lax.ppermute(array, 'z', route)  17 us
    ppermute x6, starting transfers between devices, climbed(): return lax.ppermute(array, 'z', route)  11.8 us
    ppermute x18, starting transfers between devices, flipped(): return lax.ppermute(array, ('y', 'core'), [(i, i ^ flip) for i in range(4)])  11 us
    ppermute x18, waiting for transfers between devices, flipped(): return lax.ppermute(array, ('y', 'core'), [(i, i ^ flip) for i in range(4)])  9.98 us
    ppermute x1, starting transfers between devices, shards(): grads_other = lax.ppermute(results[-1], 'tp', [(0, 1), (1, 0)])  2.94 us
    unnamed x45, local copies, waits for them, and re-layouts  2.8 us
  transfers between devices with their start and end apart: 25, of which 10 were waited for; matrix products, arithmetic and copies ran while one was open for 2% of the time, Pallas kernels for 36%

profile of v8, /device:TPU:0, one launch (start us, length us, event | category | flops | bytes accessed | tf_op | source)
XLA Modules:
  0.0 103.4 jit_solution(15425783462294006712)
XLA Ops:
  0.6 0.6 stack.34.where_ref
  1.2 3.0 %first.1 = (f32[128,128]{1,0:T(8,128)}, f32[128,128]{1,0:T(8,128)}, bf16[2,128,128]{2,1,0:T(8,128)(2,1)}, bf16[2,128,128]{2,1,0:T(8,128)(2,1)}, bf16[2,128,128]{...) custom-call(s32[5]{0:T(128)} %stack.34.where_ref, s32[3,128]{1,0:T(4,128)} %ids_ref.1, ...), custom_call_target="tpu_custom_call" | custom-call | tf_op jit(solution)/shard_map/first/pallas_call | solution.py:344
  4.3 2.9 %collective-permute-start.11 = (bf16[64,4096]{1,0:T(8,128)(2,1)}, bf16[64,4096]{1,0:T(8,128)(2,1)S(1)}, u32[]{:S(2)}, u32[]{:S(2)}) collective-permute-start(bf16[64,4096]{1,0:T(8,128)(2,1)} %get-tuple-element.59), channel_id=1, source_target_pairs={{0,1},{1,0},{2,3},{3,2},{4,5},{5,4},{6,7},{7,6},{8,9},{9,8},{10,11... | collective-permute-start | bytes 1572872 | tf_op jit(solution)/shard_map/ppermute | solution.py:411
  7.2 0.0 collective-permute-start
  7.2 1.5 %collective-permute-start.1 = (bf16[2,128,128]{2,1,0:T(8,128)(2,1)}, bf16[2,128,128]{2,1,0:T(8,128)(2,1)S(1)}, u32[]{:S(2)}, u32[]{:S(2)}) collective-permute-start(bf16[2,128,128]{2,1,0:T(8,128)(2,1)} %get-tuple-element.47), channel_id=1, source_target_pairs={{0,4},{2,6},{4,0},{6,2},{1,5},{3,7},{5,1},{7,3},{8,12},{10,14},{12... | collective-permute-start | bytes 196616 | tf_op jit(solution)/shard_map/ppermute | solution.py:382
  8.7 0.3 collective-permute-start.2
  9.1 3.0 %delta.2 = (bf16[544,128]{1,0:T(8,128)(2,1)}, bf16[544,128]{1,0:T(8,128)(2,1)}, bf16[544,128]{1,0:T(8,128)(2,1)}, bf16[544,128]{1,0:T(8,128)(2,1)}) custom-call(s32[5]{0:T(128)} %stack.34.where_ref, bf16[128,4096]{1,0:T(8,128)(2,1)} %a_ref.3, f32[32,128]{1,0:T(8,128)} %l_ref.3, bf16[64,8192]{1,0:T(8,128)(2,1)} %source_ref.1), custom_call_target="tpu_custom_call" | custom-call | tf_op jit(solution)/shard_map/delta/pallas_call | solution.py:344
  12.1 0.3 collective-permute-start.7
  12.4 0.6 collective-permute-done.2
  13.1 1.6 %collective-permute-start.10 = (bf16[4,2,128,128]{3,2,1,0:T(8,128)(2,1)S(1)}, bf16[4,2,128,128]{3,2,1,0:T(8,128)(2,1)S(1)}, u32[]{:S(2)}, u32[]{:S(2)}) collective-permute-start(bf16[4,2,128,128]{3,2,1,0:T(8,128)(2,1)S(1)} %pad_maximum_fusion.refs_1_), channel_id=1, source_target_pairs={{0,8},{8,16},{16,24},{24,0},{1,9},{9,17},{17,25},{25,1},{2,10},{10... | collective-permute-start | bytes 786440 | tf_op jit(solution)/shard_map/ppermute | solution.py:386
  14.7 1.4 %collective-permute-start.8 = (bf16[544,128]{1,0:T(8,128)(2,1)}, bf16[544,128]{1,0:T(8,128)(2,1)S(1)}, u32[]{:S(2)}, u32[]{:S(2)}) collective-permute-start(bf16[544,128]{1,0:T(8,128)(2,1)} %get-tuple-element.57), channel_id=1, source_target_pairs={{0,4},{2,6},{4,0},{6,2},{1,5},{3,7},{5,1},{7,3},{8,12},{10,14},{12... | collective-permute-start | bytes 417800 | tf_op jit(solution)/shard_map/ppermute | solution.py:382
  16.1 2.6 %collective-permute-start.15 = (bf16[4,2,128,128]{3,2,1,0:T(8,128)(2,1)S(1)}, bf16[4,2,128,128]{3,2,1,0:T(8,128)(2,1)S(1)}, u32[]{:S(2)}, u32[]{:S(2)}) collective-permute-start(bf16[4,2,128,128]{3,2,1,0:T(8,128)(2,1)S(1)} %pad_maximum_fusion.refs_1_), channel_id=1, source_target_pairs={{0,16},{8,24},{16,0},{24,8},{1,17},{9,25},{17,1},{25,9},{2,18},{10... | collective-permute-start | bytes 786440 | tf_op jit(solution)/shard_map/ppermute | solution.py:386
  18.7 3.3 %rotate.1 = (bf16[2,512,128]{2,1,0:T(8,128)(2,1)}, bf16[2,512,128]{2,1,0:T(8,128)(2,1)}, bf16[2,512,128]{2,1,0:T(8,128)(2,1)}, bf16[2,512,128]{2,1,0:T(8,128)(2,1)}) custom-call(s32[5]{0:T(128)} %stack.34.where_ref, f32[128,128]{1,0:T(8,128)} %get-tuple-element.50.cos_ref, f32[128,128]{1,0:T(8,128)} %get-tuple-element.44.sin_ref, bf16[128,4096]{1,0:T(8,128)(2,1)} %q_ref.1), custom_call_target="tpu_custom_call" | custom-call | tf_op jit(solution)/shard_map/rotate/pallas_call | solution.py:344
  22.0 0.0 collective-permute-start.4
  22.1 0.7 collective-permute-start.9
  22.8 1.3 %collective-permute-done.10.refs_1_ = bf16[4,2,128,128]{3,2,1,0:T(8,128)(2,1)S(1)} collective-permute-done((bf16[4,2,128,128]{3,2,1,0:T(8,128)(2,1)S(1)}, bf16[4,2,128,128]{3,2,1,0:T(8,128)(2,1)S(1)}, u32[]{:S(2)}, u32[]{:S(2)}) %collective-permute-start.10) | collective-permute-done | bytes 262176 | tf_op jit(solution)/shard_map/ppermute | solution.py:386
  24.1 1.4 %collective-permute-start.5 = (bf16[2,512,128]{2,1,0:T(8,128)(2,1)}, bf16[2,512,128]{2,1,0:T(8,128)(2,1)S(1)}, u32[]{:S(2)}, u32[]{:S(2)}) collective-permute-start(bf16[2,512,128]{2,1,0:T(8,128)(2,1)} %get-tuple-element.53), channel_id=1, source_target_pairs={{0,4},{2,6},{4,0},{6,2},{1,5},{3,7},{5,1},{7,3},{8,12},{10,14},{12... | collective-permute-start | bytes 786440 | tf_op jit(solution)/shard_map/ppermute | solution.py:382
  25.6 0.8 copy-done
  26.4 3.0 %delta.3 = (bf16[544,128]{1,0:T(8,128)(2,1)}, bf16[544,128]{1,0:T(8,128)(2,1)}, bf16[544,128]{1,0:T(8,128)(2,1)}, bf16[544,128]{1,0:T(8,128)(2,1)}) custom-call(s32[5]{0:T(128)} %stack.34.where_ref, bf16[128,4096]{1,0:T(8,128)(2,1)} %a_ref.3, f32[32,128]{1,0:T(8,128)} %l_ref.3, bf16[64,4096]{1,0:T(8,128)(2,1)} %copy-done), custom_call_target="tpu_custom_call" | custom-call | tf_op jit(solution)/shard_map/delta/pallas_call | solution.py:344
  29.4 0.1 collective-permute-start.12
  29.4 5.4 %collective-permute-done.15.refs_0_ = bf16[4,2,128,128]{3,2,1,0:T(8,128)(2,1)S(1)} collective-permute-done((bf16[4,2,128,128]{3,2,1,0:T(8,128)(2,1)S(1)}, bf16[4,2,128,128]{3,2,1,0:T(8,128)(2,1)S(1)}, u32[]{:S(2)}, u32[]{:S(2)}) %collective-permute-start.15) | collective-permute-done | bytes 262176 | tf_op jit(solution)/shard_map/ppermute | solution.py:386
  34.9 1.5 %collective-permute-start.13 = (bf16[544,128]{1,0:T(8,128)(2,1)}, bf16[544,128]{1,0:T(8,128)(2,1)S(1)}, u32[]{:S(2)}, u32[]{:S(2)}) collective-permute-start(bf16[544,128]{1,0:T(8,128)(2,1)} %get-tuple-element.63), channel_id=1, source_target_pairs={{0,4},{2,6},{4,0},{6,2},{1,5},{3,7},{5,1},{7,3},{8,12},{10,14},{12... | collective-permute-start | bytes 417800 | tf_op jit(solution)/shard_map/ppermute | solution.py:382
  36.4 0.1 copy.13
  36.5 0.6 reshape.14.span_ref
  37.1 1.6 %collective-permute-start.3 = (bf16[4,2,128,128]{3,2,1,0:T(8,128)(2,1)S(1)}, bf16[4,2,128,128]{3,2,1,0:T(8,128)(2,1)S(1)}, u32[]{:S(2)}, u32[]{:S(2)}) collective-permute-start(bf16[4,2,128,128]{3,2,1,0:T(8,128)(2,1)S(1)} %pad_maximum_fusion.refs_1_), channel_id=1, source_target_pairs={{0,24},{8,0},{16,8},{24,16},{1,25},{9,1},{17,9},{25,17},{2,26},{10... | collective-permute-start | bytes 786440 | tf_op jit(solution)/shard_map/ppermute | solution.py:386
  38.7 0.3 collective-permute-done.6.refs_5_
  39.0 4.1 %collective-permute-done.13.refs_12_ = bf16[544,128]{1,0:T(8,128)(2,1)S(1)} collective-permute-done((bf16[544,128]{1,0:T(8,128)(2,1)}, bf16[544,128]{1,0:T(8,128)(2,1)S(1)}, u32[]{:S(2)}, u32[]{:S(2)}) %collective-permute-start.13) | collective-permute-done | bytes 139296 | tf_op jit(solution)/shard_map/ppermute | solution.py:382
  43.1 1.9 %collective-permute-done.14.refs_13_ = bf16[544,128]{1,0:T(8,128)(2,1)S(1)} collective-permute-done((bf16[544,128]{1,0:T(8,128)(2,1)}, bf16[544,128]{1,0:T(8,128)(2,1)S(1)}, u32[]{:S(2)}, u32[]{:S(2)}) %collective-permute-start.14) | collective-permute-done | bytes 139296 | tf_op jit(solution)/shard_map/ppermute | solution.py:382
  45.1 0.6 copy-done.21
  45.6 12.2 %attend.2 = (f32[8,128,512]{2,1,0:T(8,128)}, bf16[4,2,128,128]{3,2,1,0:T(8,128)(2,1)}, bf16[4,2,128,128]{3,2,1,0:T(8,128)(2,1)}) custom-call(s32[5]{0:T(128)} %stack.34.where_ref, s32[32]{0:T(128)} %map_ref.3, s32[8]{0:T(128)} %reshape.14.span_ref, bf16[4,2,128,128]{3,2,1,0:T(8,128)(2,1)} %copy-done.12, bf16[4,2,128,128]{3,2,1,0:T(8,128)(2,1)} %copy-done.11, ...), custom_call_target="tpu_custom_call" | custom-call | flops 3221225472 | bytes 6291456 | tf_op jit(solution)/shard_map/attend/pallas_call | solution.py:344
  57.8 1.4 %collective-permute-start.16 = (bf16[4,2,128,128]{3,2,1,0:T(8,128)(2,1)}, bf16[4,2,128,128]{3,2,1,0:T(8,128)(2,1)S(1)}, u32[]{:S(2)}, u32[]{:S(2)}) collective-permute-start(bf16[4,2,128,128]{3,2,1,0:T(8,128)(2,1)} %get-tuple-element.71), channel_id=1, source_target_pairs={{0,24},{8,0},{16,8},{24,16},{1,25},{9,1},{17,9},{25,17},{2,26},{10... | collective-permute-start | bytes 786440 | tf_op jit(solution)/shard_map/ppermute | solution.py:386
  59.2 4.6 %collective-permute-start.17 = (bf16[4,2,128,128]{3,2,1,0:T(8,128)(2,1)}, bf16[4,2,128,128]{3,2,1,0:T(8,128)(2,1)S(1)}, u32[]{:S(2)}, u32[]{:S(2)}) collective-permute-start(bf16[4,2,128,128]{3,2,1,0:T(8,128)(2,1)} %get-tuple-element.72), channel_id=1, source_target_pairs={{0,16},{8,24},{16,0},{24,8},{1,17},{9,25},{17,1},{25,9},{2,18},{10... | collective-permute-start | bytes 786440 | tf_op jit(solution)/shard_map/ppermute | solution.py:386
  63.8 0.7 copy-done.15
  64.5 16.0 %attend.3 = (bf16[2,512,128]{2,1,0:T(8,128)(2,1)}, bf16[2,512,128]{2,1,0:T(8,128)(2,1)}, bf16[2,512,128]{2,1,0:T(8,128)(2,1)}, bf16[2,512,128]{2,1,0:T(8,128)(2,...) custom-call(s32[5]{0:T(128)} %stack.34.where_ref, s32[32]{0:T(128)} %map_ref.3, s32[8]{0:T(128)} %reshape.14.span_ref, ...), custom_call_target="tpu_custom_call" | custom-call | flops 3221225472 | bytes 6291456 | tf_op jit(solution)/shard_map/attend/pallas_call | solution.py:344
  80.4 1.8 %collective-permute-done.17 = bf16[4,2,128,128]{3,2,1,0:T(8,128)(2,1)S(1)} collective-permute-done((bf16[4,2,128,128]{3,2,1,0:T(8,128)(2,1)}, bf16[4,2,128,128]{3,2,1,0:T(8,128)(2,1)S(1)}, u32[]{:S(2)}, u32[]{:S(2)}) %collective-permute-start.17) | collective-permute-done | bytes 262176 | tf_op jit(solution)/shard_map/ppermute | solution.py:386
  82.2 0.1 collective-permute-start.18
  82.3 0.7 collective-permute-start.19
  83.1 1.0 collective-permute-start.20
  84.1 8.5 %collective-permute-done.21 = bf16[4,2,128,128]{3,2,1,0:T(8,128)(2,1)S(1)} collective-permute-done((bf16[4,2,128,128]{3,2,1,0:T(8,128)(2,1)}, bf16[4,2,128,128]{3,2,1,0:T(8,128)(2,1)S(1)}, u32[]{:S(2)}, u32[]{:S(2)}) %collective-permute-start.21) | collective-permute-done | bytes 262176 | tf_op jit(solution)/shard_map/ppermute | solution.py:386
  92.5 1.2 %add_convert_fusion = bf16[4,2,128,128]{3,2,1,0:T(8,128)(2,1)S(1)} fusion(bf16[4,2,128,128]{3,2,1,0:T(8,128)(2,1)S(1)} %collective-permute-done.21, bf16[4,2,128,128]{3,2,1,0:T(8,128)(2,1)S(1)} %collective-permute-done.16, f32[4,2,128,128]{3,2,1,0:T(8,128)} %get-tuple-element.79, bf16[4,2,128,128]{3,2,1,0:T(8,128)(2,1)S(1)} %collective-permute-done.17), kind=kLoop, calls=%fused_computation | loop fusion | flops 917504 | bytes 1572864 | tf_op jit(solution)/shard_map/convert.3
  93.7 0.6 slice_bitcast_fusion
  94.4 0.9 collective-permute-start.23
  95.3 0.9 collective-permute-start.22
  96.2 2.3 %collective-permute-done.24.refs_7_ = bf16[2,128,128]{2,1,0:T(8,128)(2,1)S(1)} collective-permute-done((bf16[2,128,128]{2,1,0:T(8,128)(2,1)S(1)}, bf16[2,128,128]{2,1,0:T(8,128)(2,1)S(1)}, u32[]{:S(2)}, u32[]{:S(2)}) %collective-permute-start.24) | collective-permute-done | bytes 65568 | tf_op jit(solution)/shard_map/ppermute | solution.py:382
  98.5 0.8 collective-permute-done.23.refs_6_
  99.3 0.6 copy-done.7
  99.9 0.0 copy-done.8
  99.9 3.5 %last.1 = (bf16[128,4096]{1,0:T(8,128)(2,1)}, bf16[128,512]{1,0:T(8,128)(2,1)}, bf16[128,512]{1,0:T(8,128)(2,1)}) custom-call(s32[5]{0:T(128)} %stack.34.where_ref, f32[128,128]{1,0:T(8,128)} %get-tuple-element.50.cos_ref, f32[128,128]{1,0:T(8,128)} %get-tuple-element.44.sin_ref, bf16[2,512,128]{2,1,0:T(8,128)(2,1)} %get-tuple-element.75.refs_0_, ...), custom_call_target="tpu_custom_call" | custom-call | tf_op jit(solution)/shard_map/last/pallas_call | solution.py:344
  (59 shorter events, 0.2 us)
Async XLA Ops:
  4.3 8.7 %copy-start.5 = (bf16[2,128,128]{2,1,0:T(8,128)(2,1)S(1)}, bf16[2,128,128]{2,1,0:T(8,128)(2,1)}, u32[]{:S(2)}) copy-start(bf16[2,128,128]{2,1,0:T(8,128)(2,1)} %get-tuple-element.45) | copy-start | bytes 196612
  4.3 21.3 %collective-permute-start.11 = (bf16[64,4096]{1,0:T(8,128)(2,1)}, bf16[64,4096]{1,0:T(8,128)(2,1)S(1)}, u32[]{:S(2)}, u32[]{:S(2)}) collective-permute-start(bf16[64,4096]{1,0:T(8,128)(2,1)} %get-tuple-element.59), channel_id=1, source_target_pairs={{0,1},{1,0},{2,3},{3,2},{4,5},{5,4},{6,7},{7,6},{8,9},{9,8},{10,11... | collective-permute-start | bytes 1572872 | tf_op jit(solution)/shard_map/ppermute | solution.py:411
  7.2 5.2 %collective-permute-start = (bf16[2,128,128]{2,1,0:T(8,128)(2,1)}, bf16[2,128,128]{2,1,0:T(8,128)(2,1)S(1)}, u32[]{:S(2)}, u32[]{:S(2)}) collective-permute-start(bf16[2,128,128]{2,1,0:T(8,128)(2,1)} %get-tuple-element.46), channel_id=1, source_target_pairs={{0,2},{2,0},{4,6},{6,4},{1,3},{3,1},{5,7},{7,5},{8,10},{10,8},{12,... | collective-permute-start | bytes 196616 | tf_op jit(solution)/shard_map/ppermute | solution.py:382
  7.2 5.2 %collective-permute-start.1 = (bf16[2,128,128]{2,1,0:T(8,128)(2,1)}, bf16[2,128,128]{2,1,0:T(8,128)(2,1)S(1)}, u32[]{:S(2)}, u32[]{:S(2)}) collective-permute-start(bf16[2,128,128]{2,1,0:T(8,128)(2,1)} %get-tuple-element.47), channel_id=1, source_target_pairs={{0,4},{2,6},{4,0},{6,2},{1,5},{3,7},{5,1},{7,3},{8,12},{10,14},{12... | collective-permute-start | bytes 196616 | tf_op jit(solution)/shard_map/ppermute | solution.py:382
  8.7 4.3 %collective-permute-start.2 = (bf16[2,128,128]{2,1,0:T(8,128)(2,1)}, bf16[2,128,128]{2,1,0:T(8,128)(2,1)S(1)}, u32[]{:S(2)}, u32[]{:S(2)}) collective-permute-start(bf16[2,128,128]{2,1,0:T(8,128)(2,1)} %get-tuple-element.48), channel_id=1, source_target_pairs={{0,6},{2,4},{4,2},{6,0},{1,7},{3,5},{5,3},{7,1},{8,14},{10,12},{12... | collective-permute-start | bytes 196616 | tf_op jit(solution)/shard_map/ppermute | solution.py:382
  12.1 24.3 %copy-start.9 = (s32[4,2]{0,1:T(2,128)S(1)}, s32[4,2]{0,1:T(2,128)}, u32[]{:S(2)}) copy-start(s32[4,2]{0,1:T(2,128)} %param.17) | copy-start | bytes 100
  12.1 9.9 %collective-permute-start.7 = (bf16[544,128]{1,0:T(8,128)(2,1)}, bf16[544,128]{1,0:T(8,128)(2,1)S(1)}, u32[]{:S(2)}, u32[]{:S(2)}) collective-permute-start(bf16[544,128]{1,0:T(8,128)(2,1)} %get-tuple-element.56), channel_id=1, source_target_pairs={{0,2},{2,0},{4,6},{6,4},{1,3},{3,1},{5,7},{7,5},{8,10},{10,8},{12,... | collective-permute-start | bytes 417800 | tf_op jit(solution)/shard_map/ppermute | solution.py:382
  13.0 44.8 %copy-start.1 = (bf16[4,2,128,128]{3,2,1,0:T(8,128)(2,1)}, bf16[4,2,128,128]{3,2,1,0:T(8,128)(2,1)S(1)}, u32[]{:S(2)}) copy-start(bf16[4,2,128,128]{3,2,1,0:T(8,128)(2,1)S(1)} %pad_maximum_fusion.refs_1_) | copy-start | bytes 786436
  13.1 11.1 %collective-permute-start.10 = (bf16[4,2,128,128]{3,2,1,0:T(8,128)(2,1)S(1)}, bf16[4,2,128,128]{3,2,1,0:T(8,128)(2,1)S(1)}, u32[]{:S(2)}, u32[]{:S(2)}) collective-permute-start(bf16[4,2,128,128]{3,2,1,0:T(8,128)(2,1)S(1)} %pad_maximum_fusion.refs_1_), channel_id=1, source_target_pairs={{0,8},{8,16},{16,24},{24,0},{1,9},{9,17},{17,25},{25,1},{2,10},{10... | collective-permute-start | bytes 786440 | tf_op jit(solution)/shard_map/ppermute | solution.py:386
  14.7 7.4 %collective-permute-start.8 = (bf16[544,128]{1,0:T(8,128)(2,1)}, bf16[544,128]{1,0:T(8,128)(2,1)S(1)}, u32[]{:S(2)}, u32[]{:S(2)}) collective-permute-start(bf16[544,128]{1,0:T(8,128)(2,1)} %get-tuple-element.57), channel_id=1, source_target_pairs={{0,4},{2,6},{4,0},{6,2},{1,5},{3,7},{5,1},{7,3},{8,12},{10,14},{12... | collective-permute-start | bytes 417800 | tf_op jit(solution)/shard_map/ppermute | solution.py:382
  16.1 18.7 %collective-permute-start.15 = (bf16[4,2,128,128]{3,2,1,0:T(8,128)(2,1)S(1)}, bf16[4,2,128,128]{3,2,1,0:T(8,128)(2,1)S(1)}, u32[]{:S(2)}, u32[]{:S(2)}) collective-permute-start(bf16[4,2,128,128]{3,2,1,0:T(8,128)(2,1)S(1)} %pad_maximum_fusion.refs_1_), channel_id=1, source_target_pairs={{0,16},{8,24},{16,0},{24,8},{1,17},{9,25},{17,1},{25,9},{2,18},{10... | collective-permute-start | bytes 786440 | tf_op jit(solution)/shard_map/ppermute | solution.py:386
  22.0 23.0 %copy-start.16 = (bf16[544,128]{1,0:T(8,128)(2,1)}, bf16[544,128]{1,0:T(8,128)(2,1)S(1)}, u32[]{:S(2)}) copy-start(bf16[544,128]{1,0:T(8,128)(2,1)S(1)} %collective-permute-done.7.refs_7_) | copy-start | bytes 417796
  22.0 14.4 %collective-permute-start.4 = (bf16[2,512,128]{2,1,0:T(8,128)(2,1)}, bf16[2,512,128]{2,1,0:T(8,128)(2,1)S(1)}, u32[]{:S(2)}, u32[]{:S(2)}) collective-permute-start(bf16[2,512,128]{2,1,0:T(8,128)(2,1)} %get-tuple-element.52), channel_id=1, source_target_pairs={{0,2},{2,0},{4,6},{6,4},{1,3},{3,1},{5,7},{7,5},{8,10},{10,8},{12,... | collective-permute-start | bytes 786440 | tf_op jit(solution)/shard_map/ppermute | solution.py:382
  22.1 22.9 %copy-start.17 = (bf16[544,128]{1,0:T(8,128)(2,1)}, bf16[544,128]{1,0:T(8,128)(2,1)S(1)}, u32[]{:S(2)}) copy-start(bf16[544,128]{1,0:T(8,128)(2,1)S(1)} %collective-permute-done.8.refs_8_) | copy-start | bytes 417796
  22.1 7.3 %collective-permute-start.9 = (bf16[544,128]{1,0:T(8,128)(2,1)}, bf16[544,128]{1,0:T(8,128)(2,1)S(1)}, u32[]{:S(2)}, u32[]{:S(2)}) collective-permute-start(bf16[544,128]{1,0:T(8,128)(2,1)} %get-tuple-element.58), channel_id=1, source_target_pairs={{0,6},{2,4},{4,2},{6,0},{1,7},{3,5},{5,3},{7,1},{8,14},{10,12},{12... | collective-permute-start | bytes 417800 | tf_op jit(solution)/shard_map/ppermute | solution.py:382
  24.1 20.9 %copy-start.11 = (bf16[4,2,128,128]{3,2,1,0:T(8,128)(2,1)}, bf16[4,2,128,128]{3,2,1,0:T(8,128)(2,1)S(1)}, u32[]{:S(2)}) copy-start(bf16[4,2,128,128]{3,2,1,0:T(8,128)(2,1)S(1)} %collective-permute-done.10.refs_1_) | copy-start | bytes 786436
  24.1 13.0 %collective-permute-start.5 = (bf16[2,512,128]{2,1,0:T(8,128)(2,1)}, bf16[2,512,128]{2,1,0:T(8,128)(2,1)S(1)}, u32[]{:S(2)}, u32[]{:S(2)}) collective-permute-start(bf16[2,512,128]{2,1,0:T(8,128)(2,1)} %get-tuple-element.53), channel_id=1, source_target_pairs={{0,4},{2,6},{4,0},{6,2},{1,5},{3,7},{5,1},{7,3},{8,12},{10,14},{12... | collective-permute-start | bytes 786440 | tf_op jit(solution)/shard_map/ppermute | solution.py:382
  25.6 0.8 copy-start
  25.6 13.5 %collective-permute-start.6 = (bf16[2,512,128]{2,1,0:T(8,128)(2,1)}, bf16[2,512,128]{2,1,0:T(8,128)(2,1)S(1)}, u32[]{:S(2)}, u32[]{:S(2)}) collective-permute-start(bf16[2,512,128]{2,1,0:T(8,128)(2,1)} %get-tuple-element.54), channel_id=1, source_target_pairs={{0,6},{2,4},{4,2},{6,0},{1,7},{3,5},{5,3},{7,1},{8,14},{10,12},{12... | collective-permute-start | bytes 786440 | tf_op jit(solution)/shard_map/ppermute | solution.py:382
  29.4 15.6 %copy-start.18 = (bf16[544,128]{1,0:T(8,128)(2,1)}, bf16[544,128]{1,0:T(8,128)(2,1)S(1)}, u32[]{:S(2)}) copy-start(bf16[544,128]{1,0:T(8,128)(2,1)S(1)} %collective-permute-done.9.refs_9_) | copy-start | bytes 417796
  29.4 9.7 %collective-permute-start.12 = (bf16[544,128]{1,0:T(8,128)(2,1)}, bf16[544,128]{1,0:T(8,128)(2,1)S(1)}, u32[]{:S(2)}, u32[]{:S(2)}) collective-permute-start(bf16[544,128]{1,0:T(8,128)(2,1)} %get-tuple-element.62), channel_id=1, source_target_pairs={{0,2},{2,0},{4,6},{6,4},{1,3},{3,1},{5,7},{7,5},{8,10},{10,8},{12,... | collective-permute-start | bytes 417800 | tf_op jit(solution)/shard_map/ppermute | solution.py:382
  34.9 10.2 %copy-start.12 = (bf16[4,2,128,128]{3,2,1,0:T(8,128)(2,1)}, bf16[4,2,128,128]{3,2,1,0:T(8,128)(2,1)S(1)}, u32[]{:S(2)}) copy-start(bf16[4,2,128,128]{3,2,1,0:T(8,128)(2,1)S(1)} %collective-permute-done.15.refs_0_) | copy-start | bytes 786436
  34.9 8.3 %collective-permute-start.13 = (bf16[544,128]{1,0:T(8,128)(2,1)}, bf16[544,128]{1,0:T(8,128)(2,1)S(1)}, u32[]{:S(2)}, u32[]{:S(2)}) collective-permute-start(bf16[544,128]{1,0:T(8,128)(2,1)} %get-tuple-element.63), channel_id=1, source_target_pairs={{0,4},{2,6},{4,0},{6,2},{1,5},{3,7},{5,1},{7,3},{8,12},{10,14},{12... | collective-permute-start | bytes 417800 | tf_op jit(solution)/shard_map/ppermute | solution.py:382
  36.4 8.6 %copy-start.10 = (bf16[2,512,128]{2,1,0:T(8,128)(2,1)}, bf16[2,512,128]{2,1,0:T(8,128)(2,1)S(1)}, u32[]{:S(2)}) copy-start(bf16[2,512,128]{2,1,0:T(8,128)(2,1)S(1)} %collective-permute-done.4.refs_3_) | copy-start | bytes 786436
  36.4 8.6 %collective-permute-start.14 = (bf16[544,128]{1,0:T(8,128)(2,1)}, bf16[544,128]{1,0:T(8,128)(2,1)S(1)}, u32[]{:S(2)}, u32[]{:S(2)}) collective-permute-start(bf16[544,128]{1,0:T(8,128)(2,1)} %get-tuple-element.64), channel_id=1, source_target_pairs={{0,6},{2,4},{4,2},{6,0},{1,7},{3,5},{5,3},{7,1},{8,14},{10,12},{12... | collective-permute-start | bytes 417800 | tf_op jit(solution)/shard_map/ppermute | solution.py:382
  37.1 7.9 %copy-start.13 = (bf16[2,512,128]{2,1,0:T(8,128)(2,1)}, bf16[2,512,128]{2,1,0:T(8,128)(2,1)S(1)}, u32[]{:S(2)}) copy-start(bf16[2,512,128]{2,1,0:T(8,128)(2,1)S(1)} %collective-permute-done.5.refs_4_) | copy-start | bytes 786436
  37.1 26.7 %collective-permute-start.3 = (bf16[4,2,128,128]{3,2,1,0:T(8,128)(2,1)S(1)}, bf16[4,2,128,128]{3,2,1,0:T(8,128)(2,1)S(1)}, u32[]{:S(2)}, u32[]{:S(2)}) collective-permute-start(bf16[4,2,128,128]{3,2,1,0:T(8,128)(2,1)S(1)} %pad_maximum_fusion.refs_1_), channel_id=1, source_target_pairs={{0,24},{8,0},{16,8},{24,16},{1,25},{9,1},{17,9},{25,17},{2,26},{10... | collective-permute-start | bytes 786440 | tf_op jit(solution)/shard_map/ppermute | solution.py:386
  39.0 6.0 %copy-start.14 = (bf16[2,512,128]{2,1,0:T(8,128)(2,1)}, bf16[2,512,128]{2,1,0:T(8,128)(2,1)S(1)}, u32[]{:S(2)}) copy-start(bf16[2,512,128]{2,1,0:T(8,128)(2,1)S(1)} %collective-permute-done.6.refs_5_) | copy-start | bytes 786436
  39.0 6.0 %copy-start.19 = (bf16[544,128]{1,0:T(8,128)(2,1)}, bf16[544,128]{1,0:T(8,128)(2,1)S(1)}, u32[]{:S(2)}) copy-start(bf16[544,128]{1,0:T(8,128)(2,1)S(1)} %collective-permute-done.12.refs_11_) | copy-start | bytes 417796
  43.1 1.9 %copy-start.20 = (bf16[544,128]{1,0:T(8,128)(2,1)}, bf16[544,128]{1,0:T(8,128)(2,1)S(1)}, u32[]{:S(2)}) copy-start(bf16[544,128]{1,0:T(8,128)(2,1)S(1)} %collective-permute-done.13.refs_12_) | copy-start | bytes 417796
  45.0 0.7 copy-start.21
  57.8 22.6 %collective-permute-start.16 = (bf16[4,2,128,128]{3,2,1,0:T(8,128)(2,1)}, bf16[4,2,128,128]{3,2,1,0:T(8,128)(2,1)S(1)}, u32[]{:S(2)}, u32[]{:S(2)}) collective-permute-start(bf16[4,2,128,128]{3,2,1,0:T(8,128)(2,1)} %get-tuple-element.71), channel_id=1, source_target_pairs={{0,24},{8,0},{16,8},{24,16},{1,25},{9,1},{17,9},{25,17},{2,26},{10... | collective-permute-start | bytes 786440 | tf_op jit(solution)/shard_map/ppermute | solution.py:386
  59.2 23.0 %collective-permute-start.17 = (bf16[4,2,128,128]{3,2,1,0:T(8,128)(2,1)}, bf16[4,2,128,128]{3,2,1,0:T(8,128)(2,1)S(1)}, u32[]{:S(2)}, u32[]{:S(2)}) collective-permute-start(bf16[4,2,128,128]{3,2,1,0:T(8,128)(2,1)} %get-tuple-element.72), channel_id=1, source_target_pairs={{0,16},{8,24},{16,0},{24,8},{1,17},{9,25},{17,1},{25,9},{2,18},{10... | collective-permute-start | bytes 786440 | tf_op jit(solution)/shard_map/ppermute | solution.py:386
  63.8 0.7 copy-start.15
  82.2 10.3 %collective-permute-start.21 = (bf16[4,2,128,128]{3,2,1,0:T(8,128)(2,1)}, bf16[4,2,128,128]{3,2,1,0:T(8,128)(2,1)S(1)}, u32[]{:S(2)}, u32[]{:S(2)}) collective-permute-start(bf16[4,2,128,128]{3,2,1,0:T(8,128)(2,1)} %get-tuple-element.82), channel_id=1, source_target_pairs={{0,8},{8,16},{16,24},{24,0},{1,9},{9,17},{17,25},{25,1},{2,10},{10... | collective-permute-start | bytes 786440 | tf_op jit(solution)/shard_map/ppermute | solution.py:386
  82.2 13.1 %collective-permute-start.18 = (bf16[2,512,128]{2,1,0:T(8,128)(2,1)}, bf16[2,512,128]{2,1,0:T(8,128)(2,1)S(1)}, u32[]{:S(2)}, u32[]{:S(2)}) collective-permute-start(bf16[2,512,128]{2,1,0:T(8,128)(2,1)} %get-tuple-element.76), channel_id=1, source_target_pairs={{0,2},{2,0},{4,6},{6,4},{1,3},{3,1},{5,7},{7,5},{8,10},{10,8},{12,... | collective-permute-start | bytes 786440 | tf_op jit(solution)/shard_map/ppermute | solution.py:382
  82.3 13.9 %collective-permute-start.19 = (bf16[2,512,128]{2,1,0:T(8,128)(2,1)}, bf16[2,512,128]{2,1,0:T(8,128)(2,1)S(1)}, u32[]{:S(2)}, u32[]{:S(2)}) collective-permute-start(bf16[2,512,128]{2,1,0:T(8,128)(2,1)} %get-tuple-element.77), channel_id=1, source_target_pairs={{0,4},{2,6},{4,0},{6,2},{1,5},{3,7},{5,1},{7,3},{8,12},{10,14},{12... | collective-permute-start | bytes 786440 | tf_op jit(solution)/shard_map/ppermute | solution.py:382
  83.1 13.2 %collective-permute-start.20 = (bf16[2,512,128]{2,1,0:T(8,128)(2,1)}, bf16[2,512,128]{2,1,0:T(8,128)(2,1)S(1)}, u32[]{:S(2)}, u32[]{:S(2)}) collective-permute-start(bf16[2,512,128]{2,1,0:T(8,128)(2,1)} %get-tuple-element.78), channel_id=1, source_target_pairs={{0,6},{2,4},{4,2},{6,0},{1,7},{3,5},{5,3},{7,1},{8,14},{10,12},{12... | collective-permute-start | bytes 786440 | tf_op jit(solution)/shard_map/ppermute | solution.py:382
  94.3 4.2 %collective-permute-start.24 = (bf16[2,128,128]{2,1,0:T(8,128)(2,1)S(1)}, bf16[2,128,128]{2,1,0:T(8,128)(2,1)S(1)}, u32[]{:S(2)}, u32[]{:S(2)}) collective-permute-start(bf16[2,128,128]{2,1,0:T(8,128)(2,1)S(1)} %get-tuple-element.83), channel_id=1, source_target_pairs={{0,6},{2,4},{4,2},{6,0},{1,7},{3,5},{5,3},{7,1},{8,14},{10,12},{12... | collective-permute-start | bytes 196616 | tf_op jit(solution)/shard_map/ppermute | solution.py:382
  94.4 4.9 %collective-permute-start.23 = (bf16[2,128,128]{2,1,0:T(8,128)(2,1)S(1)}, bf16[2,128,128]{2,1,0:T(8,128)(2,1)S(1)}, u32[]{:S(2)}, u32[]{:S(2)}) collective-permute-start(bf16[2,128,128]{2,1,0:T(8,128)(2,1)S(1)} %get-tuple-element.84), channel_id=1, source_target_pairs={{0,4},{2,6},{4,0},{6,2},{1,5},{3,7},{5,1},{7,3},{8,12},{10,14},{12... | collective-permute-start | bytes 196616 | tf_op jit(solution)/shard_map/ppermute | solution.py:382
  95.3 4.0 %copy-start.2 = (bf16[2,512,128]{2,1,0:T(8,128)(2,1)}, bf16[2,512,128]{2,1,0:T(8,128)(2,1)S(1)}, u32[]{:S(2)}) copy-start(bf16[2,512,128]{2,1,0:T(8,128)(2,1)S(1)} %collective-permute-done.18.refs_1_) | copy-start | bytes 786436
  95.3 4.0 %collective-permute-start.22 = (bf16[2,128,128]{2,1,0:T(8,128)(2,1)S(1)}, bf16[2,128,128]{2,1,0:T(8,128)(2,1)S(1)}, u32[]{:S(2)}, u32[]{:S(2)}) collective-permute-start(bf16[2,128,128]{2,1,0:T(8,128)(2,1)S(1)} %get-tuple-element.85), channel_id=1, source_target_pairs={{0,2},{2,0},{4,6},{6,4},{1,3},{3,1},{5,7},{7,5},{8,10},{10,8},{12,... | collective-permute-start | bytes 196616 | tf_op jit(solution)/shard_map/ppermute | solution.py:382
  96.2 3.1 %copy-start.3 = (bf16[2,512,128]{2,1,0:T(8,128)(2,1)}, bf16[2,512,128]{2,1,0:T(8,128)(2,1)S(1)}, u32[]{:S(2)}) copy-start(bf16[2,512,128]{2,1,0:T(8,128)(2,1)S(1)} %collective-permute-done.19.refs_2_) | copy-start | bytes 786436
  96.2 3.1 %copy-start.4 = (bf16[2,512,128]{2,1,0:T(8,128)(2,1)}, bf16[2,512,128]{2,1,0:T(8,128)(2,1)S(1)}, u32[]{:S(2)}) copy-start(bf16[2,512,128]{2,1,0:T(8,128)(2,1)S(1)} %collective-permute-done.20.refs_3_) | copy-start | bytes 786436
  98.5 0.8 copy-start.6
  99.3 0.6 copy-start.7
  99.3 0.6 copy-start.8

commit v9 on v8

--- a/solution.py
+++ b/solution.py
@@ -250,7 +250,7 @@
             end = jnp.where(inside, span_ref[2 * span + 1], end)
         limit = jnp.where(end > 0, end * block_len, block * block_len + within + 1)
         full = blocks_before(jnp.where(end > 0, end, block)) // chunk_blocks
-        seen = (blocks_before(jnp.maximum(end, block + 1)) + chunk_blocks - 1) // chunk_blocks
+        tail = blocks_before(jnp.maximum(end, block + 1)) - full * chunk_blocks
         dq_sum[...] = in_ref[place] if carried else jnp.zeros_like(dq_sum)
 
         def visit(chunk, size, masked):
@@ -267,7 +267,7 @@
                 positions = jnp.concatenate(
                     [
                         key_row + ordered[chunk * chunk_blocks + i] * block_len
-                        for i in range(chunk_blocks)
+                        for i in range(size // block_len)
                     ],
                     axis=0,
                 )
@@ -283,7 +283,10 @@
             dk_sum[pl.ds(at, size), :] += jnp.dot(
                 grad_s, queries, preferred_element_type=jnp.float32
             )
-            turned = [k_turn[chunk + i] for i in range(size // CHUNK)]
+            if size < CHUNK:
+                turned = [k_turn[chunk, :, :size]]
+            else:
+                turned = [k_turn[chunk + i] for i in range(size // CHUNK)]
             dq_sum[...] += jnp.dot(
                 jnp.concatenate(turned, axis=1), grad_s, preferred_element_type=jnp.float32
             )
@@ -291,7 +294,9 @@
         pairs = full // 2
         pl.loop(0, pairs)(lambda pair: visit(2 * pair, WIDE, False))
         pl.loop(2 * pairs, full)(lambda chunk: visit(chunk, CHUNK, False))
-        pl.loop(full, seen)(lambda chunk: visit(chunk, CHUNK, True))
+        short = chunk_blocks // 2
+        pl.when(tail > short)(lambda: visit(full, CHUNK, True))
+        pl.when((tail > 0) & (tail <= short))(lambda: visit(full, CHUNK // 2, True))
 
         if carries:
             dq_refs[0][place] = dq_sum[...]

time: 103 us -> 103 us (level)
  Pallas kernels: 44 us -> 48.2 us
  starting transfers between devices: 25.8 us -> 22.9 us
    pallas_call x7, Pallas kernels: 44 us -> 48.2 us  [call(): pl.pallas_call(kernel, grid_spec=pltpu.PrefetchScalarGridSpec(num_scalar_...]
    ppermute x6, starting transfers between devices: 11.8 us -> 8.89 us  [climbed(): return lax.ppermute(array, 'z', route)]
    ppermute x6, waiting for transfers between devices: 17 us -> 15.1 us  [climbed(): return lax.ppermute(array, 'z', route)]
  transfers between devices with their start and end apart: 25 -> 25, of which waited for: 10 -> 11; matrix products, arithmetic and copies ran while one was open for 2% -> 2% of each run, Pallas kernels for 36% -> 40%
where the time goes in v9:
time: 103 us; the launch traced here: 104 us
  Pallas kernels  48.2 us (47%)
  waiting for transfers between devices  26 us (25%)
  starting transfers between devices  22.9 us (22%)
  local copies, waits for them, and re-layouts  4.62 us (4%)
  other arithmetic  1.2 us (1%)
    pallas_call x7, Pallas kernels, call(): pl.pallas_call(kernel, grid_spec=pltpu.PrefetchScalarGridSpec(num_scalar_...  48.2 us
    ppermute x6, waiting for transfers between devices, climbed(): return lax.ppermute(array, 'z', route)  15.1 us
    ppermute x18, starting transfers between devices, flipped(): return lax.ppermute(array, ('y', 'core'), [(i, i ^ flip) for i in range(4)])  11 us
    ppermute x18, waiting for transfers between devices, flipped(): return lax.ppermute(array, ('y', 'core'), [(i, i ^ flip) for i in range(4)])  10.8 us
    ppermute x6, starting transfers between devices, climbed(): return lax.ppermute(array, 'z', route)  8.89 us
    ppermute x1, starting transfers between devices, shards(): grads_other = lax.ppermute(results[-1], 'tp', [(0, 1), (1, 0)])  2.94 us
    unnamed x45, local copies, waits for them, and re-layouts  2.8 us
  transfers between devices with their start and end apart: 25, of which 11 were waited for; matrix products, arithmetic and copies ran while one was open for 2% of the time, Pallas kernels for 40%

profile of v9, /device:TPU:0, one launch (start us, length us, event | category | flops | bytes accessed | tf_op | source)
XLA Modules:
  0.0 103.7 jit_solution(2750354579501574642)
XLA Ops:
  0.6 0.6 stack.34.where_ref
  1.2 3.0 %first.1 = (f32[128,128]{1,0:T(8,128)}, f32[128,128]{1,0:T(8,128)}, bf16[2,128,128]{2,1,0:T(8,128)(2,1)}, bf16[2,128,128]{2,1,0:T(8,128)(2,1)}, bf16[2,128,128]{...) custom-call(s32[5]{0:T(128)} %stack.34.where_ref, s32[3,128]{1,0:T(4,128)} %ids_ref.1, ...), custom_call_target="tpu_custom_call" | custom-call | tf_op jit(solution)/shard_map/first/pallas_call | solution.py:349
  4.3 2.9 %collective-permute-start.11 = (bf16[64,4096]{1,0:T(8,128)(2,1)}, bf16[64,4096]{1,0:T(8,128)(2,1)S(1)}, u32[]{:S(2)}, u32[]{:S(2)}) collective-permute-start(bf16[64,4096]{1,0:T(8,128)(2,1)} %get-tuple-element.59), channel_id=1, source_target_pairs={{0,1},{1,0},{2,3},{3,2},{4,5},{5,4},{6,7},{7,6},{8,9},{9,8},{10,11... | collective-permute-start | bytes 1572872 | tf_op jit(solution)/shard_map/ppermute | solution.py:416
  7.2 1.5 %collective-permute-start.1 = (bf16[2,128,128]{2,1,0:T(8,128)(2,1)}, bf16[2,128,128]{2,1,0:T(8,128)(2,1)S(1)}, u32[]{:S(2)}, u32[]{:S(2)}) collective-permute-start(bf16[2,128,128]{2,1,0:T(8,128)(2,1)} %get-tuple-element.47), channel_id=1, source_target_pairs={{0,4},{2,6},{4,0},{6,2},{1,5},{3,7},{5,1},{7,3},{8,12},{10,14},{12... | collective-permute-start | bytes 196616 | tf_op jit(solution)/shard_map/ppermute | solution.py:387
  8.7 0.3 collective-permute-start.2
  9.1 3.0 %delta.2 = (bf16[544,128]{1,0:T(8,128)(2,1)}, bf16[544,128]{1,0:T(8,128)(2,1)}, bf16[544,128]{1,0:T(8,128)(2,1)}, bf16[544,128]{1,0:T(8,128)(2,1)}) custom-call(s32[5]{0:T(128)} %stack.34.where_ref, bf16[128,4096]{1,0:T(8,128)(2,1)} %a_ref.3, f32[32,128]{1,0:T(8,128)} %l_ref.3, bf16[64,8192]{1,0:T(8,128)(2,1)} %source_ref.1), custom_call_target="tpu_custom_call" | custom-call | tf_op jit(solution)/shard_map/delta/pallas_call | solution.py:349
  12.1 0.3 collective-permute-start.7
  12.4 0.6 collective-permute-done.2
  13.1 1.6 %collective-permute-start.10 = (bf16[4,2,128,128]{3,2,1,0:T(8,128)(2,1)S(1)}, bf16[4,2,128,128]{3,2,1,0:T(8,128)(2,1)S(1)}, u32[]{:S(2)}, u32[]{:S(2)}) collective-permute-start(bf16[4,2,128,128]{3,2,1,0:T(8,128)(2,1)S(1)} %pad_maximum_fusion.refs_1_), channel_id=1, source_target_pairs={{0,8},{8,16},{16,24},{24,0},{1,9},{9,17},{17,25},{25,1},{2,10},{10... | collective-permute-start | bytes 786440 | tf_op jit(solution)/shard_map/ppermute | solution.py:391
  14.7 1.4 %collective-permute-start.8 = (bf16[544,128]{1,0:T(8,128)(2,1)}, bf16[544,128]{1,0:T(8,128)(2,1)S(1)}, u32[]{:S(2)}, u32[]{:S(2)}) collective-permute-start(bf16[544,128]{1,0:T(8,128)(2,1)} %get-tuple-element.57), channel_id=1, source_target_pairs={{0,4},{2,6},{4,0},{6,2},{1,5},{3,7},{5,1},{7,3},{8,12},{10,14},{12... | collective-permute-start | bytes 417800 | tf_op jit(solution)/shard_map/ppermute | solution.py:387
  16.1 2.6 %collective-permute-start.15 = (bf16[4,2,128,128]{3,2,1,0:T(8,128)(2,1)S(1)}, bf16[4,2,128,128]{3,2,1,0:T(8,128)(2,1)S(1)}, u32[]{:S(2)}, u32[]{:S(2)}) collective-permute-start(bf16[4,2,128,128]{3,2,1,0:T(8,128)(2,1)S(1)} %pad_maximum_fusion.refs_1_), channel_id=1, source_target_pairs={{0,16},{8,24},{16,0},{24,8},{1,17},{9,25},{17,1},{25,9},{2,18},{10... | collective-permute-start | bytes 786440 | tf_op jit(solution)/shard_map/ppermute | solution.py:391
  18.7 3.3 %rotate.1 = (bf16[2,512,128]{2,1,0:T(8,128)(2,1)}, bf16[2,512,128]{2,1,0:T(8,128)(2,1)}, bf16[2,512,128]{2,1,0:T(8,128)(2,1)}, bf16[2,512,128]{2,1,0:T(8,128)(2,1)}) custom-call(s32[5]{0:T(128)} %stack.34.where_ref, f32[128,128]{1,0:T(8,128)} %get-tuple-element.50.cos_ref, f32[128,128]{1,0:T(8,128)} %get-tuple-element.44.sin_ref, bf16[128,4096]{1,0:T(8,128)(2,1)} %q_ref.1), custom_call_target="tpu_custom_call" | custom-call | tf_op jit(solution)/shard_map/rotate/pallas_call | solution.py:349
  22.0 0.0 collective-permute-start.4
  22.1 0.7 collective-permute-start.9
  22.8 1.3 %collective-permute-done.10.refs_1_ = bf16[4,2,128,128]{3,2,1,0:T(8,128)(2,1)S(1)} collective-permute-done((bf16[4,2,128,128]{3,2,1,0:T(8,128)(2,1)S(1)}, bf16[4,2,128,128]{3,2,1,0:T(8,128)(2,1)S(1)}, u32[]{:S(2)}, u32[]{:S(2)}) %collective-permute-start.10) | collective-permute-done | bytes 262176 | tf_op jit(solution)/shard_map/ppermute | solution.py:391
  24.1 1.4 %collective-permute-start.5 = (bf16[2,512,128]{2,1,0:T(8,128)(2,1)}, bf16[2,512,128]{2,1,0:T(8,128)(2,1)S(1)}, u32[]{:S(2)}, u32[]{:S(2)}) collective-permute-start(bf16[2,512,128]{2,1,0:T(8,128)(2,1)} %get-tuple-element.53), channel_id=1, source_target_pairs={{0,4},{2,6},{4,0},{6,2},{1,5},{3,7},{5,1},{7,3},{8,12},{10,14},{12... | collective-permute-start | bytes 786440 | tf_op jit(solution)/shard_map/ppermute | solution.py:387
  25.6 0.8 copy-done
  26.4 3.0 %delta.3 = (bf16[544,128]{1,0:T(8,128)(2,1)}, bf16[544,128]{1,0:T(8,128)(2,1)}, bf16[544,128]{1,0:T(8,128)(2,1)}, bf16[544,128]{1,0:T(8,128)(2,1)}) custom-call(s32[5]{0:T(128)} %stack.34.where_ref, bf16[128,4096]{1,0:T(8,128)(2,1)} %a_ref.3, f32[32,128]{1,0:T(8,128)} %l_ref.3, bf16[64,4096]{1,0:T(8,128)(2,1)} %copy-done), custom_call_target="tpu_custom_call" | custom-call | tf_op jit(solution)/shard_map/delta/pallas_call | solution.py:349
  29.4 0.1 collective-permute-start.12
  29.4 5.4 %collective-permute-done.15.refs_0_ = bf16[4,2,128,128]{3,2,1,0:T(8,128)(2,1)S(1)} collective-permute-done((bf16[4,2,128,128]{3,2,1,0:T(8,128)(2,1)S(1)}, bf16[4,2,128,128]{3,2,1,0:T(8,128)(2,1)S(1)}, u32[]{:S(2)}, u32[]{:S(2)}) %collective-permute-start.15) | collective-permute-done | bytes 262176 | tf_op jit(solution)/shard_map/ppermute | solution.py:391
  34.9 1.5 %collective-permute-start.13 = (bf16[544,128]{1,0:T(8,128)(2,1)}, bf16[544,128]{1,0:T(8,128)(2,1)S(1)}, u32[]{:S(2)}, u32[]{:S(2)}) collective-permute-start(bf16[544,128]{1,0:T(8,128)(2,1)} %get-tuple-element.63), channel_id=1, source_target_pairs={{0,4},{2,6},{4,0},{6,2},{1,5},{3,7},{5,1},{7,3},{8,12},{10,14},{12... | collective-permute-start | bytes 417800 | tf_op jit(solution)/shard_map/ppermute | solution.py:387
  36.4 0.1 copy.13
  36.5 0.6 reshape.14.span_ref
  37.1 1.6 %collective-permute-start.3 = (bf16[4,2,128,128]{3,2,1,0:T(8,128)(2,1)S(1)}, bf16[4,2,128,128]{3,2,1,0:T(8,128)(2,1)S(1)}, u32[]{:S(2)}, u32[]{:S(2)}) collective-permute-start(bf16[4,2,128,128]{3,2,1,0:T(8,128)(2,1)S(1)} %pad_maximum_fusion.refs_1_), channel_id=1, source_target_pairs={{0,24},{8,0},{16,8},{24,16},{1,25},{9,1},{17,9},{25,17},{2,26},{10... | collective-permute-start | bytes 786440 | tf_op jit(solution)/shard_map/ppermute | solution.py:391
  38.7 0.3 collective-permute-done.6.refs_5_
  39.0 4.1 %collective-permute-done.13.refs_12_ = bf16[544,128]{1,0:T(8,128)(2,1)S(1)} collective-permute-done((bf16[544,128]{1,0:T(8,128)(2,1)}, bf16[544,128]{1,0:T(8,128)(2,1)S(1)}, u32[]{:S(2)}, u32[]{:S(2)}) %collective-permute-start.13) | collective-permute-done | bytes 139296 | tf_op jit(solution)/shard_map/ppermute | solution.py:387
  43.1 1.9 %collective-permute-done.14.refs_13_ = bf16[544,128]{1,0:T(8,128)(2,1)S(1)} collective-permute-done((bf16[544,128]{1,0:T(8,128)(2,1)}, bf16[544,128]{1,0:T(8,128)(2,1)S(1)}, u32[]{:S(2)}, u32[]{:S(2)}) %collective-permute-start.14) | collective-permute-done | bytes 139296 | tf_op jit(solution)/shard_map/ppermute | solution.py:387
  45.1 0.6 copy-done.21
  45.6 14.9 %attend.2 = (f32[8,128,512]{2,1,0:T(8,128)}, bf16[4,2,128,128]{3,2,1,0:T(8,128)(2,1)}, bf16[4,2,128,128]{3,2,1,0:T(8,128)(2,1)}) custom-call(s32[5]{0:T(128)} %stack.34.where_ref, s32[32]{0:T(128)} %map_ref.3, s32[8]{0:T(128)} %reshape.14.span_ref, bf16[4,2,128,128]{3,2,1,0:T(8,128)(2,1)} %copy-done.12, bf16[4,2,128,128]{3,2,1,0:T(8,128)(2,1)} %copy-done.11, ...), custom_call_target="tpu_custom_call" | custom-call | flops 3221225472 | bytes 6291456 | tf_op jit(solution)/shard_map/attend/pallas_call | solution.py:349
  60.6 2.1 %collective-permute-start.16 = (bf16[4,2,128,128]{3,2,1,0:T(8,128)(2,1)}, bf16[4,2,128,128]{3,2,1,0:T(8,128)(2,1)S(1)}, u32[]{:S(2)}, u32[]{:S(2)}) collective-permute-start(bf16[4,2,128,128]{3,2,1,0:T(8,128)(2,1)} %get-tuple-element.71), channel_id=1, source_target_pairs={{0,24},{8,0},{16,8},{24,16},{1,25},{9,1},{17,9},{25,17},{2,26},{10... | collective-permute-start | bytes 786440 | tf_op jit(solution)/shard_map/ppermute | solution.py:391
  62.7 0.4 collective-permute-start.17
  63.1 0.7 copy-done.15
  63.8 17.5 %attend.3 = (bf16[2,512,128]{2,1,0:T(8,128)(2,1)}, bf16[2,512,128]{2,1,0:T(8,128)(2,1)}, bf16[2,512,128]{2,1,0:T(8,128)(2,1)}, bf16[2,512,128]{2,1,0:T(8,128)(2,...) custom-call(s32[5]{0:T(128)} %stack.34.where_ref, s32[32]{0:T(128)} %map_ref.3, s32[8]{0:T(128)} %reshape.14.span_ref, ...), custom_call_target="tpu_custom_call" | custom-call | flops 3221225472 | bytes 6291456 | tf_op jit(solution)/shard_map/attend/pallas_call | solution.py:349
  81.3 0.3 collective-permute-done.17
  81.6 0.5 collective-permute-start.21
  82.1 1.2 %collective-permute-start.19 = (bf16[2,512,128]{2,1,0:T(8,128)(2,1)}, bf16[2,512,128]{2,1,0:T(8,128)(2,1)S(1)}, u32[]{:S(2)}, u32[]{:S(2)}) collective-permute-start(bf16[2,512,128]{2,1,0:T(8,128)(2,1)} %get-tuple-element.77), channel_id=1, source_target_pairs={{0,4},{2,6},{4,0},{6,2},{1,5},{3,7},{5,1},{7,3},{8,12},{10,14},{12... | collective-permute-start | bytes 786440 | tf_op jit(solution)/shard_map/ppermute | solution.py:387
  83.3 0.6 collective-permute-start.20
  84.0 8.1 %collective-permute-done.21 = bf16[4,2,128,128]{3,2,1,0:T(8,128)(2,1)S(1)} collective-permute-done((bf16[4,2,128,128]{3,2,1,0:T(8,128)(2,1)}, bf16[4,2,128,128]{3,2,1,0:T(8,128)(2,1)S(1)}, u32[]{:S(2)}, u32[]{:S(2)}) %collective-permute-start.21) | collective-permute-done | bytes 262176 | tf_op jit(solution)/shard_map/ppermute | solution.py:391
  92.0 1.2 %add_convert_fusion = bf16[4,2,128,128]{3,2,1,0:T(8,128)(2,1)S(1)} fusion(bf16[4,2,128,128]{3,2,1,0:T(8,128)(2,1)S(1)} %collective-permute-done.21, bf16[4,2,128,128]{3,2,1,0:T(8,128)(2,1)S(1)} %collective-permute-done.16, f32[4,2,128,128]{3,2,1,0:T(8,128)} %get-tuple-element.79, bf16[4,2,128,128]{3,2,1,0:T(8,128)(2,1)S(1)} %collective-permute-done.17), kind=kLoop, calls=%fused_computation | loop fusion | flops 917504 | bytes 1572864 | tf_op jit(solution)/shard_map/convert.3
  93.2 0.6 slice_bitcast_fusion
  93.8 1.1 %collective-permute-start.24 = (bf16[2,128,128]{2,1,0:T(8,128)(2,1)S(1)}, bf16[2,128,128]{2,1,0:T(8,128)(2,1)S(1)}, u32[]{:S(2)}, u32[]{:S(2)}) collective-permute-start(bf16[2,128,128]{2,1,0:T(8,128)(2,1)S(1)} %get-tuple-element.83), channel_id=1, source_target_pairs={{0,6},{2,4},{4,2},{6,0},{1,7},{3,5},{5,3},{7,1},{8,14},{10,12},{12... | collective-permute-start | bytes 196616 | tf_op jit(solution)/shard_map/ppermute | solution.py:387
  94.9 0.4 collective-permute-start.23
  95.3 0.4 collective-permute-start.22
  95.7 0.6 collective-permute-done.20.refs_3_
  96.3 1.9 %collective-permute-done.24.refs_7_ = bf16[2,128,128]{2,1,0:T(8,128)(2,1)S(1)} collective-permute-done((bf16[2,128,128]{2,1,0:T(8,128)(2,1)S(1)}, bf16[2,128,128]{2,1,0:T(8,128)(2,1)S(1)}, u32[]{:S(2)}, u32[]{:S(2)}) %collective-permute-start.24) | collective-permute-done | bytes 65568 | tf_op jit(solution)/shard_map/ppermute | solution.py:387
  98.2 1.4 %collective-permute-done.23.refs_6_ = bf16[2,128,128]{2,1,0:T(8,128)(2,1)S(1)} collective-permute-done((bf16[2,128,128]{2,1,0:T(8,128)(2,1)S(1)}, bf16[2,128,128]{2,1,0:T(8,128)(2,1)S(1)}, u32[]{:S(2)}, u32[]{:S(2)}) %collective-permute-start.23) | collective-permute-done | bytes 65568 | tf_op jit(solution)/shard_map/ppermute | solution.py:387
  99.7 0.6 copy-done.7
  100.3 3.5 %last.1 = (bf16[128,4096]{1,0:T(8,128)(2,1)}, bf16[128,512]{1,0:T(8,128)(2,1)}, bf16[128,512]{1,0:T(8,128)(2,1)}) custom-call(s32[5]{0:T(128)} %stack.34.where_ref, f32[128,128]{1,0:T(8,128)} %get-tuple-element.50.cos_ref, f32[128,128]{1,0:T(8,128)} %get-tuple-element.44.sin_ref, bf16[2,512,128]{2,1,0:T(8,128)(2,1)} %get-tuple-element.75.refs_0_, ...), custom_call_target="tpu_custom_call" | custom-call | tf_op jit(solution)/shard_map/last/pallas_call | solution.py:349
  (59 shorter events, 0.2 us)
Async XLA Ops:
  4.3 8.7 %copy-start.5 = (bf16[2,128,128]{2,1,0:T(8,128)(2,1)S(1)}, bf16[2,128,128]{2,1,0:T(8,128)(2,1)}, u32[]{:S(2)}) copy-start(bf16[2,128,128]{2,1,0:T(8,128)(2,1)} %get-tuple-element.45) | copy-start | bytes 196612
  4.3 21.3 %collective-permute-start.11 = (bf16[64,4096]{1,0:T(8,128)(2,1)}, bf16[64,4096]{1,0:T(8,128)(2,1)S(1)}, u32[]{:S(2)}, u32[]{:S(2)}) collective-permute-start(bf16[64,4096]{1,0:T(8,128)(2,1)} %get-tuple-element.59), channel_id=1, source_target_pairs={{0,1},{1,0},{2,3},{3,2},{4,5},{5,4},{6,7},{7,6},{8,9},{9,8},{10,11... | collective-permute-start | bytes 1572872 | tf_op jit(solution)/shard_map/ppermute | solution.py:416
  7.2 5.2 %collective-permute-start = (bf16[2,128,128]{2,1,0:T(8,128)(2,1)}, bf16[2,128,128]{2,1,0:T(8,128)(2,1)S(1)}, u32[]{:S(2)}, u32[]{:S(2)}) collective-permute-start(bf16[2,128,128]{2,1,0:T(8,128)(2,1)} %get-tuple-element.46), channel_id=1, source_target_pairs={{0,2},{2,0},{4,6},{6,4},{1,3},{3,1},{5,7},{7,5},{8,10},{10,8},{12,... | collective-permute-start | bytes 196616 | tf_op jit(solution)/shard_map/ppermute | solution.py:387
  7.2 5.2 %collective-permute-start.1 = (bf16[2,128,128]{2,1,0:T(8,128)(2,1)}, bf16[2,128,128]{2,1,0:T(8,128)(2,1)S(1)}, u32[]{:S(2)}, u32[]{:S(2)}) collective-permute-start(bf16[2,128,128]{2,1,0:T(8,128)(2,1)} %get-tuple-element.47), channel_id=1, source_target_pairs={{0,4},{2,6},{4,0},{6,2},{1,5},{3,7},{5,1},{7,3},{8,12},{10,14},{12... | collective-permute-start | bytes 196616 | tf_op jit(solution)/shard_map/ppermute | solution.py:387
  8.7 4.3 %collective-permute-start.2 = (bf16[2,128,128]{2,1,0:T(8,128)(2,1)}, bf16[2,128,128]{2,1,0:T(8,128)(2,1)S(1)}, u32[]{:S(2)}, u32[]{:S(2)}) collective-permute-start(bf16[2,128,128]{2,1,0:T(8,128)(2,1)} %get-tuple-element.48), channel_id=1, source_target_pairs={{0,6},{2,4},{4,2},{6,0},{1,7},{3,5},{5,3},{7,1},{8,14},{10,12},{12... | collective-permute-start | bytes 196616 | tf_op jit(solution)/shard_map/ppermute | solution.py:387
  12.1 24.3 %copy-start.9 = (s32[4,2]{0,1:T(2,128)S(1)}, s32[4,2]{0,1:T(2,128)}, u32[]{:S(2)}) copy-start(s32[4,2]{0,1:T(2,128)} %param.17) | copy-start | bytes 100
  12.1 9.9 %collective-permute-start.7 = (bf16[544,128]{1,0:T(8,128)(2,1)}, bf16[544,128]{1,0:T(8,128)(2,1)S(1)}, u32[]{:S(2)}, u32[]{:S(2)}) collective-permute-start(bf16[544,128]{1,0:T(8,128)(2,1)} %get-tuple-element.56), channel_id=1, source_target_pairs={{0,2},{2,0},{4,6},{6,4},{1,3},{3,1},{5,7},{7,5},{8,10},{10,8},{12,... | collective-permute-start | bytes 417800 | tf_op jit(solution)/shard_map/ppermute | solution.py:387
  13.0 47.5 %copy-start.1 = (bf16[4,2,128,128]{3,2,1,0:T(8,128)(2,1)}, bf16[4,2,128,128]{3,2,1,0:T(8,128)(2,1)S(1)}, u32[]{:S(2)}) copy-start(bf16[4,2,128,128]{3,2,1,0:T(8,128)(2,1)S(1)} %pad_maximum_fusion.refs_1_) | copy-start | bytes 786436
  13.1 11.1 %collective-permute-start.10 = (bf16[4,2,128,128]{3,2,1,0:T(8,128)(2,1)S(1)}, bf16[4,2,128,128]{3,2,1,0:T(8,128)(2,1)S(1)}, u32[]{:S(2)}, u32[]{:S(2)}) collective-permute-start(bf16[4,2,128,128]{3,2,1,0:T(8,128)(2,1)S(1)} %pad_maximum_fusion.refs_1_), channel_id=1, source_target_pairs={{0,8},{8,16},{16,24},{24,0},{1,9},{9,17},{17,25},{25,1},{2,10},{10... | collective-permute-start | bytes 786440 | tf_op jit(solution)/shard_map/ppermute | solution.py:391
  14.7 7.4 %collective-permute-start.8 = (bf16[544,128]{1,0:T(8,128)(2,1)}, bf16[544,128]{1,0:T(8,128)(2,1)S(1)}, u32[]{:S(2)}, u32[]{:S(2)}) collective-permute-start(bf16[544,128]{1,0:T(8,128)(2,1)} %get-tuple-element.57), channel_id=1, source_target_pairs={{0,4},{2,6},{4,0},{6,2},{1,5},{3,7},{5,1},{7,3},{8,12},{10,14},{12... | collective-permute-start | bytes 417800 | tf_op jit(solution)/shard_map/ppermute | solution.py:387
  16.1 18.7 %collective-permute-start.15 = (bf16[4,2,128,128]{3,2,1,0:T(8,128)(2,1)S(1)}, bf16[4,2,128,128]{3,2,1,0:T(8,128)(2,1)S(1)}, u32[]{:S(2)}, u32[]{:S(2)}) collective-permute-start(bf16[4,2,128,128]{3,2,1,0:T(8,128)(2,1)S(1)} %pad_maximum_fusion.refs_1_), channel_id=1, source_target_pairs={{0,16},{8,24},{16,0},{24,8},{1,17},{9,25},{17,1},{25,9},{2,18},{10... | collective-permute-start | bytes 786440 | tf_op jit(solution)/shard_map/ppermute | solution.py:391
  22.0 23.0 %copy-start.16 = (bf16[544,128]{1,0:T(8,128)(2,1)}, bf16[544,128]{1,0:T(8,128)(2,1)S(1)}, u32[]{:S(2)}) copy-start(bf16[544,128]{1,0:T(8,128)(2,1)S(1)} %collective-permute-done.7.refs_7_) | copy-start | bytes 417796
  22.0 14.4 %collective-permute-start.4 = (bf16[2,512,128]{2,1,0:T(8,128)(2,1)}, bf16[2,512,128]{2,1,0:T(8,128)(2,1)S(1)}, u32[]{:S(2)}, u32[]{:S(2)}) collective-permute-start(bf16[2,512,128]{2,1,0:T(8,128)(2,1)} %get-tuple-element.52), channel_id=1, source_target_pairs={{0,2},{2,0},{4,6},{6,4},{1,3},{3,1},{5,7},{7,5},{8,10},{10,8},{12,... | collective-permute-start | bytes 786440 | tf_op jit(solution)/shard_map/ppermute | solution.py:387
  22.1 22.9 %copy-start.17 = (bf16[544,128]{1,0:T(8,128)(2,1)}, bf16[544,128]{1,0:T(8,128)(2,1)S(1)}, u32[]{:S(2)}) copy-start(bf16[544,128]{1,0:T(8,128)(2,1)S(1)} %collective-permute-done.8.refs_8_) | copy-start | bytes 417796
  22.1 7.3 %collective-permute-start.9 = (bf16[544,128]{1,0:T(8,128)(2,1)}, bf16[544,128]{1,0:T(8,128)(2,1)S(1)}, u32[]{:S(2)}, u32[]{:S(2)}) collective-permute-start(bf16[544,128]{1,0:T(8,128)(2,1)} %get-tuple-element.58), channel_id=1, source_target_pairs={{0,6},{2,4},{4,2},{6,0},{1,7},{3,5},{5,3},{7,1},{8,14},{10,12},{12... | collective-permute-start | bytes 417800 | tf_op jit(solution)/shard_map/ppermute | solution.py:387
  24.1 20.9 %copy-start.11 = (bf16[4,2,128,128]{3,2,1,0:T(8,128)(2,1)}, bf16[4,2,128,128]{3,2,1,0:T(8,128)(2,1)S(1)}, u32[]{:S(2)}) copy-start(bf16[4,2,128,128]{3,2,1,0:T(8,128)(2,1)S(1)} %collective-permute-done.10.refs_1_) | copy-start | bytes 786436
  24.1 13.0 %collective-permute-start.5 = (bf16[2,512,128]{2,1,0:T(8,128)(2,1)}, bf16[2,512,128]{2,1,0:T(8,128)(2,1)S(1)}, u32[]{:S(2)}, u32[]{:S(2)}) collective-permute-start(bf16[2,512,128]{2,1,0:T(8,128)(2,1)} %get-tuple-element.53), channel_id=1, source_target_pairs={{0,4},{2,6},{4,0},{6,2},{1,5},{3,7},{5,1},{7,3},{8,12},{10,14},{12... | collective-permute-start | bytes 786440 | tf_op jit(solution)/shard_map/ppermute | solution.py:387
  25.6 0.8 copy-start
  25.6 13.5 %collective-permute-start.6 = (bf16[2,512,128]{2,1,0:T(8,128)(2,1)}, bf16[2,512,128]{2,1,0:T(8,128)(2,1)S(1)}, u32[]{:S(2)}, u32[]{:S(2)}) collective-permute-start(bf16[2,512,128]{2,1,0:T(8,128)(2,1)} %get-tuple-element.54), channel_id=1, source_target_pairs={{0,6},{2,4},{4,2},{6,0},{1,7},{3,5},{5,3},{7,1},{8,14},{10,12},{12... | collective-permute-start | bytes 786440 | tf_op jit(solution)/shard_map/ppermute | solution.py:387
  29.4 15.6 %copy-start.18 = (bf16[544,128]{1,0:T(8,128)(2,1)}, bf16[544,128]{1,0:T(8,128)(2,1)S(1)}, u32[]{:S(2)}) copy-start(bf16[544,128]{1,0:T(8,128)(2,1)S(1)} %collective-permute-done.9.refs_9_) | copy-start | bytes 417796
  29.4 9.7 %collective-permute-start.12 = (bf16[544,128]{1,0:T(8,128)(2,1)}, bf16[544,128]{1,0:T(8,128)(2,1)S(1)}, u32[]{:S(2)}, u32[]{:S(2)}) collective-permute-start(bf16[544,128]{1,0:T(8,128)(2,1)} %get-tuple-element.62), channel_id=1, source_target_pairs={{0,2},{2,0},{4,6},{6,4},{1,3},{3,1},{5,7},{7,5},{8,10},{10,8},{12,... | collective-permute-start | bytes 417800 | tf_op jit(solution)/shard_map/ppermute | solution.py:387
  34.9 10.2 %copy-start.12 = (bf16[4,2,128,128]{3,2,1,0:T(8,128)(2,1)}, bf16[4,2,128,128]{3,2,1,0:T(8,128)(2,1)S(1)}, u32[]{:S(2)}) copy-start(bf16[4,2,128,128]{3,2,1,0:T(8,128)(2,1)S(1)} %collective-permute-done.15.refs_0_) | copy-start | bytes 786436
  34.9 8.3 %collective-permute-start.13 = (bf16[544,128]{1,0:T(8,128)(2,1)}, bf16[544,128]{1,0:T(8,128)(2,1)S(1)}, u32[]{:S(2)}, u32[]{:S(2)}) collective-permute-start(bf16[544,128]{1,0:T(8,128)(2,1)} %get-tuple-element.63), channel_id=1, source_target_pairs={{0,4},{2,6},{4,0},{6,2},{1,5},{3,7},{5,1},{7,3},{8,12},{10,14},{12... | collective-permute-start | bytes 417800 | tf_op jit(solution)/shard_map/ppermute | solution.py:387
  36.4 8.6 %copy-start.10 = (bf16[2,512,128]{2,1,0:T(8,128)(2,1)}, bf16[2,512,128]{2,1,0:T(8,128)(2,1)S(1)}, u32[]{:S(2)}) copy-start(bf16[2,512,128]{2,1,0:T(8,128)(2,1)S(1)} %collective-permute-done.4.refs_3_) | copy-start | bytes 786436
  36.4 8.6 %collective-permute-start.14 = (bf16[544,128]{1,0:T(8,128)(2,1)}, bf16[544,128]{1,0:T(8,128)(2,1)S(1)}, u32[]{:S(2)}, u32[]{:S(2)}) collective-permute-start(bf16[544,128]{1,0:T(8,128)(2,1)} %get-tuple-element.64), channel_id=1, source_target_pairs={{0,6},{2,4},{4,2},{6,0},{1,7},{3,5},{5,3},{7,1},{8,14},{10,12},{12... | collective-permute-start | bytes 417800 | tf_op jit(solution)/shard_map/ppermute | solution.py:387
  37.1 7.9 %copy-start.13 = (bf16[2,512,128]{2,1,0:T(8,128)(2,1)}, bf16[2,512,128]{2,1,0:T(8,128)(2,1)S(1)}, u32[]{:S(2)}) copy-start(bf16[2,512,128]{2,1,0:T(8,128)(2,1)S(1)} %collective-permute-done.5.refs_4_) | copy-start | bytes 786436
  37.1 26.0 %collective-permute-start.3 = (bf16[4,2,128,128]{3,2,1,0:T(8,128)(2,1)S(1)}, bf16[4,2,128,128]{3,2,1,0:T(8,128)(2,1)S(1)}, u32[]{:S(2)}, u32[]{:S(2)}) collective-permute-start(bf16[4,2,128,128]{3,2,1,0:T(8,128)(2,1)S(1)} %pad_maximum_fusion.refs_1_), channel_id=1, source_target_pairs={{0,24},{8,0},{16,8},{24,16},{1,25},{9,1},{17,9},{25,17},{2,26},{10... | collective-permute-start | bytes 786440 | tf_op jit(solution)/shard_map/ppermute | solution.py:391
  39.0 6.0 %copy-start.14 = (bf16[2,512,128]{2,1,0:T(8,128)(2,1)}, bf16[2,512,128]{2,1,0:T(8,128)(2,1)S(1)}, u32[]{:S(2)}) copy-start(bf16[2,512,128]{2,1,0:T(8,128)(2,1)S(1)} %collective-permute-done.6.refs_5_) | copy-start | bytes 786436
  39.0 6.0 %copy-start.19 = (bf16[544,128]{1,0:T(8,128)(2,1)}, bf16[544,128]{1,0:T(8,128)(2,1)S(1)}, u32[]{:S(2)}) copy-start(bf16[544,128]{1,0:T(8,128)(2,1)S(1)} %collective-permute-done.12.refs_11_) | copy-start | bytes 417796
  43.1 1.9 %copy-start.20 = (bf16[544,128]{1,0:T(8,128)(2,1)}, bf16[544,128]{1,0:T(8,128)(2,1)S(1)}, u32[]{:S(2)}) copy-start(bf16[544,128]{1,0:T(8,128)(2,1)S(1)} %collective-permute-done.13.refs_12_) | copy-start | bytes 417796
  45.0 0.7 copy-start.21
  60.6 20.7 %collective-permute-start.16 = (bf16[4,2,128,128]{3,2,1,0:T(8,128)(2,1)}, bf16[4,2,128,128]{3,2,1,0:T(8,128)(2,1)S(1)}, u32[]{:S(2)}, u32[]{:S(2)}) collective-permute-start(bf16[4,2,128,128]{3,2,1,0:T(8,128)(2,1)} %get-tuple-element.71), channel_id=1, source_target_pairs={{0,24},{8,0},{16,8},{24,16},{1,25},{9,1},{17,9},{25,17},{2,26},{10... | collective-permute-start | bytes 786440 | tf_op jit(solution)/shard_map/ppermute | solution.py:391
  62.7 18.9 %collective-permute-start.17 = (bf16[4,2,128,128]{3,2,1,0:T(8,128)(2,1)}, bf16[4,2,128,128]{3,2,1,0:T(8,128)(2,1)S(1)}, u32[]{:S(2)}, u32[]{:S(2)}) collective-permute-start(bf16[4,2,128,128]{3,2,1,0:T(8,128)(2,1)} %get-tuple-element.72), channel_id=1, source_target_pairs={{0,16},{8,24},{16,0},{24,8},{1,17},{9,25},{17,1},{25,9},{2,18},{10... | collective-permute-start | bytes 786440 | tf_op jit(solution)/shard_map/ppermute | solution.py:391
  63.1 0.7 copy-start.15
  81.6 10.4 %collective-permute-start.21 = (bf16[4,2,128,128]{3,2,1,0:T(8,128)(2,1)}, bf16[4,2,128,128]{3,2,1,0:T(8,128)(2,1)S(1)}, u32[]{:S(2)}, u32[]{:S(2)}) collective-permute-start(bf16[4,2,128,128]{3,2,1,0:T(8,128)(2,1)} %get-tuple-element.82), channel_id=1, source_target_pairs={{0,8},{8,16},{16,24},{24,0},{1,9},{9,17},{17,25},{25,1},{2,10},{10... | collective-permute-start | bytes 786440 | tf_op jit(solution)/shard_map/ppermute | solution.py:391
  82.1 13.2 %collective-permute-start.18 = (bf16[2,512,128]{2,1,0:T(8,128)(2,1)}, bf16[2,512,128]{2,1,0:T(8,128)(2,1)S(1)}, u32[]{:S(2)}, u32[]{:S(2)}) collective-permute-start(bf16[2,512,128]{2,1,0:T(8,128)(2,1)} %get-tuple-element.76), channel_id=1, source_target_pairs={{0,2},{2,0},{4,6},{6,4},{1,3},{3,1},{5,7},{7,5},{8,10},{10,8},{12,... | collective-permute-start | bytes 786440 | tf_op jit(solution)/shard_map/ppermute | solution.py:387
  82.1 13.6 %collective-permute-start.19 = (bf16[2,512,128]{2,1,0:T(8,128)(2,1)}, bf16[2,512,128]{2,1,0:T(8,128)(2,1)S(1)}, u32[]{:S(2)}, u32[]{:S(2)}) collective-permute-start(bf16[2,512,128]{2,1,0:T(8,128)(2,1)} %get-tuple-element.77), channel_id=1, source_target_pairs={{0,4},{2,6},{4,0},{6,2},{1,5},{3,7},{5,1},{7,3},{8,12},{10,14},{12... | collective-permute-start | bytes 786440 | tf_op jit(solution)/shard_map/ppermute | solution.py:387
  83.3 12.9 %collective-permute-start.20 = (bf16[2,512,128]{2,1,0:T(8,128)(2,1)}, bf16[2,512,128]{2,1,0:T(8,128)(2,1)S(1)}, u32[]{:S(2)}, u32[]{:S(2)}) collective-permute-start(bf16[2,512,128]{2,1,0:T(8,128)(2,1)} %get-tuple-element.78), channel_id=1, source_target_pairs={{0,6},{2,4},{4,2},{6,0},{1,7},{3,5},{5,3},{7,1},{8,14},{10,12},{12... | collective-permute-start | bytes 786440 | tf_op jit(solution)/shard_map/ppermute | solution.py:387
  93.8 4.4 %collective-permute-start.24 = (bf16[2,128,128]{2,1,0:T(8,128)(2,1)S(1)}, bf16[2,128,128]{2,1,0:T(8,128)(2,1)S(1)}, u32[]{:S(2)}, u32[]{:S(2)}) collective-permute-start(bf16[2,128,128]{2,1,0:T(8,128)(2,1)S(1)} %get-tuple-element.83), channel_id=1, source_target_pairs={{0,6},{2,4},{4,2},{6,0},{1,7},{3,5},{5,3},{7,1},{8,14},{10,12},{12... | collective-permute-start | bytes 196616 | tf_op jit(solution)/shard_map/ppermute | solution.py:387
  94.9 4.7 %collective-permute-start.23 = (bf16[2,128,128]{2,1,0:T(8,128)(2,1)S(1)}, bf16[2,128,128]{2,1,0:T(8,128)(2,1)S(1)}, u32[]{:S(2)}, u32[]{:S(2)}) collective-permute-start(bf16[2,128,128]{2,1,0:T(8,128)(2,1)S(1)} %get-tuple-element.84), channel_id=1, source_target_pairs={{0,4},{2,6},{4,0},{6,2},{1,5},{3,7},{5,1},{7,3},{8,12},{10,14},{12... | collective-permute-start | bytes 196616 | tf_op jit(solution)/shard_map/ppermute | solution.py:387
  95.3 4.3 %copy-start.2 = (bf16[2,512,128]{2,1,0:T(8,128)(2,1)}, bf16[2,512,128]{2,1,0:T(8,128)(2,1)S(1)}, u32[]{:S(2)}) copy-start(bf16[2,512,128]{2,1,0:T(8,128)(2,1)S(1)} %collective-permute-done.18.refs_1_) | copy-start | bytes 786436
  95.3 4.3 %collective-permute-start.22 = (bf16[2,128,128]{2,1,0:T(8,128)(2,1)S(1)}, bf16[2,128,128]{2,1,0:T(8,128)(2,1)S(1)}, u32[]{:S(2)}, u32[]{:S(2)}) collective-permute-start(bf16[2,128,128]{2,1,0:T(8,128)(2,1)S(1)} %get-tuple-element.85), channel_id=1, source_target_pairs={{0,2},{2,0},{4,6},{6,4},{1,3},{3,1},{5,7},{7,5},{8,10},{10,8},{12,... | collective-permute-start | bytes 196616 | tf_op jit(solution)/shard_map/ppermute | solution.py:387
  95.7 3.9 %copy-start.3 = (bf16[2,512,128]{2,1,0:T(8,128)(2,1)}, bf16[2,512,128]{2,1,0:T(8,128)(2,1)S(1)}, u32[]{:S(2)}) copy-start(bf16[2,512,128]{2,1,0:T(8,128)(2,1)S(1)} %collective-permute-done.19.refs_2_) | copy-start | bytes 786436
  96.3 3.4 %copy-start.4 = (bf16[2,512,128]{2,1,0:T(8,128)(2,1)}, bf16[2,512,128]{2,1,0:T(8,128)(2,1)S(1)}, u32[]{:S(2)}) copy-start(bf16[2,512,128]{2,1,0:T(8,128)(2,1)S(1)} %collective-permute-done.20.refs_3_) | copy-start | bytes 786436
  98.2 1.5 %copy-start.6 = (bf16[2,128,128]{2,1,0:T(8,128)(2,1)}, bf16[2,128,128]{2,1,0:T(8,128)(2,1)S(1)}, u32[]{:S(2)}) copy-start(bf16[2,128,128]{2,1,0:T(8,128)(2,1)S(1)} %collective-permute-done.24.refs_7_) | copy-start | bytes 196612
  99.6 0.6 copy-start.7
  99.6 0.6 copy-start.8
